TPU v7x, 32 devices: a whole 2x2x4 slice. The times are simulated.
32 devices in a mesh: fsdp: 8 (over z, y), dp: 4 (over x, core).
Axes of the slice: x: 2, y: 2, z: 4, core: 2. Of those that a mesh axis runs over, the one named last changes fastest.
Arguments:
- images: bfloat16 [64, 14, 14, 2048], P(('fsdp', 'dp')), may hold values from -24 to 24
- valid: int32 [64], P(('fsdp', 'dp')), may hold values from 0 to 1, as said below
- cotangent: bfloat16 [64, 14, 14, 2048], P(('fsdp', 'dp')), may hold values from -24 to 24
- w_reduce: bfloat16 [2048, 1024], P('fsdp'), may hold values from -0.125 to 0.125
- gain_one: bfloat16 [1024], P('fsdp'), may hold values from 0.25 to 1.75
- shift_one: bfloat16 [1024], P('fsdp'), may hold values from -3 to 3
- w_group: bfloat16 [288, 1024], P('fsdp'), may hold values from -0.375 to 0.375
- gain_two: bfloat16 [1024], P('fsdp'), may hold values from 0.25 to 1.75
- shift_two: bfloat16 [1024], P('fsdp'), may hold values from -3 to 3
- w_expand: bfloat16 [1024, 2048], P('fsdp'), may hold values from -0.1875 to 0.1875
- gain_three: bfloat16 [2048], P('fsdp'), may hold values from 0.25 to 1.75
- shift_three: bfloat16 [2048], P('fsdp'), may hold values from -3 to 3
Outputs:
- output: bfloat16 [64, 14, 14, 2048], P(('fsdp', 'dp'))
- grad_input: bfloat16 [64, 14, 14, 2048], P(('fsdp', 'dp'))
- grad_w_reduce: float32 [2048, 1024], P('fsdp')
- grad_w_group: float32 [288, 1024], P('fsdp')
- grad_w_expand: float32 [1024, 2048], P('fsdp')
- grad_gain_one: float32 [1024], P('fsdp')
- grad_shift_one: float32 [1024], P('fsdp')
- grad_gain_two: float32 [1024], P('fsdp')
- grad_shift_two: float32 [1024], P('fsdp')
- grad_gain_three: float32 [2048], P('fsdp')
- grad_shift_three: float32 [2048], P('fsdp')
Inputs may be any that keep to these rules, and one draw needn't show every extreme that they name: At least one slot of all is valid; each slot is valid with probability 9/10.
All inputs are finite; a program needn't handle non-finite values.
Results may differ from a plain program's by a relative error of at most 0.0075.
Values may be sent and summed in bfloat16 or wider, within the bound.
No kernel may reach another device: no remote copies, remote signals or barrier semaphores. Data moves between devices by JAX's collectives and lax.ppermute only.
A program may use at most 192 MiB of HBM per device.

v0:
```python
import functools

import jax
import jax.numpy as jnp
from jax import lax
from jax.experimental import pallas as pl
from jax.experimental.pallas import tpu as pltpu
from jax.sharding import Mesh
from jax.sharding import PartitionSpec as P

GROUPS = 32
TAPS = 9
LINE = 16
BLOCK = 256
epsilon = 1e-05
BF16, F32 = jnp.bfloat16, jnp.float32
SWAP = [(0, 1), (1, 0)]
NN, NT = ((1,), (0,)), ((1,), (1,))
CHIPS = ("fsdp", "x")


def sigmoid(values):
    return 0.5 * jnp.tanh(0.5 * values) + 0.5


def dsilu(values):
    sigma = sigmoid(values)
    return sigma * (1.0 + values * (1.0 - sigma))


def dot(a, b, contract=NN):
    return lax.dot_general(a, b, (contract, ((), ())), preferred_element_type=F32)


def after(values, *others):
    return lax.optimization_barrier((values,) + others)[0]


def together(*values):
    return lax.optimization_barrier(values)


def shape(dims, dtype):
    return jax.ShapeDtypeStruct(dims, dtype)


def call(kernel, outs, args, scalars=0, scratch=(), vmem=8, name=None, flops=0):
    vm = pl.BlockSpec(memory_space=pltpu.VMEM)
    sm = pl.BlockSpec(memory_space=pltpu.SMEM)
    return pl.pallas_call(
        kernel,
        out_shape=outs,
        in_specs=[sm] * scalars + [vm] * (len(args) - scalars),
        out_specs=[vm] * len(outs),
        scratch_shapes=list(scratch),
        compiler_params=pltpu.CompilerParams(vmem_limit_bytes=vmem << 20),
        cost_estimate=pl.CostEstimate(flops=flops, bytes_accessed=1 << 20, transcendentals=0),
        name=name,
    )(*args)


def moments(total, pixels):
    mean = total[0:1, :] / pixels
    inverse = lax.rsqrt(total[1:2, :] / pixels - mean * mean + epsilon)
    return mean, inverse


def line_mask(columns, side):
    return lax.broadcasted_iota(jnp.int32, (LINE, columns), 0) < side


def column_sums(values):
    return jnp.sum(values, axis=0, keepdims=True)


def line_at(step):
    return pl.ds(pl.multiple_of(step * LINE, LINE), LINE)


def fold(values):
    return values[0:8] + values[8:16]


def part_at(part, half, at=0, length=None):
    core = lax.axis_index("core")
    side = core if part == 0 else 1 - core
    length = half if length is None else length
    return pl.ds(pl.multiple_of(side * half + at, 128), length)


def block_owner(slot):
    position = lax.axis_index("fsdp")
    way = 1 - 2 * lax.axis_index("x")
    step = (0, -way, way, 2)[slot % 4]
    owner = lax.rem(position + 2 * step + 8, 8)
    return owner if slot < 4 else owner + 1 - 2 * lax.rem(owner, 2)


def rows_of(owner, depth):
    return pl.ds(pl.multiple_of(owner * depth, 16), depth)


def pack_kernel(side, valid, weight, group, vectors, out, mask):
    depth, half = weight.shape[0], out.shape[1]
    shard, extra = group.shape[0], out.shape[0] - weight.shape[0]
    columns = part_at(0, half)
    out[0:depth, :] = weight[:, columns]
    below = [group[:, columns].astype(F32), vectors[:, columns].astype(F32)]
    if extra > shard + 1:
        below.append(jnp.zeros((extra - shard - 1, half), F32))
    out[depth : depth + extra, :] = jnp.concatenate(below, axis=0).astype(BF16)
    images = valid.shape[0]
    rows = mask.shape[0] // images
    inside = lax.broadcasted_iota(jnp.int32, (rows, 1), 0) % LINE < side
    for image in range(images):
        mask[image * rows : (image + 1) * rows, :] = jnp.where(inside, valid[image].astype(F32), 0.0)


def reduce_kernel(slots, depth, side, valid, mask, x, *refs):
    weights, (red, stats) = refs[: 2 * slots], refs[2 * slots :]
    half = weights[0].shape[1]
    for part in range(2):
        for at in range(0, half, BLOCK):
            total = None
            for slot in range(slots):
                if slots == 1:
                    piece = x[...]
                else:
                    piece = x[:, pl.ds(pl.multiple_of(block_owner(slot) * depth, 128), depth)]
                term = dot(piece, weights[2 * slot + part][0:depth, at : at + BLOCK])
                total = term if total is None else total + term
            columns = part_at(part, half, at, BLOCK)
            red[:, columns] = total
            masked = total * mask[...]
            stats[0:1, columns] = column_sums(masked)
            stats[1:2, columns] = column_sums(masked * total)
    pixels = valid[0].astype(F32)
    for image in range(1, valid.shape[0]):
        pixels = pixels + valid[image].astype(F32)
    stats[2:3, :] = jnp.full((1, stats.shape[1]), 1.0, F32) * (pixels * (side * side))


def spread_kernel(slots, depth, *refs):
    blocks, (wide, inner_vectors, outer_vectors, held, rows) = refs[: 2 * slots], refs[2 * slots :]
    extra, half = held.shape[1], held.shape[2] // 2
    for slot in range(slots):
        for part in range(2):
            held[block_owner(slot), :, part_at(part, half)] = blocks[2 * slot + part][depth : depth + extra, :].astype(F32)
    shard = rows.shape[0] // slots
    per, outer = inner_vectors.shape[1] // slots, outer_vectors.shape[1] // slots
    for owner in range(slots):
        rows[owner * shard : (owner + 1) * shard, :] = held[owner, 0:shard, :]
        for row in range(4):
            inner_vectors[row : row + 1, owner * per : (owner + 1) * per] = held[
                owner, shard : shard + 1, row * per : (row + 1) * per
            ]
        for row in range(2):
            outer_vectors[row : row + 1, owner * outer : (owner + 1) * outer] = held[
                owner, shard : shard + 1, 4 * per + row * outer : 4 * per + (row + 1) * outer
            ]
    widen(rows, wide)


def widen_kernel(weight, wide, rows):
    rows[...] = weight[...].astype(F32)
    widen(rows, wide)


def widen(weight, wide):
    taps, blocks = wide.shape[:2]
    inner = weight.shape[0] // taps
    row = lax.broadcasted_iota(jnp.int32, (BLOCK, BLOCK), 0) // inner
    column = lax.broadcasted_iota(jnp.int32, (BLOCK, BLOCK), 1) // inner
    own = row == column
    for tap in range(taps):
        for block in range(blocks):
            piece = weight[tap * inner : (tap + 1) * inner, block * BLOCK : (block + 1) * BLOCK]
            tall = jnp.concatenate([piece] * (BLOCK // inner), axis=0)
            wide[tap, block] = jnp.where(own, tall, 0.0).astype(BF16)


def fill_pads(pads, image, line, values):
    rows = pl.ds(pl.multiple_of((line + 1) * LINE, LINE), LINE)
    pads[0, image, rows, :] = pltpu.roll(values, 1, 0).astype(BF16)
    pads[1, image, rows, :] = values.astype(BF16)
    pads[2, image, rows, :] = pltpu.roll(values, LINE - 1, 0).astype(BF16)


def clear_pads(pads):
    images, rows, columns = pads.shape[1:]
    zeros = jnp.zeros((3, images, LINE, columns), BF16)
    pads[:, :, 0:LINE, :] = zeros
    pads[:, :, rows - LINE : rows, :] = zeros


def convolve(pads, wide, image, block, rows, turned=False):
    columns = slice(block * BLOCK, (block + 1) * BLOCK)
    value = None
    for tap in range(TAPS):
        top, left = divmod(TAPS - 1 - tap if turned else tap, 3)
        piece = pads[left, image, top * LINE : top * LINE + rows, columns]
        term = dot(piece, wide[tap, block], NT if turned else NN)
        value = term if value is None else value + term
    return value


def group_kernel(side, mask, total, vectors, red, wide, pads, grouped, stats):
    images, padded, width = pads.shape[1:]
    rows = side * LINE
    mean, inverse = moments(total, total[2:3, :])
    scale, bias = inverse * vectors[0:1, :], vectors[1:2, :]
    clear_pads(pads)
    inside = line_mask(width, side)

    def body(step, carry):
        normal = (red[line_at(step), :] - mean) * scale + bias
        fill_pads(pads, step // side, step % side, jnp.where(inside, normal * sigmoid(normal), 0.0))
        return carry

    lax.fori_loop(0, images * side, body, 0)
    for block in range(width // BLOCK):
        columns = slice(block * BLOCK, (block + 1) * BLOCK)
        sums = [0.0, 0.0]
        for image in range(images):
            at = slice(image * rows, (image + 1) * rows)
            value = convolve(pads, wide, image, block, rows)
            grouped[at, columns] = value
            masked = value * mask[at, :]
            sums = [sums[0] + column_sums(masked), sums[1] + column_sums(masked * value)]
        stats[0:1, columns] = sums[0]
        stats[1:2, columns] = sums[1]


def expand_kernel(side, mask, total, first, vectors, grouped, mine, other, act, expanded, stats):
    rows, width = grouped.shape
    mean, inverse = moments(total, first[2:3, :])
    scale, bias = inverse * vectors[2:3, :], vectors[3:4, :]
    inside = line_mask(width, side)

    def body(step, carry):
        at = line_at(step)
        normal = (grouped[at, :] - mean) * scale + bias
        act[at, :] = jnp.where(inside, normal * sigmoid(normal), 0.0).astype(BF16)
        return carry

    lax.fori_loop(0, rows // LINE, body, 0)
    half = mine.shape[1]
    for part, weight in enumerate((mine, other)):
        for at in range(0, half, BLOCK):
            value = dot(act[...], weight[:, at : at + BLOCK])
            columns = part_at(part, half, at, BLOCK)
            expanded[:, columns] = value
            masked = value * mask[...]
            stats[0:1, columns] = column_sums(masked)
            stats[1:2, columns] = column_sums(masked * value)


def output_kernel(side, valid, total, first, vectors, expanded, x, cotangent, output, grad, stats):
    rows, channels = expanded.shape
    mean, inverse = moments(total, first[2:3, 0:1])
    gains, bias = vectors[0:1, :], vectors[1:2, :]
    zero = jnp.zeros((8, channels), F32)

    def body(step, carry):
        image, line = step // side, step % side
        at = line_at(step)
        keep = valid[image].astype(F32)
        normed = (expanded[at, :] - mean) * inverse
        summed = normed * gains + bias + x[at, :].astype(F32)
        sigma = sigmoid(summed)
        output[image, line] = (summed * sigma * keep).astype(BF16)[0:side]
        here = cotangent[at, :].astype(F32) * keep * (sigma * (1.0 + summed * (1.0 - sigma)))
        grad[at, :] = here
        return carry[0] + fold(here), carry[1] + fold(here * normed)

    one, two = lax.fori_loop(0, rows // LINE, body, (zero, zero))
    stats[0:1, :] = column_sums(one)
    stats[1:2, :] = column_sums(two)


def back_expand_kernel(
    mask, total, sums, first, vectors, total_two, vectors_two, grad, expanded, grouped, mine, other, flat, dz, stats
):
    rows, width = grouped.shape
    pixels = first[2:3, 0:1]
    mean, inverse = moments(total, pixels)
    scale = inverse * vectors[0:1, :]
    shifted, scaled = sums[0:1, :] / pixels, sums[1:2, :] / pixels

    def body(step, carry):
        at = line_at(step)
        normed = (expanded[at, :] - mean) * inverse
        flat[at, :] = (scale * (grad[at, :] - mask[at, :] * (shifted + normed * scaled))).astype(BF16)
        return carry

    lax.fori_loop(0, rows // LINE, body, 0)
    half = mine.shape[1]
    for at in range(0, width, BLOCK):
        value = None
        for part, weight in enumerate((mine, other)):
            term = dot(flat[:, part_at(part, half)], weight[at : at + BLOCK, :], NT)
            value = term if value is None else value + term
        dz[:, at : at + BLOCK] = value
    mean_two, inverse_two = moments(total_two, first[2:3, :])
    gains, bias = vectors_two[2:3, :], vectors_two[3:4, :]
    zero = jnp.zeros((8, width), F32)

    def tail(step, carry):
        at = line_at(step)
        normed = (grouped[at, :] - mean_two) * inverse_two
        here = dz[at, :] * dsilu(normed * gains + bias)
        dz[at, :] = here
        return carry[0] + fold(here), carry[1] + fold(here * normed)

    one, two = lax.fori_loop(0, rows // LINE, tail, (zero, zero))
    stats[0:1, :] = column_sums(one)
    stats[1:2, :] = column_sums(two)


def weight_expand_kernel(act, flat, send, keep):
    half = send.shape[1]
    turned = act[...].T
    for part, out in ((1, send), (0, keep)):
        for at in range(0, half, BLOCK):
            out[:, at : at + BLOCK] = dot(turned, flat[:, part_at(part, half, at, BLOCK)]).astype(BF16)


def back_group_kernel(
    side, mask, total, sums, first, vectors, dz, grouped, red, wide, flat, dz_one, stats, pads
):
    images, padded, width = pads.shape[1:]
    rows = side * LINE
    pixels = first[2:3, :]
    mean, inverse = moments(total, pixels)
    scale = inverse * vectors[2:3, :]
    shifted, scaled = sums[0:1, :] / pixels, sums[1:2, :] / pixels
    clear_pads(pads)

    def body(step, carry):
        at = line_at(step)
        normed = (grouped[at, :] - mean) * inverse
        value = scale * (dz[at, :] - mask[at, :] * (shifted + normed * scaled))
        flat[at, :] = value.astype(BF16)
        fill_pads(pads, step // side, step % side, value)
        return carry

    lax.fori_loop(0, images * side, body, 0)
    for block in range(width // BLOCK):
        columns = slice(block * BLOCK, (block + 1) * BLOCK)
        for image in range(images):
            dz_one[image * rows : (image + 1) * rows, columns] = convolve(pads, wide, image, block, rows, True)
    mean_one, inverse_one = moments(first, pixels)
    gains, bias = vectors[0:1, :], vectors[1:2, :]
    inside = line_mask(width, side)
    zero = jnp.zeros((8, width), F32)

    def tail(step, carry):
        at = line_at(step)
        normed = (red[at, :] - mean_one) * inverse_one
        here = jnp.where(inside, dz_one[at, :] * dsilu(normed * gains + bias), 0.0)
        dz_one[at, :] = here
        return carry[0] + fold(here), carry[1] + fold(here * normed)

    one, two = lax.fori_loop(0, images * side, tail, (zero, zero))
    stats[0:1, :] = column_sums(one)
    stats[1:2, :] = column_sums(two)


def weight_group_kernel(side, pads, flat, out, rows_held):
    images, padded, width = pads.shape[1:]
    rows = side * LINE
    inner = width // GROUPS
    row = lax.broadcasted_iota(jnp.int32, (BLOCK, BLOCK), 0) // inner
    column = lax.broadcasted_iota(jnp.int32, (BLOCK, BLOCK), 1) // inner
    own = row == column
    lanes = 128 // inner
    pick_row = lax.broadcasted_iota(jnp.int32, (BLOCK, 128), 0) % inner
    pick_lane = lax.broadcasted_iota(jnp.int32, (BLOCK, 128), 1)
    picks = [
        jnp.where(pick_lane == pick_row + inner * lane, 1.0, 0.0).astype(BF16) for lane in range(lanes)
    ]
    for block in range(width // BLOCK):
        columns = slice(block * BLOCK, (block + 1) * BLOCK)
        turned = [flat[image * rows : (image + 1) * rows, columns].T for image in range(images)]
        for begin in range(0, TAPS, lanes):
            packed = None
            taps = range(begin, min(begin + lanes, TAPS))
            for tap in taps:
                top, left = divmod(tap, 3)
                value = None
                for image in range(images):
                    term = dot(turned[image], pads[left, image, top * LINE : top * LINE + rows, columns])
                    value = term if value is None else value + term
                term = dot(jnp.where(own, value, 0.0).astype(BF16), picks[tap - begin])
                packed = term if packed is None else packed + term
            length = len(taps) * inner
            rows_held[begin * inner : begin * inner + length, columns] = packed.T[0:length]
    owners, extra = out.shape[:2]
    shard = TAPS * inner // owners
    for owner in range(owners):
        out[owner] = jnp.concatenate(
            [rows_held[owner * shard : (owner + 1) * shard, :], jnp.zeros((extra - shard, width), F32)], axis=0
        ).astype(BF16)


def back_reduce_kernel(blocks, small, mask, first, sums, vectors, dz, red, turned, group, flat, send):
    rows, width = red.shape
    pixels = first[2:3, :]
    mean, inverse = moments(first, pixels)
    scale = inverse * vectors[0:1, :]
    shifted, scaled = sums[0:1, :] / pixels, sums[1:2, :] / pixels

    def body(step, carry):
        at = line_at(step)
        normed = (red[at, :] - mean) * inverse
        flat[at, :] = (scale * (dz[at, :] - mask[at, :] * (shifted + normed * scaled))).astype(BF16)
        return carry

    lax.fori_loop(0, rows // LINE, body, 0)
    tall, half = send.shape[1:]
    depth = tall - group.shape[1]
    columns = part_at(1, half)
    for block in range(blocks):
        owner = block_owner(block) if small else block
        send[block, 0:depth, :] = dot(turned[rows_of(owner, depth), :], flat[:, columns]).astype(BF16)
        send[block, depth:tall, :] = group[owner, :, columns]


def block_sum_kernel(small, places, turned, group, flat, near, *refs):
    arrived, outs = refs[: len(refs) - len(places)], refs[len(refs) - len(places) :]
    tall, half = near.shape[1:]
    depth = tall - group.shape[1]
    columns = part_at(0, half)
    for out, (block, chosen) in zip(outs, places):
        owner = block_owner(block) if small else block
        value = dot(turned[rows_of(owner, depth), :], flat[:, columns]) + near[block, 0:depth, :].astype(F32)
        more = group[owner, :, columns].astype(F32) + near[block, depth:tall, :].astype(F32)
        for other in chosen:
            value = value + arrived[other][0:depth, :].astype(F32)
            more = more + arrived[other][depth:tall, :].astype(F32)
        out[0:depth, :] = value.astype(BF16)
        out[depth:tall, :] = more.astype(BF16)


def expand_sum_kernel(places, keep, near, *refs):
    arrived, outs = refs[: len(refs) - len(places)], refs[len(refs) - len(places) :]
    depth = outs[0].shape[0]
    for out, (block, chosen) in zip(outs, places):
        rows = rows_of(block_owner(block), depth)
        value = keep[rows, :].astype(F32) + near[rows, :].astype(F32)
        for other in chosen:
            value = value + arrived[other][...].astype(F32)
        out[...] = value.astype(BF16)


def add_kernel(a, b, out):
    out[...] = (a[...].astype(F32) + b[...].astype(F32)).astype(out.dtype)


def join_kernel(mine, other, *outs):
    half = mine.shape[1]
    at = 0
    for out in outs:
        rows = out.shape[0]
        for part, values in enumerate((mine, other)):
            out[:, part_at(part, half)] = values[at : at + rows, :]
        at += -(-rows // 16) * 16


def pin_kernel(values, out):
    pass


def own_kernel(*refs):
    number = len(refs) // 3
    position = lax.axis_index("fsdp")
    for at, total in enumerate(refs[:number]):
        for row, out in ((1, refs[number + 2 * at]), (0, refs[number + 2 * at + 1])):
            length = out.shape[1]
            out[...] = total[row : row + 1, pl.ds(pl.multiple_of(position * length, 128), length)]


def grad_input_kernel(slots, depth, side, flat, grad, *refs):
    weights, (out, held) = refs[: 2 * slots], refs[2 * slots :]
    half = weights[0].shape[1]
    for slot in range(slots):
        columns = pl.ds(pl.multiple_of(block_owner(slot) * depth, 128), depth) if slots > 1 else slice(None)
        value = grad[:, columns]
        for part in range(2):
            value = value + dot(flat[:, part_at(part, half)], weights[2 * slot + part][0:depth, :], NT)
        held[:, columns] = value

    def body(step, carry):
        out[step // side, step % side] = held[line_at(step), :].astype(BF16)[0:side]
        return carry

    lax.fori_loop(0, flat.shape[0] // LINE, body, 0)


def pinned(values):
    anywhere = pl.BlockSpec(memory_space=pl.ANY)
    values = values.transpose(1, 2, 0, 3)
    values = pl.pallas_call(
        pin_kernel, out_shape=shape(values.shape, values.dtype), in_specs=[anywhere], out_specs=anywhere,
        input_output_aliases={0: 0}, compiler_params=pltpu.CompilerParams(vmem_limit_bytes=1 << 20), name="pin",
    )(values)
    return values.transpose(2, 0, 1, 3)


def swap_core(values):
    return lax.ppermute(values, "core", SWAP)


def swap_x(values):
    if lax.axis_size("x") == 2:
        return lax.ppermute(values, "x", SWAP)
    return (lax.psum(values.astype(F32), "x") - values.astype(F32)).astype(values.dtype)


def sum_chips(values, flips):
    got = [lax.ppermute(values, CHIPS, [(at, at ^ flip) for at in range(16)]) for flip in flips]
    for other in got:
        values = values + other
    return values


def along(values, way):
    pairs = [(f * 2 + x, (f + 2 * way * (1 - 2 * x)) % 8 * 2 + x) for f in range(8) for x in range(2)]
    return lax.ppermute(values, CHIPS, pairs)


def across(values):
    return lax.ppermute(values, "fsdp", [(f, f ^ 1) for f in range(8)])


def gather_blocks(own, early, late):
    first = along(own, 1)
    other = across(own)
    first, other, *early = together(first, other, *early)
    passed, second, first_other = swap_x(first), along(first, 1), across(first)
    second, passed, first_other, *late = together(second, passed, first_other, *late)
    passed_other, second_other = swap_x(first_other), across(second)
    return [own, first, passed, second, other, first_other, passed_other, second_other], early, late


def halves(values, core):
    half = values.shape[1] // 2
    return lax.dynamic_slice_in_dim(values, core * half, half, 1)


def per_device(
    images,
    valid,
    cotangent,
    w_reduce,
    gain_one,
    shift_one,
    w_group,
    gain_two,
    shift_two,
    w_expand,
    gain_three,
    shift_three,
):
    count, side, _, channels = images.shape
    width = w_reduce.shape[1]
    inner = width // GROUPS
    size = lax.axis_size("fsdp")
    small = size == 8 and lax.axis_size("x") == 2
    position, core = lax.axis_index("fsdp"), lax.axis_index("core")
    rows = count * side * LINE
    per, outer, shard, depth = gain_one.shape[0], gain_three.shape[0], w_group.shape[0], w_reduce.shape[0]
    extra = -(-(shard + 1) // 16) * 16
    half = width // 2

    def start_sum(values):
        return values + swap_core(values) if small else lax.psum(values, ("fsdp", "x", "core"))

    def plane_sum(values):
        return sum_chips(values, (1, 2, 3)) if small else values

    def line_sum(values):
        return sum_chips(values, (4, 8, 12)) if small else values

    def everywhere(values):
        return line_sum(plane_sum(start_sum(values)))

    def padded(values):
        return jnp.pad(values, ((0, 0), (0, 0), (0, LINE - side), (0, 0))).reshape(rows, channels)

    x, cot = padded(images), padded(cotangent)

    vectors, at = jnp.zeros((width,), BF16), 0
    for vector in (gain_one, shift_one, gain_two, shift_two, gain_three, shift_three):
        vectors = vectors + jnp.pad(vector, (at, width - at - vector.size))
        at += vector.size
    own, mask = call(
        functools.partial(pack_kernel, side),
        [shape((depth + extra, half), BF16), shape((rows, 1), F32)],
        [valid, w_reduce, w_group, vectors.reshape(1, width)], scalars=1, name="pack",
    )
    wide_shape = shape((TAPS, width // BLOCK, BLOCK, BLOCK), BF16)
    expand_half = halves(w_expand, core)
    if small:
        weights = []
        blocks, (x, expand_half), (turned,) = gather_blocks(own, (x, expand_half), (x.T,))
        for block in blocks:
            weights += [block, swap_core(block)]
        slots, slot_depth = size, depth
    else:
        whole = lax.all_gather(own, "fsdp", axis=0, tiled=False)
        block = whole[:, :depth].reshape(channels, half)
        weights = [block, swap_core(block)]
        slots, slot_depth, turned = 1, channels, x.T
    expand_mine = lax.all_gather(expand_half, "fsdp", axis=0, tiled=True)

    red, part = call(
        functools.partial(reduce_kernel, slots, slot_depth, side),
        [shape((rows, width), F32), shape((3, width), F32)],
        [valid, mask, x] + weights, scalars=1, name="reduce", flops=2 * rows * width * channels,
    )
    if small:
        wide, inner_vectors, outer_vectors = call(
            functools.partial(spread_kernel, slots, depth),
            [wide_shape, shape((4, width), F32), shape((2, channels), F32)],
            weights,
            scratch=[pltpu.VMEM((size, extra, width), F32), pltpu.VMEM((size * shard, width), F32)],
            name="spread", flops=1 << 28,
        )
    else:
        mine = whole[:, depth:]
        other = swap_core(mine)
        packed = jnp.concatenate([jnp.where(core == 0, mine, other), jnp.where(core == 0, other, mine)], axis=2)
        (wide,) = call(
            widen_kernel, [wide_shape], [packed[:, :shard].reshape(size * shard, width)],
            scratch=[pltpu.VMEM((size * shard, width), F32)], name="widen",
        )
        line = packed[:, shard].astype(F32)
        inner_vectors = line[:, : 4 * per].reshape(size, 4, per).transpose(1, 0, 2).reshape(4, width)
        outer_vectors = line[:, 4 * per : 4 * per + 2 * outer].reshape(size, 2, outer)
        outer_vectors = outer_vectors.transpose(1, 0, 2).reshape(2, channels)
    middle = plane_sum(start_sum(part))
    middle, wide, inner_vectors, outer_vectors = together(middle, wide, inner_vectors, outer_vectors)
    first = line_sum(middle)
    pad_shape = (3, count, (side + 2) * LINE, width)
    pads, grouped, part = call(
        functools.partial(group_kernel, side),
        [shape(pad_shape, BF16), shape((rows, width), F32), shape((2, width), F32)],
        [mask, first, inner_vectors, red, wide],
        name="group", flops=2 * TAPS * rows * width * BLOCK,
    )
    middle = plane_sum(start_sum(part))
    expand_other = swap_core(after(expand_mine, middle))
    total_two = line_sum(middle)
    act_two, expanded, part = call(
        functools.partial(expand_kernel, side),
        [shape((rows, width), BF16), shape((rows, channels), F32), shape((2, channels), F32)],
        [mask, total_two, first, inner_vectors, grouped, expand_mine, expand_other],
        name="expand", flops=2 * rows * width * channels,
    )
    total_three = everywhere(part)
    output, grad_summed, part = call(
        functools.partial(output_kernel, side),
        [shape(images.shape, BF16), shape((rows, channels), F32), shape((2, channels), F32)],
        [valid, total_three, first, outer_vectors, expanded, x, cot], scalars=1, name="output",
    )

    sums_three = everywhere(part)
    flat_three, dz_two, part = call(
        back_expand_kernel,
        [shape((rows, channels), BF16), shape((rows, width), F32), shape((2, width), F32)],
        [mask, total_three, sums_three, first, outer_vectors, total_two, inner_vectors, grad_summed, expanded, grouped,
         expand_mine, expand_other],
        name="back_expand", flops=2 * rows * width * channels,
    )
    middle = start_sum(part)
    act_two = after(act_two, middle)
    sums_two = line_sum(plane_sum(middle))
    send, keep = call(
        weight_expand_kernel,
        [shape((width, channels // 2), BF16)] * 2,
        [act_two, flat_three], name="weight_expand", flops=2 * rows * width * channels,
    )
    near_expand = swap_core(send)

    def expand_sums(places, arrived=()):
        return call(
            functools.partial(expand_sum_kernel, places),
            [shape((w_expand.shape[0], channels // 2), BF16)] * len(places),
            [keep, near_expand] + list(arrived), name="expand_sum",
        )

    if small:
        passed_other, second_other = expand_sums(((6, ()), (7, ())))
        sums_two, passed_other, second_other = together(sums_two, passed_other, second_other)
        got_expand = [swap_x(passed_other), across(second_other)]
    else:
        (chip,) = call(add_kernel, [shape(keep.shape, BF16)], [keep, near_expand], name="add")
        own_expand = lax.psum_scatter(chip, "fsdp", scatter_dimension=0, tiled=True)

    flat_two, dz_one, part = call(
        functools.partial(back_group_kernel, side),
        [shape((rows, width), BF16), shape((rows, width), F32), shape((2, width), F32)],
        [mask, total_two, sums_two, first, inner_vectors, dz_two, grouped, red, wide],
        scratch=[pltpu.VMEM(pad_shape, BF16)], name="back_group", flops=2 * TAPS * rows * width * BLOCK,
    )
    if small:
        first_other, passed, second = expand_sums(((5, (0,)), (2, ()), (3, (1,))), got_expand)
        part, first_other, passed, second = together(part, first_other, passed, second)
        got_expand = [swap_x(passed), along(second, -1), across(first_other)]
    sums_one = everywhere(part)
    if small:
        first_own, other = expand_sums(((1, (0, 1, 2)), (4, ())), got_expand)
        sums_one, first_own, other = together(sums_one, first_own, other)
        got_expand = [along(first_own, -1), across(other)]
    (group_term,) = call(
        functools.partial(weight_group_kernel, side),
        [shape((size, extra, width), BF16)],
        [pads, flat_two], scratch=[pltpu.VMEM((TAPS * inner, width), F32)], name="weight_group", flops=2 * TAPS * rows * width * BLOCK,
    )
    tall = depth + extra
    flat_one, send = call(
        functools.partial(back_reduce_kernel, size, small),
        [shape((rows, width), BF16), shape((size, tall, half), BF16)],
        [mask, first, sums_one, inner_vectors, dz_one, red, turned, group_term],
        name="back_reduce", flops=rows * width * channels,
    )
    near = swap_core(send)

    def sums(places, arrived=()):
        return call(
            functools.partial(block_sum_kernel, small, places),
            [shape((tall, half), BF16)] * len(places),
            [turned, group_term, flat_one, near] + list(arrived),
            name="block_sum", flops=2 * rows * depth * half * len(places),
        )

    def back_input(flat):
        (out,) = call(
            functools.partial(grad_input_kernel, slots, slot_depth, side),
            [shape(images.shape, BF16)],
            [flat, grad_summed] + weights,
            scratch=[pltpu.VMEM((rows, channels), F32)], name="grad_input", flops=2 * rows * width * channels,
        )
        return out

    def own_shards(*totals):
        if not small:
            cut = []
            for total, length in zip(totals, (per, per, outer)):
                cut += [lax.dynamic_slice_in_dim(total[row], position * length, length, 0) for row in (1, 0)]
            return cut
        lengths = (per, per, per, per, outer, outer)
        return [out.reshape(-1) for out in call(own_kernel, [shape((1, n), F32) for n in lengths], totals, name="own")]

    if small:
        passed_other, second_other = sums(((6, ()), (7, ())))
        got_x, got_y = swap_x(passed_other), across(second_other)
        grad_input = back_input(after(flat_one, second_other))
        (own_expand,) = expand_sums(((0, (0, 1)),), got_expand)
        got_x, grad_input, own_expand = together(got_x, grad_input, own_expand)
        first_other, passed, second = sums(((5, (0,)), (2, ()), (3, (1,))), (got_x, got_y))
        got = [swap_x(passed), along(second, -1), across(first_other)]
        output = pinned(after(output, second))
        got[0], output = together(got[0], output)
        first_own, other = sums(((1, (0, 1, 2)), (4, ())), got)
        got = [along(first_own, -1), across(other)]
        shards = own_shards(after(sums_one, first_own), sums_two, sums_three)
        grad_input = pinned(after(grad_input, first_own))
        got[0], grad_input, *shards = together(got[0], grad_input, *shards)
        (own_reduce,) = sums(((0, (0, 1)),), got)
    else:
        grad_input = back_input(flat_one)
        shards = own_shards(sums_one, sums_two, sums_three)
        whole = jnp.stack(sums(tuple((at, ()) for at in range(size)))).reshape(size * tall, half)
        own_reduce = lax.psum_scatter(whole, "fsdp", scatter_dimension=0, tiled=True)
    (own_expand,) = call(add_kernel, [shape(own_expand.shape, F32)], [own_expand, swap_x(own_expand)], name="add")
    (grad_w_expand,) = call(join_kernel, [shape(w_expand.shape, F32)], [own_expand, swap_core(own_expand)], name="join")
    (own_reduce,) = call(add_kernel, [shape(own_reduce.shape, F32)], [own_reduce, swap_x(own_reduce)], name="add")
    grad_w_reduce, grad_w_group = call(
        join_kernel,
        [shape(w_reduce.shape, F32), shape(w_group.shape, F32)],
        [own_reduce, swap_core(own_reduce)], name="join",
    )
    return (output, grad_input, grad_w_reduce, grad_w_group, grad_w_expand) + tuple(shards)


def solution(mesh):
    fsdp, dp = mesh.shape["fsdp"], mesh.shape["dp"]
    split = Mesh(mesh.devices.reshape(fsdp, dp // 2, 2), ("fsdp", "x", "core"))
    images, rows, vector = P(("fsdp", "x", "core"), None, None, None), P("fsdp", None), P("fsdp")
    return jax.shard_map(
        per_device,
        mesh=split,
        in_specs=(
            images, P(("fsdp", "x", "core")), images,
            rows, vector, vector, rows, vector, vector, rows, vector, vector,
        ),
        out_specs=(images, images, rows, rows, rows) + (vector,) * 6,
        check_vma=False,
    )
```

profile of v0, /device:TPU:0, one launch (start us, length us, event | category | flops | bytes accessed | tf_op | source)
XLA Modules:
  0.0 250.0 jit_solution(1329256857505745404)
XLA Ops:
  11.2 3.0 %collective-permute-start.1 = (bf16[304,512]{1,0:T(8,128)(2,1)S(1)}, bf16[304,512]{1,0:T(8,128)(2,1)S(1)}, u32[]{:S(2)}, u32[]{:S(2)}) collective-permute-start(bf16[304,512]{1,0:T(8,128)(2,1)S(1)} %get-tuple-element.100.refs_0_), channel_id=1, source_target_pairs={{0,4},{4,0},{8,12},{12,8},{16,20},{20,16},{24,28},{28,24},{1,5},{5... | collective-permute-start | bytes 933896 | tf_op jit(solution)/shard_map/ppermute | solution.py:533
  14.3 1.6 collective-permute-start
  15.8 3.3 %copy.31 = bf16[2,14,14,2048]{3,2,1,0:T(8,128)(2,1)} copy(bf16[2,14,14,2048]{3,0,2,1:T(2,128)(2,1)} %param.12) | data formatting | bytes 3211264 | tf_op args[0]
  19.2 3.2 %pad.37 = bf16[2,14,16,2048]{3,2,1,0:T(8,128)(2,1)} pad(bf16[2,14,14,2048]{3,2,1,0:T(8,128)(2,1)} %copy.31, bf16[]{:T(256)} %constant.2.clone.1), padding=0_0x0_0x0_2x0_0 | pad | bytes 3440642 | tf_op jit(solution)/shard_map/jit(_pad)/pad | solution.py:589
  23.0 1.9 collective-permute-done.refs_2_
  25.5 1.6 collective-permute-start.3
  27.2 2.8 %copy.32 = bf16[448,2048]{0,1:T(8,128)(2,1)S(1)} copy(bf16[448,2048]{1,0:T(8,128)(2,1)} %bitcast.22) | data formatting | bytes 3670016 | tf_op jit(solution)/shard_map/reshape | solution.py:589
  30.6 2.6 %collective-permute-done.4.refs_10_ = bf16[304,512]{1,0:T(8,128)(2,1)} collective-permute-done((bf16[304,512]{1,0:T(8,128)(2,1)S(1)}, bf16[304,512]{1,0:T(8,128)(2,1)}, u32[]{:S(2)}, u32[]{:S(2)}) %collective-permute-start.4) | collective-permute-done | bytes 311328 | tf_op jit(solution)/shard_map/ppermute | solution.py:533
  33.8 3.3 %collective-permute-done.2.refs_6_ = bf16[304,512]{1,0:T(8,128)(2,1)} collective-permute-done((bf16[304,512]{1,0:T(8,128)(2,1)S(1)}, bf16[304,512]{1,0:T(8,128)(2,1)}, u32[]{:S(2)}, u32[]{:S(2)}) %collective-permute-start.2) | collective-permute-done | bytes 311328 | tf_op jit(solution)/shard_map/ppermute | solution.py:529
  37.1 1.5 collective-permute-start.13
  39.3 6.2 %collective-permute-done.13.refs_14_ = bf16[304,512]{1,0:T(8,128)(2,1)S(1)} collective-permute-done((bf16[304,512]{1,0:T(8,128)(2,1)}, bf16[304,512]{1,0:T(8,128)(2,1)S(1)}, u32[]{:S(2)}, u32[]{:S(2)}) %collective-permute-start.13) | collective-permute-done | bytes 311328 | tf_op jit(solution)/shard_map/ppermute | solution.py:533
  47.5 1.6 copy-done.2
  49.2 3.4 %reduce.1 = (f32[448,1024]{1,0:T(8,128)S(1)}, f32[3,1024]{1,0:T(4,128)S(1)}) custom-call(s32[2]{0:T(128)S(1)} %copy-done.33, f32[448,1]{1,0:T(8,128)S(1)} %get-tuple-element.103.mask, bf16[448,2048]{1,0:T(8,128)(2,1)S(1)} %bitcast.23, bf16[304,512]{1,0:T(8,128)(2,1)S(1)} %get-tuple-element.100.refs_0_, bf16[304,512]{1,0:T(8,128)(2,1)} %collective-permute-done.5.refs_1_, ...), custom_call_target="tpu_custom_call" | custom-call | flops 1879048192 | bytes 1048576 | tf_op jit(solution)/shard_map/reduce/pallas_call | solution.py:50
  53.8 1.5 collective-permute-start.18
  55.3 1.5 collective-permute-start.17
  57.4 2.2 spread.1
  60.5 3.4 %collective-permute-start.21 = (f32[3,1024]{1,0:T(4,128)S(1)}, f32[3,1024]{1,0:T(4,128)S(1)}, u32[]{:S(2)}, u32[]{:S(2)}) collective-permute-start(f32[3,1024]{1,0:T(4,128)S(1)} %add_add_fusion.5), channel_id=1, source_target_pairs={{0,24},{2,26},{4,28},{6,30},{8,16},{10,18},{12,20},{14,22},{16,8},... | collective-permute-start | bytes 36872 | tf_op jit(solution)/shard_map/ppermute | solution.py:521
  65.0 1.5 collective-permute-done.21
  66.4 2.2 collective-permute-done.20
  68.7 3.5 %group.3 = (bf16[3,2,256,1024]{3,2,1,0:T(8,128)(2,1)S(1)}, f32[448,1024]{1,0:T(8,128)S(1)}, f32[2,1024]{1,0:T(2,128)S(1)}) custom-call(f32[448,1]{1,0:T(8,128)S(1)} %get-tuple-element.103.mask, f32[3,1024]{1,0:T(4,128)S(1)} %add_add_fusion.4.total.first, f32[4,1024]{1,0:T(4,128)S(1)} %get-tuple-element.114.vectors.vectors_two, ...), custom_call_target="tpu_custom_call" | custom-call | flops 2113929216 | bytes 1048576 | tf_op jit(solution)/shard_map/group/pallas_call | solution.py:50
  73.4 1.7 copy-done.34
  76.2 1.5 collective-permute-start.25
  82.3 1.6 collective-permute-start.28
  84.1 2.6 %collective-permute-start.26 = (f32[2,1024]{1,0:T(2,128)S(1)}, f32[2,1024]{1,0:T(2,128)S(1)}, u32[]{:S(2)}, u32[]{:S(2)}) collective-permute-start(f32[2,1024]{1,0:T(2,128)S(1)} %add_add_fusion.11), channel_id=1, source_target_pairs={{0,8},{2,10},{4,12},{6,14},{8,0},{10,2},{12,4},{14,6},{16,24},{18,... | collective-permute-start | bytes 24584 | tf_op jit(solution)/shard_map/ppermute | solution.py:521
  88.5 1.5 copy-done.7
  90.0 1.6 copy-done.28
  91.6 3.1 %expand.1 = (bf16[448,1024]{1,0:T(8,128)(2,1)S(1)}, f32[448,2048]{1,0:T(8,128)S(1)}, f32[2,2048]{1,0:T(2,128)S(1)}) custom-call(f32[448,1]{1,0:T(8,128)S(1)} %get-tuple-element.103.mask, f32[2,1024]{1,0:T(2,128)S(1)} %add_add_fusion.10.total.total_two, f32[3,1024]{1,0:T(4,128)S(1)} %add_add_fusion.4.total.first, ...), custom_call_target="tpu_custom_call" | custom-call | flops 1879048192 | bytes 1048576 | tf_op jit(solution)/shard_map/expand/pallas_call | solution.py:50
  95.9 1.6 collective-permute-start.33
  102.4 2.5 collective-permute-start.36
  108.0 1.5 collective-permute-done.35
  109.7 4.2 %output.1 = (bf16[2,14,14,2048]{3,2,1,0:T(8,128)(2,1)S(1)}, f32[448,2048]{1,0:T(8,128)S(1)}, f32[2,2048]{1,0:T(2,128)S(1)}) custom-call(s32[2]{0:T(128)S(1)} %copy-done.33, f32[2,2048]{1,0:T(2,128)S(1)} %add_add_fusion.2.total, f32[3,1024]{1,0:T(4,128)S(1)} %add_add_fusion.4.total.first, f32[2,2048]{1,0:T(2,128)S(1)} %get-tuple-element.123.vectors, ...), custom_call_target="tpu_custom_call" | custom-call | bytes 1048576 | tf_op jit(solution)/shard_map/output/pallas_call | solution.py:50
  115.3 1.4 collective-permute-start.40
  117.5 1.3 collective-permute-start.38
  121.3 1.7 collective-permute-start.43
  123.8 1.9 collective-permute-start.41
  127.8 6.6 %back_expand.1 = (bf16[448,2048]{1,0:T(8,128)(2,1)S(1)}, f32[448,1024]{1,0:T(8,128)S(1)}, f32[2,1024]{1,0:T(2,128)S(1)}) custom-call(f32[448,1]{1,0:T(8,128)S(1)} %get-tuple-element.103.mask, f32[2,2048]{1,0:T(2,128)S(1)} %add_add_fusion.2.total, f32[2,2048]{1,0:T(2,128)S(1)} %add_add_fusion.sums.refs_2_, f32[3,1024]{1,0:T(4,128)S(1)} %add_add_fusion.4.total.first, ...), custom_call_target="tpu_custom_call" | custom-call | flops 1879048192 | bytes 1048576 | tf_op jit(solution)/shard_map/back_expand/pallas_call | solution.py:50
  135.6 2.4 weight_expand.1
  138.3 1.5 collective-permute-start.47
  139.8 1.2 collective-permute-start.46
  144.7 2.3 collective-permute-start.50
  150.2 1.4 collective-permute-done.49
  153.8 7.2 %back_group.1 = (bf16[448,1024]{1,0:T(8,128)(2,1)S(1)}, f32[448,1024]{1,0:T(8,128)S(1)}, f32[2,1024]{1,0:T(2,128)S(1)}) custom-call(f32[448,1]{1,0:T(8,128)S(1)} %get-tuple-element.103.mask, f32[2,1024]{1,0:T(2,128)S(1)} %add_add_fusion.10.total.total_two, f32[2,1024]{1,0:T(2,128)S(1)} %add_add_fusion.8.sums.refs_1_, ...), custom_call_target="tpu_custom_call" | custom-call | flops 2113929216 | bytes 1048576 | tf_op jit(solution)/shard_map/back_group/pallas_call | solution.py:50
  162.6 1.5 collective-permute-start.57
  168.6 1.7 collective-permute-start.60
  171.4 2.2 collective-permute-start.62
  175.2 7.2 %weight_group.1.group = bf16[8,48,1024]{2,1,0:T(8,128)(2,1)S(1)} custom-call(bf16[3,2,256,1024]{3,2,1,0:T(8,128)(2,1)S(1)} %copy-done.35, bf16[448,1024]{1,0:T(8,128)(2,1)S(1)} %get-tuple-element.137.flat), custom_call_target="tpu_custom_call" | custom-call | flops 2113929216 | bytes 1048576 | tf_op jit(solution)/shard_map/weight_group/pallas_call | solution.py:50
  182.7 3.5 %back_reduce.1 = (bf16[448,1024]{1,0:T(8,128)(2,1)S(1)}, bf16[8,304,512]{2,1,0:T(8,128)(2,1)S(1)}) custom-call(f32[448,1]{1,0:T(8,128)S(1)} %get-tuple-element.103.mask, f32[3,1024]{1,0:T(4,128)S(1)} %add_add_fusion.4.total.first, f32[2,1024]{1,0:T(2,128)S(1)} %add_add_fusion.6.sums.refs_0_, f32[4,1024]{1,0:T(4,128)S(1)} %get-tuple-element.114.vectors.vectors_two, ...), custom_call_target="tpu_custom_call" | custom-call | flops 939524096 | bytes 1048576 | tf_op jit(solution)/shard_map/back_reduce/pallas_call | solution.py:50
  186.3 3.6 %collective-permute-start.66 = (bf16[128,1024]{1,0:T(8,128)(2,1)S(1)}, bf16[128,1024]{1,0:T(8,128)(2,1)S(1)}, u32[]{:S(2)}, u32[]{:S(2)}) collective-permute-start(bf16[128,1024]{1,0:T(8,128)(2,1)S(1)} %get-tuple-element.157), channel_id=1, source_target_pairs={{0,24},{2,10},{4,28},{6,14},{8,0},{10,18},{12,4},{14,22},{16,8},{1... | collective-permute-start | bytes 786440 | tf_op jit(solution)/shard_map/ppermute | solution.py:529
  191.6 2.6 %collective-permute-start.65 = (bf16[304,512]{1,0:T(8,128)(2,1)S(1)}, bf16[304,512]{1,0:T(8,128)(2,1)S(1)}, u32[]{:S(2)}, u32[]{:S(2)}) collective-permute-start(bf16[304,512]{1,0:T(8,128)(2,1)S(1)} %get-tuple-element.154), channel_id=1, source_target_pairs={{0,2},{2,0},{1,3},{3,1},{4,6},{6,4},{5,7},{7,5},{8,10},{10,8},{9,1... | collective-permute-start | bytes 933896 | tf_op jit(solution)/shard_map/ppermute | solution.py:516
  196.2 3.0 %collective-permute-done.67.refs_1_ = bf16[128,1024]{1,0:T(8,128)(2,1)S(1)} collective-permute-done((bf16[128,1024]{1,0:T(8,128)(2,1)S(1)}, bf16[128,1024]{1,0:T(8,128)(2,1)S(1)}, u32[]{:S(2)}, u32[]{:S(2)}) %collective-permute-start.67) | collective-permute-done | bytes 262176 | tf_op jit(solution)/shard_map/ppermute | solution.py:533
  199.4 4.0 %grad_input.1 = bf16[2,14,14,2048]{3,2,1,0:T(8,128)(2,1)S(1)} custom-call(bf16[448,1024]{1,0:T(8,128)(2,1)S(1)} %get-tuple-element.156.flat, f32[448,2048]{1,0:T(8,128)S(1)} %get-tuple-element.126.grad, bf16[304,512]{1,0:T(8,128)(2,1)S(1)} %get-tuple-element.100.refs_0_, bf16[304,512]{1,0:T(8,128)(2,1)} %collective-permute-done.5.refs_1_, ...), custom_call_target="tpu_custom_call" | custom-call | flops 1879048192 | bytes 1048576 | tf_op jit(solution)/shard_map/grad_input/pallas_call | solution.py:50
  203.4 1.6 collective-permute-done.68.refs_1_
  205.8 1.3 collective-permute-start.71
  207.1 2.5 collective-permute-start.70
  209.5 2.8 %copy.40 = bf16[2,14,14,2048]{3,0,2,1:T(2,128)(2,1)} copy(bf16[2,14,14,2048]{3,2,1,0:T(8,128)(2,1)S(1)} %get-tuple-element.163) | data formatting | bytes 3211264 | tf_op jit(solution)/shard_map/optimization_barrier | solution.py:36
  212.4 2.0 collective-permute-done.69.refs_0_
  216.0 4.1 %collective-permute-start.72 = (bf16[304,512]{1,0:T(8,128)(2,1)S(1)}, bf16[304,512]{1,0:T(8,128)(2,1)S(1)}, u32[]{:S(2)}, u32[]{:S(2)}) collective-permute-start(bf16[304,512]{1,0:T(8,128)(2,1)S(1)} %get-tuple-element.167), channel_id=1, source_target_pairs={{0,24},{2,10},{4,28},{6,14},{8,0},{10,18},{12,4},{14,22},{16,8},{1... | collective-permute-start | bytes 933896 | tf_op jit(solution)/shard_map/ppermute | solution.py:529
  220.0 1.2 collective-permute-start.73
  221.8 2.8 %copy.39 = bf16[2,14,14,2048]{3,0,2,1:T(2,128)(2,1)} copy(bf16[2,14,14,2048]{3,2,1,0:T(8,128)(2,1)S(1)} %grad_input.1) | data formatting | bytes 3211264 | tf_op jit(solution)/shard_map/optimization_barrier | solution.py:36
  224.6 2.3 collective-permute-done.73.refs_1_
  227.3 1.5 collective-permute-start.74
  229.4 6.7 %collective-permute-done.74.b = bf16[304,512]{1,0:T(8,128)(2,1)S(1)} collective-permute-done((bf16[304,512]{1,0:T(8,128)(2,1)S(1)}, bf16[304,512]{1,0:T(8,128)(2,1)S(1)}, u32[]{:S(2)}, u32[]{:S(2)}) %collective-permute-start.74) | collective-permute-done | bytes 311328 | tf_op jit(solution)/shard_map/ppermute | solution.py:516
  236.3 2.7 %collective-permute-done.76.b = bf16[128,1024]{1,0:T(8,128)(2,1)S(1)} collective-permute-done((bf16[128,1024]{1,0:T(8,128)(2,1)S(1)}, bf16[128,1024]{1,0:T(8,128)(2,1)S(1)}, u32[]{:S(2)}, u32[]{:S(2)}) %collective-permute-start.76) | collective-permute-done | bytes 262176 | tf_op jit(solution)/shard_map/ppermute | solution.py:516
  239.1 1.9 collective-permute-done.77.other
  (229 shorter events, 68.4 us)
Async XLA Ops:
  7.2 75.0 %all-gather.2.cloned.1.call-start = ((), (), s32[]{:S(2)}) async-start(), calls=%async_computation | async-start | bytes 2359296 | tf_op jit(solution)/shard_map/all_gather | solution.py:615
  11.2 11.8 %collective-permute-start.1 = (bf16[304,512]{1,0:T(8,128)(2,1)S(1)}, bf16[304,512]{1,0:T(8,128)(2,1)S(1)}, u32[]{:S(2)}, u32[]{:S(2)}) collective-permute-start(bf16[304,512]{1,0:T(8,128)(2,1)S(1)} %get-tuple-element.100.refs_0_), channel_id=1, source_target_pairs={{0,4},{4,0},{8,12},{12,8},{16,20},{20,16},{24,28},{28,24},{1,5},{5... | collective-permute-start | bytes 933896 | tf_op jit(solution)/shard_map/ppermute | solution.py:533
  14.3 10.7 %collective-permute-start = (bf16[304,512]{1,0:T(8,128)(2,1)S(1)}, bf16[304,512]{1,0:T(8,128)(2,1)S(1)}, u32[]{:S(2)}, u32[]{:S(2)}) collective-permute-start(bf16[304,512]{1,0:T(8,128)(2,1)S(1)} %get-tuple-element.100.refs_0_), channel_id=1, source_target_pairs={{0,8},{2,26},{4,12},{6,30},{8,16},{10,2},{12,20},{14,6},{16,24},{1... | collective-permute-start | bytes 933896 | tf_op jit(solution)/shard_map/ppermute | solution.py:529
  25.0 8.1 %collective-permute-start.4 = (bf16[304,512]{1,0:T(8,128)(2,1)S(1)}, bf16[304,512]{1,0:T(8,128)(2,1)}, u32[]{:S(2)}, u32[]{:S(2)}) collective-permute-start(bf16[304,512]{1,0:T(8,128)(2,1)S(1)} %collective-permute-done.refs_2_), channel_id=1, source_target_pairs={{0,4},{4,0},{8,12},{12,8},{16,20},{20,16},{24,28},{28,24},{1,5},{5... | collective-permute-start | bytes 933896 | tf_op jit(solution)/shard_map/ppermute | solution.py:533
  25.5 8.2 %collective-permute-start.3 = (bf16[304,512]{1,0:T(8,128)(2,1)S(1)}, bf16[304,512]{1,0:T(8,128)(2,1)}, u32[]{:S(2)}, u32[]{:S(2)}) collective-permute-start(bf16[304,512]{1,0:T(8,128)(2,1)S(1)} %collective-permute-done.refs_2_), channel_id=1, source_target_pairs={{0,2},{2,0},{1,3},{3,1},{4,6},{6,4},{5,7},{7,5},{8,10},{10,8},{9,1... | collective-permute-start | bytes 933896 | tf_op jit(solution)/shard_map/ppermute | solution.py:516
  27.2 10.0 %collective-permute-start.2 = (bf16[304,512]{1,0:T(8,128)(2,1)S(1)}, bf16[304,512]{1,0:T(8,128)(2,1)}, u32[]{:S(2)}, u32[]{:S(2)}) collective-permute-start(bf16[304,512]{1,0:T(8,128)(2,1)S(1)} %collective-permute-done.refs_2_), channel_id=1, source_target_pairs={{0,8},{2,26},{4,12},{6,30},{8,16},{10,2},{12,20},{14,6},{16,24},{1... | collective-permute-start | bytes 933896 | tf_op jit(solution)/shard_map/ppermute | solution.py:529
  27.2 11.5 %collective-permute-start.5 = (bf16[304,512]{1,0:T(8,128)(2,1)S(1)}, bf16[304,512]{1,0:T(8,128)(2,1)}, u32[]{:S(2)}, u32[]{:S(2)}) collective-permute-start(bf16[304,512]{1,0:T(8,128)(2,1)S(1)} %get-tuple-element.100.refs_0_), channel_id=1, source_target_pairs={{0,1},{1,0},{2,3},{3,2},{4,5},{5,4},{6,7},{7,6},{8,9},{9,8},{10,11... | collective-permute-start | bytes 933896 | tf_op jit(solution)/shard_map/ppermute | solution.py:511
  30.0 9.2 %collective-permute-start.6 = (bf16[304,512]{1,0:T(8,128)(2,1)S(1)}, bf16[304,512]{1,0:T(8,128)(2,1)S(1)}, u32[]{:S(2)}, u32[]{:S(2)}) collective-permute-start(bf16[304,512]{1,0:T(8,128)(2,1)S(1)} %collective-permute-done.refs_2_), channel_id=1, source_target_pairs={{0,1},{1,0},{2,3},{3,2},{4,5},{5,4},{6,7},{7,6},{8,9},{9,8},{10,11... | collective-permute-start | bytes 933896 | tf_op jit(solution)/shard_map/ppermute | solution.py:511
  33.1 5.6 %collective-permute-start.9 = (bf16[304,512]{1,0:T(8,128)(2,1)S(1)}, bf16[304,512]{1,0:T(8,128)(2,1)S(1)}, u32[]{:S(2)}, u32[]{:S(2)}) collective-permute-start(bf16[304,512]{1,0:T(8,128)(2,1)S(1)} %collective-permute-done.1.refs_8_), channel_id=1, source_target_pairs={{0,1},{1,0},{2,3},{3,2},{4,5},{5,4},{6,7},{7,6},{8,9},{9,8},{10,11... | collective-permute-start | bytes 933896 | tf_op jit(solution)/shard_map/ppermute | solution.py:511
  37.1 8.3 %collective-permute-start.13 = (bf16[304,512]{1,0:T(8,128)(2,1)}, bf16[304,512]{1,0:T(8,128)(2,1)S(1)}, u32[]{:S(2)}, u32[]{:S(2)}) collective-permute-start(bf16[304,512]{1,0:T(8,128)(2,1)} %collective-permute-done.2.refs_6_), channel_id=1, source_target_pairs={{0,4},{4,0},{8,12},{12,8},{16,20},{20,16},{24,28},{28,24},{1,5},{5... | collective-permute-start | bytes 933896 | tf_op jit(solution)/shard_map/ppermute | solution.py:533
  38.7 7.1 %collective-permute-start.11 = (bf16[304,512]{1,0:T(8,128)(2,1)}, bf16[304,512]{1,0:T(8,128)(2,1)S(1)}, u32[]{:S(2)}, u32[]{:S(2)}) collective-permute-start(bf16[304,512]{1,0:T(8,128)(2,1)} %collective-permute-done.4.refs_10_), channel_id=1, source_target_pairs={{0,2},{2,0},{1,3},{3,1},{4,6},{6,4},{5,7},{7,5},{8,10},{10,8},{9,1... | collective-permute-start | bytes 933896 | tf_op jit(solution)/shard_map/ppermute | solution.py:516
  38.7 7.3 %collective-permute-start.8 = (bf16[304,512]{1,0:T(8,128)(2,1)}, bf16[304,512]{1,0:T(8,128)(2,1)S(1)}, u32[]{:S(2)}, u32[]{:S(2)}) collective-permute-start(bf16[304,512]{1,0:T(8,128)(2,1)} %collective-permute-done.2.refs_6_), channel_id=1, source_target_pairs={{0,1},{1,0},{2,3},{3,2},{4,5},{5,4},{6,7},{7,6},{8,9},{9,8},{10,11... | collective-permute-start | bytes 933896 | tf_op jit(solution)/shard_map/ppermute | solution.py:511
  38.7 7.3 %collective-permute-start.10 = (bf16[304,512]{1,0:T(8,128)(2,1)}, bf16[304,512]{1,0:T(8,128)(2,1)S(1)}, u32[]{:S(2)}, u32[]{:S(2)}) collective-permute-start(bf16[304,512]{1,0:T(8,128)(2,1)} %collective-permute-done.4.refs_10_), channel_id=1, source_target_pairs={{0,1},{1,0},{2,3},{3,2},{4,5},{5,4},{6,7},{7,6},{8,9},{9,8},{10,11... | collective-permute-start | bytes 933896 | tf_op jit(solution)/shard_map/ppermute | solution.py:511
  39.2 6.8 %collective-permute-start.7 = (bf16[304,512]{1,0:T(8,128)(2,1)}, bf16[304,512]{1,0:T(8,128)(2,1)S(1)}, u32[]{:S(2)}, u32[]{:S(2)}) collective-permute-start(bf16[304,512]{1,0:T(8,128)(2,1)} %collective-permute-done.3.refs_4_), channel_id=1, source_target_pairs={{0,1},{1,0},{2,3},{3,2},{4,5},{5,4},{6,7},{7,6},{8,9},{9,8},{10,11... | collective-permute-start | bytes 933896 | tf_op jit(solution)/shard_map/ppermute | solution.py:511
  53.8 5.7 %collective-permute-start.18 = (f32[3,1024]{1,0:T(4,128)S(1)}, f32[3,1024]{1,0:T(4,128)S(1)}, u32[]{:S(2)}, u32[]{:S(2)}) collective-permute-start(f32[3,1024]{1,0:T(4,128)S(1)} %add.168), channel_id=1, source_target_pairs={{0,6},{2,4},{4,2},{6,0},{8,14},{10,12},{12,10},{14,8},{16,22},{18,... | collective-permute-start | bytes 36872 | tf_op jit(solution)/shard_map/ppermute | solution.py:521
  55.3 4.3 %collective-permute-start.17 = (f32[3,1024]{1,0:T(4,128)S(1)}, f32[3,1024]{1,0:T(4,128)S(1)}, u32[]{:S(2)}, u32[]{:S(2)}) collective-permute-start(f32[3,1024]{1,0:T(4,128)S(1)} %add.168), channel_id=1, source_target_pairs={{0,4},{2,6},{4,0},{6,2},{8,12},{10,14},{12,8},{14,10},{16,20},{18,... | collective-permute-start | bytes 36872 | tf_op jit(solution)/shard_map/ppermute | solution.py:521
  56.7 3.7 %collective-permute-start.16 = (f32[3,1024]{1,0:T(4,128)S(1)}, f32[3,1024]{1,0:T(4,128)S(1)}, u32[]{:S(2)}, u32[]{:S(2)}) collective-permute-start(f32[3,1024]{1,0:T(4,128)S(1)} %add.168), channel_id=1, source_target_pairs={{0,2},{2,0},{4,6},{6,4},{8,10},{10,8},{12,14},{14,12},{16,18},{18,... | collective-permute-start | bytes 36872 | tf_op jit(solution)/shard_map/ppermute | solution.py:521
  60.5 5.9 %collective-permute-start.21 = (f32[3,1024]{1,0:T(4,128)S(1)}, f32[3,1024]{1,0:T(4,128)S(1)}, u32[]{:S(2)}, u32[]{:S(2)}) collective-permute-start(f32[3,1024]{1,0:T(4,128)S(1)} %add_add_fusion.5), channel_id=1, source_target_pairs={{0,24},{2,26},{4,28},{6,30},{8,16},{10,18},{12,20},{14,22},{16,8},... | collective-permute-start | bytes 36872 | tf_op jit(solution)/shard_map/ppermute | solution.py:521
  63.9 4.7 %collective-permute-start.20 = (f32[3,1024]{1,0:T(4,128)S(1)}, f32[3,1024]{1,0:T(4,128)S(1)}, u32[]{:S(2)}, u32[]{:S(2)}) collective-permute-start(f32[3,1024]{1,0:T(4,128)S(1)} %add_add_fusion.5), channel_id=1, source_target_pairs={{0,16},{2,18},{4,20},{6,22},{8,24},{10,26},{12,28},{14,30},{16,0},... | collective-permute-start | bytes 36872 | tf_op jit(solution)/shard_map/ppermute | solution.py:521
  63.9 4.7 %collective-permute-start.19 = (f32[3,1024]{1,0:T(4,128)S(1)}, f32[3,1024]{1,0:T(4,128)S(1)}, u32[]{:S(2)}, u32[]{:S(2)}) collective-permute-start(f32[3,1024]{1,0:T(4,128)S(1)} %add_add_fusion.5), channel_id=1, source_target_pairs={{0,8},{2,10},{4,12},{6,14},{8,0},{10,2},{12,4},{14,6},{16,24},{18,... | collective-permute-start | bytes 36872 | tf_op jit(solution)/shard_map/ppermute | solution.py:521
  76.2 4.5 %collective-permute-start.25 = (f32[2,1024]{1,0:T(2,128)S(1)}, f32[2,1024]{1,0:T(2,128)S(1)}, u32[]{:S(2)}, u32[]{:S(2)}) collective-permute-start(f32[2,1024]{1,0:T(2,128)S(1)} %add.175), channel_id=1, source_target_pairs={{0,6},{2,4},{4,2},{6,0},{8,14},{10,12},{12,10},{14,8},{16,22},{18,... | collective-permute-start | bytes 24584 | tf_op jit(solution)/shard_map/ppermute | solution.py:521
  82.2 6.3 %collective-permute-start.29 = (bf16[1024,1024]{1,0:T(8,128)(2,1)}, bf16[1024,1024]{1,0:T(8,128)(2,1)S(1)}, u32[]{:S(2)}, u32[]{:S(2)}) collective-permute-start(bf16[1024,1024]{1,0:T(8,128)(2,1)} %all-gather.2.cloned.1.call-done.mine), channel_id=1, source_target_pairs={{0,1},{1,0},{2,3},{3,2},{4,5},{5,4},{6,7},{7,6},{8,9},{9,8},{10,11... | collective-permute-start | bytes 6291464 | tf_op jit(solution)/shard_map/ppermute | solution.py:511
  82.3 5.6 %collective-permute-start.28 = (f32[2,1024]{1,0:T(2,128)S(1)}, f32[2,1024]{1,0:T(2,128)S(1)}, u32[]{:S(2)}, u32[]{:S(2)}) collective-permute-start(f32[2,1024]{1,0:T(2,128)S(1)} %add_add_fusion.11), channel_id=1, source_target_pairs={{0,24},{2,26},{4,28},{6,30},{8,16},{10,18},{12,20},{14,22},{16,8},... | collective-permute-start | bytes 24584 | tf_op jit(solution)/shard_map/ppermute | solution.py:521
  83.9 4.6 %collective-permute-start.27 = (f32[2,1024]{1,0:T(2,128)S(1)}, f32[2,1024]{1,0:T(2,128)S(1)}, u32[]{:S(2)}, u32[]{:S(2)}) collective-permute-start(f32[2,1024]{1,0:T(2,128)S(1)} %add_add_fusion.11), channel_id=1, source_target_pairs={{0,16},{2,18},{4,20},{6,22},{8,24},{10,26},{12,28},{14,30},{16,0},... | collective-permute-start | bytes 24584 | tf_op jit(solution)/shard_map/ppermute | solution.py:521
  84.1 4.3 %collective-permute-start.26 = (f32[2,1024]{1,0:T(2,128)S(1)}, f32[2,1024]{1,0:T(2,128)S(1)}, u32[]{:S(2)}, u32[]{:S(2)}) collective-permute-start(f32[2,1024]{1,0:T(2,128)S(1)} %add_add_fusion.11), channel_id=1, source_target_pairs={{0,8},{2,10},{4,12},{6,14},{8,0},{10,2},{12,4},{14,6},{16,24},{18,... | collective-permute-start | bytes 24584 | tf_op jit(solution)/shard_map/ppermute | solution.py:521
  95.9 4.7 %collective-permute-start.33 = (f32[2,2048]{1,0:T(2,128)S(1)}, f32[2,2048]{1,0:T(2,128)S(1)}, u32[]{:S(2)}, u32[]{:S(2)}) collective-permute-start(f32[2,2048]{1,0:T(2,128)S(1)} %add.182), channel_id=1, source_target_pairs={{0,6},{2,4},{4,2},{6,0},{8,14},{10,12},{12,10},{14,8},{16,22},{18,... | collective-permute-start | bytes 49160 | tf_op jit(solution)/shard_map/ppermute | solution.py:521
  97.5 3.7 %collective-permute-start.32 = (f32[2,2048]{1,0:T(2,128)S(1)}, f32[2,2048]{1,0:T(2,128)S(1)}, u32[]{:S(2)}, u32[]{:S(2)}) collective-permute-start(f32[2,2048]{1,0:T(2,128)S(1)} %add.182), channel_id=1, source_target_pairs={{0,4},{2,6},{4,0},{6,2},{8,12},{10,14},{12,8},{14,10},{16,20},{18,... | collective-permute-start | bytes 49160 | tf_op jit(solution)/shard_map/ppermute | solution.py:521
  98.7 3.7 %collective-permute-start.31 = (f32[2,2048]{1,0:T(2,128)S(1)}, f32[2,2048]{1,0:T(2,128)S(1)}, u32[]{:S(2)}, u32[]{:S(2)}) collective-permute-start(f32[2,2048]{1,0:T(2,128)S(1)} %add.182), channel_id=1, source_target_pairs={{0,2},{2,0},{4,6},{6,4},{8,10},{10,8},{12,14},{14,12},{16,18},{18,... | collective-permute-start | bytes 49160 | tf_op jit(solution)/shard_map/ppermute | solution.py:521
  102.4 5.6 %collective-permute-start.36 = (f32[2,2048]{1,0:T(2,128)S(1)}, f32[2,2048]{1,0:T(2,128)S(1)}, u32[]{:S(2)}, u32[]{:S(2)}) collective-permute-start(f32[2,2048]{1,0:T(2,128)S(1)} %add_add_fusion.3), channel_id=1, source_target_pairs={{0,24},{2,26},{4,28},{6,30},{8,16},{10,18},{12,20},{14,22},{16,8},... | collective-permute-start | bytes 49160 | tf_op jit(solution)/shard_map/ppermute | solution.py:521
  104.9 4.6 %collective-permute-start.35 = (f32[2,2048]{1,0:T(2,128)S(1)}, f32[2,2048]{1,0:T(2,128)S(1)}, u32[]{:S(2)}, u32[]{:S(2)}) collective-permute-start(f32[2,2048]{1,0:T(2,128)S(1)} %add_add_fusion.3), channel_id=1, source_target_pairs={{0,16},{2,18},{4,20},{6,22},{8,24},{10,26},{12,28},{14,30},{16,0},... | collective-permute-start | bytes 49160 | tf_op jit(solution)/shard_map/ppermute | solution.py:521
  105.9 3.8 %collective-permute-start.34 = (f32[2,2048]{1,0:T(2,128)S(1)}, f32[2,2048]{1,0:T(2,128)S(1)}, u32[]{:S(2)}, u32[]{:S(2)}) collective-permute-start(f32[2,2048]{1,0:T(2,128)S(1)} %add_add_fusion.3), channel_id=1, source_target_pairs={{0,8},{2,10},{4,12},{6,14},{8,0},{10,2},{12,4},{14,6},{16,24},{18,... | collective-permute-start | bytes 49160 | tf_op jit(solution)/shard_map/ppermute | solution.py:521
  115.3 4.7 %collective-permute-start.40 = (f32[2,2048]{1,0:T(2,128)S(1)}, f32[2,2048]{1,0:T(2,128)S(1)}, u32[]{:S(2)}, u32[]{:S(2)}) collective-permute-start(f32[2,2048]{1,0:T(2,128)S(1)} %add.189), channel_id=1, source_target_pairs={{0,6},{2,4},{4,2},{6,0},{8,14},{10,12},{12,10},{14,8},{16,22},{18,... | collective-permute-start | bytes 49160 | tf_op jit(solution)/shard_map/ppermute | solution.py:521
  116.7 3.7 %collective-permute-start.39 = (f32[2,2048]{1,0:T(2,128)S(1)}, f32[2,2048]{1,0:T(2,128)S(1)}, u32[]{:S(2)}, u32[]{:S(2)}) collective-permute-start(f32[2,2048]{1,0:T(2,128)S(1)} %add.189), channel_id=1, source_target_pairs={{0,4},{2,6},{4,0},{6,2},{8,12},{10,14},{12,8},{14,10},{16,20},{18,... | collective-permute-start | bytes 49160 | tf_op jit(solution)/shard_map/ppermute | solution.py:521
  117.5 3.7 %collective-permute-start.38 = (f32[2,2048]{1,0:T(2,128)S(1)}, f32[2,2048]{1,0:T(2,128)S(1)}, u32[]{:S(2)}, u32[]{:S(2)}) collective-permute-start(f32[2,2048]{1,0:T(2,128)S(1)} %add.189), channel_id=1, source_target_pairs={{0,2},{2,0},{4,6},{6,4},{8,10},{10,8},{12,14},{14,12},{16,18},{18,... | collective-permute-start | bytes 49160 | tf_op jit(solution)/shard_map/ppermute | solution.py:521
  121.3 5.6 %collective-permute-start.43 = (f32[2,2048]{1,0:T(2,128)S(1)}, f32[2,2048]{1,0:T(2,128)S(1)}, u32[]{:S(2)}, u32[]{:S(2)}) collective-permute-start(f32[2,2048]{1,0:T(2,128)S(1)} %add_add_fusion.1), channel_id=1, source_target_pairs={{0,24},{2,26},{4,28},{6,30},{8,16},{10,18},{12,20},{14,22},{16,8},... | collective-permute-start | bytes 49160 | tf_op jit(solution)/shard_map/ppermute | solution.py:521
  123.0 4.7 %collective-permute-start.42 = (f32[2,2048]{1,0:T(2,128)S(1)}, f32[2,2048]{1,0:T(2,128)S(1)}, u32[]{:S(2)}, u32[]{:S(2)}) collective-permute-start(f32[2,2048]{1,0:T(2,128)S(1)} %add_add_fusion.1), channel_id=1, source_target_pairs={{0,16},{2,18},{4,20},{6,22},{8,24},{10,26},{12,28},{14,30},{16,0},... | collective-permute-start | bytes 49160 | tf_op jit(solution)/shard_map/ppermute | solution.py:521
  123.8 3.9 %collective-permute-start.41 = (f32[2,2048]{1,0:T(2,128)S(1)}, f32[2,2048]{1,0:T(2,128)S(1)}, u32[]{:S(2)}, u32[]{:S(2)}) collective-permute-start(f32[2,2048]{1,0:T(2,128)S(1)} %add_add_fusion.1), channel_id=1, source_target_pairs={{0,8},{2,10},{4,12},{6,14},{8,0},{10,2},{12,4},{14,6},{16,24},{18,... | collective-permute-start | bytes 49160 | tf_op jit(solution)/shard_map/ppermute | solution.py:521
  138.0 13.6 %collective-permute-start.51 = (bf16[1024,1024]{1,0:T(8,128)(2,1)S(1)}, bf16[1024,1024]{1,0:T(8,128)(2,1)S(1)}, u32[]{:S(2)}, u32[]{:S(2)}) collective-permute-start(bf16[1024,1024]{1,0:T(8,128)(2,1)S(1)} %get-tuple-element.132), channel_id=1, source_target_pairs={{0,1},{1,0},{2,3},{3,2},{4,5},{5,4},{6,7},{7,6},{8,9},{9,8},{10,11... | collective-permute-start | bytes 6291464 | tf_op jit(solution)/shard_map/ppermute | solution.py:511
  138.3 4.5 %collective-permute-start.47 = (f32[2,1024]{1,0:T(2,128)S(1)}, f32[2,1024]{1,0:T(2,128)S(1)}, u32[]{:S(2)}, u32[]{:S(2)}) collective-permute-start(f32[2,1024]{1,0:T(2,128)S(1)} %add.196), channel_id=1, source_target_pairs={{0,6},{2,4},{4,2},{6,0},{8,14},{10,12},{12,10},{14,8},{16,22},{18,... | collective-permute-start | bytes 24584 | tf_op jit(solution)/shard_map/ppermute | solution.py:521
  144.7 5.5 %collective-permute-start.50 = (f32[2,1024]{1,0:T(2,128)S(1)}, f32[2,1024]{1,0:T(2,128)S(1)}, u32[]{:S(2)}, u32[]{:S(2)}) collective-permute-start(f32[2,1024]{1,0:T(2,128)S(1)} %add_add_fusion.9), channel_id=1, source_target_pairs={{0,24},{2,26},{4,28},{6,30},{8,16},{10,18},{12,20},{14,22},{16,8},... | collective-permute-start | bytes 24584 | tf_op jit(solution)/shard_map/ppermute | solution.py:521
  147.0 4.5 %collective-permute-start.49 = (f32[2,1024]{1,0:T(2,128)S(1)}, f32[2,1024]{1,0:T(2,128)S(1)}, u32[]{:S(2)}, u32[]{:S(2)}) collective-permute-start(f32[2,1024]{1,0:T(2,128)S(1)} %add_add_fusion.9), channel_id=1, source_target_pairs={{0,16},{2,18},{4,20},{6,22},{8,24},{10,26},{12,28},{14,30},{16,0},... | collective-permute-start | bytes 24584 | tf_op jit(solution)/shard_map/ppermute | solution.py:521
  147.9 3.7 %collective-permute-start.48 = (f32[2,1024]{1,0:T(2,128)S(1)}, f32[2,1024]{1,0:T(2,128)S(1)}, u32[]{:S(2)}, u32[]{:S(2)}) collective-permute-start(f32[2,1024]{1,0:T(2,128)S(1)} %add_add_fusion.9), channel_id=1, source_target_pairs={{0,8},{2,10},{4,12},{6,14},{8,0},{10,2},{12,4},{14,6},{16,24},{18,... | collective-permute-start | bytes 24584 | tf_op jit(solution)/shard_map/ppermute | solution.py:521
  151.8 9.2 %collective-permute-start.52 = (bf16[128,1024]{1,0:T(8,128)(2,1)S(1)}, bf16[128,1024]{1,0:T(8,128)(2,1)S(1)}, u32[]{:S(2)}, u32[]{:S(2)}) collective-permute-start(bf16[128,1024]{1,0:T(8,128)(2,1)S(1)} %get-tuple-element.139), channel_id=1, source_target_pairs={{0,2},{2,0},{1,3},{3,1},{4,6},{6,4},{5,7},{7,5},{8,10},{10,8},{9,1... | collective-permute-start | bytes 786440 | tf_op jit(solution)/shard_map/ppermute | solution.py:516
  152.6 8.4 %collective-permute-start.53 = (bf16[128,1024]{1,0:T(8,128)(2,1)S(1)}, bf16[128,1024]{1,0:T(8,128)(2,1)S(1)}, u32[]{:S(2)}, u32[]{:S(2)}) collective-permute-start(bf16[128,1024]{1,0:T(8,128)(2,1)S(1)} %get-tuple-element.140), channel_id=1, source_target_pairs={{0,4},{4,0},{8,12},{12,8},{16,20},{20,16},{24,28},{28,24},{1,5},{5... | collective-permute-start | bytes 786440 | tf_op jit(solution)/shard_map/ppermute | solution.py:533
  162.6 4.5 %collective-permute-start.57 = (f32[2,1024]{1,0:T(2,128)S(1)}, f32[2,1024]{1,0:T(2,128)S(1)}, u32[]{:S(2)}, u32[]{:S(2)}) collective-permute-start(f32[2,1024]{1,0:T(2,128)S(1)} %add.203), channel_id=1, source_target_pairs={{0,6},{2,4},{4,2},{6,0},{8,14},{10,12},{12,10},{14,8},{16,22},{18,... | collective-permute-start | bytes 24584 | tf_op jit(solution)/shard_map/ppermute | solution.py:521
  168.6 5.9 %collective-permute-start.60 = (f32[2,1024]{1,0:T(2,128)S(1)}, f32[2,1024]{1,0:T(2,128)S(1)}, u32[]{:S(2)}, u32[]{:S(2)}) collective-permute-start(f32[2,1024]{1,0:T(2,128)S(1)} %add_add_fusion.7), channel_id=1, source_target_pairs={{0,24},{2,26},{4,28},{6,30},{8,16},{10,18},{12,20},{14,22},{16,8},... | collective-permute-start | bytes 24584 | tf_op jit(solution)/shard_map/ppermute | solution.py:521
  170.3 12.1 %collective-permute-start.61 = (bf16[128,1024]{1,0:T(8,128)(2,1)S(1)}, bf16[128,1024]{1,0:T(8,128)(2,1)S(1)}, u32[]{:S(2)}, u32[]{:S(2)}) collective-permute-start(bf16[128,1024]{1,0:T(8,128)(2,1)S(1)} %get-tuple-element.145), channel_id=1, source_target_pairs={{0,2},{2,0},{1,3},{3,1},{4,6},{6,4},{5,7},{7,5},{8,10},{10,8},{9,1... | collective-permute-start | bytes 786440 | tf_op jit(solution)/shard_map/ppermute | solution.py:516
  171.4 11.1 %collective-permute-start.62 = (bf16[128,1024]{1,0:T(8,128)(2,1)S(1)}, bf16[128,1024]{1,0:T(8,128)(2,1)S(1)}, u32[]{:S(2)}, u32[]{:S(2)}) collective-permute-start(bf16[128,1024]{1,0:T(8,128)(2,1)S(1)} %get-tuple-element.146), channel_id=1, source_target_pairs={{0,24},{2,10},{4,28},{6,14},{8,0},{10,18},{12,4},{14,22},{16,8},{1... | collective-permute-start | bytes 786440 | tf_op jit(solution)/shard_map/ppermute | solution.py:529
  173.6 8.9 %collective-permute-start.63 = (bf16[128,1024]{1,0:T(8,128)(2,1)S(1)}, bf16[128,1024]{1,0:T(8,128)(2,1)S(1)}, u32[]{:S(2)}, u32[]{:S(2)}) collective-permute-start(bf16[128,1024]{1,0:T(8,128)(2,1)S(1)} %get-tuple-element.147), channel_id=1, source_target_pairs={{0,4},{4,0},{8,12},{12,8},{16,20},{20,16},{24,28},{28,24},{1,5},{5... | collective-permute-start | bytes 786440 | tf_op jit(solution)/shard_map/ppermute | solution.py:533
  174.4 8.0 %collective-permute-start.59 = (f32[2,1024]{1,0:T(2,128)S(1)}, f32[2,1024]{1,0:T(2,128)S(1)}, u32[]{:S(2)}, u32[]{:S(2)}) collective-permute-start(f32[2,1024]{1,0:T(2,128)S(1)} %add_add_fusion.7), channel_id=1, source_target_pairs={{0,16},{2,18},{4,20},{6,22},{8,24},{10,26},{12,28},{14,30},{16,0},... | collective-permute-start | bytes 24584 | tf_op jit(solution)/shard_map/ppermute | solution.py:521
  174.6 7.9 %collective-permute-start.58 = (f32[2,1024]{1,0:T(2,128)S(1)}, f32[2,1024]{1,0:T(2,128)S(1)}, u32[]{:S(2)}, u32[]{:S(2)}) collective-permute-start(f32[2,1024]{1,0:T(2,128)S(1)} %add_add_fusion.7), channel_id=1, source_target_pairs={{0,8},{2,10},{4,12},{6,14},{8,0},{10,2},{12,4},{14,6},{16,24},{18,... | collective-permute-start | bytes 24584 | tf_op jit(solution)/shard_map/ppermute | solution.py:521
  186.3 4.9 %collective-permute-start.64 = (bf16[8,304,512]{2,1,0:T(8,128)(2,1)S(1)}, bf16[8,304,512]{2,1,0:T(8,128)(2,1)S(1)}, u32[]{:S(2)}, u32[]{:S(2)}) collective-permute-start(bf16[8,304,512]{2,1,0:T(8,128)(2,1)S(1)} %get-tuple-element.153), channel_id=1, source_target_pairs={{0,1},{1,0},{2,3},{3,2},{4,5},{5,4},{6,7},{7,6},{8,9},{9,8},{10,11... | collective-permute-start | bytes 7471112 | tf_op jit(solution)/shard_map/ppermute | solution.py:511
  186.3 9.8 %collective-permute-start.66 = (bf16[128,1024]{1,0:T(8,128)(2,1)S(1)}, bf16[128,1024]{1,0:T(8,128)(2,1)S(1)}, u32[]{:S(2)}, u32[]{:S(2)}) collective-permute-start(bf16[128,1024]{1,0:T(8,128)(2,1)S(1)} %get-tuple-element.157), channel_id=1, source_target_pairs={{0,24},{2,10},{4,28},{6,14},{8,0},{10,18},{12,4},{14,22},{16,8},{1... | collective-permute-start | bytes 786440 | tf_op jit(solution)/shard_map/ppermute | solution.py:529
  190.0 9.1 %collective-permute-start.67 = (bf16[128,1024]{1,0:T(8,128)(2,1)S(1)}, bf16[128,1024]{1,0:T(8,128)(2,1)S(1)}, u32[]{:S(2)}, u32[]{:S(2)}) collective-permute-start(bf16[128,1024]{1,0:T(8,128)(2,1)S(1)} %get-tuple-element.158), channel_id=1, source_target_pairs={{0,4},{4,0},{8,12},{12,8},{16,20},{20,16},{24,28},{28,24},{1,5},{5... | collective-permute-start | bytes 786440 | tf_op jit(solution)/shard_map/ppermute | solution.py:533
  191.6 11.8 %collective-permute-start.65 = (bf16[304,512]{1,0:T(8,128)(2,1)S(1)}, bf16[304,512]{1,0:T(8,128)(2,1)S(1)}, u32[]{:S(2)}, u32[]{:S(2)}) collective-permute-start(bf16[304,512]{1,0:T(8,128)(2,1)S(1)} %get-tuple-element.154), channel_id=1, source_target_pairs={{0,2},{2,0},{1,3},{3,1},{4,6},{6,4},{5,7},{7,5},{8,10},{10,8},{9,1... | collective-permute-start | bytes 933896 | tf_op jit(solution)/shard_map/ppermute | solution.py:516
  194.4 10.7 %collective-permute-start.68 = (bf16[304,512]{1,0:T(8,128)(2,1)S(1)}, bf16[304,512]{1,0:T(8,128)(2,1)S(1)}, u32[]{:S(2)}, u32[]{:S(2)}) collective-permute-start(bf16[304,512]{1,0:T(8,128)(2,1)S(1)} %get-tuple-element.155), channel_id=1, source_target_pairs={{0,4},{4,0},{8,12},{12,8},{16,20},{20,16},{24,28},{28,24},{1,5},{5... | collective-permute-start | bytes 933896 | tf_op jit(solution)/shard_map/ppermute | solution.py:533
  205.7 8.7 %collective-permute-start.69 = (bf16[304,512]{1,0:T(8,128)(2,1)S(1)}, bf16[304,512]{1,0:T(8,128)(2,1)S(1)}, u32[]{:S(2)}, u32[]{:S(2)}) collective-permute-start(bf16[304,512]{1,0:T(8,128)(2,1)S(1)} %get-tuple-element.160), channel_id=1, source_target_pairs={{0,2},{2,0},{1,3},{3,1},{4,6},{6,4},{5,7},{7,5},{8,10},{10,8},{9,1... | collective-permute-start | bytes 933896 | tf_op jit(solution)/shard_map/ppermute | solution.py:516
  205.8 8.7 %collective-permute-start.71 = (bf16[304,512]{1,0:T(8,128)(2,1)S(1)}, bf16[304,512]{1,0:T(8,128)(2,1)S(1)}, u32[]{:S(2)}, u32[]{:S(2)}) collective-permute-start(bf16[304,512]{1,0:T(8,128)(2,1)S(1)} %get-tuple-element.166), channel_id=1, source_target_pairs={{0,4},{4,0},{8,12},{12,8},{16,20},{20,16},{24,28},{28,24},{1,5},{5... | collective-permute-start | bytes 933896 | tf_op jit(solution)/shard_map/ppermute | solution.py:533
  207.1 8.3 %collective-permute-start.70 = (bf16[304,512]{1,0:T(8,128)(2,1)S(1)}, bf16[304,512]{1,0:T(8,128)(2,1)S(1)}, u32[]{:S(2)}, u32[]{:S(2)}) collective-permute-start(bf16[304,512]{1,0:T(8,128)(2,1)S(1)} %get-tuple-element.162), channel_id=1, source_target_pairs={{0,24},{2,10},{4,28},{6,14},{8,0},{10,18},{12,4},{14,22},{16,8},{1... | collective-permute-start | bytes 933896 | tf_op jit(solution)/shard_map/ppermute | solution.py:529
  216.0 8.7 %collective-permute-start.72 = (bf16[304,512]{1,0:T(8,128)(2,1)S(1)}, bf16[304,512]{1,0:T(8,128)(2,1)S(1)}, u32[]{:S(2)}, u32[]{:S(2)}) collective-permute-start(bf16[304,512]{1,0:T(8,128)(2,1)S(1)} %get-tuple-element.167), channel_id=1, source_target_pairs={{0,24},{2,10},{4,28},{6,14},{8,0},{10,18},{12,4},{14,22},{16,8},{1... | collective-permute-start | bytes 933896 | tf_op jit(solution)/shard_map/ppermute | solution.py:529
  220.0 6.9 %collective-permute-start.73 = (bf16[304,512]{1,0:T(8,128)(2,1)S(1)}, bf16[304,512]{1,0:T(8,128)(2,1)S(1)}, u32[]{:S(2)}, u32[]{:S(2)}) collective-permute-start(bf16[304,512]{1,0:T(8,128)(2,1)S(1)} %get-tuple-element.179), channel_id=1, source_target_pairs={{0,4},{4,0},{8,12},{12,8},{16,20},{20,16},{24,28},{28,24},{1,5},{5... | collective-permute-start | bytes 933896 | tf_op jit(solution)/shard_map/ppermute | solution.py:533
  227.3 8.8 %collective-permute-start.74 = (bf16[304,512]{1,0:T(8,128)(2,1)S(1)}, bf16[304,512]{1,0:T(8,128)(2,1)S(1)}, u32[]{:S(2)}, u32[]{:S(2)}) collective-permute-start(bf16[304,512]{1,0:T(8,128)(2,1)S(1)} %block_sum.7.a), channel_id=1, source_target_pairs={{0,2},{2,0},{1,3},{3,1},{4,6},{6,4},{5,7},{7,5},{8,10},{10,8},{9,1... | collective-permute-start | bytes 933896 | tf_op jit(solution)/shard_map/ppermute | solution.py:516
  228.8 10.1 %collective-permute-start.76 = (bf16[128,1024]{1,0:T(8,128)(2,1)S(1)}, bf16[128,1024]{1,0:T(8,128)(2,1)S(1)}, u32[]{:S(2)}, u32[]{:S(2)}) collective-permute-start(bf16[128,1024]{1,0:T(8,128)(2,1)S(1)} %expand_sum.7.a), channel_id=1, source_target_pairs={{0,2},{2,0},{1,3},{3,1},{4,6},{6,4},{5,7},{7,5},{8,10},{10,8},{9,1... | collective-permute-start | bytes 786440 | tf_op jit(solution)/shard_map/ppermute | solution.py:516
  236.2 5.8 %collective-permute-start.75 = (f32[304,512]{1,0:T(8,128)S(1)}, f32[304,512]{1,0:T(8,128)S(1)}, u32[]{:S(2)}, u32[]{:S(2)}) collective-permute-start(f32[304,512]{1,0:T(8,128)S(1)} %add.251.mine), channel_id=1, source_target_pairs={{0,1},{1,0},{2,3},{3,2},{4,5},{5,4},{6,7},{7,6},{8,9},{9,8},{10,11... | collective-permute-start | bytes 1867784 | tf_op jit(solution)/shard_map/ppermute | solution.py:511
  (54 other events, 416.9 us)
Sparse Core Ops, SparseCore 0:
  25.1 51.8 all-gather.1
where the time goes:
time: 250 us
  starting transfers between devices  82.2 us (33%)
  waiting for transfers between devices  71.4 us (29%)
  Pallas kernels  53.6 us (21%)
  local copies, waits for them, and re-layouts  26.9 us (11%)
  between operations  14.9 us (6%)
    pallas_call x25, Pallas kernels, call(): pl.pallas_call(kernel, out_shape=outs, in_specs=[sm] * scalars + [vm] * (...  53.6 us
    ppermute x36, starting transfers between devices, sum_chips(): lax.ppermute(values, CHIPS, [(at, at ^ flip) for at in range(16)])  45.8 us
    ppermute x36, waiting for transfers between devices, sum_chips(): lax.ppermute(values, CHIPS, [(at, at ^ flip) for at in range(16)])  26 us
    ppermute x9, waiting for transfers between devices, across(): return lax.ppermute(values, 'fsdp', [(f, f ^ 1) for f in range(8)])  15.7 us
    unnamed x80, local copies, waits for them, and re-layouts  14.3 us
    ppermute x6, starting transfers between devices, along(): return lax.ppermute(values, CHIPS, pairs)  14 us
    ppermute x8, waiting for transfers between devices, swap_x(): return lax.ppermute(values, 'x', SWAP)  12.4 us
    ppermute x9, starting transfers between devices, across(): return lax.ppermute(values, 'fsdp', [(f, f ^ 1) for f in range(8)])  11.7 us
  transfers between devices with their start and end apart: 79, of which 52 were waited for; matrix products, arithmetic and copies ran while one was open for 7% of the time, Pallas kernels for 12%

commit v1 on v0

v1 whole, which is shorter than its diff:
```python
import functools

import jax
import jax.numpy as jnp
from jax import lax
from jax.experimental import pallas as pl
from jax.experimental.pallas import tpu as pltpu
from jax.sharding import Mesh
from jax.sharding import PartitionSpec as P

GROUPS = 32
TAPS = 9
LINE = 16
CHUNK = 512
UNROLL = 7
LANES = 128
BLOCK = 256
epsilon = 1e-05
BF16, F32 = jnp.bfloat16, jnp.float32
SWAP = [(0, 1), (1, 0)]
NN, NT = ((1,), (0,)), ((1,), (1,))
CHIPS = ("fsdp", "x")


def silu_half(half):
    return half + half * jnp.tanh(half)


def dsilu_twice(half):
    turned = jnp.tanh(half)
    upper = 1.0 + turned
    return upper * (1.0 + half * (1.0 - turned)), upper


def dot(a, b, contract=NN):
    return lax.dot_general(a, b, (contract, ((), ())), preferred_element_type=F32)


def after(values, *others):
    return lax.optimization_barrier((values,) + others)[0]


def together(*values):
    return lax.optimization_barrier(values)


def shape(dims, dtype):
    return jax.ShapeDtypeStruct(dims, dtype)


def call(kernel, outs, args, scalars=0, scratch=(), vmem=8, name=None, flops=0, anywhere=False, aliases=()):
    vm = pl.BlockSpec(memory_space=pltpu.VMEM)
    given = pl.BlockSpec(memory_space=pl.ANY) if anywhere else vm
    sm = pl.BlockSpec(memory_space=pltpu.SMEM)
    return pl.pallas_call(
        kernel,
        out_shape=outs,
        in_specs=[sm] * scalars + [given] * (len(args) - scalars),
        out_specs=[vm] * len(outs),
        scratch_shapes=list(scratch),
        compiler_params=pltpu.CompilerParams(vmem_limit_bytes=vmem << 20),
        cost_estimate=pl.CostEstimate(flops=flops, bytes_accessed=1 << 20, transcendentals=0),
        input_output_aliases=dict(aliases),
        name=name,
    )(*args)


def moments(total, pixels):
    mean = total[0:1, :] / pixels
    inverse = lax.rsqrt(total[1:2, :] / pixels - mean * mean + epsilon)
    return mean, inverse


def chunks(columns):
    return [slice(at, min(at + CHUNK, columns)) for at in range(0, columns, CHUNK)]


def line_mask(columns, side):
    return lax.broadcasted_iota(jnp.int32, (LINE, columns), 0) < side


def each_line(lines, body):
    lax.fori_loop(0, lines, lambda step, none: body(step) or none, 0, unroll=UNROLL)


def each_line_summed(lines, width, body):
    zero = jnp.zeros((8, width), F32)

    def step_sums(step, carry):
        one, two = body(step)
        return carry[0] + fold(one), carry[1] + fold(two)

    one, two = lax.fori_loop(0, lines, step_sums, (zero, zero), unroll=UNROLL)
    return column_sums(one), column_sums(two)


def across_lanes(mask, columns):
    return jnp.concatenate([mask] * (columns // LANES), axis=1)


def column_sums(values):
    return jnp.sum(values, axis=0, keepdims=True)


def line_at(step):
    return pl.ds(pl.multiple_of(step * LINE, LINE), LINE)


def fold(values):
    return values[0:8] + values[8:16]


def part_at(part, half, at=0, length=None):
    core = lax.axis_index("core")
    side = core if part == 0 else 1 - core
    length = half if length is None else length
    return pl.ds(pl.multiple_of(side * half + at, 128), length)


def block_owner(slot):
    position = lax.axis_index("fsdp")
    way = 1 - 2 * lax.axis_index("x")
    step = (0, -way, way, 2)[slot % 4]
    owner = lax.rem(position + 2 * step + 8, 8)
    return owner if slot < 4 else owner + 1 - 2 * lax.rem(owner, 2)


def rows_of(owner, depth):
    return pl.ds(pl.multiple_of(owner * depth, 16), depth)


def pack_kernel(side, valid, weight, group, vectors, out, mask, held, row, sems):
    depth, half = weight.shape[0], out.shape[1]
    shard, extra = group.shape[0], out.shape[0] - weight.shape[0]
    columns = part_at(0, half)
    copies = [
        pltpu.make_async_copy(group, held, sems.at[0]),
        pltpu.make_async_copy(vectors, row, sems.at[1]),
        pltpu.make_async_copy(weight.at[:, columns], out.at[pl.ds(0, depth)], sems.at[2]),
    ]
    for copy in copies:
        copy.start()
    images = valid.shape[0]
    rows = mask.shape[0] // images
    inside = lax.broadcasted_iota(jnp.int32, (rows, LANES), 0) % LINE < side
    for image in range(images):
        mask[image * rows : (image + 1) * rows, :] = jnp.where(inside, valid[image].astype(F32), 0.0)
    copies[0].wait()
    copies[1].wait()
    below = [held[:, columns].astype(F32), row[:, columns].astype(F32)]
    if extra > shard + 1:
        below.append(jnp.zeros((extra - shard - 1, half), F32))
    out[depth : depth + extra, :] = jnp.concatenate(below, axis=0).astype(BF16)
    copies[2].wait()


def reduce_kernel(part, slots, depth, side, valid, mask, x, *refs):
    weights, (red, stats) = refs[:slots], refs[-2:]
    half = weights[0].shape[1]
    for at in range(0, half, BLOCK):
        total = None
        for slot in range(slots):
            if slots == 1:
                piece = x[...]
            else:
                piece = x[:, pl.ds(pl.multiple_of(block_owner(slot) * depth, 128), depth)]
            term = dot(piece, weights[slot][0:depth, at : at + BLOCK])
            total = term if total is None else total + term
        columns = part_at(part, half, at, BLOCK)
        red[:, columns] = total
        masked = total * across_lanes(mask[...], BLOCK)
        stats[0:1, columns] = column_sums(masked)
        stats[1:2, columns] = column_sums(masked * total)
    pixels = valid[0].astype(F32)
    for image in range(1, valid.shape[0]):
        pixels = pixels + valid[image].astype(F32)
    columns = part_at(part, half)
    stats[2:3, columns] = jnp.full((1, half), 1.0, F32) * (pixels * (side * side))


def spread_kernel(slots, depth, *refs):
    blocks, (wide, wide_turned, inner_vectors, outer_vectors, held, rows) = refs[: 2 * slots], refs[2 * slots :]
    extra, half = held.shape[1], held.shape[2] // 2
    for slot in range(slots):
        for part in range(2):
            held[block_owner(slot), :, part_at(part, half)] = blocks[2 * slot + part][depth : depth + extra, :].astype(F32)
    shard = rows.shape[0] // slots
    per, outer = inner_vectors.shape[1] // slots, outer_vectors.shape[1] // slots
    for owner in range(slots):
        rows[owner * shard : (owner + 1) * shard, :] = held[owner, 0:shard, :]
        for row in range(4):
            inner_vectors[row : row + 1, owner * per : (owner + 1) * per] = held[
                owner, shard : shard + 1, row * per : (row + 1) * per
            ]
        for row in range(2):
            outer_vectors[row : row + 1, owner * outer : (owner + 1) * outer] = held[
                owner, shard : shard + 1, 4 * per + row * outer : 4 * per + (row + 1) * outer
            ]
    widen(rows, wide, wide_turned)


def widen_kernel(weight, wide, wide_turned, rows):
    rows[...] = weight[...].astype(F32)
    widen(rows, wide, wide_turned)


def widen(weight, wide, wide_turned):
    taps, blocks = wide.shape[:2]
    inner = weight.shape[0] // taps
    row = lax.broadcasted_iota(jnp.int32, (BLOCK, BLOCK), 0) // inner
    column = lax.broadcasted_iota(jnp.int32, (BLOCK, BLOCK), 1) // inner
    own = row == column
    for tap in range(taps):
        for block in range(blocks):
            piece = weight[tap * inner : (tap + 1) * inner, block * BLOCK : (block + 1) * BLOCK]
            tall = jnp.concatenate([piece] * (BLOCK // inner), axis=0)
            dense = jnp.where(own, tall, 0.0)
            wide[tap, block] = dense.astype(BF16)
            wide_turned[tap, block] = dense.T.astype(BF16)


def fill_pads(pads, columns, image, line, values):
    rows = pl.ds(pl.multiple_of((line + 1) * LINE, LINE), LINE)
    pads[0, image, rows, columns] = pltpu.roll(values, 1, 0).astype(BF16)
    pads[1, image, rows, columns] = values.astype(BF16)
    pads[2, image, rows, columns] = pltpu.roll(values, LINE - 1, 0).astype(BF16)


def clear_pads(pads):
    images, rows, columns = pads.shape[1:]
    zeros = jnp.zeros((3, images, LINE, columns), BF16)
    pads[:, :, 0:LINE, :] = zeros
    pads[:, :, rows - LINE : rows, :] = zeros


def convolve(pads, wide, image, block, rows, turned=False):
    columns = slice(block * BLOCK, (block + 1) * BLOCK)
    value = None
    for tap in range(TAPS):
        top, left = divmod(TAPS - 1 - tap if turned else tap, 3)
        piece = pads[left, image, top * LINE : top * LINE + rows, columns]
        term = dot(piece, wide[tap, block])
        value = term if value is None else value + term
    return value


def group_kernel(side, mask, total, vectors, red, wide, pads, grouped, stats):
    images, padded, width = pads.shape[1:]
    rows = side * LINE
    mean, inverse = moments(total, total[2:3, :])
    scale, bias = 0.5 * inverse * vectors[0:1, :], 0.5 * vectors[1:2, :]
    clear_pads(pads)
    for part in chunks(width):
        inside = line_mask(part.stop - part.start, side)

        def body(step):
            half = (red[line_at(step), part] - mean[:, part]) * scale[:, part] + bias[:, part]
            fill_pads(pads, part, step // side, step % side, jnp.where(inside, silu_half(half), 0.0))

        each_line(images * side, body)
    for block in range(width // BLOCK):
        columns = slice(block * BLOCK, (block + 1) * BLOCK)
        sums = [0.0, 0.0]
        for image in range(images):
            at = slice(image * rows, (image + 1) * rows)
            value = convolve(pads, wide, image, block, rows)
            grouped[at, columns] = value
            masked = value * across_lanes(mask[at, :], BLOCK)
            sums = [sums[0] + column_sums(masked), sums[1] + column_sums(masked * value)]
        stats[0:1, columns] = sums[0]
        stats[1:2, columns] = sums[1]


def pair_slots(slots):
    return [(0,)] if slots == 1 else [(slot, slot + slots // 2) for slot in range(slots // 2)]


def pair_rows(weights, pair, part, columns=slice(None)):
    return jnp.concatenate([weights[2 * slot + part][:, columns] for slot in pair], axis=0)


def expand_kernel(slots, side, mask, total, first, vectors, grouped, *refs):
    weights, (act, expanded, stats, held) = refs[: 2 * slots], refs[2 * slots :]
    rows, width = grouped.shape
    mean, inverse = moments(total, first[2:3, :])
    scale, bias = 0.5 * inverse * vectors[2:3, :], 0.5 * vectors[3:4, :]
    for part in chunks(width):
        inside = line_mask(part.stop - part.start, side)

        def body(step):
            at = line_at(step)
            half = (grouped[at, part] - mean[:, part]) * scale[:, part] + bias[:, part]
            held[at, part] = jnp.where(inside, silu_half(half), 0.0).astype(BF16)

        each_line(rows // LINE, body)
    depth, half = weights[0].shape
    pairs = pair_slots(slots)
    for at, slot in enumerate(slot for pair in pairs for slot in pair):
        columns = pl.ds(pl.multiple_of(block_owner(slot) * depth, 128), depth) if slots > 1 else slice(None)
        act[:, at * depth : (at + 1) * depth] = held[:, columns]
    tall = depth * len(pairs[0])
    for part in range(2):
        for at in range(0, half, BLOCK):
            value = None
            for index, pair in enumerate(pairs):
                weight = pair_rows(weights, pair, part, slice(at, at + BLOCK))
                term = dot(act[:, index * tall : (index + 1) * tall], weight)
                value = term if value is None else value + term
            columns = part_at(part, half, at, BLOCK)
            expanded[:, columns] = value
            masked = value * across_lanes(mask[...], BLOCK)
            stats[0:1, columns] = column_sums(masked)
            stats[1:2, columns] = column_sums(masked * value)


def output_kernel(side, valid, total, first, vectors, expanded, x, cotangent, output, grad, stats):
    rows, channels = expanded.shape
    mean, inverse = moments(total, first[2:3, 0:1])
    scale, bias = inverse * vectors[0:1, :], vectors[1:2, :]
    for part in chunks(channels):

        def body(step):
            image, line = step // side, step % side
            at = line_at(step)
            keep = 0.5 * valid[image].astype(F32)
            centered = expanded[at, part] - mean[:, part]
            half = (centered * scale[:, part] + (bias[:, part] + x[at, part].astype(F32))) * keep
            slope, upper = dsilu_twice(half)
            output[image, line, :, part] = (half * upper).astype(BF16)[0:side]
            here = cotangent[at, part].astype(F32) * keep * slope
            grad[at, part] = here
            return here, here * centered

        one, two = each_line_summed(rows // LINE, part.stop - part.start, body)
        stats[0:1, part] = one
        stats[1:2, part] = two * inverse[:, part]


def back_expand_kernel(
    slots, mask, total, sums, first, vectors, total_two, vectors_two, grad, expanded, grouped, *refs
):
    weights, (flat, dz, stats) = refs[: 2 * slots], refs[2 * slots :]
    rows, width = grouped.shape
    pixels = first[2:3, 0:1]
    mean, inverse = moments(total, pixels)
    scale = inverse * vectors[0:1, :]
    shifted, scaled = scale * sums[0:1, :] / pixels, scale * inverse * sums[1:2, :] / pixels
    for part in chunks(expanded.shape[1]):

        def body(step):
            at = line_at(step)
            common = shifted[:, part] + (expanded[at, part] - mean[:, part]) * scaled[:, part]
            flat[at, part] = (scale[:, part] * grad[at, part] - across_lanes(mask[at, :], part.stop - part.start) * common).astype(BF16)

        each_line(rows // LINE, body)
    depth, half = weights[0].shape
    for pair in pair_slots(slots):
        for at in range(0, depth * len(pair), BLOCK):
            value = None
            for part in range(2):
                weight = pair_rows(weights, pair, part) if slots > 1 else weights[part][at : at + BLOCK, :]
                term = dot(flat[:, part_at(part, half)], weight, NT)
                value = term if value is None else value + term
            if slots == 1:
                dz[:, at : at + BLOCK] = value
            else:
                for index, slot in enumerate(pair):
                    columns = pl.ds(pl.multiple_of(block_owner(slot) * depth, 128), depth)
                    dz[:, columns] = value[:, index * depth : (index + 1) * depth]
    mean_two, inverse_two = moments(total_two, first[2:3, :])
    before_norm(dz, grouped, mean_two, inverse_two, vectors_two[2:3, :], vectors_two[3:4, :], stats)


def before_norm(dz, hidden, mean, inverse, gain, shift, stats, side=None):
    scale, bias = 0.5 * inverse * gain, 0.5 * shift
    rows, width = hidden.shape
    for part in chunks(width):
        inside = None if side is None else line_mask(part.stop - part.start, side)

        def body(step):
            at = line_at(step)
            centered = hidden[at, part] - mean[:, part]
            slope, _ = dsilu_twice(centered * scale[:, part] + bias[:, part])
            here = dz[at, part] * slope
            if side is not None:
                here = jnp.where(inside, here, 0.0)
            dz[at, part] = here
            return here, here * centered

        one, two = each_line_summed(rows // LINE, part.stop - part.start, body)
        stats[0:1, part] = 0.5 * one
        stats[1:2, part] = 0.5 * inverse[:, part] * two


def weight_expand_kernel(act, flat, send, keep):
    half = send.shape[1]
    turned = act[...].T
    for part, out in ((1, send), (0, keep)):
        for at in range(0, half, BLOCK):
            out[:, at : at + BLOCK] = dot(turned, flat[:, part_at(part, half, at, BLOCK)]).astype(BF16)


def back_group_kernel(
    side, mask, total, sums, first, vectors, dz, grouped, red, wide, flat, dz_one, stats, pads
):
    images, padded, width = pads.shape[1:]
    rows = side * LINE
    pixels = first[2:3, :]
    mean, inverse = moments(total, pixels)
    scale = inverse * vectors[2:3, :]
    shifted, scaled = scale * sums[0:1, :] / pixels, scale * inverse * sums[1:2, :] / pixels
    scale = 0.5 * scale
    clear_pads(pads)
    for part in chunks(width):

        def body(step):
            at = line_at(step)
            common = shifted[:, part] + (grouped[at, part] - mean[:, part]) * scaled[:, part]
            value = scale[:, part] * dz[at, part] - across_lanes(mask[at, :], part.stop - part.start) * common
            flat[at, part] = value.astype(BF16)
            fill_pads(pads, part, step // side, step % side, value)

        each_line(images * side, body)
    for block in range(width // BLOCK):
        columns = slice(block * BLOCK, (block + 1) * BLOCK)
        for image in range(images):
            dz_one[image * rows : (image + 1) * rows, columns] = convolve(pads, wide, image, block, rows, True)
    mean_one, inverse_one = moments(first, pixels)
    before_norm(dz_one, red, mean_one, inverse_one, vectors[0:1, :], vectors[1:2, :], stats, side)


def weight_group_kernel(side, pads, flat, out, held):
    images, padded, width = pads.shape[1:]
    rows = side * LINE
    inner = width // GROUPS
    row = lax.broadcasted_iota(jnp.int32, (LANES, LANES), 0) // inner
    column = lax.broadcasted_iota(jnp.int32, (LANES, LANES), 1) // inner
    own = row == column
    for at in range(0, width, LANES):
        columns = slice(at, at + LANES)
        moved = []
        for tap in range(TAPS):
            top, left = divmod(tap, 3)
            pieces = [pads[left, image, top * LINE : top * LINE + rows, columns] for image in range(images)]
            moved.append(jnp.concatenate(pieces, axis=0))
        product = dot(flat[:, columns].T, jnp.concatenate(moved, axis=1))
        for tap in range(TAPS):
            kept = jnp.where(own, product[:, tap * LANES : (tap + 1) * LANES].T, 0.0)
            value = kept[0:inner]
            for begin in range(inner, LANES, inner):
                value = value + kept[begin : begin + inner]
            held[tap * inner : (tap + 1) * inner, columns] = value
    owners, extra = out.shape[:2]
    shard = TAPS * inner // owners
    zeros = jnp.zeros((extra - shard, width), F32)
    for owner in range(owners):
        rows_here = held[owner * shard : (owner + 1) * shard, :]
        out[owner] = jnp.concatenate([rows_here, zeros], axis=0).astype(BF16)


def back_reduce_kernel(
    small, blocks, mask, first, sums, vectors, dz, red, turned, group, flat, send
):
    rows, width = red.shape
    pixels = first[2:3, :]
    mean, inverse = moments(first, pixels)
    scale = inverse * vectors[0:1, :]
    shifted, scaled = scale * sums[0:1, :] / pixels, scale * inverse * sums[1:2, :] / pixels
    scale = 0.5 * scale
    for part in chunks(width):

        def body(step):
            at = line_at(step)
            common = shifted[:, part] + (red[at, part] - mean[:, part]) * scaled[:, part]
            flat[at, part] = (scale[:, part] * dz[at, part] - across_lanes(mask[at, :], part.stop - part.start) * common).astype(BF16)

        each_line(rows // LINE, body)
    send_kernel(small, blocks, turned, group, flat, send)


def send_kernel(small, blocks, turned, group, flat, send):
    tall, half = send.shape[1:]
    depth = tall - group.shape[1]
    columns = part_at(1, half)
    for at, block in enumerate(blocks):
        owner = block_owner(block) if small else block
        send[at, 0:depth, :] = dot(turned[rows_of(owner, depth), :], flat[:, columns]).astype(BF16)
        send[at, depth:tall, :] = group[owner, :, columns]


def block_sum_kernel(small, places, turned, group, flat, near, *refs):
    arrived, outs = refs[: len(refs) - len(places)], refs[len(refs) - len(places) :]
    tall, half = near.shape[1:]
    depth = tall - group.shape[1]
    columns = part_at(0, half)
    for out, (block, at, chosen) in zip(outs, places):
        owner = block_owner(block) if small else block
        value = dot(turned[rows_of(owner, depth), :], flat[:, columns]) + near[at, 0:depth, :].astype(F32)
        more = group[owner, :, columns].astype(F32) + near[at, depth:tall, :].astype(F32)
        for other in chosen:
            value = value + arrived[other][0:depth, :].astype(F32)
            more = more + arrived[other][depth:tall, :].astype(F32)
        out[0:depth, :] = value.astype(BF16)
        out[depth:tall, :] = more.astype(BF16)


def expand_sum_kernel(places, keep, near, *refs):
    arrived, outs = refs[: len(refs) - len(places)], refs[len(refs) - len(places) :]
    depth = outs[0].shape[0]
    for out, (block, chosen) in zip(outs, places):
        at = block % 4 * 2 + block // 4
        rows = slice(at * depth, (at + 1) * depth)
        value = keep[rows, :].astype(F32) + near[rows, :].astype(F32)
        for other in chosen:
            value = value + arrived[other][...].astype(F32)
        out[...] = value.astype(BF16)


def add_kernel(a, b, out):
    out[...] = (a[...].astype(F32) + b[...].astype(F32)).astype(out.dtype)


def join_kernel(mine, mine_x, other, other_x, *outs):
    half = mine.shape[1]
    at = 0
    for out in outs:
        rows = out.shape[0]
        for part, terms in enumerate(((mine, mine_x), (other, other_x))):
            values = [term[at : at + -(-rows // 16) * 16, :].astype(F32) for term in terms]
            out[:, part_at(part, half)] = (values[0] + values[1])[0:rows]
        at += -(-rows // 16) * 16


def turn_kernel(values, out):
    out[...] = values[...].T


def pin_kernel(values, out):
    pass


def own_kernel(*refs):
    number = len(refs) // 3
    position = lax.axis_index("fsdp")
    for at, total in enumerate(refs[:number]):
        for row, out in ((1, refs[number + 2 * at]), (0, refs[number + 2 * at + 1])):
            length = out.shape[1]
            out[...] = total[row : row + 1, pl.ds(pl.multiple_of(position * length, 128), length)]


def grad_input_kernel(slots, depth, side, flat, grad, *refs):
    weights, (out, held) = refs[: 2 * slots], refs[2 * slots :]
    half = weights[0].shape[1]
    for slot in range(slots):
        columns = pl.ds(pl.multiple_of(block_owner(slot) * depth, 128), depth) if slots > 1 else slice(None)
        value = grad[:, columns]
        for part in range(2):
            value = value + dot(flat[:, part_at(part, half)], weights[2 * slot + part][0:depth, :], NT)
        held[:, columns] = value

    def body(step, carry):
        out[step // side, step % side] = held[line_at(step), :].astype(BF16)[0:side]
        return carry

    lax.fori_loop(0, flat.shape[0] // LINE, body, 0)


def pinned(values):
    anywhere = pl.BlockSpec(memory_space=pl.ANY)
    values = values.transpose(1, 2, 0, 3)
    values = pl.pallas_call(
        pin_kernel, out_shape=shape(values.shape, values.dtype), in_specs=[anywhere], out_specs=anywhere,
        input_output_aliases={0: 0}, compiler_params=pltpu.CompilerParams(vmem_limit_bytes=1 << 20), name="pin",
    )(values)
    return values.transpose(2, 0, 1, 3)


def swap_core(values):
    return lax.ppermute(values, "core", SWAP)


def swap_x(values):
    if lax.axis_size("x") == 2:
        return lax.ppermute(values, "x", SWAP)
    return (lax.psum(values.astype(F32), "x") - values.astype(F32)).astype(values.dtype)


def sum_chips(values, flips):
    got = [lax.ppermute(values, CHIPS, [(at, at ^ flip) for at in range(16)]) for flip in flips]
    for other in got:
        values = values + other
    return values


def along(values, way):
    pairs = [(f * 2 + x, (f + 2 * way * (1 - 2 * x)) % 8 * 2 + x) for f in range(8) for x in range(2)]
    return lax.ppermute(values, CHIPS, pairs)


def across(values):
    return lax.ppermute(values, "fsdp", [(f, f ^ 1) for f in range(8)])


def gather_blocks(own, early, late, beside):
    first = along(own, 1)
    other = across(own)
    first, other, *early = together(first, other, *early)
    passed, second, first_other = swap_x(first), along(first, 1), across(first)
    second, passed, first_other, *late = together(second, passed, first_other, *late)
    passed_other, second_other, beside = swap_x(first_other), across(second), along(beside(early), 1)
    blocks = [own, first, passed, second, other, first_other, passed_other, second_other]
    *blocks, beside = together(*blocks, beside)
    return blocks, early, late, beside


def halves(values, core):
    half = values.shape[1] // 2
    return lax.dynamic_slice_in_dim(values, core * half, half, 1)


def per_device(
    images,
    valid,
    cotangent,
    w_reduce,
    gain_one,
    shift_one,
    w_group,
    gain_two,
    shift_two,
    w_expand,
    gain_three,
    shift_three,
):
    count, side, _, channels = images.shape
    width = w_reduce.shape[1]
    inner = width // GROUPS
    size = lax.axis_size("fsdp")
    small = size == 8 and lax.axis_size("x") == 2
    position, core = lax.axis_index("fsdp"), lax.axis_index("core")
    rows = count * side * LINE
    per, outer, shard, depth = gain_one.shape[0], gain_three.shape[0], w_group.shape[0], w_reduce.shape[0]
    extra = -(-(shard + 1) // 16) * 16
    half = width // 2

    def start_sum(values):
        return values + swap_core(values) if small else lax.psum(values, ("fsdp", "x", "core"))

    def plane_sum(values):
        return sum_chips(values, (1, 2, 3)) if small else values

    def line_sum(values):
        return sum_chips(values, (4, 8, 12)) if small else values

    def everywhere(values):
        return line_sum(plane_sum(start_sum(values)))


    def padded(values):
        return jnp.pad(values, ((0, 0), (0, 0), (0, LINE - side), (0, 0))).reshape(rows, channels)

    x, cot = padded(images), padded(cotangent)

    vectors, at = jnp.zeros((width,), BF16), 0
    for vector in (gain_one, shift_one, gain_two, shift_two, gain_three, shift_three):
        vectors = vectors + jnp.pad(vector, (at, width - at - vector.size))
        at += vector.size
    own, mask = call(
        functools.partial(pack_kernel, side),
        [shape((depth + extra, half), BF16), shape((rows, LANES), F32)],
        [valid, w_reduce, w_group, vectors.reshape(1, width)], scalars=1, anywhere=True, vmem=60, name="pack",
        scratch=[pltpu.VMEM((shard, width), BF16), pltpu.VMEM((1, width), BF16), pltpu.SemaphoreType.DMA((3,))],
    )
    wide_shape = shape((TAPS, width // BLOCK, BLOCK, BLOCK), BF16)
    expand_own = halves(w_expand, core)
    if small:
        (turned,) = call(turn_kernel, [shape((channels, rows), BF16)], [x], name="turn")
        blocks, (x, expand_own), (turned,), expand_first = gather_blocks(
            own, (x, expand_own), (turned,), lambda early: early[1]
        )
        moving = [across(expand_first), swap_x(expand_first)]
        slots, slot_depth = size, depth
    else:
        whole = lax.all_gather(own, "fsdp", axis=0, tiled=False)
        block = whole[:, :depth].reshape(channels, half)
        blocks = [block]
        slots, slot_depth, turned = 1, channels, x.T
        expand_mine = lax.all_gather(expand_own, "fsdp", axis=0, tiled=True)
        expand_weights = [expand_mine, swap_core(expand_mine)]

    far = [swap_core(block) for block in blocks]
    weights = [half for pair in zip(blocks, far) for half in pair]

    def reduce_part(part, weights, *before):
        return call(
            functools.partial(reduce_kernel, part, slots, slot_depth, side),
            [shape((rows, width), F32), shape((3, width), F32)],
            [valid, mask, x, *weights, *before], scalars=1, name="reduce", flops=rows * width * channels,
            aliases=((3 + slots, 0), (4 + slots, 1)) if before else (),
        )

    red, part = reduce_part(1, far, *reduce_part(0, blocks))
    if small:
        wide, wide_turned, inner_vectors, outer_vectors = call(
            functools.partial(spread_kernel, slots, depth),
            [wide_shape, wide_shape, shape((4, width), F32), shape((2, channels), F32)],
            weights,
            scratch=[pltpu.VMEM((size, extra, width), F32), pltpu.VMEM((size * shard, width), F32)],
            name="spread", flops=1 << 28,
        )
    else:
        mine = whole[:, depth:]
        other = swap_core(mine)
        packed = jnp.concatenate([jnp.where(core == 0, mine, other), jnp.where(core == 0, other, mine)], axis=2)
        wide, wide_turned = call(
            widen_kernel, [wide_shape, wide_shape], [packed[:, :shard].reshape(size * shard, width)],
            scratch=[pltpu.VMEM((size * shard, width), F32)], name="widen",
        )
        line = packed[:, shard].astype(F32)
        inner_vectors = line[:, : 4 * per].reshape(size, 4, per).transpose(1, 0, 2).reshape(4, width)
        outer_vectors = line[:, 4 * per : 4 * per + 2 * outer].reshape(size, 2, outer)
        outer_vectors = outer_vectors.transpose(1, 0, 2).reshape(2, channels)
    middle = line_sum(start_sum(part))
    middle, wide, wide_turned, inner_vectors, outer_vectors = together(
        middle, wide, wide_turned, inner_vectors, outer_vectors
    )
    if small:
        middle, first_other, passed, expand_first = together(middle, *moving, expand_first)
        second = along(expand_first, 1)
    first = plane_sum(middle)
    if small:
        first, first_other, expand_own = together(first, first_other, expand_own)
        moving = [swap_x(first_other), across(expand_own)]
    pad_shape = (3, count, (side + 2) * LINE, width)
    pads, grouped, part = call(
        functools.partial(group_kernel, side),
        [shape(pad_shape, BF16), shape((rows, width), F32), shape((2, width), F32)],
        [mask, first, inner_vectors, red, wide],
        name="group", flops=2 * TAPS * rows * width * BLOCK,
    )
    if small:
        part, second = together(part, second)
        second_other = across(second)
    middle = line_sum(start_sum(part))
    if small:
        middle, passed_other, other, second_other = together(middle, *moving, second_other)
        expand_weights = []
        for block in (expand_own, expand_first, passed, second, other, first_other, passed_other, second_other):
            expand_weights += [block, swap_core(block)]
    total_two = plane_sum(middle)
    act_two, expanded, part = call(
        functools.partial(expand_kernel, slots, side),
        [shape((rows, width), BF16), shape((rows, channels), F32), shape((2, channels), F32)],
        [mask, total_two, first, inner_vectors, grouped] + expand_weights,
        scratch=[pltpu.VMEM((rows, width), BF16)], name="expand", flops=2 * rows * width * channels,
    )
    total_three = everywhere(part)
    output, grad_summed, part = call(
        functools.partial(output_kernel, side),
        [shape(images.shape, BF16), shape((rows, channels), F32), shape((2, channels), F32)],
        [valid, total_three, first, outer_vectors, expanded, x, cot], scalars=1, name="output",
    )

    sums_three = everywhere(part)
    flat_three, dz_two, part = call(
        functools.partial(back_expand_kernel, slots),
        [shape((rows, channels), BF16), shape((rows, width), F32), shape((2, width), F32)],
        [mask, total_three, sums_three, first, outer_vectors, total_two, inner_vectors, grad_summed, expanded, grouped]
        + expand_weights,
        name="back_expand", flops=2 * rows * width * channels,
    )
    middle = start_sum(part)
    act_two = after(act_two, middle)
    send, keep = call(
        weight_expand_kernel,
        [shape((width, channels // 2), BF16)] * 2,
        [act_two, flat_three], name="weight_expand", flops=2 * rows * width * channels,
    )
    near_expand = swap_core(send)
    middle = plane_sum(middle)

    def expand_sums(places, arrived=()):
        return call(
            functools.partial(expand_sum_kernel, places),
            [shape((w_expand.shape[0], channels // 2), BF16)] * len(places),
            [keep, near_expand] + list(arrived), name="expand_sum",
        )

    if small:
        middle, *moving = together(middle, *expand_sums(((6, ()), (7, ()))))
        moving = [swap_x(moving[0]), across(moving[1])]
        sums_two, *moving = together(line_sum(middle), *moving)
        sums_two, expand_first_other, expand_passed, expand_second, expand_other = together(
            sums_two, *expand_sums(((5, (0,)), (2, ()), (3, (1,)), (4, ())), moving)
        )
        expand_second = along(expand_second, -1)
    else:
        sums_two = line_sum(middle)
        (chip,) = call(add_kernel, [shape(keep.shape, BF16)], [keep, near_expand], name="add")
        own_expand = lax.psum_scatter(chip, "fsdp", scatter_dimension=0, tiled=True)
    flat_two, dz_one, part = call(
        functools.partial(back_group_kernel, side),
        [shape((rows, width), BF16), shape((rows, width), F32), shape((2, width), F32)],
        [mask, total_two, sums_two, first, inner_vectors, dz_two, grouped, red, wide_turned],
        scratch=[pltpu.VMEM(pad_shape, BF16)], name="back_group", flops=2 * TAPS * rows * width * BLOCK,
    )

    middle = start_sum(part)
    flat_two = after(flat_two, middle)
    (group_term,) = call(
        functools.partial(weight_group_kernel, side),
        [shape((size, extra, width), BF16)],
        [pads, flat_two], scratch=[pltpu.VMEM((TAPS * inner, width), F32)], name="weight_group",
        flops=2 * TAPS * rows * width * BLOCK,
    )
    middle, group_term = together(plane_sum(middle), group_term)
    if small:
        middle, expand_second, expand_first_other, expand_passed, expand_other = together(
            middle, expand_second, expand_first_other, expand_passed, expand_other
        )
        moving = [swap_x(expand_passed), expand_second, across(expand_first_other), across(expand_other)]
    sums_one = line_sum(middle)
    tall = depth + extra
    early = (6, 7) if small else tuple(range(size))
    flat_one, send = call(
        functools.partial(back_reduce_kernel, small, early),
        [shape((rows, width), BF16), shape((len(early), tall, half), BF16)],
        [mask, first, sums_one, inner_vectors, dz_one, red, turned, group_term],
        name="back_reduce", flops=2 * rows * depth * half * len(early),
    )
    near = swap_core(send)

    def sums(places, near, arrived=()):
        return call(
            functools.partial(block_sum_kernel, small, places),
            [shape((tall, half), BF16)] * len(places),
            [turned, group_term, flat_one, near] + list(arrived),
            name="block_sum", flops=2 * rows * depth * half * len(places),
        )

    def back_input(flat):
        (out,) = call(
            functools.partial(grad_input_kernel, slots, slot_depth, side),
            [shape(images.shape, BF16)],
            [flat, grad_summed] + weights,
            scratch=[pltpu.VMEM((rows, channels), F32)], name="grad_input", flops=2 * rows * width * channels,
        )
        return out

    def own_shards(*totals):
        if not small:
            cut = []
            for total, length in zip(totals, (per, per, outer)):
                cut += [lax.dynamic_slice_in_dim(total[row], position * length, length, 0) for row in (1, 0)]
            return cut
        lengths = (per, per, per, per, outer, outer)
        return [out.reshape(-1) for out in call(own_kernel, [shape((1, n), F32) for n in lengths], totals, name="own")]

    def join(own, far, outs):
        return call(
            join_kernel, [shape(out.shape, F32) for out in outs], [own, far, swap_core(own), swap_core(far)], name="join"
        )

    if small:
        late = (0, 1, 2, 3, 4, 5)
        (send,) = call(
            functools.partial(send_kernel, small, late),
            [shape((len(late), tall, half), BF16)],
            [turned, group_term, flat_one], name="send", flops=2 * rows * depth * half * len(late),
        )
        near_late = swap_core(send)
        passed_other, second_other = sums(((6, 0, ()), (7, 1, ())), near)
        second_other, *expand_moving = together(second_other, *moving)
        (expand_first_own,) = expand_sums(((1, (0, 1, 2)),), expand_moving[:3])
        moving = [swap_x(passed_other), across(second_other)]
        expand_first_own = along(expand_first_own, -1)
        grad_input = back_input(after(flat_one, second_other))
        moving[0], grad_input, expand_first_own = together(moving[0], grad_input, expand_first_own)
        (own_expand,) = expand_sums(((0, (0, 1)),), [expand_first_own, expand_moving[3]])
        first_other, passed, second = sums(((5, 5, (0,)), (2, 2, ()), (3, 3, (1,))), near_late, moving)
        moving = [swap_x(passed), along(second, -1), across(first_other)]
        output = pinned(after(output, second))
        moving[0], output = together(moving[0], output)
        first_own, other = sums(((1, 1, (0, 1, 2)), (4, 4, ())), near_late, moving)
        moving = [along(first_own, -1), across(other)]
        shards = own_shards(after(sums_one, first_own), sums_two, sums_three)
        grad_input, own_expand = pinned(after(grad_input, first_own)), after(own_expand, first_own)
        far_expand = swap_x(own_expand)
        moving[0], grad_input, far_expand, *shards = together(moving[0], grad_input, far_expand, *shards)
        (own_reduce,) = sums(((0, 0, (0, 1)),), near_late, moving)
        own_expand, far_expand = after(own_expand, own_reduce), after(far_expand, own_reduce)
        (grad_w_expand,) = join(own_expand, far_expand, [w_expand])
    else:
        grad_input = back_input(flat_one)
        shards = own_shards(sums_one, sums_two, sums_three)
        whole = jnp.stack(sums(tuple((at, at, ()) for at in range(size)), near)).reshape(size * tall, half)
        own_reduce = lax.psum_scatter(whole, "fsdp", scatter_dimension=0, tiled=True)
        (grad_w_expand,) = join(own_expand, swap_x(own_expand), [w_expand])
    grad_w_reduce, grad_w_group = join(own_reduce, swap_x(own_reduce), [w_reduce, w_group])
    return (output, grad_input, grad_w_reduce, grad_w_group, grad_w_expand) + tuple(shards)


def solution(mesh):
    fsdp, dp = mesh.shape["fsdp"], mesh.shape["dp"]
    split = Mesh(mesh.devices.reshape(fsdp, dp // 2, 2), ("fsdp", "x", "core"))
    images, rows, vector = P(("fsdp", "x", "core"), None, None, None), P("fsdp", None), P("fsdp")
    return jax.shard_map(
        per_device,
        mesh=split,
        in_specs=(
            images, P(("fsdp", "x", "core")), images,
            rows, vector, vector, rows, vector, vector, rows, vector, vector,
        ),
        out_specs=(images, images, rows, rows, rows) + (vector,) * 6,
        check_vma=False,
    )
```

time: 250 us -> 233 us (0.932)
  waiting for transfers between devices: 71.4 us -> 95.8 us
  local copies, waits for them, and re-layouts: 26.9 us -> 9.64 us
  between operations: 14.9 us -> 1.2 us
  Pallas kernels: 53.6 us -> 42 us
    ppermute x6 -> x8, waiting for transfers between devices: 7.1 us -> 18.7 us  [along(): return lax.ppermute(values, CHIPS, pairs)]
    pallas_call x25 -> x26, Pallas kernels: 53.6 us -> 42 us  [call(): pl.pallas_call(kernel, out_shape=outs, in_specs=[sm] * scalars + [given]...]
    unnamed x80 -> x14, local copies, waits for them, and re-layouts: 14.3 us -> 2.81 us
    ppermute x9 -> x12, waiting for transfers between devices: 15.7 us -> 22.9 us  [across(): return lax.ppermute(values, 'fsdp', [(f, f ^ 1) for f in range(8)])]
    ppermute x8 -> x10, waiting for transfers between devices: 12.4 us -> 16.6 us  [swap_x(): return lax.ppermute(values, 'x', SWAP)]
    ppermute x6 -> x8, starting transfers between devices: 14 us -> 9.96 us  [along(): return lax.ppermute(values, CHIPS, pairs)]
    pad x2, local copies, waits for them, and re-layouts: 3.41 us -> 0.57 us  [padded(): jnp.pad(values, ((0, 0), (0, 0), (0, LINE - side), (0, 0)))]
    reshape x1 -> x0, local copies, waits for them, and re-layouts: 2.8 us -> none  [padded(): jnp.pad(values, ((0, 0), (0, 0), (0, LINE - side), (0, 0)))]
  transfers between devices with their start and end apart: 79 -> 95, of which waited for: 52 -> 57; matrix products, arithmetic and copies ran while one was open for 7% -> 4% of each run, Pallas kernels for 12% -> 7%
where the time goes in v1:
time: 233 us
  waiting for transfers between devices  95.8 us (41%)
  starting transfers between devices  83.3 us (36%)
  Pallas kernels  42 us (18%)
  local copies, waits for them, and re-layouts  9.64 us (4%)
    ppermute x36, starting transfers between devices, sum_chips(): lax.ppermute(values, CHIPS, [(at, at ^ flip) for at in range(16)])  47.8 us
    pallas_call x26, Pallas kernels, call(): pl.pallas_call(kernel, out_shape=outs, in_specs=[sm] * scalars + [given]...  42 us
    ppermute x36, waiting for transfers between devices, sum_chips(): lax.ppermute(values, CHIPS, [(at, at ^ flip) for at in range(16)])  26.5 us
    ppermute x12, waiting for transfers between devices, across(): return lax.ppermute(values, 'fsdp', [(f, f ^ 1) for f in range(8)])  22.9 us
    ppermute x8, waiting for transfers between devices, along(): return lax.ppermute(values, CHIPS, pairs)  18.7 us
    ppermute x10, waiting for transfers between devices, swap_x(): return lax.ppermute(values, 'x', SWAP)  16.6 us
    ppermute x12, starting transfers between devices, across(): return lax.ppermute(values, 'fsdp', [(f, f ^ 1) for f in range(8)])  12.3 us
    ppermute x29, waiting for transfers between devices, swap_core(): return lax.ppermute(values, 'core', SWAP)  11.2 us
  transfers between devices with their start and end apart: 95, of which 57 were waited for; matrix products, arithmetic and copies ran while one was open for 4% of the time, Pallas kernels for 7%

profile of v1, /device:TPU:0, one launch (start us, length us, event | category | flops | bytes accessed | tf_op | source)
XLA Modules:
  0.0 232.9 jit_solution(6280423749600697520)
XLA Ops:
  2.1 2.5 %pack.1 = (bf16[304,512]{1,0:T(8,128)(2,1)}, f32[448,128]{1,0:T(8,128)}) custom-call(s32[2]{0:T(128)} %valid.7, bf16[256,1024]{1,0:T(8,128)(2,1)} %weight.1, bf16[36,1024]{1,0:T(8,128)(2,1)} %group.2, bf16[1,1024]{1,0:T(2,128)(2,1)} %reshape.49.vectors), custom_call_target="tpu_custom_call" | custom-call | bytes 1048576 | tf_op jit(solution)/shard_map/pack/pallas_call | solution.py:55
  4.6 3.0 %collective-permute-start.1 = (bf16[304,512]{1,0:T(8,128)(2,1)}, bf16[304,512]{1,0:T(8,128)(2,1)S(1)}, u32[]{:S(2)}, u32[]{:S(2)}) collective-permute-start(bf16[304,512]{1,0:T(8,128)(2,1)} %get-tuple-element.152.refs_0_), channel_id=1, source_target_pairs={{0,4},{4,0},{8,12},{12,8},{16,20},{20,16},{24,28},{28,24},{1,5},{5... | collective-permute-start | bytes 933896 | tf_op jit(solution)/shard_map/ppermute | solution.py:601
  7.6 1.6 collective-permute-start
  9.2 2.1 copy.31
  11.6 3.6 %collective-permute-done.1.refs_4_.refs_8_ = bf16[304,512]{1,0:T(8,128)(2,1)S(1)} collective-permute-done((bf16[304,512]{1,0:T(8,128)(2,1)}, bf16[304,512]{1,0:T(8,128)(2,1)S(1)}, u32[]{:S(2)}, u32[]{:S(2)}) %collective-permute-start.1) | collective-permute-done | bytes 311328 | tf_op jit(solution)/shard_map/ppermute | solution.py:601
  15.2 3.4 %collective-permute-done.refs_1_.refs_2_ = bf16[304,512]{1,0:T(8,128)(2,1)S(1)} collective-permute-done((bf16[304,512]{1,0:T(8,128)(2,1)}, bf16[304,512]{1,0:T(8,128)(2,1)S(1)}, u32[]{:S(2)}, u32[]{:S(2)}) %collective-permute-start) | collective-permute-done | bytes 311328 | tf_op jit(solution)/shard_map/ppermute | solution.py:597
  20.8 5.7 %collective-permute-done.4.refs_5_.refs_10_ = bf16[304,512]{1,0:T(8,128)(2,1)S(1)} collective-permute-done((bf16[304,512]{1,0:T(8,128)(2,1)S(1)}, bf16[304,512]{1,0:T(8,128)(2,1)S(1)}, u32[]{:S(2)}, u32[]{:S(2)}) %collective-permute-start.4) | collective-permute-done | bytes 311328 | tf_op jit(solution)/shard_map/ppermute | solution.py:601
  27.0 2.7 %collective-permute-done.2.refs_3_.refs_6_ = bf16[304,512]{1,0:T(8,128)(2,1)S(1)} collective-permute-done((bf16[304,512]{1,0:T(8,128)(2,1)S(1)}, bf16[304,512]{1,0:T(8,128)(2,1)S(1)}, u32[]{:S(2)}, u32[]{:S(2)}) %collective-permute-start.2) | collective-permute-done | bytes 311328 | tf_op jit(solution)/shard_map/ppermute | solution.py:597
  29.6 1.5 collective-permute-start.6
  31.2 8.2 %collective-permute-done.7.refs_2_ = bf16[128,1024]{1,0:T(8,128)(2,1)S(1)} collective-permute-done((bf16[128,1024]{1,0:T(8,128)(2,1)S(1)}, bf16[128,1024]{1,0:T(8,128)(2,1)S(1)}, u32[]{:S(2)}, u32[]{:S(2)}) %collective-permute-start.7) | collective-permute-done | bytes 262176 | tf_op jit(solution)/shard_map/ppermute | solution.py:597
  42.0 1.7 reduce.2
  44.1 1.7 reduce.3
  47.1 3.4 %collective-permute-start.19 = (f32[3,1024]{1,0:T(4,128)S(1)}, f32[3,1024]{1,0:T(4,128)S(1)}, u32[]{:S(2)}, u32[]{:S(2)}) collective-permute-start(f32[3,1024]{1,0:T(4,128)S(1)} %add.166), channel_id=1, source_target_pairs={{0,24},{2,26},{4,28},{6,30},{8,16},{10,18},{12,20},{14,22},{16,8},... | collective-permute-start | bytes 36872 | tf_op jit(solution)/shard_map/ppermute | solution.py:589
  51.5 1.6 spread.1
  53.1 2.0 collective-permute-done.18
  56.4 1.4 collective-permute-start.23
  60.1 1.4 collective-permute-done.22
  62.5 3.4 %group.3 = (bf16[3,2,256,1024]{3,2,1,0:T(8,128)(2,1)S(1)}, f32[448,1024]{1,0:T(8,128)S(1)}, f32[2,1024]{1,0:T(2,128)S(1)}) custom-call(f32[448,128]{1,0:T(8,128)S(1)} %copy-done.2, f32[3,1024]{1,0:T(4,128)S(1)} %add_add_fusion.4.total.first, f32[4,1024]{1,0:T(4,128)S(1)} %get-tuple-element.172.vectors.vectors_two, f32[448,1024]{1,0:T(8,128)S(1)} %get-tuple-element.173.red, ...), custom_call_target="tpu_custom_call" | custom-call | flops 2113929216 | bytes 1048576 | tf_op jit(solution)/shard_map/group/pallas_call | solution.py:55
  68.0 2.1 collective-permute-start.29
  70.6 1.5 collective-permute-start.32
  72.1 2.3 %collective-permute-start.27 = (f32[2,1024]{1,0:T(2,128)S(1)}, f32[2,1024]{1,0:T(2,128)S(1)}, u32[]{:S(2)}, u32[]{:S(2)}) collective-permute-start(f32[2,1024]{1,0:T(2,128)S(1)} %add.173), channel_id=1, source_target_pairs={{0,8},{2,10},{4,12},{6,14},{8,0},{10,2},{12,4},{14,6},{16,24},{18,... | collective-permute-start | bytes 24584 | tf_op jit(solution)/shard_map/ppermute | solution.py:589
  74.4 2.2 collective-permute-done.28
  77.2 2.1 collective-permute-done.31.refs_8_
  79.3 4.5 %collective-permute-done.32.refs_14_ = bf16[128,1024]{1,0:T(8,128)(2,1)S(1)} collective-permute-done((bf16[128,1024]{1,0:T(8,128)(2,1)S(1)}, bf16[128,1024]{1,0:T(8,128)(2,1)S(1)}, u32[]{:S(2)}, u32[]{:S(2)}) %collective-permute-start.32) | collective-permute-done | bytes 262176 | tf_op jit(solution)/shard_map/ppermute | solution.py:601
  83.8 1.7 collective-permute-start.35
  85.5 1.5 collective-permute-start.34
  89.1 1.5 collective-permute-done.33
  90.7 1.5 collective-permute-done.43.refs_15_
  92.2 2.8 %expand.1 = (bf16[448,1024]{1,0:T(8,128)(2,1)S(1)}, f32[448,2048]{1,0:T(8,128)S(1)}, f32[2,2048]{1,0:T(2,128)S(1)}) custom-call(f32[448,128]{1,0:T(8,128)S(1)} %copy-done.2, f32[2,1024]{1,0:T(2,128)S(1)} %add_add_fusion.10.total.total_two, f32[3,1024]{1,0:T(4,128)S(1)} %add_add_fusion.4.total.first, f32[4,1024]{1,0:T(4,128)S(1)} %get-tuple-element.172.vectors.vectors_two, ...), custom_call_target="tpu_custom_call" | custom-call | flops 1879048192 | bytes 1048576 | tf_op jit(solution)/shard_map/expand/pallas_call | solution.py:55
  96.5 1.5 collective-permute-start.46
  98.0 1.8 collective-permute-start.45
  101.8 1.9 collective-permute-start.50
  103.7 2.6 %collective-permute-start.48 = (f32[2,2048]{1,0:T(2,128)S(1)}, f32[2,2048]{1,0:T(2,128)S(1)}, u32[]{:S(2)}, u32[]{:S(2)}) collective-permute-start(f32[2,2048]{1,0:T(2,128)S(1)} %add_add_fusion.3), channel_id=1, source_target_pairs={{0,8},{2,10},{4,12},{6,14},{8,0},{10,2},{12,4},{14,6},{16,24},{18,... | collective-permute-start | bytes 49160 | tf_op jit(solution)/shard_map/ppermute | solution.py:589
  108.3 3.4 %output.1 = (bf16[2,14,14,2048]{3,2,1,0:T(8,128)(2,1)S(1)}, f32[448,2048]{1,0:T(8,128)S(1)}, f32[2,2048]{1,0:T(2,128)S(1)}) custom-call(s32[2]{0:T(128)S(1)} %copy-done.4, f32[2,2048]{1,0:T(2,128)S(1)} %add_add_fusion.2.total, f32[3,1024]{1,0:T(4,128)S(1)} %add_add_fusion.4.total.first, f32[2,2048]{1,0:T(2,128)S(1)} %get-tuple-element.188.vectors, ...), custom_call_target="tpu_custom_call" | custom-call | bytes 1048576 | tf_op jit(solution)/shard_map/output/pallas_call | solution.py:55
  113.0 1.4 collective-permute-start.54
  114.5 1.5 collective-permute-start.53
  118.2 1.5 collective-permute-done.52
  119.7 2.4 %collective-permute-start.57 = (f32[2,2048]{1,0:T(2,128)S(1)}, f32[2,2048]{1,0:T(2,128)S(1)}, u32[]{:S(2)}, u32[]{:S(2)}) collective-permute-start(f32[2,2048]{1,0:T(2,128)S(1)} %add_add_fusion.1), channel_id=1, source_target_pairs={{0,24},{2,26},{4,28},{6,30},{8,16},{10,18},{12,20},{14,22},{16,8},... | collective-permute-start | bytes 49160 | tf_op jit(solution)/shard_map/ppermute | solution.py:589
  127.0 4.5 %back_expand.1 = (bf16[448,2048]{1,0:T(8,128)(2,1)S(1)}, f32[448,1024]{1,0:T(8,128)S(1)}, f32[2,1024]{1,0:T(2,128)S(1)}) custom-call(f32[448,128]{1,0:T(8,128)S(1)} %copy-done.2, f32[2,2048]{1,0:T(2,128)S(1)} %add_add_fusion.2.total, f32[2,2048]{1,0:T(2,128)S(1)} %add_add_fusion.sums.refs_2_, f32[3,1024]{1,0:T(4,128)S(1)} %add_add_fusion.4.total.first, ...), custom_call_target="tpu_custom_call" | custom-call | flops 1879048192 | bytes 1048576 | tf_op jit(solution)/shard_map/back_expand/pallas_call | solution.py:55
  132.8 2.4 %weight_expand.1 = (bf16[1024,1024]{1,0:T(8,128)(2,1)S(1)}, bf16[1024,1024]{1,0:T(8,128)(2,1)S(1)}) custom-call(bf16[448,1024]{1,0:T(8,128)(2,1)S(1)} %get-tuple-element.194.act, bf16[448,2048]{1,0:T(8,128)(2,1)S(1)} %get-tuple-element.195.flat), custom_call_target="tpu_custom_call" | custom-call | flops 1879048192 | bytes 1048576 | tf_op jit(solution)/shard_map/weight_expand/pallas_call | solution.py:55
  137.3 1.7 collective-permute-start.59
  141.1 1.7 collective-permute-start.66
  143.3 1.4 collective-permute-start.65
  145.7 2.0 collective-permute-start.63
  149.7 4.3 %back_group.1 = (bf16[448,1024]{1,0:T(8,128)(2,1)S(1)}, f32[448,1024]{1,0:T(8,128)S(1)}, f32[2,1024]{1,0:T(2,128)S(1)}) custom-call(f32[448,128]{1,0:T(8,128)S(1)} %copy-done.2, f32[2,1024]{1,0:T(2,128)S(1)} %add_add_fusion.10.total.total_two, f32[2,1024]{1,0:T(2,128)S(1)} %add_add_fusion.8.sums.refs_1_, f32[3,1024]{1,0:T(4,128)S(1)} %add_add_fusion.4.total.first, ...), custom_call_target="tpu_custom_call" | custom-call | flops 2113929216 | bytes 1048576 | tf_op jit(solution)/shard_map/back_group/pallas_call | solution.py:55
  154.1 2.5 %collective-permute-start.72 = (bf16[128,1024]{1,0:T(8,128)(2,1)S(1)}, bf16[128,1024]{1,0:T(8,128)(2,1)S(1)}, u32[]{:S(2)}, u32[]{:S(2)}) collective-permute-start(bf16[128,1024]{1,0:T(8,128)(2,1)S(1)} %get-tuple-element.219), channel_id=1, source_target_pairs={{0,24},{2,10},{4,28},{6,14},{8,0},{10,18},{12,4},{14,22},{16,8},{1... | collective-permute-start | bytes 786440 | tf_op jit(solution)/shard_map/ppermute | solution.py:597
  158.3 1.8 collective-permute-start.69
  160.1 2.4 %weight_group.1.group = bf16[8,48,1024]{2,1,0:T(8,128)(2,1)S(1)} custom-call(bf16[3,2,256,1024]{3,2,1,0:T(8,128)(2,1)S(1)} %get-tuple-element.214.pads, bf16[448,1024]{1,0:T(8,128)(2,1)S(1)} %get-tuple-element.216.flat), custom_call_target="tpu_custom_call" | custom-call | flops 2113929216 | bytes 1048576 | tf_op jit(solution)/shard_map/weight_group/pallas_call | solution.py:55
  163.0 4.0 %collective-permute-start.75 = (f32[2,1024]{1,0:T(2,128)S(1)}, f32[2,1024]{1,0:T(2,128)S(1)}, u32[]{:S(2)}, u32[]{:S(2)}) collective-permute-start(f32[2,1024]{1,0:T(2,128)S(1)} %add_add_fusion.7), channel_id=1, source_target_pairs={{0,24},{2,26},{4,28},{6,30},{8,16},{10,18},{12,20},{14,22},{16,8},... | collective-permute-start | bytes 24584 | tf_op jit(solution)/shard_map/ppermute | solution.py:589
  168.6 2.9 %collective-permute-done.74 = f32[2,1024]{1,0:T(2,128)S(1)} collective-permute-done((f32[2,1024]{1,0:T(2,128)S(1)}, f32[2,1024]{1,0:T(2,128)S(1)}, u32[]{:S(2)}, u32[]{:S(2)}) %collective-permute-start.74) | collective-permute-done | bytes 8224 | tf_op jit(solution)/shard_map/ppermute | solution.py:589
  176.8 1.5 collective-permute-done.77.near
  179.5 3.6 %collective-permute-done.79.refs_0_ = bf16[128,1024]{1,0:T(8,128)(2,1)S(1)} collective-permute-done((bf16[128,1024]{1,0:T(8,128)(2,1)S(1)}, bf16[128,1024]{1,0:T(8,128)(2,1)S(1)}, u32[]{:S(2)}, u32[]{:S(2)}) %collective-permute-start.79) | collective-permute-done | bytes 262176 | tf_op jit(solution)/shard_map/ppermute | solution.py:584
  184.0 4.4 %collective-permute-done.81.refs_1_ = bf16[128,1024]{1,0:T(8,128)(2,1)S(1)} collective-permute-done((bf16[128,1024]{1,0:T(8,128)(2,1)S(1)}, bf16[128,1024]{1,0:T(8,128)(2,1)S(1)}, u32[]{:S(2)}, u32[]{:S(2)}) %collective-permute-start.81) | collective-permute-done | bytes 262176 | tf_op jit(solution)/shard_map/ppermute | solution.py:601
  189.7 1.8 collective-permute-start.82
  191.5 3.2 %grad_input.1 = bf16[2,14,14,2048]{3,2,1,0:T(8,128)(2,1)S(1)} custom-call(bf16[448,1024]{1,0:T(8,128)(2,1)S(1)} %get-tuple-element.234.flat, f32[448,2048]{1,0:T(8,128)S(1)} %get-tuple-element.191.grad, bf16[304,512]{1,0:T(8,128)(2,1)S(1)} %copy-done.3, bf16[304,512]{1,0:T(8,128)(2,1)S(1)} %collective-permute-done.8.refs_0_.refs_1_, ...), custom_call_target="tpu_custom_call" | custom-call | flops 1879048192 | bytes 1048576 | tf_op jit(solution)/shard_map/grad_input/pallas_call | solution.py:55
  194.8 2.2 collective-permute-done.82.refs_0_
  197.7 3.3 %collective-permute-start.84 = (bf16[304,512]{1,0:T(8,128)(2,1)S(1)}, bf16[304,512]{1,0:T(8,128)(2,1)S(1)}, u32[]{:S(2)}, u32[]{:S(2)}) collective-permute-start(bf16[304,512]{1,0:T(8,128)(2,1)S(1)} %get-tuple-element.239), channel_id=1, source_target_pairs={{0,2},{2,0},{1,3},{3,1},{4,6},{6,4},{5,7},{7,5},{8,10},{10,8},{9,1... | collective-permute-start | bytes 933896 | tf_op jit(solution)/shard_map/ppermute | solution.py:584
  202.5 2.8 %copy.36 = bf16[2,14,14,2048]{3,0,2,1:T(2,128)(2,1)} copy(bf16[2,14,14,2048]{3,2,1,0:T(8,128)(2,1)S(1)} %get-tuple-element.242) | data formatting | bytes 3211264 | tf_op jit(solution)/shard_map/optimization_barrier | solution.py:40
  206.2 1.7 collective-permute-done.86.refs_2_
  209.3 2.5 %collective-permute-start.87 = (bf16[304,512]{1,0:T(8,128)(2,1)S(1)}, bf16[304,512]{1,0:T(8,128)(2,1)S(1)}, u32[]{:S(2)}, u32[]{:S(2)}) collective-permute-start(bf16[304,512]{1,0:T(8,128)(2,1)S(1)} %get-tuple-element.246), channel_id=1, source_target_pairs={{0,24},{2,10},{4,28},{6,14},{8,0},{10,18},{12,4},{14,22},{16,8},{1... | collective-permute-start | bytes 933896 | tf_op jit(solution)/shard_map/ppermute | solution.py:597
  213.2 2.8 %copy.35 = bf16[2,14,14,2048]{3,0,2,1:T(2,128)(2,1)} copy(bf16[2,14,14,2048]{3,2,1,0:T(8,128)(2,1)S(1)} %grad_input.1) | data formatting | bytes 3211264 | tf_op jit(solution)/shard_map/optimization_barrier | solution.py:40
  216.1 4.9 %collective-permute-done.88.mine_x = bf16[128,1024]{1,0:T(8,128)(2,1)S(1)} collective-permute-done((bf16[128,1024]{1,0:T(8,128)(2,1)S(1)}, bf16[128,1024]{1,0:T(8,128)(2,1)S(1)}, u32[]{:S(2)}, u32[]{:S(2)}) %collective-permute-start.88) | collective-permute-done | bytes 262176 | tf_op jit(solution)/shard_map/ppermute | solution.py:584
  221.5 6.8 %collective-permute-done.90.mine_x = bf16[304,512]{1,0:T(8,128)(2,1)S(1)} collective-permute-done((bf16[304,512]{1,0:T(8,128)(2,1)S(1)}, bf16[304,512]{1,0:T(8,128)(2,1)S(1)}, u32[]{:S(2)}, u32[]{:S(2)}) %collective-permute-start.90) | collective-permute-done | bytes 311328 | tf_op jit(solution)/shard_map/ppermute | solution.py:584
  228.8 1.5 collective-permute-done.93.other
  (193 shorter events, 64.7 us)
Async XLA Ops:
  4.6 10.6 %collective-permute-start.1 = (bf16[304,512]{1,0:T(8,128)(2,1)}, bf16[304,512]{1,0:T(8,128)(2,1)S(1)}, u32[]{:S(2)}, u32[]{:S(2)}) collective-permute-start(bf16[304,512]{1,0:T(8,128)(2,1)} %get-tuple-element.152.refs_0_), channel_id=1, source_target_pairs={{0,4},{4,0},{8,12},{12,8},{16,20},{20,16},{24,28},{28,24},{1,5},{5... | collective-permute-start | bytes 933896 | tf_op jit(solution)/shard_map/ppermute | solution.py:601
  7.6 10.9 %collective-permute-start = (bf16[304,512]{1,0:T(8,128)(2,1)}, bf16[304,512]{1,0:T(8,128)(2,1)S(1)}, u32[]{:S(2)}, u32[]{:S(2)}) collective-permute-start(bf16[304,512]{1,0:T(8,128)(2,1)} %get-tuple-element.152.refs_0_), channel_id=1, source_target_pairs={{0,8},{2,26},{4,12},{6,30},{8,16},{10,2},{12,20},{14,6},{16,24},{1... | collective-permute-start | bytes 933896 | tf_op jit(solution)/shard_map/ppermute | solution.py:597
  18.5 8.0 %collective-permute-start.4 = (bf16[304,512]{1,0:T(8,128)(2,1)S(1)}, bf16[304,512]{1,0:T(8,128)(2,1)S(1)}, u32[]{:S(2)}, u32[]{:S(2)}) collective-permute-start(bf16[304,512]{1,0:T(8,128)(2,1)S(1)} %collective-permute-done.refs_1_.refs_2_), channel_id=1, source_target_pairs={{0,4},{4,0},{8,12},{12,8},{16,20},{20,16},{24,28},{28,24},{1,5},{5... | collective-permute-start | bytes 933896 | tf_op jit(solution)/shard_map/ppermute | solution.py:601
  19.0 7.9 %collective-permute-start.3 = (bf16[304,512]{1,0:T(8,128)(2,1)S(1)}, bf16[304,512]{1,0:T(8,128)(2,1)S(1)}, u32[]{:S(2)}, u32[]{:S(2)}) collective-permute-start(bf16[304,512]{1,0:T(8,128)(2,1)S(1)} %collective-permute-done.refs_1_.refs_2_), channel_id=1, source_target_pairs={{0,2},{2,0},{1,3},{3,1},{4,6},{6,4},{5,7},{7,5},{8,10},{10,8},{9,1... | collective-permute-start | bytes 933896 | tf_op jit(solution)/shard_map/ppermute | solution.py:584
  19.9 9.8 %collective-permute-start.2 = (bf16[304,512]{1,0:T(8,128)(2,1)S(1)}, bf16[304,512]{1,0:T(8,128)(2,1)S(1)}, u32[]{:S(2)}, u32[]{:S(2)}) collective-permute-start(bf16[304,512]{1,0:T(8,128)(2,1)S(1)} %collective-permute-done.refs_1_.refs_2_), channel_id=1, source_target_pairs={{0,8},{2,26},{4,12},{6,30},{8,16},{10,2},{12,20},{14,6},{16,24},{1... | collective-permute-start | bytes 933896 | tf_op jit(solution)/shard_map/ppermute | solution.py:597
  29.6 9.7 %collective-permute-start.6 = (bf16[304,512]{1,0:T(8,128)(2,1)S(1)}, bf16[304,512]{1,0:T(8,128)(2,1)S(1)}, u32[]{:S(2)}, u32[]{:S(2)}) collective-permute-start(bf16[304,512]{1,0:T(8,128)(2,1)S(1)} %collective-permute-done.2.refs_3_.refs_6_), channel_id=1, source_target_pairs={{0,4},{4,0},{8,12},{12,8},{16,20},{20,16},{24,28},{28,24},{1,5},{5... | collective-permute-start | bytes 933896 | tf_op jit(solution)/shard_map/ppermute | solution.py:601
  31.2 8.2 %collective-permute-start.5 = (bf16[304,512]{1,0:T(8,128)(2,1)S(1)}, bf16[304,512]{1,0:T(8,128)(2,1)S(1)}, u32[]{:S(2)}, u32[]{:S(2)}) collective-permute-start(bf16[304,512]{1,0:T(8,128)(2,1)S(1)} %collective-permute-done.4.refs_5_.refs_10_), channel_id=1, source_target_pairs={{0,2},{2,0},{1,3},{3,1},{4,6},{6,4},{5,7},{7,5},{8,10},{10,8},{9,1... | collective-permute-start | bytes 933896 | tf_op jit(solution)/shard_map/ppermute | solution.py:584
  31.2 8.2 %collective-permute-start.7 = (bf16[128,1024]{1,0:T(8,128)(2,1)S(1)}, bf16[128,1024]{1,0:T(8,128)(2,1)S(1)}, u32[]{:S(2)}, u32[]{:S(2)}) collective-permute-start(bf16[128,1024]{1,0:T(8,128)(2,1)S(1)} %constant_dynamic-slice_fusion.refs_0_), channel_id=1, source_target_pairs={{0,8},{2,26},{4,12},{6,30},{8,16},{10,2},{12,20},{14,6},{16,24},{1... | collective-permute-start | bytes 786440 | tf_op jit(solution)/shard_map/ppermute | solution.py:597
  46.0 9.1 %collective-permute-start.21 = (bf16[128,1024]{1,0:T(8,128)(2,1)S(1)}, bf16[128,1024]{1,0:T(8,128)(2,1)S(1)}, u32[]{:S(2)}, u32[]{:S(2)}) collective-permute-start(bf16[128,1024]{1,0:T(8,128)(2,1)S(1)} %collective-permute-done.7.refs_2_), channel_id=1, source_target_pairs={{0,2},{2,0},{1,3},{3,1},{4,6},{6,4},{5,7},{7,5},{8,10},{10,8},{9,1... | collective-permute-start | bytes 786440 | tf_op jit(solution)/shard_map/ppermute | solution.py:584
  46.3 8.9 %collective-permute-start.20 = (bf16[128,1024]{1,0:T(8,128)(2,1)S(1)}, bf16[128,1024]{1,0:T(8,128)(2,1)S(1)}, u32[]{:S(2)}, u32[]{:S(2)}) collective-permute-start(bf16[128,1024]{1,0:T(8,128)(2,1)S(1)} %collective-permute-done.7.refs_2_), channel_id=1, source_target_pairs={{0,4},{4,0},{8,12},{12,8},{16,20},{20,16},{24,28},{28,24},{1,5},{5... | collective-permute-start | bytes 786440 | tf_op jit(solution)/shard_map/ppermute | solution.py:601
  47.1 6.0 %collective-permute-start.19 = (f32[3,1024]{1,0:T(4,128)S(1)}, f32[3,1024]{1,0:T(4,128)S(1)}, u32[]{:S(2)}, u32[]{:S(2)}) collective-permute-start(f32[3,1024]{1,0:T(4,128)S(1)} %add.166), channel_id=1, source_target_pairs={{0,24},{2,26},{4,28},{6,30},{8,16},{10,18},{12,20},{14,22},{16,8},... | collective-permute-start | bytes 36872 | tf_op jit(solution)/shard_map/ppermute | solution.py:589
  50.4 4.6 %collective-permute-start.18 = (f32[3,1024]{1,0:T(4,128)S(1)}, f32[3,1024]{1,0:T(4,128)S(1)}, u32[]{:S(2)}, u32[]{:S(2)}) collective-permute-start(f32[3,1024]{1,0:T(4,128)S(1)} %add.166), channel_id=1, source_target_pairs={{0,16},{2,18},{4,20},{6,22},{8,24},{10,26},{12,28},{14,30},{16,0},... | collective-permute-start | bytes 36872 | tf_op jit(solution)/shard_map/ppermute | solution.py:589
  50.4 4.6 %collective-permute-start.17 = (f32[3,1024]{1,0:T(4,128)S(1)}, f32[3,1024]{1,0:T(4,128)S(1)}, u32[]{:S(2)}, u32[]{:S(2)}) collective-permute-start(f32[3,1024]{1,0:T(4,128)S(1)} %add.166), channel_id=1, source_target_pairs={{0,8},{2,10},{4,12},{6,14},{8,0},{10,2},{12,4},{14,6},{16,24},{18,... | collective-permute-start | bytes 36872 | tf_op jit(solution)/shard_map/ppermute | solution.py:589
  55.1 4.7 %collective-permute-start.24 = (f32[3,1024]{1,0:T(4,128)S(1)}, f32[3,1024]{1,0:T(4,128)S(1)}, u32[]{:S(2)}, u32[]{:S(2)}) collective-permute-start(f32[3,1024]{1,0:T(4,128)S(1)} %add_add_fusion.5), channel_id=1, source_target_pairs={{0,6},{2,4},{4,2},{6,0},{8,14},{10,12},{12,10},{14,8},{16,22},{18,... | collective-permute-start | bytes 36872 | tf_op jit(solution)/shard_map/ppermute | solution.py:589
  58.7 8.2 %collective-permute-start.25 = (bf16[128,1024]{1,0:T(8,128)(2,1)S(1)}, bf16[128,1024]{1,0:T(8,128)(2,1)S(1)}, u32[]{:S(2)}, u32[]{:S(2)}) collective-permute-start(bf16[128,1024]{1,0:T(8,128)(2,1)S(1)} %collective-permute-done.7.refs_2_), channel_id=1, source_target_pairs={{0,8},{2,26},{4,12},{6,30},{8,16},{10,2},{12,20},{14,6},{16,24},{1... | collective-permute-start | bytes 786440 | tf_op jit(solution)/shard_map/ppermute | solution.py:597
  61.6 10.6 %collective-permute-start.30 = (bf16[128,1024]{1,0:T(8,128)(2,1)S(1)}, bf16[128,1024]{1,0:T(8,128)(2,1)S(1)}, u32[]{:S(2)}, u32[]{:S(2)}) collective-permute-start(bf16[128,1024]{1,0:T(8,128)(2,1)S(1)} %collective-permute-done.20.refs_10_), channel_id=1, source_target_pairs={{0,2},{2,0},{1,3},{3,1},{4,6},{6,4},{5,7},{7,5},{8,10},{10,8},{9,1... | collective-permute-start | bytes 786440 | tf_op jit(solution)/shard_map/ppermute | solution.py:584
  68.0 6.4 %collective-permute-start.29 = (f32[2,1024]{1,0:T(2,128)S(1)}, f32[2,1024]{1,0:T(2,128)S(1)}, u32[]{:S(2)}, u32[]{:S(2)}) collective-permute-start(f32[2,1024]{1,0:T(2,128)S(1)} %add.173), channel_id=1, source_target_pairs={{0,24},{2,26},{4,28},{6,30},{8,16},{10,18},{12,20},{14,22},{16,8},... | collective-permute-start | bytes 24584 | tf_op jit(solution)/shard_map/ppermute | solution.py:589
  70.1 9.2 %collective-permute-start.31 = (bf16[128,1024]{1,0:T(8,128)(2,1)S(1)}, bf16[128,1024]{1,0:T(8,128)(2,1)S(1)}, u32[]{:S(2)}, u32[]{:S(2)}) collective-permute-start(bf16[128,1024]{1,0:T(8,128)(2,1)S(1)} %constant_dynamic-slice_fusion.refs_0_), channel_id=1, source_target_pairs={{0,4},{4,0},{8,12},{12,8},{16,20},{20,16},{24,28},{28,24},{1,5},{5... | collective-permute-start | bytes 786440 | tf_op jit(solution)/shard_map/ppermute | solution.py:601
  70.6 13.2 %collective-permute-start.32 = (bf16[128,1024]{1,0:T(8,128)(2,1)S(1)}, bf16[128,1024]{1,0:T(8,128)(2,1)S(1)}, u32[]{:S(2)}, u32[]{:S(2)}) collective-permute-start(bf16[128,1024]{1,0:T(8,128)(2,1)S(1)} %collective-permute-done.25.refs_6_), channel_id=1, source_target_pairs={{0,4},{4,0},{8,12},{12,8},{16,20},{20,16},{24,28},{28,24},{1,5},{5... | collective-permute-start | bytes 786440 | tf_op jit(solution)/shard_map/ppermute | solution.py:601
  72.1 4.5 %collective-permute-start.28 = (f32[2,1024]{1,0:T(2,128)S(1)}, f32[2,1024]{1,0:T(2,128)S(1)}, u32[]{:S(2)}, u32[]{:S(2)}) collective-permute-start(f32[2,1024]{1,0:T(2,128)S(1)} %add.173), channel_id=1, source_target_pairs={{0,16},{2,18},{4,20},{6,22},{8,24},{10,26},{12,28},{14,30},{16,0},... | collective-permute-start | bytes 24584 | tf_op jit(solution)/shard_map/ppermute | solution.py:589
  72.1 4.5 %collective-permute-start.27 = (f32[2,1024]{1,0:T(2,128)S(1)}, f32[2,1024]{1,0:T(2,128)S(1)}, u32[]{:S(2)}, u32[]{:S(2)}) collective-permute-start(f32[2,1024]{1,0:T(2,128)S(1)} %add.173), channel_id=1, source_target_pairs={{0,8},{2,10},{4,12},{6,14},{8,0},{10,2},{12,4},{14,6},{16,24},{18,... | collective-permute-start | bytes 24584 | tf_op jit(solution)/shard_map/ppermute | solution.py:589
  74.4 12.6 %collective-permute-start.38 = (bf16[128,1024]{1,0:T(8,128)(2,1)S(1)}, bf16[128,1024]{1,0:T(8,128)(2,1)S(1)}, u32[]{:S(2)}, u32[]{:S(2)}) collective-permute-start(bf16[128,1024]{1,0:T(8,128)(2,1)S(1)} %collective-permute-done.21.refs_4_), channel_id=1, source_target_pairs={{0,1},{1,0},{2,3},{3,2},{4,5},{5,4},{6,7},{7,6},{8,9},{9,8},{10,11... | collective-permute-start | bytes 786440 | tf_op jit(solution)/shard_map/ppermute | solution.py:579
  76.7 10.6 %collective-permute-start.37 = (bf16[128,1024]{1,0:T(8,128)(2,1)S(1)}, bf16[128,1024]{1,0:T(8,128)(2,1)S(1)}, u32[]{:S(2)}, u32[]{:S(2)}) collective-permute-start(bf16[128,1024]{1,0:T(8,128)(2,1)S(1)} %collective-permute-done.7.refs_2_), channel_id=1, source_target_pairs={{0,1},{1,0},{2,3},{3,2},{4,5},{5,4},{6,7},{7,6},{8,9},{9,8},{10,11... | collective-permute-start | bytes 786440 | tf_op jit(solution)/shard_map/ppermute | solution.py:579
  76.7 10.6 %collective-permute-start.41 = (bf16[128,1024]{1,0:T(8,128)(2,1)S(1)}, bf16[128,1024]{1,0:T(8,128)(2,1)S(1)}, u32[]{:S(2)}, u32[]{:S(2)}) collective-permute-start(bf16[128,1024]{1,0:T(8,128)(2,1)S(1)} %collective-permute-done.20.refs_10_), channel_id=1, source_target_pairs={{0,1},{1,0},{2,3},{3,2},{4,5},{5,4},{6,7},{7,6},{8,9},{9,8},{10,11... | collective-permute-start | bytes 786440 | tf_op jit(solution)/shard_map/ppermute | solution.py:579
  83.8 4.5 %collective-permute-start.35 = (f32[2,1024]{1,0:T(2,128)S(1)}, f32[2,1024]{1,0:T(2,128)S(1)}, u32[]{:S(2)}, u32[]{:S(2)}) collective-permute-start(f32[2,1024]{1,0:T(2,128)S(1)} %add_add_fusion.11), channel_id=1, source_target_pairs={{0,6},{2,4},{4,2},{6,0},{8,14},{10,12},{12,10},{14,8},{16,22},{18,... | collective-permute-start | bytes 24584 | tf_op jit(solution)/shard_map/ppermute | solution.py:589
  96.3 4.7 %collective-permute-start.47 = (f32[2,2048]{1,0:T(2,128)S(1)}, f32[2,2048]{1,0:T(2,128)S(1)}, u32[]{:S(2)}, u32[]{:S(2)}) collective-permute-start(f32[2,2048]{1,0:T(2,128)S(1)} %add.180), channel_id=1, source_target_pairs={{0,6},{2,4},{4,2},{6,0},{8,14},{10,12},{12,10},{14,8},{16,22},{18,... | collective-permute-start | bytes 49160 | tf_op jit(solution)/shard_map/ppermute | solution.py:589
  96.5 4.4 %collective-permute-start.46 = (f32[2,2048]{1,0:T(2,128)S(1)}, f32[2,2048]{1,0:T(2,128)S(1)}, u32[]{:S(2)}, u32[]{:S(2)}) collective-permute-start(f32[2,2048]{1,0:T(2,128)S(1)} %add.180), channel_id=1, source_target_pairs={{0,4},{2,6},{4,0},{6,2},{8,12},{10,14},{12,8},{14,10},{16,20},{18,... | collective-permute-start | bytes 49160 | tf_op jit(solution)/shard_map/ppermute | solution.py:589
  101.8 5.6 %collective-permute-start.50 = (f32[2,2048]{1,0:T(2,128)S(1)}, f32[2,2048]{1,0:T(2,128)S(1)}, u32[]{:S(2)}, u32[]{:S(2)}) collective-permute-start(f32[2,2048]{1,0:T(2,128)S(1)} %add_add_fusion.3), channel_id=1, source_target_pairs={{0,24},{2,26},{4,28},{6,30},{8,16},{10,18},{12,20},{14,22},{16,8},... | collective-permute-start | bytes 49160 | tf_op jit(solution)/shard_map/ppermute | solution.py:589
  103.7 4.6 %collective-permute-start.49 = (f32[2,2048]{1,0:T(2,128)S(1)}, f32[2,2048]{1,0:T(2,128)S(1)}, u32[]{:S(2)}, u32[]{:S(2)}) collective-permute-start(f32[2,2048]{1,0:T(2,128)S(1)} %add_add_fusion.3), channel_id=1, source_target_pairs={{0,16},{2,18},{4,20},{6,22},{8,24},{10,26},{12,28},{14,30},{16,0},... | collective-permute-start | bytes 49160 | tf_op jit(solution)/shard_map/ppermute | solution.py:589
  103.7 4.6 %collective-permute-start.48 = (f32[2,2048]{1,0:T(2,128)S(1)}, f32[2,2048]{1,0:T(2,128)S(1)}, u32[]{:S(2)}, u32[]{:S(2)}) collective-permute-start(f32[2,2048]{1,0:T(2,128)S(1)} %add_add_fusion.3), channel_id=1, source_target_pairs={{0,8},{2,10},{4,12},{6,14},{8,0},{10,2},{12,4},{14,6},{16,24},{18,... | collective-permute-start | bytes 49160 | tf_op jit(solution)/shard_map/ppermute | solution.py:589
  113.0 4.7 %collective-permute-start.54 = (f32[2,2048]{1,0:T(2,128)S(1)}, f32[2,2048]{1,0:T(2,128)S(1)}, u32[]{:S(2)}, u32[]{:S(2)}) collective-permute-start(f32[2,2048]{1,0:T(2,128)S(1)} %add.187), channel_id=1, source_target_pairs={{0,6},{2,4},{4,2},{6,0},{8,14},{10,12},{12,10},{14,8},{16,22},{18,... | collective-permute-start | bytes 49160 | tf_op jit(solution)/shard_map/ppermute | solution.py:589
  116.0 3.7 %collective-permute-start.52 = (f32[2,2048]{1,0:T(2,128)S(1)}, f32[2,2048]{1,0:T(2,128)S(1)}, u32[]{:S(2)}, u32[]{:S(2)}) collective-permute-start(f32[2,2048]{1,0:T(2,128)S(1)} %add.187), channel_id=1, source_target_pairs={{0,2},{2,0},{4,6},{6,4},{8,10},{10,8},{12,14},{14,12},{16,18},{18,... | collective-permute-start | bytes 49160 | tf_op jit(solution)/shard_map/ppermute | solution.py:589
  119.7 5.8 %collective-permute-start.57 = (f32[2,2048]{1,0:T(2,128)S(1)}, f32[2,2048]{1,0:T(2,128)S(1)}, u32[]{:S(2)}, u32[]{:S(2)}) collective-permute-start(f32[2,2048]{1,0:T(2,128)S(1)} %add_add_fusion.1), channel_id=1, source_target_pairs={{0,24},{2,26},{4,28},{6,30},{8,16},{10,18},{12,20},{14,22},{16,8},... | collective-permute-start | bytes 49160 | tf_op jit(solution)/shard_map/ppermute | solution.py:589
  122.2 4.6 %collective-permute-start.56 = (f32[2,2048]{1,0:T(2,128)S(1)}, f32[2,2048]{1,0:T(2,128)S(1)}, u32[]{:S(2)}, u32[]{:S(2)}) collective-permute-start(f32[2,2048]{1,0:T(2,128)S(1)} %add_add_fusion.1), channel_id=1, source_target_pairs={{0,16},{2,18},{4,20},{6,22},{8,24},{10,26},{12,28},{14,30},{16,0},... | collective-permute-start | bytes 49160 | tf_op jit(solution)/shard_map/ppermute | solution.py:589
  135.2 5.7 %collective-permute-start.62 = (bf16[1024,1024]{1,0:T(8,128)(2,1)S(1)}, bf16[1024,1024]{1,0:T(8,128)(2,1)S(1)}, u32[]{:S(2)}, u32[]{:S(2)}) collective-permute-start(bf16[1024,1024]{1,0:T(8,128)(2,1)S(1)} %get-tuple-element.197), channel_id=1, source_target_pairs={{0,1},{1,0},{2,3},{3,2},{4,5},{5,4},{6,7},{7,6},{8,9},{9,8},{10,11... | collective-permute-start | bytes 6291464 | tf_op jit(solution)/shard_map/ppermute | solution.py:579
  135.4 4.6 %collective-permute-start.61 = (f32[2,1024]{1,0:T(2,128)S(1)}, f32[2,1024]{1,0:T(2,128)S(1)}, u32[]{:S(2)}, u32[]{:S(2)}) collective-permute-start(f32[2,1024]{1,0:T(2,128)S(1)} %add.194), channel_id=1, source_target_pairs={{0,6},{2,4},{4,2},{6,0},{8,14},{10,12},{12,10},{14,8},{16,22},{18,... | collective-permute-start | bytes 24584 | tf_op jit(solution)/shard_map/ppermute | solution.py:589
  136.0 4.0 %collective-permute-start.60 = (f32[2,1024]{1,0:T(2,128)S(1)}, f32[2,1024]{1,0:T(2,128)S(1)}, u32[]{:S(2)}, u32[]{:S(2)}) collective-permute-start(f32[2,1024]{1,0:T(2,128)S(1)} %add.194), channel_id=1, source_target_pairs={{0,4},{2,6},{4,0},{6,2},{8,12},{10,14},{12,8},{14,10},{16,20},{18,... | collective-permute-start | bytes 24584 | tf_op jit(solution)/shard_map/ppermute | solution.py:589
  141.1 8.3 %collective-permute-start.66 = (bf16[128,1024]{1,0:T(8,128)(2,1)S(1)}, bf16[128,1024]{1,0:T(8,128)(2,1)S(1)}, u32[]{:S(2)}, u32[]{:S(2)}) collective-permute-start(bf16[128,1024]{1,0:T(8,128)(2,1)S(1)} %get-tuple-element.201), channel_id=1, source_target_pairs={{0,2},{2,0},{1,3},{3,1},{4,6},{6,4},{5,7},{7,5},{8,10},{10,8},{9,1... | collective-permute-start | bytes 786440 | tf_op jit(solution)/shard_map/ppermute | solution.py:584
  142.8 6.6 %collective-permute-start.67 = (bf16[128,1024]{1,0:T(8,128)(2,1)S(1)}, bf16[128,1024]{1,0:T(8,128)(2,1)S(1)}, u32[]{:S(2)}, u32[]{:S(2)}) collective-permute-start(bf16[128,1024]{1,0:T(8,128)(2,1)S(1)} %get-tuple-element.202), channel_id=1, source_target_pairs={{0,4},{4,0},{8,12},{12,8},{16,20},{20,16},{24,28},{28,24},{1,5},{5... | collective-permute-start | bytes 786440 | tf_op jit(solution)/shard_map/ppermute | solution.py:601
  143.3 5.4 %collective-permute-start.65 = (f32[2,1024]{1,0:T(2,128)S(1)}, f32[2,1024]{1,0:T(2,128)S(1)}, u32[]{:S(2)}, u32[]{:S(2)}) collective-permute-start(f32[2,1024]{1,0:T(2,128)S(1)} %add_add_fusion.9), channel_id=1, source_target_pairs={{0,24},{2,26},{4,28},{6,30},{8,16},{10,18},{12,20},{14,22},{16,8},... | collective-permute-start | bytes 24584 | tf_op jit(solution)/shard_map/ppermute | solution.py:589
  144.7 4.5 %collective-permute-start.64 = (f32[2,1024]{1,0:T(2,128)S(1)}, f32[2,1024]{1,0:T(2,128)S(1)}, u32[]{:S(2)}, u32[]{:S(2)}) collective-permute-start(f32[2,1024]{1,0:T(2,128)S(1)} %add_add_fusion.9), channel_id=1, source_target_pairs={{0,16},{2,18},{4,20},{6,22},{8,24},{10,26},{12,28},{14,30},{16,0},... | collective-permute-start | bytes 24584 | tf_op jit(solution)/shard_map/ppermute | solution.py:589
  154.1 9.0 %collective-permute-start.72 = (bf16[128,1024]{1,0:T(8,128)(2,1)S(1)}, bf16[128,1024]{1,0:T(8,128)(2,1)S(1)}, u32[]{:S(2)}, u32[]{:S(2)}) collective-permute-start(bf16[128,1024]{1,0:T(8,128)(2,1)S(1)} %get-tuple-element.219), channel_id=1, source_target_pairs={{0,24},{2,10},{4,28},{6,14},{8,0},{10,18},{12,4},{14,22},{16,8},{1... | collective-permute-start | bytes 786440 | tf_op jit(solution)/shard_map/ppermute | solution.py:597
  156.6 5.9 %collective-permute-start.71 = (f32[2,1024]{1,0:T(2,128)S(1)}, f32[2,1024]{1,0:T(2,128)S(1)}, u32[]{:S(2)}, u32[]{:S(2)}) collective-permute-start(f32[2,1024]{1,0:T(2,128)S(1)} %add.201), channel_id=1, source_target_pairs={{0,6},{2,4},{4,2},{6,0},{8,14},{10,12},{12,10},{14,8},{16,22},{18,... | collective-permute-start | bytes 24584 | tf_op jit(solution)/shard_map/ppermute | solution.py:589
  157.5 5.0 %collective-permute-start.70 = (f32[2,1024]{1,0:T(2,128)S(1)}, f32[2,1024]{1,0:T(2,128)S(1)}, u32[]{:S(2)}, u32[]{:S(2)}) collective-permute-start(f32[2,1024]{1,0:T(2,128)S(1)} %add.201), channel_id=1, source_target_pairs={{0,4},{2,6},{4,0},{6,2},{8,12},{10,14},{12,8},{14,10},{16,20},{18,... | collective-permute-start | bytes 24584 | tf_op jit(solution)/shard_map/ppermute | solution.py:589
  158.3 4.2 %collective-permute-start.69 = (f32[2,1024]{1,0:T(2,128)S(1)}, f32[2,1024]{1,0:T(2,128)S(1)}, u32[]{:S(2)}, u32[]{:S(2)}) collective-permute-start(f32[2,1024]{1,0:T(2,128)S(1)} %add.201), channel_id=1, source_target_pairs={{0,2},{2,0},{4,6},{6,4},{8,10},{10,8},{12,14},{14,12},{16,18},{18,... | collective-permute-start | bytes 24584 | tf_op jit(solution)/shard_map/ppermute | solution.py:589
  163.0 5.6 %collective-permute-start.75 = (f32[2,1024]{1,0:T(2,128)S(1)}, f32[2,1024]{1,0:T(2,128)S(1)}, u32[]{:S(2)}, u32[]{:S(2)}) collective-permute-start(f32[2,1024]{1,0:T(2,128)S(1)} %add_add_fusion.7), channel_id=1, source_target_pairs={{0,24},{2,26},{4,28},{6,30},{8,16},{10,18},{12,20},{14,22},{16,8},... | collective-permute-start | bytes 24584 | tf_op jit(solution)/shard_map/ppermute | solution.py:589
  167.0 4.5 %collective-permute-start.74 = (f32[2,1024]{1,0:T(2,128)S(1)}, f32[2,1024]{1,0:T(2,128)S(1)}, u32[]{:S(2)}, u32[]{:S(2)}) collective-permute-start(f32[2,1024]{1,0:T(2,128)S(1)} %add_add_fusion.7), channel_id=1, source_target_pairs={{0,16},{2,18},{4,20},{6,22},{8,24},{10,26},{12,28},{14,30},{16,0},... | collective-permute-start | bytes 24584 | tf_op jit(solution)/shard_map/ppermute | solution.py:589
  167.0 4.5 %collective-permute-start.73 = (f32[2,1024]{1,0:T(2,128)S(1)}, f32[2,1024]{1,0:T(2,128)S(1)}, u32[]{:S(2)}, u32[]{:S(2)}) collective-permute-start(f32[2,1024]{1,0:T(2,128)S(1)} %add_add_fusion.7), channel_id=1, source_target_pairs={{0,8},{2,10},{4,12},{6,14},{8,0},{10,2},{12,4},{14,6},{16,24},{18,... | collective-permute-start | bytes 24584 | tf_op jit(solution)/shard_map/ppermute | solution.py:589
  173.5 23.4 %collective-permute-start.76 = (bf16[6,304,512]{2,1,0:T(8,128)(2,1)S(1)}, bf16[6,304,512]{2,1,0:T(8,128)(2,1)S(1)}, u32[]{:S(2)}, u32[]{:S(2)}) collective-permute-start(bf16[6,304,512]{2,1,0:T(8,128)(2,1)S(1)} %send.1), channel_id=1, source_target_pairs={{0,1},{1,0},{2,3},{3,2},{4,5},{5,4},{6,7},{7,6},{8,9},{9,8},{10,11... | collective-permute-start | bytes 5603336 | tf_op jit(solution)/shard_map/ppermute | solution.py:579
  173.6 4.7 %collective-permute-start.77 = (bf16[2,304,512]{2,1,0:T(8,128)(2,1)S(1)}, bf16[2,304,512]{2,1,0:T(8,128)(2,1)S(1)}, u32[]{:S(2)}, u32[]{:S(2)}) collective-permute-start(bf16[2,304,512]{2,1,0:T(8,128)(2,1)S(1)} %get-tuple-element.226), channel_id=1, source_target_pairs={{0,1},{1,0},{2,3},{3,2},{4,5},{5,4},{6,7},{7,6},{8,9},{9,8},{10,11... | collective-permute-start | bytes 1867784 | tf_op jit(solution)/shard_map/ppermute | solution.py:579
  174.1 9.0 %collective-permute-start.79 = (bf16[128,1024]{1,0:T(8,128)(2,1)S(1)}, bf16[128,1024]{1,0:T(8,128)(2,1)S(1)}, u32[]{:S(2)}, u32[]{:S(2)}) collective-permute-start(bf16[128,1024]{1,0:T(8,128)(2,1)S(1)} %get-tuple-element.229), channel_id=1, source_target_pairs={{0,2},{2,0},{1,3},{3,1},{4,6},{6,4},{5,7},{7,5},{8,10},{10,8},{9,1... | collective-permute-start | bytes 786440 | tf_op jit(solution)/shard_map/ppermute | solution.py:584
  174.8 9.2 %collective-permute-start.80 = (bf16[128,1024]{1,0:T(8,128)(2,1)S(1)}, bf16[128,1024]{1,0:T(8,128)(2,1)S(1)}, u32[]{:S(2)}, u32[]{:S(2)}) collective-permute-start(bf16[128,1024]{1,0:T(8,128)(2,1)S(1)} %get-tuple-element.231), channel_id=1, source_target_pairs={{0,4},{4,0},{8,12},{12,8},{16,20},{20,16},{24,28},{28,24},{1,5},{5... | collective-permute-start | bytes 786440 | tf_op jit(solution)/shard_map/ppermute | solution.py:601
  175.6 12.8 %collective-permute-start.81 = (bf16[128,1024]{1,0:T(8,128)(2,1)S(1)}, bf16[128,1024]{1,0:T(8,128)(2,1)S(1)}, u32[]{:S(2)}, u32[]{:S(2)}) collective-permute-start(bf16[128,1024]{1,0:T(8,128)(2,1)S(1)} %get-tuple-element.232), channel_id=1, source_target_pairs={{0,4},{4,0},{8,12},{12,8},{16,20},{20,16},{24,28},{28,24},{1,5},{5... | collective-permute-start | bytes 786440 | tf_op jit(solution)/shard_map/ppermute | solution.py:601
  178.8 18.2 %collective-permute-start.78 = (bf16[304,512]{1,0:T(8,128)(2,1)S(1)}, bf16[304,512]{1,0:T(8,128)(2,1)S(1)}, u32[]{:S(2)}, u32[]{:S(2)}) collective-permute-start(bf16[304,512]{1,0:T(8,128)(2,1)S(1)} %get-tuple-element.227), channel_id=1, source_target_pairs={{0,2},{2,0},{1,3},{3,1},{4,6},{6,4},{5,7},{7,5},{8,10},{10,8},{9,1... | collective-permute-start | bytes 933896 | tf_op jit(solution)/shard_map/ppermute | solution.py:584
  188.4 8.5 %collective-permute-start.83 = (bf16[304,512]{1,0:T(8,128)(2,1)S(1)}, bf16[304,512]{1,0:T(8,128)(2,1)S(1)}, u32[]{:S(2)}, u32[]{:S(2)}) collective-permute-start(bf16[304,512]{1,0:T(8,128)(2,1)S(1)} %get-tuple-element.233), channel_id=1, source_target_pairs={{0,4},{4,0},{8,12},{12,8},{16,20},{20,16},{24,28},{28,24},{1,5},{5... | collective-permute-start | bytes 933896 | tf_op jit(solution)/shard_map/ppermute | solution.py:601
  189.7 7.2 %collective-permute-start.82 = (bf16[128,1024]{1,0:T(8,128)(2,1)S(1)}, bf16[128,1024]{1,0:T(8,128)(2,1)S(1)}, u32[]{:S(2)}, u32[]{:S(2)}) collective-permute-start(bf16[128,1024]{1,0:T(8,128)(2,1)S(1)} %expand_sum.6), channel_id=1, source_target_pairs={{0,24},{2,10},{4,28},{6,14},{8,0},{10,18},{12,4},{14,22},{16,8},{1... | collective-permute-start | bytes 786440 | tf_op jit(solution)/shard_map/ppermute | solution.py:597
  197.7 8.5 %collective-permute-start.84 = (bf16[304,512]{1,0:T(8,128)(2,1)S(1)}, bf16[304,512]{1,0:T(8,128)(2,1)S(1)}, u32[]{:S(2)}, u32[]{:S(2)}) collective-permute-start(bf16[304,512]{1,0:T(8,128)(2,1)S(1)} %get-tuple-element.239), channel_id=1, source_target_pairs={{0,2},{2,0},{1,3},{3,1},{4,6},{6,4},{5,7},{7,5},{8,10},{10,8},{9,1... | collective-permute-start | bytes 933896 | tf_op jit(solution)/shard_map/ppermute | solution.py:584
  200.9 6.9 %collective-permute-start.86 = (bf16[304,512]{1,0:T(8,128)(2,1)S(1)}, bf16[304,512]{1,0:T(8,128)(2,1)S(1)}, u32[]{:S(2)}, u32[]{:S(2)}) collective-permute-start(bf16[304,512]{1,0:T(8,128)(2,1)S(1)} %get-tuple-element.245), channel_id=1, source_target_pairs={{0,4},{4,0},{8,12},{12,8},{16,20},{20,16},{24,28},{28,24},{1,5},{5... | collective-permute-start | bytes 933896 | tf_op jit(solution)/shard_map/ppermute | solution.py:601
  201.4 7.3 %collective-permute-start.85 = (bf16[304,512]{1,0:T(8,128)(2,1)S(1)}, bf16[304,512]{1,0:T(8,128)(2,1)S(1)}, u32[]{:S(2)}, u32[]{:S(2)}) collective-permute-start(bf16[304,512]{1,0:T(8,128)(2,1)S(1)} %get-tuple-element.241), channel_id=1, source_target_pairs={{0,24},{2,10},{4,28},{6,14},{8,0},{10,18},{12,4},{14,22},{16,8},{1... | collective-permute-start | bytes 933896 | tf_op jit(solution)/shard_map/ppermute | solution.py:597
  209.3 11.6 %collective-permute-start.87 = (bf16[304,512]{1,0:T(8,128)(2,1)S(1)}, bf16[304,512]{1,0:T(8,128)(2,1)S(1)}, u32[]{:S(2)}, u32[]{:S(2)}) collective-permute-start(bf16[304,512]{1,0:T(8,128)(2,1)S(1)} %get-tuple-element.246), channel_id=1, source_target_pairs={{0,24},{2,10},{4,28},{6,14},{8,0},{10,18},{12,4},{14,22},{16,8},{1... | collective-permute-start | bytes 933896 | tf_op jit(solution)/shard_map/ppermute | solution.py:597
  211.9 9.1 %collective-permute-start.89 = (bf16[304,512]{1,0:T(8,128)(2,1)S(1)}, bf16[304,512]{1,0:T(8,128)(2,1)S(1)}, u32[]{:S(2)}, u32[]{:S(2)}) collective-permute-start(bf16[304,512]{1,0:T(8,128)(2,1)S(1)} %get-tuple-element.261), channel_id=1, source_target_pairs={{0,4},{4,0},{8,12},{12,8},{16,20},{20,16},{24,28},{28,24},{1,5},{5... | collective-permute-start | bytes 933896 | tf_op jit(solution)/shard_map/ppermute | solution.py:601
  212.5 8.4 %collective-permute-start.88 = (bf16[128,1024]{1,0:T(8,128)(2,1)S(1)}, bf16[128,1024]{1,0:T(8,128)(2,1)S(1)}, u32[]{:S(2)}, u32[]{:S(2)}) collective-permute-start(bf16[128,1024]{1,0:T(8,128)(2,1)S(1)} %expand_sum.7.mine), channel_id=1, source_target_pairs={{0,2},{2,0},{1,3},{3,1},{4,6},{6,4},{5,7},{7,5},{8,10},{10,8},{9,1... | collective-permute-start | bytes 786440 | tf_op jit(solution)/shard_map/ppermute | solution.py:584
  221.4 7.0 %collective-permute-start.90 = (bf16[304,512]{1,0:T(8,128)(2,1)S(1)}, bf16[304,512]{1,0:T(8,128)(2,1)S(1)}, u32[]{:S(2)}, u32[]{:S(2)}) collective-permute-start(bf16[304,512]{1,0:T(8,128)(2,1)S(1)} %block_sum.7.mine), channel_id=1, source_target_pairs={{0,2},{2,0},{1,3},{3,1},{4,6},{6,4},{5,7},{7,5},{8,10},{10,8},{9,1... | collective-permute-start | bytes 933896 | tf_op jit(solution)/shard_map/ppermute | solution.py:584
  221.4 10.3 %collective-permute-start.91 = (bf16[304,512]{1,0:T(8,128)(2,1)S(1)}, bf16[304,512]{1,0:T(8,128)(2,1)S(1)}, u32[]{:S(2)}, u32[]{:S(2)}) collective-permute-start(bf16[304,512]{1,0:T(8,128)(2,1)S(1)} %block_sum.7.mine), channel_id=1, source_target_pairs={{0,1},{1,0},{2,3},{3,2},{4,5},{5,4},{6,7},{7,6},{8,9},{9,8},{10,11... | collective-permute-start | bytes 933896 | tf_op jit(solution)/shard_map/ppermute | solution.py:579
  (37 other events, 186.3 us)

commit v2 on v1

--- a/solution.py
+++ b/solution.py
@@ -678,7 +678,7 @@
         blocks, (x, expand_own), (turned,), expand_first = gather_blocks(
             own, (x, expand_own), (turned,), lambda early: early[1]
         )
-        moving = [across(expand_first), swap_x(expand_first)]
+        second, other = along(expand_first, 1), across(expand_own)
         slots, slot_depth = size, depth
     else:
         whole = lax.all_gather(own, "fsdp", axis=0, tiled=False)
@@ -720,17 +720,19 @@
         inner_vectors = line[:, : 4 * per].reshape(size, 4, per).transpose(1, 0, 2).reshape(4, width)
         outer_vectors = line[:, 4 * per : 4 * per + 2 * outer].reshape(size, 2, outer)
         outer_vectors = outer_vectors.transpose(1, 0, 2).reshape(2, channels)
-    middle = line_sum(start_sum(part))
+    middle = start_sum(part)
+    if small:
+        middle, other = together(middle, other)
     middle, wide, wide_turned, inner_vectors, outer_vectors = together(
-        middle, wide, wide_turned, inner_vectors, outer_vectors
-    )
-    if small:
-        middle, first_other, passed, expand_first = together(middle, *moving, expand_first)
-        second = along(expand_first, 1)
-    first = plane_sum(middle)
-    if small:
-        first, first_other, expand_own = together(first, first_other, expand_own)
-        moving = [swap_x(first_other), across(expand_own)]
+        plane_sum(middle), wide, wide_turned, inner_vectors, outer_vectors
+    )
+    if small:
+        middle, second, expand_first = together(middle, second, expand_first)
+        first_other, passed = across(expand_first), swap_x(expand_first)
+    first = line_sum(middle)
+    if small:
+        first, first_other, second = together(first, first_other, second)
+        second_other, passed_other = across(second), swap_x(first_other)
     pad_shape = (3, count, (side + 2) * LINE, width)
     pads, grouped, part = call(
         functools.partial(group_kernel, side),
@@ -739,11 +741,10 @@
         name="group", flops=2 * TAPS * rows * width * BLOCK,
     )
     if small:
-        part, second = together(part, second)
-        second_other = across(second)
+        part, passed = together(part, passed)
     middle = line_sum(start_sum(part))
     if small:
-        middle, passed_other, other, second_other = together(middle, *moving, second_other)
+        middle, passed_other, second_other = together(middle, passed_other, second_other)
         expand_weights = []
         for block in (expand_own, expand_first, passed, second, other, first_other, passed_other, second_other):
             expand_weights += [block, swap_core(block)]
@@ -793,7 +794,7 @@
         sums_two, expand_first_other, expand_passed, expand_second, expand_other = together(
             sums_two, *expand_sums(((5, (0,)), (2, ()), (3, (1,)), (4, ())), moving)
         )
-        expand_second = along(expand_second, -1)
+        expand_second, expand_other = along(expand_second, -1), across(expand_other)
     else:
         sums_two = line_sum(middle)
         (chip,) = call(add_kernel, [shape(keep.shape, BF16)], [keep, near_expand], name="add")
@@ -818,8 +819,11 @@
         middle, expand_second, expand_first_other, expand_passed, expand_other = together(
             middle, expand_second, expand_first_other, expand_passed, expand_other
         )
-        moving = [swap_x(expand_passed), expand_second, across(expand_first_other), across(expand_other)]
+        moving = [swap_x(expand_passed), across(expand_first_other)]
     sums_one = line_sum(middle)
+    if small:
+        sums_one, *moving = together(sums_one, *moving)
+        (expand_first_own,) = expand_sums(((1, (0, 1, 2)),), moving + [expand_second])
     tall = depth + extra
     early = (6, 7) if small else tuple(range(size))
     flat_one, send = call(
@@ -870,13 +874,12 @@
         )
         near_late = swap_core(send)
         passed_other, second_other = sums(((6, 0, ()), (7, 1, ())), near)
-        second_other, *expand_moving = together(second_other, *moving)
-        (expand_first_own,) = expand_sums(((1, (0, 1, 2)),), expand_moving[:3])
+        second_other, expand_first_own = together(second_other, expand_first_own)
         moving = [swap_x(passed_other), across(second_other)]
         expand_first_own = along(expand_first_own, -1)
         grad_input = back_input(after(flat_one, second_other))
         moving[0], grad_input, expand_first_own = together(moving[0], grad_input, expand_first_own)
-        (own_expand,) = expand_sums(((0, (0, 1)),), [expand_first_own, expand_moving[3]])
+        (own_expand,) = expand_sums(((0, (0, 1)),), [expand_first_own, expand_other])
         first_other, passed, second = sums(((5, 5, (0,)), (2, 2, ()), (3, 3, (1,))), near_late, moving)
         moving = [swap_x(passed), along(second, -1), across(first_other)]
         output = pinned(after(output, second))

time: 233 us -> 225 us (0.966)
  waiting for transfers between devices: 95.8 us -> 87.6 us
    ppermute x12, waiting for transfers between devices: 22.9 us -> 15.7 us  [across(): return lax.ppermute(values, 'fsdp', [(f, f ^ 1) for f in range(8)])]
    ppermute x29, waiting for transfers between devices: 11.2 us -> 14.5 us  [swap_core(): return lax.ppermute(values, 'core', SWAP)]
  transfers between devices with their start and end apart: 95 -> 95, of which waited for: 57 -> 59; matrix products, arithmetic and copies ran while one was open for 4% -> 4% of each run, Pallas kernels for 7% -> 8%
where the time goes in v2:
time: 225 us
  waiting for transfers between devices  87.6 us (39%)
  starting transfers between devices  83.8 us (37%)
  Pallas kernels  42.1 us (19%)
  local copies, waits for them, and re-layouts  9.64 us (4%)
    ppermute x36, starting transfers between devices, sum_chips(): lax.ppermute(values, CHIPS, [(at, at ^ flip) for at in range(16)])  46.8 us
    pallas_call x26, Pallas kernels, call(): pl.pallas_call(kernel, out_shape=outs, in_specs=[sm] * scalars + [given]...  42.1 us
    ppermute x36, waiting for transfers between devices, sum_chips(): lax.ppermute(values, CHIPS, [(at, at ^ flip) for at in range(16)])  24.5 us
    ppermute x8, waiting for transfers between devices, along(): return lax.ppermute(values, CHIPS, pairs)  18.3 us
    ppermute x12, waiting for transfers between devices, across(): return lax.ppermute(values, 'fsdp', [(f, f ^ 1) for f in range(8)])  15.7 us
    ppermute x10, waiting for transfers between devices, swap_x(): return lax.ppermute(values, 'x', SWAP)  14.6 us
    ppermute x29, waiting for transfers between devices, swap_core(): return lax.ppermute(values, 'core', SWAP)  14.5 us
    ppermute x12, starting transfers between devices, across(): return lax.ppermute(values, 'fsdp', [(f, f ^ 1) for f in range(8)])  14.4 us
  transfers between devices with their start and end apart: 95, of which 59 were waited for; matrix products, arithmetic and copies ran while one was open for 4% of the time, Pallas kernels for 8%

profile of v2, /device:TPU:0, one launch (start us, length us, event | category | flops | bytes accessed | tf_op | source)
XLA Modules:
  0.0 225.3 jit_solution(7280286357703656320)
XLA Ops:
  2.1 2.5 %pack.1 = (bf16[304,512]{1,0:T(8,128)(2,1)}, f32[448,128]{1,0:T(8,128)}) custom-call(s32[2]{0:T(128)} %valid.7, bf16[256,1024]{1,0:T(8,128)(2,1)} %weight.1, bf16[36,1024]{1,0:T(8,128)(2,1)} %group.2, bf16[1,1024]{1,0:T(2,128)(2,1)} %reshape.49.vectors), custom_call_target="tpu_custom_call" | custom-call | bytes 1048576 | tf_op jit(solution)/shard_map/pack/pallas_call | solution.py:55
  4.6 3.0 %collective-permute-start.1 = (bf16[304,512]{1,0:T(8,128)(2,1)}, bf16[304,512]{1,0:T(8,128)(2,1)S(1)}, u32[]{:S(2)}, u32[]{:S(2)}) collective-permute-start(bf16[304,512]{1,0:T(8,128)(2,1)} %get-tuple-element.152.refs_0_), channel_id=1, source_target_pairs={{0,4},{4,0},{8,12},{12,8},{16,20},{20,16},{24,28},{28,24},{1,5},{5... | collective-permute-start | bytes 933896 | tf_op jit(solution)/shard_map/ppermute | solution.py:601
  7.6 1.6 collective-permute-start
  9.2 2.1 copy.31
  11.6 3.6 %collective-permute-done.1.refs_4_.refs_8_ = bf16[304,512]{1,0:T(8,128)(2,1)S(1)} collective-permute-done((bf16[304,512]{1,0:T(8,128)(2,1)}, bf16[304,512]{1,0:T(8,128)(2,1)S(1)}, u32[]{:S(2)}, u32[]{:S(2)}) %collective-permute-start.1) | collective-permute-done | bytes 311328 | tf_op jit(solution)/shard_map/ppermute | solution.py:601
  15.2 3.4 %collective-permute-done.refs_1_.refs_2_ = bf16[304,512]{1,0:T(8,128)(2,1)S(1)} collective-permute-done((bf16[304,512]{1,0:T(8,128)(2,1)}, bf16[304,512]{1,0:T(8,128)(2,1)S(1)}, u32[]{:S(2)}, u32[]{:S(2)}) %collective-permute-start) | collective-permute-done | bytes 311328 | tf_op jit(solution)/shard_map/ppermute | solution.py:597
  20.8 5.7 %collective-permute-done.4.refs_5_.refs_10_ = bf16[304,512]{1,0:T(8,128)(2,1)S(1)} collective-permute-done((bf16[304,512]{1,0:T(8,128)(2,1)S(1)}, bf16[304,512]{1,0:T(8,128)(2,1)S(1)}, u32[]{:S(2)}, u32[]{:S(2)}) %collective-permute-start.4) | collective-permute-done | bytes 311328 | tf_op jit(solution)/shard_map/ppermute | solution.py:601
  27.0 2.7 %collective-permute-done.2.refs_3_.refs_6_ = bf16[304,512]{1,0:T(8,128)(2,1)S(1)} collective-permute-done((bf16[304,512]{1,0:T(8,128)(2,1)S(1)}, bf16[304,512]{1,0:T(8,128)(2,1)S(1)}, u32[]{:S(2)}, u32[]{:S(2)}) %collective-permute-start.2) | collective-permute-done | bytes 311328 | tf_op jit(solution)/shard_map/ppermute | solution.py:597
  29.6 1.5 collective-permute-start.6
  31.2 8.2 %collective-permute-done.7.refs_2_ = bf16[128,1024]{1,0:T(8,128)(2,1)S(1)} collective-permute-done((bf16[128,1024]{1,0:T(8,128)(2,1)S(1)}, bf16[128,1024]{1,0:T(8,128)(2,1)S(1)}, u32[]{:S(2)}, u32[]{:S(2)}) %collective-permute-start.7) | collective-permute-done | bytes 262176 | tf_op jit(solution)/shard_map/ppermute | solution.py:597
  42.9 1.7 reduce.2
  44.6 1.7 reduce.3
  47.5 3.2 %collective-permute-done.17.refs_8_ = bf16[128,1024]{1,0:T(8,128)(2,1)S(1)} collective-permute-done((bf16[128,1024]{1,0:T(8,128)(2,1)S(1)}, bf16[128,1024]{1,0:T(8,128)(2,1)S(1)}, u32[]{:S(2)}, u32[]{:S(2)}) %collective-permute-start.17) | collective-permute-done | bytes 262176 | tf_op jit(solution)/shard_map/ppermute | solution.py:601
  52.4 1.8 collective-permute-start.18
  54.2 1.6 spread.1
  56.8 1.5 collective-permute-start.25
  58.4 1.9 collective-permute-start.24
  60.3 2.4 %collective-permute-start.22 = (f32[3,1024]{1,0:T(4,128)S(1)}, f32[3,1024]{1,0:T(4,128)S(1)}, u32[]{:S(2)}, u32[]{:S(2)}) collective-permute-start(f32[3,1024]{1,0:T(4,128)S(1)} %add_add_fusion.5), channel_id=1, source_target_pairs={{0,8},{2,10},{4,12},{6,14},{8,0},{10,2},{12,4},{14,6},{16,24},{18,... | collective-permute-start | bytes 36872 | tf_op jit(solution)/shard_map/ppermute | solution.py:589
  65.0 3.5 %group.3 = (bf16[3,2,256,1024]{3,2,1,0:T(8,128)(2,1)S(1)}, f32[448,1024]{1,0:T(8,128)S(1)}, f32[2,1024]{1,0:T(2,128)S(1)}) custom-call(f32[448,128]{1,0:T(8,128)S(1)} %copy-done.2, f32[3,1024]{1,0:T(4,128)S(1)} %add_add_fusion.4.total.first, f32[4,1024]{1,0:T(4,128)S(1)} %get-tuple-element.174.vectors.vectors_two, f32[448,1024]{1,0:T(8,128)S(1)} %get-tuple-element.175.red, ...), custom_call_target="tpu_custom_call" | custom-call | flops 2113929216 | bytes 1048576 | tf_op jit(solution)/shard_map/group/pallas_call | solution.py:55
  70.7 2.1 collective-permute-start.30
  72.8 1.7 collective-permute-start.31
  75.0 1.5 collective-permute-start.28
  76.6 2.5 %collective-permute-done.29 = f32[2,1024]{1,0:T(2,128)S(1)} collective-permute-done((f32[2,1024]{1,0:T(2,128)S(1)}, f32[2,1024]{1,0:T(2,128)S(1)}, u32[]{:S(2)}, u32[]{:S(2)}) %collective-permute-start.29) | collective-permute-done | bytes 8224 | tf_op jit(solution)/shard_map/ppermute | solution.py:589
  79.6 1.3 collective-permute-done.31.refs_12_
  80.9 1.5 collective-permute-done.32.refs_14_
  84.1 1.7 collective-permute-start.33
  89.3 2.8 %expand.1 = (bf16[448,1024]{1,0:T(8,128)(2,1)S(1)}, f32[448,2048]{1,0:T(8,128)S(1)}, f32[2,2048]{1,0:T(2,128)S(1)}) custom-call(f32[448,128]{1,0:T(8,128)S(1)} %copy-done.2, f32[2,1024]{1,0:T(2,128)S(1)} %add_add_fusion.10.total.total_two, f32[3,1024]{1,0:T(4,128)S(1)} %add_add_fusion.4.total.first, f32[4,1024]{1,0:T(4,128)S(1)} %get-tuple-element.174.vectors.vectors_two, ...), custom_call_target="tpu_custom_call" | custom-call | flops 1879048192 | bytes 1048576 | tf_op jit(solution)/shard_map/expand/pallas_call | solution.py:55
  93.3 1.7 collective-permute-start.47
  95.1 1.5 collective-permute-start.46
  98.8 1.5 collective-permute-done.45
  100.3 1.9 collective-permute-start.50
  103.2 1.6 collective-permute-start.48
  107.1 3.4 %output.1 = (bf16[2,14,14,2048]{3,2,1,0:T(8,128)(2,1)S(1)}, f32[448,2048]{1,0:T(8,128)S(1)}, f32[2,2048]{1,0:T(2,128)S(1)}) custom-call(s32[2]{0:T(128)S(1)} %copy-done.4, f32[2,2048]{1,0:T(2,128)S(1)} %add_add_fusion.2.total, f32[3,1024]{1,0:T(4,128)S(1)} %add_add_fusion.4.total.first, f32[2,2048]{1,0:T(2,128)S(1)} %get-tuple-element.188.vectors, ...), custom_call_target="tpu_custom_call" | custom-call | bytes 1048576 | tf_op jit(solution)/shard_map/output/pallas_call | solution.py:55
  112.9 1.2 collective-permute-start.53
  117.9 2.2 collective-permute-start.57
  120.4 2.0 collective-permute-start.55
  124.7 4.5 %back_expand.1 = (bf16[448,2048]{1,0:T(8,128)(2,1)S(1)}, f32[448,1024]{1,0:T(8,128)S(1)}, f32[2,1024]{1,0:T(2,128)S(1)}) custom-call(f32[448,128]{1,0:T(8,128)S(1)} %copy-done.2, f32[2,2048]{1,0:T(2,128)S(1)} %add_add_fusion.2.total, f32[2,2048]{1,0:T(2,128)S(1)} %add_add_fusion.sums.refs_2_, f32[3,1024]{1,0:T(4,128)S(1)} %add_add_fusion.4.total.first, ...), custom_call_target="tpu_custom_call" | custom-call | flops 1879048192 | bytes 1048576 | tf_op jit(solution)/shard_map/back_expand/pallas_call | solution.py:55
  130.5 2.4 %weight_expand.1 = (bf16[1024,1024]{1,0:T(8,128)(2,1)S(1)}, bf16[1024,1024]{1,0:T(8,128)(2,1)S(1)}) custom-call(bf16[448,1024]{1,0:T(8,128)(2,1)S(1)} %get-tuple-element.194.act, bf16[448,2048]{1,0:T(8,128)(2,1)S(1)} %get-tuple-element.195.flat), custom_call_target="tpu_custom_call" | custom-call | flops 1879048192 | bytes 1048576 | tf_op jit(solution)/shard_map/weight_expand/pallas_call | solution.py:55
  133.1 1.7 collective-permute-start.61
  134.8 1.5 collective-permute-start.60
  138.5 1.5 collective-permute-done.59
  141.5 1.7 collective-permute-start.65
  144.1 1.8 collective-permute-start.63
  148.2 4.3 %back_group.1 = (bf16[448,1024]{1,0:T(8,128)(2,1)S(1)}, f32[448,1024]{1,0:T(8,128)S(1)}, f32[2,1024]{1,0:T(2,128)S(1)}) custom-call(f32[448,128]{1,0:T(8,128)S(1)} %copy-done.2, f32[2,1024]{1,0:T(2,128)S(1)} %add_add_fusion.10.total.total_two, f32[2,1024]{1,0:T(2,128)S(1)} %add_add_fusion.8.sums.refs_1_, f32[3,1024]{1,0:T(4,128)S(1)} %add_add_fusion.4.total.first, ...), custom_call_target="tpu_custom_call" | custom-call | flops 2113929216 | bytes 1048576 | tf_op jit(solution)/shard_map/back_group/pallas_call | solution.py:55
  152.5 2.3 %collective-permute-start.72 = (bf16[128,1024]{1,0:T(8,128)(2,1)S(1)}, bf16[128,1024]{1,0:T(8,128)(2,1)S(1)}, u32[]{:S(2)}, u32[]{:S(2)}) collective-permute-start(bf16[128,1024]{1,0:T(8,128)(2,1)S(1)} %get-tuple-element.219), channel_id=1, source_target_pairs={{0,24},{2,10},{4,28},{6,14},{8,0},{10,18},{12,4},{14,22},{16,8},{1... | collective-permute-start | bytes 786440 | tf_op jit(solution)/shard_map/ppermute | solution.py:597
  157.1 1.5 collective-permute-start.70
  159.5 2.4 %weight_group.1.group = bf16[8,48,1024]{2,1,0:T(8,128)(2,1)S(1)} custom-call(bf16[3,2,256,1024]{3,2,1,0:T(8,128)(2,1)S(1)} %get-tuple-element.214.pads, bf16[448,1024]{1,0:T(8,128)(2,1)S(1)} %get-tuple-element.216.flat), custom_call_target="tpu_custom_call" | custom-call | flops 2113929216 | bytes 1048576 | tf_op jit(solution)/shard_map/weight_group/pallas_call | solution.py:55
  161.8 1.8 collective-permute-done.70
  164.4 1.5 collective-permute-start.78
  165.9 1.9 collective-permute-start.76
  168.0 2.4 %collective-permute-start.74 = (f32[2,1024]{1,0:T(2,128)S(1)}, f32[2,1024]{1,0:T(2,128)S(1)}, u32[]{:S(2)}, u32[]{:S(2)}) collective-permute-start(f32[2,1024]{1,0:T(2,128)S(1)} %add_add_fusion.7), channel_id=1, source_target_pairs={{0,8},{2,10},{4,12},{6,14},{8,0},{10,2},{12,4},{14,6},{16,24},{18,... | collective-permute-start | bytes 24584 | tf_op jit(solution)/shard_map/ppermute | solution.py:589
  175.1 4.0 %collective-permute-done.80.near = bf16[2,304,512]{2,1,0:T(8,128)(2,1)S(1)} collective-permute-done((bf16[2,304,512]{2,1,0:T(8,128)(2,1)S(1)}, bf16[2,304,512]{2,1,0:T(8,128)(2,1)S(1)}, u32[]{:S(2)}, u32[]{:S(2)}) %collective-permute-start.80) | collective-permute-done | bytes 622624 | tf_op jit(solution)/shard_map/ppermute | solution.py:579
  181.3 2.2 collective-permute-start.82
  183.4 3.2 %grad_input.1 = bf16[2,14,14,2048]{3,2,1,0:T(8,128)(2,1)S(1)} custom-call(bf16[448,1024]{1,0:T(8,128)(2,1)S(1)} %get-tuple-element.236.flat, f32[448,2048]{1,0:T(8,128)S(1)} %get-tuple-element.191.grad, bf16[304,512]{1,0:T(8,128)(2,1)S(1)} %copy-done.3, bf16[304,512]{1,0:T(8,128)(2,1)S(1)} %collective-permute-done.8.refs_0_.refs_1_, ...), custom_call_target="tpu_custom_call" | custom-call | flops 1879048192 | bytes 1048576 | tf_op jit(solution)/shard_map/grad_input/pallas_call | solution.py:55
  186.6 2.5 %collective-permute-done.82.refs_0_ = bf16[128,1024]{1,0:T(8,128)(2,1)S(1)} collective-permute-done((bf16[128,1024]{1,0:T(8,128)(2,1)S(1)}, bf16[128,1024]{1,0:T(8,128)(2,1)S(1)}, u32[]{:S(2)}, u32[]{:S(2)}) %collective-permute-start.82) | collective-permute-done | bytes 262176 | tf_op jit(solution)/shard_map/ppermute | solution.py:597
  190.1 2.8 %collective-permute-start.84 = (bf16[304,512]{1,0:T(8,128)(2,1)S(1)}, bf16[304,512]{1,0:T(8,128)(2,1)S(1)}, u32[]{:S(2)}, u32[]{:S(2)}) collective-permute-start(bf16[304,512]{1,0:T(8,128)(2,1)S(1)} %get-tuple-element.239), channel_id=1, source_target_pairs={{0,2},{2,0},{1,3},{3,1},{4,6},{6,4},{5,7},{7,5},{8,10},{10,8},{9,1... | collective-permute-start | bytes 933896 | tf_op jit(solution)/shard_map/ppermute | solution.py:584
  194.9 2.8 %copy.36 = bf16[2,14,14,2048]{3,0,2,1:T(2,128)(2,1)} copy(bf16[2,14,14,2048]{3,2,1,0:T(8,128)(2,1)S(1)} %get-tuple-element.242) | data formatting | bytes 3211264 | tf_op jit(solution)/shard_map/optimization_barrier | solution.py:40
  197.7 1.3 collective-permute-done.84.refs_0_
  199.0 1.5 collective-permute-done.86.refs_2_
  202.0 2.9 %collective-permute-start.87 = (bf16[304,512]{1,0:T(8,128)(2,1)S(1)}, bf16[304,512]{1,0:T(8,128)(2,1)S(1)}, u32[]{:S(2)}, u32[]{:S(2)}) collective-permute-start(bf16[304,512]{1,0:T(8,128)(2,1)S(1)} %get-tuple-element.246), channel_id=1, source_target_pairs={{0,24},{2,10},{4,28},{6,14},{8,0},{10,18},{12,4},{14,22},{16,8},{1... | collective-permute-start | bytes 933896 | tf_op jit(solution)/shard_map/ppermute | solution.py:597
  206.8 2.8 %copy.35 = bf16[2,14,14,2048]{3,0,2,1:T(2,128)(2,1)} copy(bf16[2,14,14,2048]{3,2,1,0:T(8,128)(2,1)S(1)} %grad_input.1) | data formatting | bytes 3211264 | tf_op jit(solution)/shard_map/optimization_barrier | solution.py:40
  209.6 3.8 %collective-permute-done.88.mine_x = bf16[128,1024]{1,0:T(8,128)(2,1)S(1)} collective-permute-done((bf16[128,1024]{1,0:T(8,128)(2,1)S(1)}, bf16[128,1024]{1,0:T(8,128)(2,1)S(1)}, u32[]{:S(2)}, u32[]{:S(2)}) %collective-permute-start.88) | collective-permute-done | bytes 262176 | tf_op jit(solution)/shard_map/ppermute | solution.py:584
  213.9 6.8 %collective-permute-done.90.mine_x = bf16[304,512]{1,0:T(8,128)(2,1)S(1)} collective-permute-done((bf16[304,512]{1,0:T(8,128)(2,1)S(1)}, bf16[304,512]{1,0:T(8,128)(2,1)S(1)}, u32[]{:S(2)}, u32[]{:S(2)}) %collective-permute-start.90) | collective-permute-done | bytes 311328 | tf_op jit(solution)/shard_map/ppermute | solution.py:584
  221.2 1.5 collective-permute-done.93.other
  (193 shorter events, 67.0 us)
Async XLA Ops:
  4.6 10.6 %collective-permute-start.1 = (bf16[304,512]{1,0:T(8,128)(2,1)}, bf16[304,512]{1,0:T(8,128)(2,1)S(1)}, u32[]{:S(2)}, u32[]{:S(2)}) collective-permute-start(bf16[304,512]{1,0:T(8,128)(2,1)} %get-tuple-element.152.refs_0_), channel_id=1, source_target_pairs={{0,4},{4,0},{8,12},{12,8},{16,20},{20,16},{24,28},{28,24},{1,5},{5... | collective-permute-start | bytes 933896 | tf_op jit(solution)/shard_map/ppermute | solution.py:601
  7.6 10.9 %collective-permute-start = (bf16[304,512]{1,0:T(8,128)(2,1)}, bf16[304,512]{1,0:T(8,128)(2,1)S(1)}, u32[]{:S(2)}, u32[]{:S(2)}) collective-permute-start(bf16[304,512]{1,0:T(8,128)(2,1)} %get-tuple-element.152.refs_0_), channel_id=1, source_target_pairs={{0,8},{2,26},{4,12},{6,30},{8,16},{10,2},{12,20},{14,6},{16,24},{1... | collective-permute-start | bytes 933896 | tf_op jit(solution)/shard_map/ppermute | solution.py:597
  18.5 8.0 %collective-permute-start.4 = (bf16[304,512]{1,0:T(8,128)(2,1)S(1)}, bf16[304,512]{1,0:T(8,128)(2,1)S(1)}, u32[]{:S(2)}, u32[]{:S(2)}) collective-permute-start(bf16[304,512]{1,0:T(8,128)(2,1)S(1)} %collective-permute-done.refs_1_.refs_2_), channel_id=1, source_target_pairs={{0,4},{4,0},{8,12},{12,8},{16,20},{20,16},{24,28},{28,24},{1,5},{5... | collective-permute-start | bytes 933896 | tf_op jit(solution)/shard_map/ppermute | solution.py:601
  19.0 7.9 %collective-permute-start.3 = (bf16[304,512]{1,0:T(8,128)(2,1)S(1)}, bf16[304,512]{1,0:T(8,128)(2,1)S(1)}, u32[]{:S(2)}, u32[]{:S(2)}) collective-permute-start(bf16[304,512]{1,0:T(8,128)(2,1)S(1)} %collective-permute-done.refs_1_.refs_2_), channel_id=1, source_target_pairs={{0,2},{2,0},{1,3},{3,1},{4,6},{6,4},{5,7},{7,5},{8,10},{10,8},{9,1... | collective-permute-start | bytes 933896 | tf_op jit(solution)/shard_map/ppermute | solution.py:584
  19.9 9.8 %collective-permute-start.2 = (bf16[304,512]{1,0:T(8,128)(2,1)S(1)}, bf16[304,512]{1,0:T(8,128)(2,1)S(1)}, u32[]{:S(2)}, u32[]{:S(2)}) collective-permute-start(bf16[304,512]{1,0:T(8,128)(2,1)S(1)} %collective-permute-done.refs_1_.refs_2_), channel_id=1, source_target_pairs={{0,8},{2,26},{4,12},{6,30},{8,16},{10,2},{12,20},{14,6},{16,24},{1... | collective-permute-start | bytes 933896 | tf_op jit(solution)/shard_map/ppermute | solution.py:597
  29.6 9.7 %collective-permute-start.6 = (bf16[304,512]{1,0:T(8,128)(2,1)S(1)}, bf16[304,512]{1,0:T(8,128)(2,1)S(1)}, u32[]{:S(2)}, u32[]{:S(2)}) collective-permute-start(bf16[304,512]{1,0:T(8,128)(2,1)S(1)} %collective-permute-done.2.refs_3_.refs_6_), channel_id=1, source_target_pairs={{0,4},{4,0},{8,12},{12,8},{16,20},{20,16},{24,28},{28,24},{1,5},{5... | collective-permute-start | bytes 933896 | tf_op jit(solution)/shard_map/ppermute | solution.py:601
  31.2 8.2 %collective-permute-start.5 = (bf16[304,512]{1,0:T(8,128)(2,1)S(1)}, bf16[304,512]{1,0:T(8,128)(2,1)S(1)}, u32[]{:S(2)}, u32[]{:S(2)}) collective-permute-start(bf16[304,512]{1,0:T(8,128)(2,1)S(1)} %collective-permute-done.4.refs_5_.refs_10_), channel_id=1, source_target_pairs={{0,2},{2,0},{1,3},{3,1},{4,6},{6,4},{5,7},{7,5},{8,10},{10,8},{9,1... | collective-permute-start | bytes 933896 | tf_op jit(solution)/shard_map/ppermute | solution.py:584
  31.2 8.2 %collective-permute-start.7 = (bf16[128,1024]{1,0:T(8,128)(2,1)S(1)}, bf16[128,1024]{1,0:T(8,128)(2,1)S(1)}, u32[]{:S(2)}, u32[]{:S(2)}) collective-permute-start(bf16[128,1024]{1,0:T(8,128)(2,1)S(1)} %constant_dynamic-slice_fusion.refs_0_), channel_id=1, source_target_pairs={{0,8},{2,26},{4,12},{6,30},{8,16},{10,2},{12,20},{14,6},{16,24},{1... | collective-permute-start | bytes 786440 | tf_op jit(solution)/shard_map/ppermute | solution.py:597
  40.4 4.1 %collective-permute-start.12 = (bf16[304,512]{1,0:T(8,128)(2,1)S(1)}, bf16[304,512]{1,0:T(8,128)(2,1)S(1)}, u32[]{:S(2)}, u32[]{:S(2)}) collective-permute-start(bf16[304,512]{1,0:T(8,128)(2,1)S(1)} %collective-permute-done.1.refs_4_.refs_8_), channel_id=1, source_target_pairs={{0,1},{1,0},{2,3},{3,2},{4,5},{5,4},{6,7},{7,6},{8,9},{9,8},{10,11... | collective-permute-start | bytes 933896 | tf_op jit(solution)/shard_map/ppermute | solution.py:579
  42.4 8.3 %collective-permute-start.17 = (bf16[128,1024]{1,0:T(8,128)(2,1)S(1)}, bf16[128,1024]{1,0:T(8,128)(2,1)S(1)}, u32[]{:S(2)}, u32[]{:S(2)}) collective-permute-start(bf16[128,1024]{1,0:T(8,128)(2,1)S(1)} %constant_dynamic-slice_fusion.refs_0_), channel_id=1, source_target_pairs={{0,4},{4,0},{8,12},{12,8},{16,20},{20,16},{24,28},{28,24},{1,5},{5... | collective-permute-start | bytes 786440 | tf_op jit(solution)/shard_map/ppermute | solution.py:601
  46.3 10.5 %collective-permute-start.21 = (bf16[128,1024]{1,0:T(8,128)(2,1)S(1)}, bf16[128,1024]{1,0:T(8,128)(2,1)S(1)}, u32[]{:S(2)}, u32[]{:S(2)}) collective-permute-start(bf16[128,1024]{1,0:T(8,128)(2,1)S(1)} %collective-permute-done.7.refs_2_), channel_id=1, source_target_pairs={{0,8},{2,26},{4,12},{6,30},{8,16},{10,2},{12,20},{14,6},{16,24},{1... | collective-permute-start | bytes 786440 | tf_op jit(solution)/shard_map/ppermute | solution.py:597
  50.7 5.1 %collective-permute-start.20 = (f32[3,1024]{1,0:T(4,128)S(1)}, f32[3,1024]{1,0:T(4,128)S(1)}, u32[]{:S(2)}, u32[]{:S(2)}) collective-permute-start(f32[3,1024]{1,0:T(4,128)S(1)} %add.166), channel_id=1, source_target_pairs={{0,6},{2,4},{4,2},{6,0},{8,14},{10,12},{12,10},{14,8},{16,22},{18,... | collective-permute-start | bytes 36872 | tf_op jit(solution)/shard_map/ppermute | solution.py:589
  51.3 4.5 %collective-permute-start.19 = (f32[3,1024]{1,0:T(4,128)S(1)}, f32[3,1024]{1,0:T(4,128)S(1)}, u32[]{:S(2)}, u32[]{:S(2)}) collective-permute-start(f32[3,1024]{1,0:T(4,128)S(1)} %add.166), channel_id=1, source_target_pairs={{0,4},{2,6},{4,0},{6,2},{8,12},{10,14},{12,8},{14,10},{16,20},{18,... | collective-permute-start | bytes 36872 | tf_op jit(solution)/shard_map/ppermute | solution.py:589
  56.8 8.1 %collective-permute-start.25 = (bf16[128,1024]{1,0:T(8,128)(2,1)S(1)}, bf16[128,1024]{1,0:T(8,128)(2,1)S(1)}, u32[]{:S(2)}, u32[]{:S(2)}) collective-permute-start(bf16[128,1024]{1,0:T(8,128)(2,1)S(1)} %collective-permute-done.7.refs_2_), channel_id=1, source_target_pairs={{0,4},{4,0},{8,12},{12,8},{16,20},{20,16},{24,28},{28,24},{1,5},{5... | collective-permute-start | bytes 786440 | tf_op jit(solution)/shard_map/ppermute | solution.py:601
  58.4 5.5 %collective-permute-start.24 = (f32[3,1024]{1,0:T(4,128)S(1)}, f32[3,1024]{1,0:T(4,128)S(1)}, u32[]{:S(2)}, u32[]{:S(2)}) collective-permute-start(f32[3,1024]{1,0:T(4,128)S(1)} %add_add_fusion.5), channel_id=1, source_target_pairs={{0,24},{2,26},{4,28},{6,30},{8,16},{10,18},{12,20},{14,22},{16,8},... | collective-permute-start | bytes 36872 | tf_op jit(solution)/shard_map/ppermute | solution.py:589
  60.3 4.6 %collective-permute-start.23 = (f32[3,1024]{1,0:T(4,128)S(1)}, f32[3,1024]{1,0:T(4,128)S(1)}, u32[]{:S(2)}, u32[]{:S(2)}) collective-permute-start(f32[3,1024]{1,0:T(4,128)S(1)} %add_add_fusion.5), channel_id=1, source_target_pairs={{0,16},{2,18},{4,20},{6,22},{8,24},{10,26},{12,28},{14,30},{16,0},... | collective-permute-start | bytes 36872 | tf_op jit(solution)/shard_map/ppermute | solution.py:589
  60.3 4.6 %collective-permute-start.22 = (f32[3,1024]{1,0:T(4,128)S(1)}, f32[3,1024]{1,0:T(4,128)S(1)}, u32[]{:S(2)}, u32[]{:S(2)}) collective-permute-start(f32[3,1024]{1,0:T(4,128)S(1)} %add_add_fusion.5), channel_id=1, source_target_pairs={{0,8},{2,10},{4,12},{6,14},{8,0},{10,2},{12,4},{14,6},{16,24},{18,... | collective-permute-start | bytes 36872 | tf_op jit(solution)/shard_map/ppermute | solution.py:589
  62.8 6.8 %collective-permute-start.26 = (bf16[128,1024]{1,0:T(8,128)(2,1)S(1)}, bf16[128,1024]{1,0:T(8,128)(2,1)S(1)}, u32[]{:S(2)}, u32[]{:S(2)}) collective-permute-start(bf16[128,1024]{1,0:T(8,128)(2,1)S(1)} %collective-permute-done.7.refs_2_), channel_id=1, source_target_pairs={{0,2},{2,0},{1,3},{3,1},{4,6},{6,4},{5,7},{7,5},{8,10},{10,8},{9,1... | collective-permute-start | bytes 786440 | tf_op jit(solution)/shard_map/ppermute | solution.py:584
  70.7 5.9 %collective-permute-start.30 = (f32[2,1024]{1,0:T(2,128)S(1)}, f32[2,1024]{1,0:T(2,128)S(1)}, u32[]{:S(2)}, u32[]{:S(2)}) collective-permute-start(f32[2,1024]{1,0:T(2,128)S(1)} %add.173), channel_id=1, source_target_pairs={{0,24},{2,26},{4,28},{6,30},{8,16},{10,18},{12,20},{14,22},{16,8},... | collective-permute-start | bytes 24584 | tf_op jit(solution)/shard_map/ppermute | solution.py:589
  72.8 8.1 %collective-permute-start.31 = (bf16[128,1024]{1,0:T(8,128)(2,1)S(1)}, bf16[128,1024]{1,0:T(8,128)(2,1)S(1)}, u32[]{:S(2)}, u32[]{:S(2)}) collective-permute-start(bf16[128,1024]{1,0:T(8,128)(2,1)S(1)} %collective-permute-done.25.refs_10_), channel_id=1, source_target_pairs={{0,2},{2,0},{1,3},{3,1},{4,6},{6,4},{5,7},{7,5},{8,10},{10,8},{9,1... | collective-permute-start | bytes 786440 | tf_op jit(solution)/shard_map/ppermute | solution.py:584
  74.5 4.5 %collective-permute-start.29 = (f32[2,1024]{1,0:T(2,128)S(1)}, f32[2,1024]{1,0:T(2,128)S(1)}, u32[]{:S(2)}, u32[]{:S(2)}) collective-permute-start(f32[2,1024]{1,0:T(2,128)S(1)} %add.173), channel_id=1, source_target_pairs={{0,16},{2,18},{4,20},{6,22},{8,24},{10,26},{12,28},{14,30},{16,0},... | collective-permute-start | bytes 24584 | tf_op jit(solution)/shard_map/ppermute | solution.py:589
  74.5 7.8 %collective-permute-start.32 = (bf16[128,1024]{1,0:T(8,128)(2,1)S(1)}, bf16[128,1024]{1,0:T(8,128)(2,1)S(1)}, u32[]{:S(2)}, u32[]{:S(2)}) collective-permute-start(bf16[128,1024]{1,0:T(8,128)(2,1)S(1)} %collective-permute-done.21.refs_6_), channel_id=1, source_target_pairs={{0,4},{4,0},{8,12},{12,8},{16,20},{20,16},{24,28},{28,24},{1,5},{5... | collective-permute-start | bytes 786440 | tf_op jit(solution)/shard_map/ppermute | solution.py:601
  75.0 4.1 %collective-permute-start.28 = (f32[2,1024]{1,0:T(2,128)S(1)}, f32[2,1024]{1,0:T(2,128)S(1)}, u32[]{:S(2)}, u32[]{:S(2)}) collective-permute-start(f32[2,1024]{1,0:T(2,128)S(1)} %add.173), channel_id=1, source_target_pairs={{0,8},{2,10},{4,12},{6,14},{8,0},{10,2},{12,4},{14,6},{16,24},{18,... | collective-permute-start | bytes 24584 | tf_op jit(solution)/shard_map/ppermute | solution.py:589
  76.6 7.5 %collective-permute-start.36 = (bf16[128,1024]{1,0:T(8,128)(2,1)S(1)}, bf16[128,1024]{1,0:T(8,128)(2,1)S(1)}, u32[]{:S(2)}, u32[]{:S(2)}) collective-permute-start(bf16[128,1024]{1,0:T(8,128)(2,1)S(1)} %constant_dynamic-slice_fusion.refs_0_), channel_id=1, source_target_pairs={{0,1},{1,0},{2,3},{3,2},{4,5},{5,4},{6,7},{7,6},{8,9},{9,8},{10,11... | collective-permute-start | bytes 786440 | tf_op jit(solution)/shard_map/ppermute | solution.py:579
  79.1 6.8 %collective-permute-start.40 = (bf16[128,1024]{1,0:T(8,128)(2,1)S(1)}, bf16[128,1024]{1,0:T(8,128)(2,1)S(1)}, u32[]{:S(2)}, u32[]{:S(2)}) collective-permute-start(bf16[128,1024]{1,0:T(8,128)(2,1)S(1)} %collective-permute-done.17.refs_8_), channel_id=1, source_target_pairs={{0,1},{1,0},{2,3},{3,2},{4,5},{5,4},{6,7},{7,6},{8,9},{9,8},{10,11... | collective-permute-start | bytes 786440 | tf_op jit(solution)/shard_map/ppermute | solution.py:579
  79.1 6.8 %collective-permute-start.37 = (bf16[128,1024]{1,0:T(8,128)(2,1)S(1)}, bf16[128,1024]{1,0:T(8,128)(2,1)S(1)}, u32[]{:S(2)}, u32[]{:S(2)}) collective-permute-start(bf16[128,1024]{1,0:T(8,128)(2,1)S(1)} %collective-permute-done.7.refs_2_), channel_id=1, source_target_pairs={{0,1},{1,0},{2,3},{3,2},{4,5},{5,4},{6,7},{7,6},{8,9},{9,8},{10,11... | collective-permute-start | bytes 786440 | tf_op jit(solution)/shard_map/ppermute | solution.py:579
  82.3 4.5 %collective-permute-start.35 = (f32[2,1024]{1,0:T(2,128)S(1)}, f32[2,1024]{1,0:T(2,128)S(1)}, u32[]{:S(2)}, u32[]{:S(2)}) collective-permute-start(f32[2,1024]{1,0:T(2,128)S(1)} %add_add_fusion.11), channel_id=1, source_target_pairs={{0,6},{2,4},{4,2},{6,0},{8,14},{10,12},{12,10},{14,8},{16,22},{18,... | collective-permute-start | bytes 24584 | tf_op jit(solution)/shard_map/ppermute | solution.py:589
  93.3 4.7 %collective-permute-start.47 = (f32[2,2048]{1,0:T(2,128)S(1)}, f32[2,2048]{1,0:T(2,128)S(1)}, u32[]{:S(2)}, u32[]{:S(2)}) collective-permute-start(f32[2,2048]{1,0:T(2,128)S(1)} %add.180), channel_id=1, source_target_pairs={{0,6},{2,4},{4,2},{6,0},{8,14},{10,12},{12,10},{14,8},{16,22},{18,... | collective-permute-start | bytes 49160 | tf_op jit(solution)/shard_map/ppermute | solution.py:589
  100.3 5.6 %collective-permute-start.50 = (f32[2,2048]{1,0:T(2,128)S(1)}, f32[2,2048]{1,0:T(2,128)S(1)}, u32[]{:S(2)}, u32[]{:S(2)}) collective-permute-start(f32[2,2048]{1,0:T(2,128)S(1)} %add_add_fusion.3), channel_id=1, source_target_pairs={{0,24},{2,26},{4,28},{6,30},{8,16},{10,18},{12,20},{14,22},{16,8},... | collective-permute-start | bytes 49160 | tf_op jit(solution)/shard_map/ppermute | solution.py:589
  102.3 4.6 %collective-permute-start.49 = (f32[2,2048]{1,0:T(2,128)S(1)}, f32[2,2048]{1,0:T(2,128)S(1)}, u32[]{:S(2)}, u32[]{:S(2)}) collective-permute-start(f32[2,2048]{1,0:T(2,128)S(1)} %add_add_fusion.3), channel_id=1, source_target_pairs={{0,16},{2,18},{4,20},{6,22},{8,24},{10,26},{12,28},{14,30},{16,0},... | collective-permute-start | bytes 49160 | tf_op jit(solution)/shard_map/ppermute | solution.py:589
  103.2 3.9 %collective-permute-start.48 = (f32[2,2048]{1,0:T(2,128)S(1)}, f32[2,2048]{1,0:T(2,128)S(1)}, u32[]{:S(2)}, u32[]{:S(2)}) collective-permute-start(f32[2,2048]{1,0:T(2,128)S(1)} %add_add_fusion.3), channel_id=1, source_target_pairs={{0,8},{2,10},{4,12},{6,14},{8,0},{10,2},{12,4},{14,6},{16,24},{18,... | collective-permute-start | bytes 49160 | tf_op jit(solution)/shard_map/ppermute | solution.py:589
  111.8 4.7 %collective-permute-start.54 = (f32[2,2048]{1,0:T(2,128)S(1)}, f32[2,2048]{1,0:T(2,128)S(1)}, u32[]{:S(2)}, u32[]{:S(2)}) collective-permute-start(f32[2,2048]{1,0:T(2,128)S(1)} %add.187), channel_id=1, source_target_pairs={{0,6},{2,4},{4,2},{6,0},{8,14},{10,12},{12,10},{14,8},{16,22},{18,... | collective-permute-start | bytes 49160 | tf_op jit(solution)/shard_map/ppermute | solution.py:589
  117.9 5.6 %collective-permute-start.57 = (f32[2,2048]{1,0:T(2,128)S(1)}, f32[2,2048]{1,0:T(2,128)S(1)}, u32[]{:S(2)}, u32[]{:S(2)}) collective-permute-start(f32[2,2048]{1,0:T(2,128)S(1)} %add_add_fusion.1), channel_id=1, source_target_pairs={{0,24},{2,26},{4,28},{6,30},{8,16},{10,18},{12,20},{14,22},{16,8},... | collective-permute-start | bytes 49160 | tf_op jit(solution)/shard_map/ppermute | solution.py:589
  120.1 4.6 %collective-permute-start.56 = (f32[2,2048]{1,0:T(2,128)S(1)}, f32[2,2048]{1,0:T(2,128)S(1)}, u32[]{:S(2)}, u32[]{:S(2)}) collective-permute-start(f32[2,2048]{1,0:T(2,128)S(1)} %add_add_fusion.1), channel_id=1, source_target_pairs={{0,16},{2,18},{4,20},{6,22},{8,24},{10,26},{12,28},{14,30},{16,0},... | collective-permute-start | bytes 49160 | tf_op jit(solution)/shard_map/ppermute | solution.py:589
  120.4 4.3 %collective-permute-start.55 = (f32[2,2048]{1,0:T(2,128)S(1)}, f32[2,2048]{1,0:T(2,128)S(1)}, u32[]{:S(2)}, u32[]{:S(2)}) collective-permute-start(f32[2,2048]{1,0:T(2,128)S(1)} %add_add_fusion.1), channel_id=1, source_target_pairs={{0,8},{2,10},{4,12},{6,14},{8,0},{10,2},{12,4},{14,6},{16,24},{18,... | collective-permute-start | bytes 49160 | tf_op jit(solution)/shard_map/ppermute | solution.py:589
  132.9 7.1 %collective-permute-start.62 = (bf16[1024,1024]{1,0:T(8,128)(2,1)S(1)}, bf16[1024,1024]{1,0:T(8,128)(2,1)S(1)}, u32[]{:S(2)}, u32[]{:S(2)}) collective-permute-start(bf16[1024,1024]{1,0:T(8,128)(2,1)S(1)} %get-tuple-element.197), channel_id=1, source_target_pairs={{0,1},{1,0},{2,3},{3,2},{4,5},{5,4},{6,7},{7,6},{8,9},{9,8},{10,11... | collective-permute-start | bytes 6291464 | tf_op jit(solution)/shard_map/ppermute | solution.py:579
  133.1 4.5 %collective-permute-start.61 = (f32[2,1024]{1,0:T(2,128)S(1)}, f32[2,1024]{1,0:T(2,128)S(1)}, u32[]{:S(2)}, u32[]{:S(2)}) collective-permute-start(f32[2,1024]{1,0:T(2,128)S(1)} %add.194), channel_id=1, source_target_pairs={{0,6},{2,4},{4,2},{6,0},{8,14},{10,12},{12,10},{14,8},{16,22},{18,... | collective-permute-start | bytes 24584 | tf_op jit(solution)/shard_map/ppermute | solution.py:589
  140.2 7.7 %collective-permute-start.66 = (bf16[128,1024]{1,0:T(8,128)(2,1)S(1)}, bf16[128,1024]{1,0:T(8,128)(2,1)S(1)}, u32[]{:S(2)}, u32[]{:S(2)}) collective-permute-start(bf16[128,1024]{1,0:T(8,128)(2,1)S(1)} %get-tuple-element.201), channel_id=1, source_target_pairs={{0,2},{2,0},{1,3},{3,1},{4,6},{6,4},{5,7},{7,5},{8,10},{10,8},{9,1... | collective-permute-start | bytes 786440 | tf_op jit(solution)/shard_map/ppermute | solution.py:584
  140.5 7.3 %collective-permute-start.67 = (bf16[128,1024]{1,0:T(8,128)(2,1)S(1)}, bf16[128,1024]{1,0:T(8,128)(2,1)S(1)}, u32[]{:S(2)}, u32[]{:S(2)}) collective-permute-start(bf16[128,1024]{1,0:T(8,128)(2,1)S(1)} %get-tuple-element.202), channel_id=1, source_target_pairs={{0,4},{4,0},{8,12},{12,8},{16,20},{20,16},{24,28},{28,24},{1,5},{5... | collective-permute-start | bytes 786440 | tf_op jit(solution)/shard_map/ppermute | solution.py:601
  141.5 5.4 %collective-permute-start.65 = (f32[2,1024]{1,0:T(2,128)S(1)}, f32[2,1024]{1,0:T(2,128)S(1)}, u32[]{:S(2)}, u32[]{:S(2)}) collective-permute-start(f32[2,1024]{1,0:T(2,128)S(1)} %add_add_fusion.9), channel_id=1, source_target_pairs={{0,24},{2,26},{4,28},{6,30},{8,16},{10,18},{12,20},{14,22},{16,8},... | collective-permute-start | bytes 24584 | tf_op jit(solution)/shard_map/ppermute | solution.py:589
  143.2 4.5 %collective-permute-start.64 = (f32[2,1024]{1,0:T(2,128)S(1)}, f32[2,1024]{1,0:T(2,128)S(1)}, u32[]{:S(2)}, u32[]{:S(2)}) collective-permute-start(f32[2,1024]{1,0:T(2,128)S(1)} %add_add_fusion.9), channel_id=1, source_target_pairs={{0,16},{2,18},{4,20},{6,22},{8,24},{10,26},{12,28},{14,30},{16,0},... | collective-permute-start | bytes 24584 | tf_op jit(solution)/shard_map/ppermute | solution.py:589
  152.5 11.1 %collective-permute-start.72 = (bf16[128,1024]{1,0:T(8,128)(2,1)S(1)}, bf16[128,1024]{1,0:T(8,128)(2,1)S(1)}, u32[]{:S(2)}, u32[]{:S(2)}) collective-permute-start(bf16[128,1024]{1,0:T(8,128)(2,1)S(1)} %get-tuple-element.219), channel_id=1, source_target_pairs={{0,24},{2,10},{4,28},{6,14},{8,0},{10,18},{12,4},{14,22},{16,8},{1... | collective-permute-start | bytes 786440 | tf_op jit(solution)/shard_map/ppermute | solution.py:597
  154.9 8.8 %collective-permute-start.73 = (bf16[128,1024]{1,0:T(8,128)(2,1)S(1)}, bf16[128,1024]{1,0:T(8,128)(2,1)S(1)}, u32[]{:S(2)}, u32[]{:S(2)}) collective-permute-start(bf16[128,1024]{1,0:T(8,128)(2,1)S(1)} %get-tuple-element.222), channel_id=1, source_target_pairs={{0,4},{4,0},{8,12},{12,8},{16,20},{20,16},{24,28},{28,24},{1,5},{5... | collective-permute-start | bytes 786440 | tf_op jit(solution)/shard_map/ppermute | solution.py:601
  155.9 5.9 %collective-permute-start.71 = (f32[2,1024]{1,0:T(2,128)S(1)}, f32[2,1024]{1,0:T(2,128)S(1)}, u32[]{:S(2)}, u32[]{:S(2)}) collective-permute-start(f32[2,1024]{1,0:T(2,128)S(1)} %add.201), channel_id=1, source_target_pairs={{0,6},{2,4},{4,2},{6,0},{8,14},{10,12},{12,10},{14,8},{16,22},{18,... | collective-permute-start | bytes 24584 | tf_op jit(solution)/shard_map/ppermute | solution.py:589
  157.1 6.5 %collective-permute-start.70 = (f32[2,1024]{1,0:T(2,128)S(1)}, f32[2,1024]{1,0:T(2,128)S(1)}, u32[]{:S(2)}, u32[]{:S(2)}) collective-permute-start(f32[2,1024]{1,0:T(2,128)S(1)} %add.201), channel_id=1, source_target_pairs={{0,4},{2,6},{4,0},{6,2},{8,12},{10,14},{12,8},{14,10},{16,20},{18,... | collective-permute-start | bytes 24584 | tf_op jit(solution)/shard_map/ppermute | solution.py:589
  158.6 5.0 %collective-permute-start.69 = (f32[2,1024]{1,0:T(2,128)S(1)}, f32[2,1024]{1,0:T(2,128)S(1)}, u32[]{:S(2)}, u32[]{:S(2)}) collective-permute-start(f32[2,1024]{1,0:T(2,128)S(1)} %add.201), channel_id=1, source_target_pairs={{0,2},{2,0},{4,6},{6,4},{8,10},{10,8},{12,14},{14,12},{16,18},{18,... | collective-permute-start | bytes 24584 | tf_op jit(solution)/shard_map/ppermute | solution.py:589
  163.6 8.8 %collective-permute-start.77 = (bf16[128,1024]{1,0:T(8,128)(2,1)S(1)}, bf16[128,1024]{1,0:T(8,128)(2,1)S(1)}, u32[]{:S(2)}, u32[]{:S(2)}) collective-permute-start(bf16[128,1024]{1,0:T(8,128)(2,1)S(1)} %get-tuple-element.224), channel_id=1, source_target_pairs={{0,2},{2,0},{1,3},{3,1},{4,6},{6,4},{5,7},{7,5},{8,10},{10,8},{9,1... | collective-permute-start | bytes 786440 | tf_op jit(solution)/shard_map/ppermute | solution.py:584
  164.4 8.0 %collective-permute-start.78 = (bf16[128,1024]{1,0:T(8,128)(2,1)S(1)}, bf16[128,1024]{1,0:T(8,128)(2,1)S(1)}, u32[]{:S(2)}, u32[]{:S(2)}) collective-permute-start(bf16[128,1024]{1,0:T(8,128)(2,1)S(1)} %get-tuple-element.225), channel_id=1, source_target_pairs={{0,4},{4,0},{8,12},{12,8},{16,20},{20,16},{24,28},{28,24},{1,5},{5... | collective-permute-start | bytes 786440 | tf_op jit(solution)/shard_map/ppermute | solution.py:601
  165.9 5.4 %collective-permute-start.76 = (f32[2,1024]{1,0:T(2,128)S(1)}, f32[2,1024]{1,0:T(2,128)S(1)}, u32[]{:S(2)}, u32[]{:S(2)}) collective-permute-start(f32[2,1024]{1,0:T(2,128)S(1)} %add_add_fusion.7), channel_id=1, source_target_pairs={{0,24},{2,26},{4,28},{6,30},{8,16},{10,18},{12,20},{14,22},{16,8},... | collective-permute-start | bytes 24584 | tf_op jit(solution)/shard_map/ppermute | solution.py:589
  167.8 4.5 %collective-permute-start.75 = (f32[2,1024]{1,0:T(2,128)S(1)}, f32[2,1024]{1,0:T(2,128)S(1)}, u32[]{:S(2)}, u32[]{:S(2)}) collective-permute-start(f32[2,1024]{1,0:T(2,128)S(1)} %add_add_fusion.7), channel_id=1, source_target_pairs={{0,16},{2,18},{4,20},{6,22},{8,24},{10,26},{12,28},{14,30},{16,0},... | collective-permute-start | bytes 24584 | tf_op jit(solution)/shard_map/ppermute | solution.py:589
  168.0 4.4 %collective-permute-start.74 = (f32[2,1024]{1,0:T(2,128)S(1)}, f32[2,1024]{1,0:T(2,128)S(1)}, u32[]{:S(2)}, u32[]{:S(2)}) collective-permute-start(f32[2,1024]{1,0:T(2,128)S(1)} %add_add_fusion.7), channel_id=1, source_target_pairs={{0,8},{2,10},{4,12},{6,14},{8,0},{10,2},{12,4},{14,6},{16,24},{18,... | collective-permute-start | bytes 24584 | tf_op jit(solution)/shard_map/ppermute | solution.py:589
  174.4 15.0 %collective-permute-start.79 = (bf16[6,304,512]{2,1,0:T(8,128)(2,1)S(1)}, bf16[6,304,512]{2,1,0:T(8,128)(2,1)S(1)}, u32[]{:S(2)}, u32[]{:S(2)}) collective-permute-start(bf16[6,304,512]{2,1,0:T(8,128)(2,1)S(1)} %send.1), channel_id=1, source_target_pairs={{0,1},{1,0},{2,3},{3,2},{4,5},{5,4},{6,7},{7,6},{8,9},{9,8},{10,11... | collective-permute-start | bytes 5603336 | tf_op jit(solution)/shard_map/ppermute | solution.py:579
  174.4 4.7 %collective-permute-start.80 = (bf16[2,304,512]{2,1,0:T(8,128)(2,1)S(1)}, bf16[2,304,512]{2,1,0:T(8,128)(2,1)S(1)}, u32[]{:S(2)}, u32[]{:S(2)}) collective-permute-start(bf16[2,304,512]{2,1,0:T(8,128)(2,1)S(1)} %get-tuple-element.229), channel_id=1, source_target_pairs={{0,1},{1,0},{2,3},{3,2},{4,5},{5,4},{6,7},{7,6},{8,9},{9,8},{10,11... | collective-permute-start | bytes 1867784 | tf_op jit(solution)/shard_map/ppermute | solution.py:579
  179.6 9.5 %collective-permute-start.81 = (bf16[304,512]{1,0:T(8,128)(2,1)S(1)}, bf16[304,512]{1,0:T(8,128)(2,1)S(1)}, u32[]{:S(2)}, u32[]{:S(2)}) collective-permute-start(bf16[304,512]{1,0:T(8,128)(2,1)S(1)} %get-tuple-element.230), channel_id=1, source_target_pairs={{0,2},{2,0},{1,3},{3,1},{4,6},{6,4},{5,7},{7,5},{8,10},{10,8},{9,1... | collective-permute-start | bytes 933896 | tf_op jit(solution)/shard_map/ppermute | solution.py:584
  180.3 9.1 %collective-permute-start.83 = (bf16[304,512]{1,0:T(8,128)(2,1)S(1)}, bf16[304,512]{1,0:T(8,128)(2,1)S(1)}, u32[]{:S(2)}, u32[]{:S(2)}) collective-permute-start(bf16[304,512]{1,0:T(8,128)(2,1)S(1)} %get-tuple-element.235), channel_id=1, source_target_pairs={{0,4},{4,0},{8,12},{12,8},{16,20},{20,16},{24,28},{28,24},{1,5},{5... | collective-permute-start | bytes 933896 | tf_op jit(solution)/shard_map/ppermute | solution.py:601
  181.3 7.9 %collective-permute-start.82 = (bf16[128,1024]{1,0:T(8,128)(2,1)S(1)}, bf16[128,1024]{1,0:T(8,128)(2,1)S(1)}, u32[]{:S(2)}, u32[]{:S(2)}) collective-permute-start(bf16[128,1024]{1,0:T(8,128)(2,1)S(1)} %expand_sum.6), channel_id=1, source_target_pairs={{0,24},{2,10},{4,28},{6,14},{8,0},{10,18},{12,4},{14,22},{16,8},{1... | collective-permute-start | bytes 786440 | tf_op jit(solution)/shard_map/ppermute | solution.py:597
  190.1 9.0 %collective-permute-start.84 = (bf16[304,512]{1,0:T(8,128)(2,1)S(1)}, bf16[304,512]{1,0:T(8,128)(2,1)S(1)}, u32[]{:S(2)}, u32[]{:S(2)}) collective-permute-start(bf16[304,512]{1,0:T(8,128)(2,1)S(1)} %get-tuple-element.239), channel_id=1, source_target_pairs={{0,2},{2,0},{1,3},{3,1},{4,6},{6,4},{5,7},{7,5},{8,10},{10,8},{9,1... | collective-permute-start | bytes 933896 | tf_op jit(solution)/shard_map/ppermute | solution.py:584
  192.9 7.6 %collective-permute-start.86 = (bf16[304,512]{1,0:T(8,128)(2,1)S(1)}, bf16[304,512]{1,0:T(8,128)(2,1)S(1)}, u32[]{:S(2)}, u32[]{:S(2)}) collective-permute-start(bf16[304,512]{1,0:T(8,128)(2,1)S(1)} %get-tuple-element.245), channel_id=1, source_target_pairs={{0,4},{4,0},{8,12},{12,8},{16,20},{20,16},{24,28},{28,24},{1,5},{5... | collective-permute-start | bytes 933896 | tf_op jit(solution)/shard_map/ppermute | solution.py:601
  194.1 7.4 %collective-permute-start.85 = (bf16[304,512]{1,0:T(8,128)(2,1)S(1)}, bf16[304,512]{1,0:T(8,128)(2,1)S(1)}, u32[]{:S(2)}, u32[]{:S(2)}) collective-permute-start(bf16[304,512]{1,0:T(8,128)(2,1)S(1)} %get-tuple-element.241), channel_id=1, source_target_pairs={{0,24},{2,10},{4,28},{6,14},{8,0},{10,18},{12,4},{14,22},{16,8},{1... | collective-permute-start | bytes 933896 | tf_op jit(solution)/shard_map/ppermute | solution.py:597
  202.0 11.3 %collective-permute-start.87 = (bf16[304,512]{1,0:T(8,128)(2,1)S(1)}, bf16[304,512]{1,0:T(8,128)(2,1)S(1)}, u32[]{:S(2)}, u32[]{:S(2)}) collective-permute-start(bf16[304,512]{1,0:T(8,128)(2,1)S(1)} %get-tuple-element.246), channel_id=1, source_target_pairs={{0,24},{2,10},{4,28},{6,14},{8,0},{10,18},{12,4},{14,22},{16,8},{1... | collective-permute-start | bytes 933896 | tf_op jit(solution)/shard_map/ppermute | solution.py:597
  204.9 8.4 %collective-permute-start.89 = (bf16[304,512]{1,0:T(8,128)(2,1)S(1)}, bf16[304,512]{1,0:T(8,128)(2,1)S(1)}, u32[]{:S(2)}, u32[]{:S(2)}) collective-permute-start(bf16[304,512]{1,0:T(8,128)(2,1)S(1)} %get-tuple-element.261), channel_id=1, source_target_pairs={{0,4},{4,0},{8,12},{12,8},{16,20},{20,16},{24,28},{28,24},{1,5},{5... | collective-permute-start | bytes 933896 | tf_op jit(solution)/shard_map/ppermute | solution.py:601
  206.1 7.3 %collective-permute-start.88 = (bf16[128,1024]{1,0:T(8,128)(2,1)S(1)}, bf16[128,1024]{1,0:T(8,128)(2,1)S(1)}, u32[]{:S(2)}, u32[]{:S(2)}) collective-permute-start(bf16[128,1024]{1,0:T(8,128)(2,1)S(1)} %expand_sum.7.mine), channel_id=1, source_target_pairs={{0,2},{2,0},{1,3},{3,1},{4,6},{6,4},{5,7},{7,5},{8,10},{10,8},{9,1... | collective-permute-start | bytes 786440 | tf_op jit(solution)/shard_map/ppermute | solution.py:584
  213.7 7.0 %collective-permute-start.90 = (bf16[304,512]{1,0:T(8,128)(2,1)S(1)}, bf16[304,512]{1,0:T(8,128)(2,1)S(1)}, u32[]{:S(2)}, u32[]{:S(2)}) collective-permute-start(bf16[304,512]{1,0:T(8,128)(2,1)S(1)} %block_sum.7.mine), channel_id=1, source_target_pairs={{0,2},{2,0},{1,3},{3,1},{4,6},{6,4},{5,7},{7,5},{8,10},{10,8},{9,1... | collective-permute-start | bytes 933896 | tf_op jit(solution)/shard_map/ppermute | solution.py:584
  213.8 10.3 %collective-permute-start.91 = (bf16[304,512]{1,0:T(8,128)(2,1)S(1)}, bf16[304,512]{1,0:T(8,128)(2,1)S(1)}, u32[]{:S(2)}, u32[]{:S(2)}) collective-permute-start(bf16[304,512]{1,0:T(8,128)(2,1)S(1)} %block_sum.7.mine), channel_id=1, source_target_pairs={{0,1},{1,0},{2,3},{3,2},{4,5},{5,4},{6,7},{7,6},{8,9},{9,8},{10,11... | collective-permute-start | bytes 933896 | tf_op jit(solution)/shard_map/ppermute | solution.py:579
  (37 other events, 189.4 us)

commit v3 on v2

v3 whole, which is shorter than its diff:
```python
import functools

import jax
import jax.numpy as jnp
from jax import lax
from jax.experimental import pallas as pl
from jax.experimental.pallas import tpu as pltpu
from jax.sharding import Mesh
from jax.sharding import PartitionSpec as P

GROUPS = 32
TAPS = 9
LINE = 16
CHUNK = 512
UNROLL = 7
LANES = 128
BLOCK = 256
epsilon = 1e-05
BF16, F32 = jnp.bfloat16, jnp.float32
SWAP = [(0, 1), (1, 0)]
NN, NT = ((1,), (0,)), ((1,), (1,))
CHIPS = ("fsdp", "x")


def silu_half(half):
    return half + half * jnp.tanh(half)


def dsilu_twice(half):
    turned = jnp.tanh(half)
    upper = 1.0 + turned
    return upper * (1.0 + half * (1.0 - turned)), upper


def dot(a, b, contract=NN):
    return lax.dot_general(a, b, (contract, ((), ())), preferred_element_type=F32)


def after(values, *others):
    return lax.optimization_barrier((values,) + others)[0]


def together(*values):
    return lax.optimization_barrier(values)


def shape(dims, dtype):
    return jax.ShapeDtypeStruct(dims, dtype)


def call(kernel, outs, args, scalars=0, scratch=(), vmem=8, name=None, flops=0, anywhere=False, aliases=()):
    vm = pl.BlockSpec(memory_space=pltpu.VMEM)
    given = pl.BlockSpec(memory_space=pl.ANY) if anywhere else vm
    sm = pl.BlockSpec(memory_space=pltpu.SMEM)
    return pl.pallas_call(
        kernel,
        out_shape=outs,
        in_specs=[sm] * scalars + [given] * (len(args) - scalars),
        out_specs=[vm] * len(outs),
        scratch_shapes=list(scratch),
        compiler_params=pltpu.CompilerParams(vmem_limit_bytes=vmem << 20),
        cost_estimate=pl.CostEstimate(flops=flops, bytes_accessed=1 << 20, transcendentals=0),
        input_output_aliases=dict(aliases),
        name=name,
    )(*args)


def moments(total, pixels):
    mean = total[0:1, :] / pixels
    inverse = lax.rsqrt(total[1:2, :] / pixels - mean * mean + epsilon)
    return mean, inverse


def chunks(columns):
    return [slice(at, min(at + CHUNK, columns)) for at in range(0, columns, CHUNK)]


def line_mask(columns, side):
    return lax.broadcasted_iota(jnp.int32, (LINE, columns), 0) < side


def each_line(lines, body):
    lax.fori_loop(0, lines, lambda step, none: body(step) or none, 0, unroll=UNROLL)


def each_line_summed(lines, width, body):
    zero = jnp.zeros((8, width), F32)

    def step_sums(step, carry):
        one, two = body(step)
        return carry[0] + fold(one), carry[1] + fold(two)

    one, two = lax.fori_loop(0, lines, step_sums, (zero, zero), unroll=UNROLL)
    return column_sums(one), column_sums(two)


def across_lanes(mask, columns):
    return jnp.concatenate([mask] * (columns // LANES), axis=1)


def column_sums(values):
    return jnp.sum(values, axis=0, keepdims=True)


def line_at(step):
    return pl.ds(pl.multiple_of(step * LINE, LINE), LINE)


def fold(values):
    return values[0:8] + values[8:16]


def part_at(part, half, at=0, length=None):
    core = lax.axis_index("core")
    side = core if part == 0 else 1 - core
    length = half if length is None else length
    return pl.ds(pl.multiple_of(side * half + at, 128), length)


def block_owner(slot):
    position = lax.axis_index("fsdp")
    way = 1 - 2 * lax.axis_index("x")
    step = (0, -way, way, 2)[slot % 4]
    owner = lax.rem(position + 2 * step + 8, 8)
    return owner if slot < 4 else owner + 1 - 2 * lax.rem(owner, 2)


def rows_of(owner, depth):
    return pl.ds(pl.multiple_of(owner * depth, 16), depth)


def pack_kernel(weight, group, vectors, out, held, row, sems):
    depth, half = weight.shape[0], out.shape[1]
    shard, extra = group.shape[0], out.shape[0] - weight.shape[0]
    columns = part_at(0, half)
    copies = [
        pltpu.make_async_copy(group, held, sems.at[0]),
        pltpu.make_async_copy(vectors, row, sems.at[1]),
        pltpu.make_async_copy(weight.at[:, columns], out.at[pl.ds(0, depth)], sems.at[2]),
    ]
    for copy in copies:
        copy.start()
    copies[0].wait()
    copies[1].wait()
    below = [held[:, columns].astype(F32), row[...].astype(F32)]
    if extra > shard + 2:
        below.append(jnp.zeros((extra - shard - 2, half), F32))
    out[depth : depth + extra, :] = jnp.concatenate(below, axis=0).astype(BF16)
    copies[2].wait()


def turn_kernel(side, valid, x, x_other, turned, mask):
    rows = x.shape[0]
    turned[:, 0:rows] = x[...].T
    turned[:, rows : 2 * rows] = x_other[...].T
    images = valid.shape[0]
    rows = 2 * rows // images
    inside = lax.broadcasted_iota(jnp.int32, (rows, LANES), 0) % LINE < side
    for image in range(images):
        mask[image * rows : (image + 1) * rows, :] = jnp.where(inside, valid[image].astype(F32), 0.0)


def reduce_kernel(slots, depth, side, valid, mask, x, x_other, *refs):
    weights, (red, stats) = refs[:slots], refs[slots:]
    half, rows = red.shape[1], x.shape[0]
    for at in range(0, half, BLOCK):
        sums = [0.0, 0.0]
        for begin, pixels in ((0, x), (rows, x_other)):
            total = None
            for slot in range(slots):
                if slots == 1:
                    piece = pixels[...]
                else:
                    piece = pixels[:, pl.ds(pl.multiple_of(block_owner(slot) * depth, 128), depth)]
                term = dot(piece, weights[slot][0:depth, at : at + BLOCK])
                total = term if total is None else total + term
            red[begin : begin + rows, at : at + BLOCK] = total
            masked = total * across_lanes(mask[begin : begin + rows, :], BLOCK)
            sums = [sums[0] + column_sums(masked), sums[1] + column_sums(masked * total)]
        stats[0:1, at : at + BLOCK] = sums[0]
        stats[1:2, at : at + BLOCK] = sums[1]
    pixels = valid[0].astype(F32)
    for image in range(1, valid.shape[0]):
        pixels = pixels + valid[image].astype(F32)
    stats[2:3, :] = jnp.full((1, half), 1.0, F32) * (pixels * (side * side))


def spread_kernel(slots, depth, *refs):
    blocks, (wide, wide_turned, inner_vectors, outer_vectors, held, rows) = refs[:slots], refs[slots:]
    extra = held.shape[1]
    for slot in range(slots):
        held[block_owner(slot)] = blocks[slot][depth : depth + extra, :].astype(F32)
    shard, ours = rows.shape[0] // slots, slots // 2
    per, outer = inner_vectors.shape[1] // ours, outer_vectors.shape[1] // ours
    core = lax.axis_index("core")
    for owner in range(slots):
        rows[owner * shard : (owner + 1) * shard, :] = held[owner, 0:shard, :]
    for at in range(ours):
        owner = core * ours + at
        for row in range(4):
            inner_vectors[row : row + 1, at * per : (at + 1) * per] = held[
                owner, shard : shard + 1, row * per : (row + 1) * per
            ]
        for row in range(2):
            outer_vectors[row : row + 1, at * outer : (at + 1) * outer] = held[
                owner, shard + 1 : shard + 2, row * outer : (row + 1) * outer
            ]
    widen(rows, wide, wide_turned)


def widen_kernel(weight, wide, wide_turned, rows):
    rows[...] = weight[...].astype(F32)
    widen(rows, wide, wide_turned)


def widen(weight, wide, wide_turned):
    taps, blocks = wide.shape[:2]
    inner = weight.shape[0] // taps
    row = lax.broadcasted_iota(jnp.int32, (BLOCK, BLOCK), 0) // inner
    column = lax.broadcasted_iota(jnp.int32, (BLOCK, BLOCK), 1) // inner
    own = row == column
    for tap in range(taps):
        for block in range(blocks):
            piece = weight[tap * inner : (tap + 1) * inner, block * BLOCK : (block + 1) * BLOCK]
            tall = jnp.concatenate([piece] * (BLOCK // inner), axis=0)
            dense = jnp.where(own, tall, 0.0)
            wide[tap, block] = dense.astype(BF16)
            wide_turned[tap, block] = dense.T.astype(BF16)


def fill_pads(pads, columns, image, line, values):
    rows = pl.ds(pl.multiple_of((line + 1) * LINE, LINE), LINE)
    pads[0, image, rows, columns] = pltpu.roll(values, 1, 0).astype(BF16)
    pads[1, image, rows, columns] = values.astype(BF16)
    pads[2, image, rows, columns] = pltpu.roll(values, LINE - 1, 0).astype(BF16)


def clear_pads(pads):
    images, rows, columns = pads.shape[1:]
    zeros = jnp.zeros((3, images, LINE, columns), BF16)
    pads[:, :, 0:LINE, :] = zeros
    pads[:, :, rows - LINE : rows, :] = zeros


def convolve(pads, wide, image, block, rows, turned=False):
    columns = slice(block * BLOCK, (block + 1) * BLOCK)
    value = None
    for tap in range(TAPS):
        top, left = divmod(TAPS - 1 - tap if turned else tap, 3)
        piece = pads[left, image, top * LINE : top * LINE + rows, columns]
        term = dot(piece, wide[tap, block])
        value = term if value is None else value + term
    return value


def group_kernel(side, mask, total, vectors, red, wide, pads, grouped, stats):
    images, padded, width = pads.shape[1:]
    rows = side * LINE
    mean, inverse = moments(total, total[2:3, :])
    scale, bias = 0.5 * inverse * vectors[0:1, :], 0.5 * vectors[1:2, :]
    clear_pads(pads)
    for part in chunks(width):
        inside = line_mask(part.stop - part.start, side)

        def body(step):
            half = (red[line_at(step), part] - mean[:, part]) * scale[:, part] + bias[:, part]
            fill_pads(pads, part, step // side, step % side, jnp.where(inside, silu_half(half), 0.0))

        each_line(images * side, body)
    for block in range(width // BLOCK):
        columns = slice(block * BLOCK, (block + 1) * BLOCK)
        sums = [0.0, 0.0]
        for image in range(images):
            at = slice(image * rows, (image + 1) * rows)
            value = convolve(pads, wide, image, block, rows)
            grouped[at, columns] = value
            masked = value * across_lanes(mask[at, :], BLOCK)
            sums = [sums[0] + column_sums(masked), sums[1] + column_sums(masked * value)]
        stats[0:1, columns] = sums[0]
        stats[1:2, columns] = sums[1]


def act_kernel(side, total, first, vectors, grouped, act):
    rows, width = grouped.shape
    mean, inverse = moments(total, first[2:3, :])
    scale, bias = 0.5 * inverse * vectors[2:3, :], 0.5 * vectors[3:4, :]
    for part in chunks(width):
        inside = line_mask(part.stop - part.start, side)

        def body(step):
            at = line_at(step)
            half = (grouped[at, part] - mean[:, part]) * scale[:, part] + bias[:, part]
            act[at, part] = jnp.where(inside, silu_half(half), 0.0).astype(BF16)

        each_line(rows // LINE, body)


def assemble_kernel(*refs):
    blocks, out = refs[:-1], refs[-1]
    depth = blocks[0].shape[0]
    for slot, block in enumerate(blocks):
        out[rows_of(block_owner(slot), depth), :] = block[...]


def expand_kernel(mask, act_mine, act_far, weight, act, expanded, stats):
    rows, half = act_mine.shape
    middle = rows // 2
    act[:, part_at(0, half)] = act_mine[...]
    act[0:middle, part_at(1, half)] = act_far[middle:rows, :]
    act[middle:rows, part_at(1, half)] = act_far[0:middle, :]
    for at in range(0, weight.shape[1], BLOCK):
        sums = [0.0, 0.0]
        for begin in (0, middle):
            here = slice(begin, begin + middle)
            value = dot(act[here, :], weight[:, at : at + BLOCK])
            expanded[here, at : at + BLOCK] = value
            masked = value * across_lanes(mask[here, :], BLOCK)
            sums = [sums[0] + column_sums(masked), sums[1] + column_sums(masked * value)]
        stats[0:1, at : at + BLOCK] = sums[0]
        stats[1:2, at : at + BLOCK] = sums[1]


def output_kernel(
    side, valid, total, first, vectors, expanded, x, x_other, cotangent, cotangent_far, keep_out, send_out, grad, stats
):
    rows, channels = expanded.shape
    middle = rows // 2
    mean, inverse = moments(total, first[2:3, 0:1])
    scale, bias = inverse * vectors[0:1, :], vectors[1:2, :]
    for part in chunks(channels):
        length = part.stop - part.start
        whole = part_at(0, channels, part.start, length)
        ends = []
        for begin, pixels, incoming, columns, out in (
            (0, x, cotangent, whole, keep_out), (middle, x_other, cotangent_far, part, send_out)
        ):

            def body(step):
                at = line_at(step)
                here = pl.ds(pl.multiple_of(begin + step * LINE, LINE), LINE)
                keep = 0.5 * valid[(begin // LINE + step) // side].astype(F32)
                centered = expanded[here, part] - mean[:, part]
                half = (centered * scale[:, part] + (bias[:, part] + pixels[at, whole].astype(F32))) * keep
                slope, upper = dsilu_twice(half)
                out[at, part] = (half * upper).astype(BF16)
                value = incoming[at, columns].astype(F32) * keep * slope
                grad[here, part] = value
                return value, value * centered

            ends.append(each_line_summed(middle // LINE, length, body))
        stats[0:1, part] = ends[0][0] + ends[1][0]
        stats[1:2, part] = (ends[0][1] + ends[1][1]) * inverse[:, part]


def back_expand_kernel(mask, total, sums, first, vectors, grad, expanded, weight, flat, send):
    rows, channels = expanded.shape
    pixels = first[2:3, 0:1]
    mean, inverse = moments(total, pixels)
    scale = inverse * vectors[0:1, :]
    shifted, scaled = scale * sums[0:1, :] / pixels, scale * inverse * sums[1:2, :] / pixels
    for part in chunks(channels):

        def body(step):
            at = line_at(step)
            common = shifted[:, part] + (expanded[at, part] - mean[:, part]) * scaled[:, part]
            counted = across_lanes(mask[at, :], part.stop - part.start)
            flat[at, part] = (scale[:, part] * grad[at, part] - counted * common).astype(BF16)

        each_line(rows // LINE, body)
    back_part_kernel(1, flat, weight, send)


def back_part_kernel(part, flat, weight, out):
    half = out.shape[1]
    for at in range(0, half, BLOCK):
        rows = pl.ds(pl.multiple_of(part_at(part, half).start + at, BLOCK), BLOCK)
        out[:, at : at + BLOCK] = dot(flat[...], weight[rows, :], NT).astype(out.dtype)


def back_act_kernel(total, first, vectors, mine, far, grouped, dz, stats):
    mean, inverse = moments(total, first[2:3, :])
    lines = grouped.shape[0] // LINE

    def gradient(step, part):
        there = lax.rem(step + lines // 2, lines)
        return mine[line_at(step), part] + far[line_at(there), part].astype(F32)

    before_norm(dz, gradient, grouped, mean, inverse, vectors[2:3, :], vectors[3:4, :], stats)


def before_norm(dz, gradient, hidden, mean, inverse, gain, shift, stats, side=None):
    scale, bias = 0.5 * inverse * gain, 0.5 * shift
    rows, width = hidden.shape
    for part in chunks(width):
        inside = None if side is None else line_mask(part.stop - part.start, side)

        def body(step):
            at = line_at(step)
            centered = hidden[at, part] - mean[:, part]
            slope, _ = dsilu_twice(centered * scale[:, part] + bias[:, part])
            here = gradient(step, part) * slope
            if side is not None:
                here = jnp.where(inside, here, 0.0)
            dz[at, part] = here
            return here, here * centered

        one, two = each_line_summed(rows // LINE, part.stop - part.start, body)
        stats[0:1, part] = 0.5 * one
        stats[1:2, part] = 0.5 * inverse[:, part] * two


def weight_expand_kernel(act, flat, out):
    turned = act[...].T
    for at in range(0, out.shape[1], BLOCK):
        out[:, at : at + BLOCK] = dot(turned, flat[:, at : at + BLOCK]).astype(BF16)


def back_group_kernel(
    side, mask, total, sums, first, vectors, dz, grouped, red, wide, flat, dz_one, stats, pads
):
    images, padded, width = pads.shape[1:]
    rows = side * LINE
    pixels = first[2:3, :]
    mean, inverse = moments(total, pixels)
    scale = inverse * vectors[2:3, :]
    shifted, scaled = scale * sums[0:1, :] / pixels, scale * inverse * sums[1:2, :] / pixels
    scale = 0.5 * scale
    clear_pads(pads)
    for part in chunks(width):

        def body(step):
            at = line_at(step)
            common = shifted[:, part] + (grouped[at, part] - mean[:, part]) * scaled[:, part]
            value = scale[:, part] * dz[at, part] - across_lanes(mask[at, :], part.stop - part.start) * common
            flat[at, part] = value.astype(BF16)
            fill_pads(pads, part, step // side, step % side, value)

        each_line(images * side, body)
    for block in range(width // BLOCK):
        columns = slice(block * BLOCK, (block + 1) * BLOCK)
        for image in range(images):
            dz_one[image * rows : (image + 1) * rows, columns] = convolve(pads, wide, image, block, rows, True)
    mean_one, inverse_one = moments(first, pixels)

    def gradient(step, part):
        return dz_one[line_at(step), part]

    before_norm(dz_one, gradient, red, mean_one, inverse_one, vectors[0:1, :], vectors[1:2, :], stats, side)


def weight_group_kernel(side, inner, pads, flat, out, held):
    images, padded, width = pads.shape[1:]
    rows = side * LINE
    row = lax.broadcasted_iota(jnp.int32, (LANES, LANES), 0) // inner
    column = lax.broadcasted_iota(jnp.int32, (LANES, LANES), 1) // inner
    own = row == column
    for at in range(0, width, LANES):
        columns = slice(at, at + LANES)
        moved = []
        for tap in range(TAPS):
            top, left = divmod(tap, 3)
            pieces = [pads[left, image, top * LINE : top * LINE + rows, columns] for image in range(images)]
            moved.append(jnp.concatenate(pieces, axis=0))
        product = dot(flat[:, columns].T, jnp.concatenate(moved, axis=1))
        for tap in range(TAPS):
            kept = jnp.where(own, product[:, tap * LANES : (tap + 1) * LANES].T, 0.0)
            value = kept[0:inner]
            for begin in range(inner, LANES, inner):
                value = value + kept[begin : begin + inner]
            held[tap * inner : (tap + 1) * inner, columns] = value
    owners, extra = out.shape[:2]
    shard = TAPS * inner // owners
    zeros = jnp.zeros((extra - shard, width), F32)
    for owner in range(owners):
        rows_here = held[owner * shard : (owner + 1) * shard, :]
        out[owner] = jnp.concatenate([rows_here, zeros], axis=0).astype(BF16)


def back_reduce_kernel(small, places, mask, first, sums, vectors, dz, red, turned, group, flat, *outs):
    rows, width = red.shape
    pixels = first[2:3, :]
    mean, inverse = moments(first, pixels)
    scale = inverse * vectors[0:1, :]
    shifted, scaled = scale * sums[0:1, :] / pixels, scale * inverse * sums[1:2, :] / pixels
    scale = 0.5 * scale
    for part in chunks(width):

        def body(step):
            at = line_at(step)
            common = shifted[:, part] + (red[at, part] - mean[:, part]) * scaled[:, part]
            counted = across_lanes(mask[at, :], part.stop - part.start)
            flat[at, part] = (scale[:, part] * dz[at, part] - counted * common).astype(BF16)

        each_line(rows // LINE, body)
    block_sum_kernel(small, places, turned, group, flat, *outs)


def block_sum_kernel(small, places, turned, group, flat, *refs):
    arrived, outs = refs[: len(refs) - len(places)], refs[len(refs) - len(places) :]
    tall, half = outs[0].shape
    depth = tall - group.shape[1]
    for out, (block, chosen) in zip(outs, places):
        owner = block_owner(block) if small else block
        value = dot(turned[rows_of(owner, depth), :], flat[...])
        more = group[owner].astype(F32)
        for other in chosen:
            value = value + arrived[other][0:depth, :].astype(F32)
            more = more + arrived[other][depth:tall, :].astype(F32)
        out[0:depth, :] = value.astype(BF16)
        out[depth:tall, :] = more.astype(BF16)


def expand_sum_kernel(places, keep, *refs):
    arrived, outs = refs[: len(refs) - len(places)], refs[len(refs) - len(places) :]
    depth = outs[0].shape[0]
    for out, (block, chosen) in zip(outs, places):
        value = keep[rows_of(block_owner(block), depth), :]
        if chosen:
            value = value.astype(F32)
            for other in chosen:
                value = value + arrived[other][...].astype(F32)
        out[...] = value.astype(BF16)


def join_kernel(mine, mine_x, other, other_x, *outs):
    half = mine.shape[1]
    at = 0
    for out in outs:
        rows = out.shape[0]
        for part, terms in enumerate(((mine, mine_x), (other, other_x))):
            values = [term[at : at + -(-rows // 16) * 16, :].astype(F32) for term in terms]
            out[:, part_at(part, half)] = (values[0] + values[1])[0:rows]
        at += -(-rows // 16) * 16


def pin_kernel(values, out):
    pass


def own_kernel(sizes, near, far, *outs):
    position, core, ours = lax.axis_index("fsdp"), lax.axis_index("core"), lax.axis_size("fsdp") // 2
    side, place, at = position // ours, lax.rem(position, ours), 0
    for index, length in enumerate(sizes):
        columns = pl.ds(pl.multiple_of(at + place * length, 128), length)
        for row, out in ((1, outs[2 * index]), (0, outs[2 * index + 1])):
            out[...] = jnp.where(side == core, near[row : row + 1, columns], far[row : row + 1, columns])
        at += ours * length


def back_input_kernel(slots, depth, begin, flat, grad, *refs):
    weights, refs = refs[:slots], refs[slots:]
    half = grad.shape[1]
    out, held = refs[-2:]
    rows = slice(begin, begin + held.shape[0])
    for slot in range(slots):
        columns = pl.ds(pl.multiple_of(block_owner(slot) * depth, 128), depth) if slots > 1 else slice(None)
        held[:, columns] = dot(flat[rows, :], weights[slot][0:depth, :], NT)
    columns = part_at(0, half)
    held[:, columns] = held[:, columns] + grad[rows, :]
    if len(refs) == 2:
        out[...] = held[...].astype(BF16)
        return
    far = refs[0]
    side = out.shape[1]

    def body(step):
        at = line_at(step)
        out[step // side, step % side] = (held[at, :] + far[at, :].astype(F32)).astype(BF16)[0:side]

    each_line(held.shape[0] // LINE, body)


def far_half_kernel(values, out):
    out[...] = values[:, part_at(1, out.shape[1])]


def image_kernel(keep, far, out):
    half, side = keep.shape[1], out.shape[1]

    def body(step):
        at = line_at(step)
        for part, values in enumerate((keep, far)):
            out[step // side, step % side, :, part_at(part, half)] = values[at, :][0:side]

    each_line(keep.shape[0] // LINE, body)


def pinned(values):
    anywhere = pl.BlockSpec(memory_space=pl.ANY)
    values = values.transpose(1, 2, 0, 3)
    values = pl.pallas_call(
        pin_kernel, out_shape=shape(values.shape, values.dtype), in_specs=[anywhere], out_specs=anywhere,
        input_output_aliases={0: 0}, compiler_params=pltpu.CompilerParams(vmem_limit_bytes=1 << 20), name="pin",
    )(values)
    return values.transpose(2, 0, 1, 3)


def swap_core(values):
    return lax.ppermute(values, "core", SWAP)


def swap_x(values):
    if lax.axis_size("x") == 2:
        return lax.ppermute(values, "x", SWAP)
    return (lax.psum(values.astype(F32), "x") - values.astype(F32)).astype(values.dtype)


def sum_chips(values, flips):
    got = [lax.ppermute(values, CHIPS, [(at, at ^ flip) for at in range(16)]) for flip in flips]
    for other in got:
        values = values + other
    return values


def along(values, way):
    pairs = [(f * 2 + x, (f + 2 * way * (1 - 2 * x)) % 8 * 2 + x) for f in range(8) for x in range(2)]
    return lax.ppermute(values, CHIPS, pairs)


def across(values):
    return lax.ppermute(values, "fsdp", [(f, f ^ 1) for f in range(8)])


def halves(values, core):
    half = values.shape[1] // 2
    return lax.dynamic_slice_in_dim(values, core * half, half, 1)


def both(near, far, core):
    first, second = jnp.where(core == 0, near, far), jnp.where(core == 0, far, near)
    return jnp.concatenate([first, second], axis=-1)


def per_device(
    images,
    valid,
    cotangent,
    w_reduce,
    gain_one,
    shift_one,
    w_group,
    gain_two,
    shift_two,
    w_expand,
    gain_three,
    shift_three,
):
    count, side, _, channels = images.shape
    width = w_reduce.shape[1]
    inner = width // GROUPS
    size = lax.axis_size("fsdp")
    small = size == 8 and lax.axis_size("x") == 2
    position, core = lax.axis_index("fsdp"), lax.axis_index("core")
    rows = count * side * LINE
    per, outer, shard, depth = gain_one.shape[0], gain_three.shape[0], w_group.shape[0], w_reduce.shape[0]
    extra = -(-(shard + 2) // 16) * 16
    half, half_out = width // 2, channels // 2

    def plane_sum(values):
        return sum_chips(values, (1, 2, 3)) if small else lax.psum(values, CHIPS)

    def line_sum(values):
        return sum_chips(values, (4, 8, 12)) if small else values

    def everywhere(values):
        return line_sum(plane_sum(values))

    def padded(values):
        return jnp.pad(values, ((0, 0), (0, 0), (0, LINE - side), (0, 0))).reshape(rows, channels)

    vectors = jnp.zeros((2 * half,), BF16)
    for at, vector in (
        (0, gain_one), (per, shift_one), (2 * per, gain_two), (3 * per, shift_two),
        (half, gain_three), (half + outer, shift_three),
    ):
        vectors = vectors + jnp.pad(vector, (at, 2 * half - at - vector.size))
    (own,) = call(
        pack_kernel, [shape((depth + extra, half), BF16)], [w_reduce, w_group, vectors.reshape(2, half)],
        anywhere=True, vmem=60, name="pack",
        scratch=[pltpu.VMEM((shard, width), BF16), pltpu.VMEM((2, half), BF16), pltpu.SemaphoreType.DMA((3,))],
    )
    wide_shape = shape((TAPS, half // BLOCK, BLOCK, BLOCK), BF16)
    expand_own, x = halves(w_expand, core), padded(images)

    def turn(x, x_other, valid_other):
        valid_both = jnp.concatenate([valid, valid_other])
        turned, mask = call(
            functools.partial(turn_kernel, side),
            [shape((channels, 2 * rows), BF16), shape((2 * rows, LANES), F32)],
            [valid_both, x, x_other], scalars=1, name="turn",
        )
        return valid_both, turned, mask

    if small:
        first = along(own, 1)
        other = across(own)
        first, other, x, expand_own = together(first, other, x, expand_own)
        x_other, valid_other = swap_core(x), swap_core(valid)
        passed, second, first_other = swap_x(first), along(first, 1), across(first)
        second, passed, first_other, x_other, valid_other = together(second, passed, first_other, x_other, valid_other)
        passed_other, second_other, expand_first = swap_x(first_other), across(second), along(expand_own, 1)
        valid_both, turned, mask = turn(x, x_other, valid_other)
        weights = [own, first, passed, second, other, first_other, passed_other, second_other]
        *weights, expand_first, turned, mask = together(*weights, expand_first, turned, mask)
        second, other = along(expand_first, 1), across(expand_own)
        slots, slot_depth = size, depth
    else:
        x_other, valid_other = swap_core(x), swap_core(valid)
        valid_both, turned, mask = turn(x, x_other, valid_other)
        whole = lax.all_gather(own, "fsdp", axis=0, tiled=False)
        weights = [whole[:, :depth].reshape(channels, half)]
        slots, slot_depth = 1, channels

    pixels, across_cores = 2 * rows, 2 * count
    red, part = call(
        functools.partial(reduce_kernel, slots, slot_depth, side),
        [shape((pixels, half), F32), shape((3, half), F32)],
        [valid_both, mask, x, x_other, *weights], scalars=1, name="reduce", flops=2 * rows * width * channels,
    )
    if small:
        wide, wide_turned, inner_vectors, outer_vectors = call(
            functools.partial(spread_kernel, slots, depth),
            [wide_shape, wide_shape, shape((4, half), F32), shape((2, half_out), F32)],
            weights,
            scratch=[pltpu.VMEM((size, extra, half), F32), pltpu.VMEM((size * shard, half), F32)],
            name="spread", flops=1 << 28,
        )
        middle, wide, wide_turned, inner_vectors, outer_vectors = together(
            plane_sum(part), wide, wide_turned, inner_vectors, outer_vectors
        )
        middle, second, other, expand_first = together(middle, second, other, expand_first)
        first_other, passed = across(expand_first), swap_x(expand_first)
        first = line_sum(middle)
        first, first_other, second = together(first, first_other, second)
        second_other, passed_other = across(second), swap_x(first_other)
    else:
        packed = whole[:, depth:]
        wide, wide_turned = call(
            widen_kernel, [wide_shape, wide_shape], [packed[:, :shard].reshape(size * shard, half)],
            scratch=[pltpu.VMEM((size * shard, half), F32)], name="widen",
        )
        line = packed[:, shard, : 4 * per].astype(F32).reshape(size, 4, per).transpose(1, 0, 2).reshape(4, width)
        inner_vectors = halves(line, core)
        line = packed[:, shard + 1, : 2 * outer].astype(F32).reshape(size, 2, outer).transpose(1, 0, 2)
        outer_vectors = halves(line.reshape(2, channels), core)
        first = everywhere(part)
    pad_shape = (3, across_cores, (side + 2) * LINE, half)
    pads, grouped, part = call(
        functools.partial(group_kernel, side),
        [shape(pad_shape, BF16), shape((pixels, half), F32), shape((2, half), F32)],
        [mask, first, inner_vectors, red, wide],
        name="group", flops=2 * TAPS * rows * width * BLOCK,
    )
    if small:
        part, passed = together(part, passed)
        middle = line_sum(part)
        middle, passed_other, second_other = together(middle, passed_other, second_other)
        blocks = (expand_own, expand_first, passed, second, other, first_other, passed_other, second_other)
        total_two = plane_sum(middle)
    else:
        total_two = everywhere(part)
    (act_mine,) = call(
        functools.partial(act_kernel, side), [shape((pixels, half), BF16)], [total_two, first, inner_vectors, grouped],
        name="act",
    )
    act_far = swap_core(act_mine)
    if small:
        act_mine, *blocks = together(act_mine, *blocks)
        (weight_three,) = call(assemble_kernel, [shape((width, half_out), BF16)], blocks, name="assemble")
    else:
        weight_three = lax.all_gather(expand_own, "fsdp", axis=0, tiled=True)
    act_two, expanded, part = call(
        expand_kernel,
        [shape((pixels, width), BF16), shape((pixels, half_out), F32), shape((2, half_out), F32)],
        [mask, act_mine, act_far, weight_three],
        name="expand", flops=2 * rows * width * channels,
    )
    cot = padded(after(cotangent, grouped))
    cot_far = swap_core(call(far_half_kernel, [shape((rows, half_out), BF16)], [cot], name="far_half")[0])
    middle, cot, cot_far = together(plane_sum(part), cot, cot_far)
    total_three = line_sum(middle)
    keep_out, send_out, grad_summed, part = call(
        functools.partial(output_kernel, side),
        [shape((rows, half_out), BF16), shape((rows, half_out), BF16), shape((pixels, half_out), F32),
         shape((2, half_out), F32)],
        [valid_both, total_three, first, outer_vectors, expanded, x, x_other, cot, cot_far], scalars=1, name="output",
    )

    sums_three = everywhere(part)
    flat_three, send = call(
        back_expand_kernel,
        [shape((pixels, half_out), BF16), shape((pixels, half), BF16)],
        [mask, total_three, sums_three, first, outer_vectors, grad_summed, expanded, weight_three],
        name="back_expand", flops=rows * width * channels,
    )
    far = swap_core(send)
    (mine,) = call(
        functools.partial(back_part_kernel, 0), [shape((pixels, half), F32)], [flat_three, weight_three],
        name="back_part", flops=rows * width * channels,
    )
    dz_two, part = call(
        back_act_kernel,
        [shape((pixels, half), F32), shape((2, half), F32)],
        [total_two, first, inner_vectors, mine, far, grouped], name="back_act",
    )
    (expand_term,) = call(
        weight_expand_kernel, [shape((width, half_out), BF16)], [after(act_two, part), flat_three],
        name="weight_expand", flops=2 * rows * width * channels,
    )
    far_out = swap_core(after(send_out, part))
    middle = plane_sum(part)

    def expand_sums(places, arrived=()):
        return call(
            functools.partial(expand_sum_kernel, places),
            [shape((w_expand.shape[0], half_out), BF16)] * len(places),
            [expand_term] + list(arrived), name="expand_sum",
        )

    if small:
        middle, *moving = together(middle, *expand_sums(((6, ()), (7, ()))))
        moving = [swap_x(moving[0]), across(moving[1])]
        sums_two, *moving = together(line_sum(middle), *moving)
        sums_two, expand_first_other, expand_passed, expand_second, expand_other = together(
            sums_two, *expand_sums(((5, (0,)), (2, ()), (3, (1,)), (4, ())), moving)
        )
        expand_second, expand_other = along(expand_second, -1), across(expand_other)
    else:
        sums_two = line_sum(middle)
        own_expand = lax.psum_scatter(expand_term, "fsdp", scatter_dimension=0, tiled=True)
    flat_two, dz_one, part = call(
        functools.partial(back_group_kernel, side),
        [shape((pixels, half), BF16), shape((pixels, half), F32), shape((2, half), F32)],
        [mask, total_two, sums_two, first, inner_vectors, dz_two, grouped, red, wide_turned],
        scratch=[pltpu.VMEM(pad_shape, BF16)], name="back_group", flops=2 * TAPS * rows * width * BLOCK,
    )
    (group_term,) = call(
        functools.partial(weight_group_kernel, side, inner),
        [shape((size, extra, half), BF16)],
        [pads, after(flat_two, part)], scratch=[pltpu.VMEM((TAPS * inner, half), F32)], name="weight_group",
        flops=2 * TAPS * rows * width * BLOCK,
    )
    middle, group_term = together(plane_sum(part), group_term)
    if small:
        middle, expand_second, expand_first_other, expand_passed, expand_other = together(
            middle, expand_second, expand_first_other, expand_passed, expand_other
        )
        moving = [swap_x(expand_passed), across(expand_first_other)]
    sums_one = line_sum(middle)
    if small:
        sums_one, *moving = together(sums_one, *moving)
        (expand_first_own,) = expand_sums(((1, (0, 1, 2)),), moving + [expand_second])
    tall = depth + extra
    places = ((6, ()), (7, ())) if small else tuple((at, ()) for at in range(size))
    flat_one, *moving = call(
        functools.partial(back_reduce_kernel, small, places),
        [shape((pixels, half), BF16)] + [shape((tall, half), BF16)] * len(places),
        [mask, first, sums_one, inner_vectors, dz_one, red, turned, group_term],
        name="back_reduce", flops=2 * rows * depth * width * len(places),
    )

    def sums(places, arrived):
        return call(
            functools.partial(block_sum_kernel, small, places),
            [shape((tall, half), BF16)] * len(places),
            [turned, group_term, flat_one] + list(arrived),
            name="block_sum", flops=2 * rows * depth * width * len(places),
        )

    def back_input(begin, flat, *far):
        out = shape(images.shape, BF16) if far else shape((rows, channels), BF16)
        return call(
            functools.partial(back_input_kernel, slots, slot_depth, begin),
            [out], [flat, grad_summed, *weights, *far],
            scratch=[pltpu.VMEM((rows, channels), F32)], name="back_input", flops=rows * width * channels,
        )[0]

    def own_shards(totals):
        near = jnp.concatenate(totals, axis=1)
        far = swap_core(near)
        lengths = (per, per, outer)
        if small:
            outs = call(
                functools.partial(own_kernel, lengths), [shape((1, n), F32) for n in lengths for _ in range(2)], [near, far],
                name="own",
            )
            return [out.reshape(-1) for out in outs]
        cut, at = [], 0
        for total, length in zip(totals, lengths):
            whole = both(total, far[:, at : at + total.shape[1]], core)
            at += total.shape[1]
            cut += [lax.dynamic_slice_in_dim(whole[row], position * length, length, 0) for row in (1, 0)]
        return cut

    def image_of(far_out):
        return call(image_kernel, [shape(images.shape, BF16)], [keep_out, far_out], name="image")[0]

    def join(own, far, outs):
        return call(
            join_kernel, [shape(out.shape, F32) for out in outs], [own, far, swap_core(own), swap_core(far)], name="join"
        )

    if small:
        flat_here = after(flat_one, *moving)
        moving[1], expand_first_own = together(moving[1], expand_first_own)
        moving = [swap_x(moving[0]), across(moving[1])]
        expand_first_own = along(expand_first_own, -1)
        far_input = swap_core(back_input(rows, flat_here))
        moving[0], far_input, expand_first_own = together(moving[0], far_input, expand_first_own)
        (own_expand,) = expand_sums(((0, (0, 1)),), [expand_first_own, expand_other])
        first_other, passed, second = sums(((5, (0,)), (2, ()), (3, (1,))), moving)
        moving = [swap_x(passed), along(second, -1), across(first_other)]
        far_out, second = together(far_out, second)
        grad_input, output = back_input(0, after(flat_one, second), far_input), pinned(image_of(far_out))
        moving[0], grad_input, output = together(moving[0], grad_input, output)
        first_own, other = sums(((1, (0, 1, 2)), (4, ())), moving)
        moving = [along(first_own, -1), across(other)]
        shards = own_shards([after(sums_one, first_own), sums_two, sums_three])
        grad_input, own_expand = pinned(after(grad_input, first_own)), after(own_expand, first_own)
        far_expand = swap_x(own_expand)
        moving[0], grad_input, far_expand, *shards = together(moving[0], grad_input, far_expand, *shards)
        (own_reduce,) = sums(((0, (0, 1)),), moving)
        own_expand, far_expand = after(own_expand, own_reduce), after(far_expand, own_reduce)
        (grad_w_expand,) = join(own_expand, far_expand, [w_expand])
        far_reduce, grad_w_expand = together(swap_x(own_reduce), grad_w_expand)
    else:
        grad_input, output = back_input(0, flat_one, swap_core(back_input(rows, flat_one))), image_of(far_out)
        shards = own_shards([sums_one, sums_two, sums_three])
        whole = jnp.stack(moving).reshape(size * tall, half)
        own_reduce = lax.psum_scatter(whole, "fsdp", scatter_dimension=0, tiled=True)
        (grad_w_expand,) = join(own_expand, swap_x(own_expand), [w_expand])
        far_reduce = swap_x(own_reduce)
    grad_w_reduce, grad_w_group = join(own_reduce, far_reduce, [w_reduce, w_group])
    return (output, grad_input, grad_w_reduce, grad_w_group, grad_w_expand) + tuple(shards)


def solution(mesh):
    fsdp, dp = mesh.shape["fsdp"], mesh.shape["dp"]
    split = Mesh(mesh.devices.reshape(fsdp, dp // 2, 2), ("fsdp", "x", "core"))
    images, rows, vector = P(("fsdp", "x", "core"), None, None, None), P("fsdp", None), P("fsdp")
    return jax.shard_map(
        per_device,
        mesh=split,
        in_specs=(
            images, P(("fsdp", "x", "core")), images,
            rows, vector, vector, rows, vector, vector, rows, vector, vector,
        ),
        out_specs=(images, images, rows, rows, rows) + (vector,) * 6,
        check_vma=False,
    )
```

time: 225 us -> 208 us (0.924)
  waiting for transfers between devices: 87.6 us -> 75 us
  starting transfers between devices: 83.8 us -> 80.3 us
    ppermute x10, waiting for transfers between devices: 14.6 us -> 6.59 us  [swap_x(): return lax.ppermute(values, 'x', SWAP)]
    ppermute x29 -> x12, waiting for transfers between devices: 14.5 us -> 7.09 us  [swap_core(): return lax.ppermute(values, 'core', SWAP)]
    ppermute x8, waiting for transfers between devices: 18.3 us -> 21.5 us  [along(): return lax.ppermute(values, CHIPS, pairs)]
    ppermute x29 -> x12, starting transfers between devices: 4.97 us -> 1.86 us  [swap_core(): return lax.ppermute(values, 'core', SWAP)]
    pallas_call x0 -> x1, local copies, waits for them, and re-layouts: none -> 2.82 us  [call(): pl.pallas_call(kernel, out_shape=outs, in_specs=[sm] * scalars + [given]...]
    optimization_barrier x2 -> x1, local copies, waits for them, and re-layouts: 5.64 us -> 2.82 us  [after(): return lax.optimization_barrier((values,) + others)[0]]
    ppermute x36, starting transfers between devices: 46.8 us -> 49.6 us  [sum_chips(): lax.ppermute(values, CHIPS, [(at, at ^ flip) for at in range(16)])]
    pallas_call x26 -> x30, Pallas kernels: 42.1 us -> 41 us  [call(): pl.pallas_call(kernel, out_shape=outs, in_specs=[sm] * scalars + [given]...]
  transfers between devices with their start and end apart: 95 -> 78, of which waited for: 59 -> 46; matrix products, arithmetic and copies ran while one was open for 4% -> 4% of each run, Pallas kernels for 8% -> 11%
where the time goes in v3:
time: 208 us
  starting transfers between devices  80.3 us (39%)
  waiting for transfers between devices  75 us (36%)
  Pallas kernels  41 us (20%)
  local copies, waits for them, and re-layouts  9.57 us (5%)
    ppermute x36, starting transfers between devices, sum_chips(): lax.ppermute(values, CHIPS, [(at, at ^ flip) for at in range(16)])  49.6 us
    pallas_call x30, Pallas kernels, call(): pl.pallas_call(kernel, out_shape=outs, in_specs=[sm] * scalars + [given]...  41 us
    ppermute x36, waiting for transfers between devices, sum_chips(): lax.ppermute(values, CHIPS, [(at, at ^ flip) for at in range(16)])  25.4 us
    ppermute x8, waiting for transfers between devices, along(): return lax.ppermute(values, CHIPS, pairs)  21.5 us
    ppermute x12, waiting for transfers between devices, across(): return lax.ppermute(values, 'fsdp', [(f, f ^ 1) for f in range(8)])  14.5 us
    ppermute x12, starting transfers between devices, across(): return lax.ppermute(values, 'fsdp', [(f, f ^ 1) for f in range(8)])  13.5 us
    ppermute x8, starting transfers between devices, along(): return lax.ppermute(values, CHIPS, pairs)  8.36 us
    ppermute x12, waiting for transfers between devices, swap_core(): return lax.ppermute(values, 'core', SWAP)  7.09 us
  transfers between devices with their start and end apart: 78, of which 46 were waited for; matrix products, arithmetic and copies ran while one was open for 4% of the time, Pallas kernels for 11%

profile of v3, /device:TPU:0, one launch (start us, length us, event | category | flops | bytes accessed | tf_op | source)
XLA Modules:
  0.0 208.1 jit_solution(12225502026463911067)
XLA Ops:
  2.1 1.8 pack.1.refs_0_
  3.8 3.0 %collective-permute-start.1 = (bf16[304,512]{1,0:T(8,128)(2,1)}, bf16[304,512]{1,0:T(8,128)(2,1)S(1)}, u32[]{:S(2)}, u32[]{:S(2)}) collective-permute-start(bf16[304,512]{1,0:T(8,128)(2,1)} %pack.1.refs_0_), channel_id=1, source_target_pairs={{0,4},{4,0},{8,12},{12,8},{16,20},{20,16},{24,28},{28,24},{1,5},{5... | collective-permute-start | bytes 933896 | tf_op jit(solution)/shard_map/ppermute | solution.py:621
  6.9 1.6 collective-permute-start
  8.4 2.1 %copy.29 = bf16[2,14,14,2048]{3,2,1,0:T(8,128)(2,1)S(1)} copy(bf16[2,14,14,2048]{3,0,2,1:T(2,128)(2,1)} %param.12) | data formatting | bytes 3211264
  10.8 3.6 %collective-permute-done.1.refs_4_ = bf16[304,512]{1,0:T(8,128)(2,1)S(1)} collective-permute-done((bf16[304,512]{1,0:T(8,128)(2,1)}, bf16[304,512]{1,0:T(8,128)(2,1)S(1)}, u32[]{:S(2)}, u32[]{:S(2)}) %collective-permute-start.1) | collective-permute-done | bytes 311328 | tf_op jit(solution)/shard_map/ppermute | solution.py:621
  14.4 3.4 %collective-permute-done.refs_1_ = bf16[304,512]{1,0:T(8,128)(2,1)S(1)} collective-permute-done((bf16[304,512]{1,0:T(8,128)(2,1)}, bf16[304,512]{1,0:T(8,128)(2,1)S(1)}, u32[]{:S(2)}, u32[]{:S(2)}) %collective-permute-start) | collective-permute-done | bytes 311328 | tf_op jit(solution)/shard_map/ppermute | solution.py:617
  19.5 2.1 %collective-permute-done.6 = s32[2]{0:T(128)S(1)} collective-permute-done((s32[2]{0:T(128)S(1)}, s32[2]{0:T(128)S(1)}, u32[]{:S(2)}, u32[]{:S(2)}) %collective-permute-start.6) | collective-permute-done | bytes 40 | tf_op jit(solution)/shard_map/ppermute | solution.py:599
  21.6 6.0 %collective-permute-done.4.refs_5_ = bf16[304,512]{1,0:T(8,128)(2,1)S(1)} collective-permute-done((bf16[304,512]{1,0:T(8,128)(2,1)S(1)}, bf16[304,512]{1,0:T(8,128)(2,1)S(1)}, u32[]{:S(2)}, u32[]{:S(2)}) %collective-permute-start.4) | collective-permute-done | bytes 311328 | tf_op jit(solution)/shard_map/ppermute | solution.py:621
  27.8 3.0 %collective-permute-done.2.refs_3_ = bf16[304,512]{1,0:T(8,128)(2,1)S(1)} collective-permute-done((bf16[304,512]{1,0:T(8,128)(2,1)S(1)}, bf16[304,512]{1,0:T(8,128)(2,1)S(1)}, u32[]{:S(2)}, u32[]{:S(2)}) %collective-permute-start.2) | collective-permute-done | bytes 311328 | tf_op jit(solution)/shard_map/ppermute | solution.py:617
  30.8 1.5 collective-permute-start.8
  32.9 2.2 %turn.1 = (bf16[2048,896]{1,0:T(8,128)(2,1)S(1)}, f32[896,128]{1,0:T(8,128)S(1)}) custom-call(s32[4]{0:T(128)S(1)} %pad_add_fusion.1.valid, bf16[448,2048]{1,0:T(8,128)(2,1)S(1)} %bitcast.17, bf16[448,2048]{1,0:T(8,128)(2,1)S(1)} %collective-permute-done.5.x_other), custom_call_target="tpu_custom_call" | custom-call | bytes 1048576 | tf_op jit(solution)/shard_map/turn/pallas_call | solution.py:55
  35.1 6.3 %collective-permute-done.9.refs_1_ = bf16[128,1024]{1,0:T(8,128)(2,1)S(1)} collective-permute-done((bf16[128,1024]{1,0:T(8,128)(2,1)S(1)}, bf16[128,1024]{1,0:T(8,128)(2,1)S(1)}, u32[]{:S(2)}, u32[]{:S(2)}) %collective-permute-start.9) | collective-permute-done | bytes 262176 | tf_op jit(solution)/shard_map/ppermute | solution.py:617
  41.4 2.7 %reduce.1 = (f32[896,512]{1,0:T(8,128)S(1)}, f32[3,512]{1,0:T(4,128)S(1)}) custom-call(s32[4]{0:T(128)S(1)} %pad_add_fusion.1.valid, f32[896,128]{1,0:T(8,128)S(1)} %get-tuple-element.170.mask, bf16[448,2048]{1,0:T(8,128)(2,1)S(1)} %bitcast.18, bf16[448,2048]{1,0:T(8,128)(2,1)S(1)} %collective-permute-done.5.x_other, bf16[304,512]{1,0:T(8,128)(2,1)S(1)} %copy-done.2, ...), custom_call_target="tpu_custom_call" | custom-call | flops 1879048192 | bytes 1048576 | tf_op jit(solution)/shard_map/reduce/pallas_call | solution.py:55
  44.1 4.5 %collective-permute-start.12 = (f32[3,512]{1,0:T(4,128)S(1)}, f32[3,512]{1,0:T(4,128)S(1)}, u32[]{:S(2)}, u32[]{:S(2)}) collective-permute-start(f32[3,512]{1,0:T(4,128)S(1)} %get-tuple-element.179), channel_id=1, source_target_pairs={{0,6},{2,4},{4,2},{6,0},{8,14},{10,12},{12,10},{14,8},{16,22},{18,... | collective-permute-start | bytes 18440 | tf_op jit(solution)/shard_map/ppermute | solution.py:609
  50.3 1.9 collective-permute-done.11
  53.1 1.2 collective-permute-start.18
  54.4 4.4 %collective-permute-start.15 = (f32[3,512]{1,0:T(4,128)S(1)}, f32[3,512]{1,0:T(4,128)S(1)}, u32[]{:S(2)}, u32[]{:S(2)}) collective-permute-start(f32[3,512]{1,0:T(4,128)S(1)} %add_add_fusion.5), channel_id=1, source_target_pairs={{0,8},{2,10},{4,12},{6,14},{8,0},{10,2},{12,4},{14,6},{16,24},{18,... | collective-permute-start | bytes 18440 | tf_op jit(solution)/shard_map/ppermute | solution.py:609
  62.3 3.5 %group.3 = (bf16[3,4,256,512]{3,2,1,0:T(8,128)(2,1)S(1)}, f32[896,512]{1,0:T(8,128)S(1)}, f32[2,512]{1,0:T(2,128)S(1)}) custom-call(f32[896,128]{1,0:T(8,128)S(1)} %get-tuple-element.170.mask, f32[3,512]{1,0:T(4,128)S(1)} %add_add_fusion.4.total.first, f32[4,512]{1,0:T(4,128)S(1)} %get-tuple-element.190.vectors, f32[896,512]{1,0:T(8,128)S(1)} %get-tuple-element.191.red, ...), custom_call_target="tpu_custom_call" | custom-call | flops 2113929216 | bytes 1048576 | tf_op jit(solution)/shard_map/group/pallas_call | solution.py:55
  65.8 1.6 collective-permute-start.22
  68.5 1.8 collective-permute-start.20
  72.1 2.6 %collective-permute-start.27 = (f32[2,512]{1,0:T(2,128)S(1)}, f32[2,512]{1,0:T(2,128)S(1)}, u32[]{:S(2)}, u32[]{:S(2)}) collective-permute-start(f32[2,512]{1,0:T(2,128)S(1)} %add_add_fusion.11), channel_id=1, source_target_pairs={{0,6},{2,4},{4,2},{6,0},{8,14},{10,12},{12,10},{14,8},{16,22},{18,... | collective-permute-start | bytes 12296 | tf_op jit(solution)/shard_map/ppermute | solution.py:609
  76.7 1.6 collective-permute-done.26
  82.2 2.3 %expand.1 = (bf16[896,1024]{1,0:T(8,128)(2,1)S(1)}, f32[896,1024]{1,0:T(8,128)S(1)}, f32[2,1024]{1,0:T(2,128)S(1)}) custom-call(f32[896,128]{1,0:T(8,128)S(1)} %get-tuple-element.170.mask, bf16[896,512]{1,0:T(8,128)(2,1)S(1)} %act.1.act_mine, bf16[896,512]{1,0:T(8,128)(2,1)S(1)} %collective-permute-done.28.act_far, bf16[1024,1024]{1,0:T(8,128)(2,1)S(1)} %assemble.1.weight), custom_call_target="tpu_custom_call" | custom-call | flops 1879048192 | bytes 1048576 | tf_op jit(solution)/shard_map/expand/pallas_call | solution.py:55
  86.2 1.9 collective-permute-start.29
  89.8 2.2 %collective-permute-start.35 = (f32[2,1024]{1,0:T(2,128)S(1)}, f32[2,1024]{1,0:T(2,128)S(1)}, u32[]{:S(2)}, u32[]{:S(2)}) collective-permute-start(f32[2,1024]{1,0:T(2,128)S(1)} %add_add_fusion.3), channel_id=1, source_target_pairs={{0,24},{2,26},{4,28},{6,30},{8,16},{10,18},{12,20},{14,22},{16,8},... | collective-permute-start | bytes 24584 | tf_op jit(solution)/shard_map/ppermute | solution.py:609
  93.1 1.2 collective-permute-start.33
  95.4 1.2 collective-permute-done.34
  96.8 3.4 %output.1 = (bf16[448,1024]{1,0:T(8,128)(2,1)S(1)}, bf16[448,1024]{1,0:T(8,128)(2,1)S(1)}, f32[896,1024]{1,0:T(8,128)S(1)}, f32[2,1024]{1,0:T(2,128)S(1)}) custom-call(s32[4]{0:T(128)S(1)} %pad_add_fusion.1.valid, f32[2,1024]{1,0:T(2,128)S(1)} %add_add_fusion.2.total, f32[3,512]{1,0:T(4,128)S(1)} %add_add_fusion.4.total.first, ...), custom_call_target="tpu_custom_call" | custom-call | bytes 1048576 | tf_op jit(solution)/shard_map/output/pallas_call | solution.py:55
  100.2 2.8 %collective-permute-start.38 = (f32[2,1024]{1,0:T(2,128)S(1)}, f32[2,1024]{1,0:T(2,128)S(1)}, u32[]{:S(2)}, u32[]{:S(2)}) collective-permute-start(f32[2,1024]{1,0:T(2,128)S(1)} %get-tuple-element.219), channel_id=1, source_target_pairs={{0,6},{2,4},{4,2},{6,0},{8,14},{10,12},{12,10},{14,8},{16,22},{18,... | collective-permute-start | bytes 24584 | tf_op jit(solution)/shard_map/ppermute | solution.py:609
  104.9 1.8 collective-permute-done.37
  107.5 1.6 collective-permute-start.41
  110.1 1.8 collective-permute-start.39
  113.7 2.2 %back_expand.1 = (bf16[896,1024]{1,0:T(8,128)(2,1)S(1)}, bf16[896,512]{1,0:T(8,128)(2,1)S(1)}) custom-call(f32[896,128]{1,0:T(8,128)S(1)} %get-tuple-element.170.mask, f32[2,1024]{1,0:T(2,128)S(1)} %add_add_fusion.2.total, f32[2,1024]{1,0:T(2,128)S(1)} %add_add_fusion.sums, f32[3,512]{1,0:T(4,128)S(1)} %add_add_fusion.4.total.first, ...), custom_call_target="tpu_custom_call" | custom-call | flops 939524096 | bytes 1048576 | tf_op jit(solution)/shard_map/back_expand/pallas_call | solution.py:55
  116.0 1.2 back_part.1.mine
  117.2 1.3 collective-permute-done.42.far
  118.5 1.3 back_act.1
  121.4 1.9 collective-permute-start.43
  123.3 2.4 %weight_expand.1.keep = bf16[1024,1024]{1,0:T(8,128)(2,1)S(1)} custom-call(bf16[896,1024]{1,0:T(8,128)(2,1)S(1)} %get-tuple-element.225.act, bf16[896,1024]{1,0:T(8,128)(2,1)S(1)} %get-tuple-element.221.flat), custom_call_target="tpu_custom_call" | custom-call | flops 1879048192 | bytes 1048576 | tf_op jit(solution)/shard_map/weight_expand/pallas_call | solution.py:55
  126.9 1.2 collective-permute-start.50
  128.1 2.4 %collective-permute-start.48 = (f32[2,512]{1,0:T(2,128)S(1)}, f32[2,512]{1,0:T(2,128)S(1)}, u32[]{:S(2)}, u32[]{:S(2)}) collective-permute-start(f32[2,512]{1,0:T(2,128)S(1)} %add_add_fusion.9), channel_id=1, source_target_pairs={{0,24},{2,26},{4,28},{6,30},{8,16},{10,18},{12,20},{14,22},{16,8},... | collective-permute-start | bytes 12296 | tf_op jit(solution)/shard_map/ppermute | solution.py:609
  133.5 1.5 collective-permute-done.47
  135.3 4.1 %back_group.1 = (bf16[896,512]{1,0:T(8,128)(2,1)S(1)}, f32[896,512]{1,0:T(8,128)S(1)}, f32[2,512]{1,0:T(2,128)S(1)}) custom-call(f32[896,128]{1,0:T(8,128)S(1)} %get-tuple-element.170.mask, f32[2,512]{1,0:T(2,128)S(1)} %add_add_fusion.10.total, f32[2,512]{1,0:T(2,128)S(1)} %add_add_fusion.8.sums, f32[3,512]{1,0:T(4,128)S(1)} %add_add_fusion.4.total.first, ...), custom_call_target="tpu_custom_call" | custom-call | flops 2113929216 | bytes 1048576 | tf_op jit(solution)/shard_map/back_group/pallas_call | solution.py:55
  139.4 1.2 collective-permute-start.53
  140.7 1.3 collective-permute-start.52
  143.0 1.4 collective-permute-start.54
  145.3 1.7 weight_group.1.group
  147.0 2.3 %collective-permute-done.54.refs_2_ = bf16[128,1024]{1,0:T(8,128)(2,1)S(1)} collective-permute-done((bf16[128,1024]{1,0:T(8,128)(2,1)S(1)}, bf16[128,1024]{1,0:T(8,128)(2,1)S(1)}, u32[]{:S(2)}, u32[]{:S(2)}) %collective-permute-start.54) | collective-permute-done | bytes 262176 | tf_op jit(solution)/shard_map/ppermute | solution.py:617
  149.4 2.3 %collective-permute-done.55.refs_1_ = bf16[128,1024]{1,0:T(8,128)(2,1)S(1)} collective-permute-done((bf16[128,1024]{1,0:T(8,128)(2,1)S(1)}, bf16[128,1024]{1,0:T(8,128)(2,1)S(1)}, u32[]{:S(2)}, u32[]{:S(2)}) %collective-permute-start.55) | collective-permute-done | bytes 262176 | tf_op jit(solution)/shard_map/ppermute | solution.py:621
  153.0 3.2 %collective-permute-start.58 = (f32[2,512]{1,0:T(2,128)S(1)}, f32[2,512]{1,0:T(2,128)S(1)}, u32[]{:S(2)}, u32[]{:S(2)}) collective-permute-start(f32[2,512]{1,0:T(2,128)S(1)} %add_add_fusion.7), channel_id=1, source_target_pairs={{0,24},{2,26},{4,28},{6,30},{8,16},{10,18},{12,20},{14,22},{16,8},... | collective-permute-start | bytes 12296 | tf_op jit(solution)/shard_map/ppermute | solution.py:609
  158.4 2.3 %collective-permute-done.57 = f32[2,512]{1,0:T(2,128)S(1)} collective-permute-done((f32[2,512]{1,0:T(2,128)S(1)}, f32[2,512]{1,0:T(2,128)S(1)}, u32[]{:S(2)}, u32[]{:S(2)}) %collective-permute-start.57) | collective-permute-done | bytes 4128 | tf_op jit(solution)/shard_map/ppermute | solution.py:609
  160.7 1.2 back_reduce.1
  161.9 1.7 back_input.2
  164.3 1.8 collective-permute-start.64
  166.2 1.7 collective-permute-start.63
  167.8 6.4 %collective-permute-done.63.refs_0_ = bf16[128,1024]{1,0:T(8,128)(2,1)S(1)} collective-permute-done((bf16[128,1024]{1,0:T(8,128)(2,1)S(1)}, bf16[128,1024]{1,0:T(8,128)(2,1)S(1)}, u32[]{:S(2)}, u32[]{:S(2)}) %collective-permute-start.63) | collective-permute-done | bytes 262176 | tf_op jit(solution)/shard_map/ppermute | solution.py:617
  175.2 3.6 %collective-permute-start.65 = (bf16[304,512]{1,0:T(8,128)(2,1)S(1)}, bf16[304,512]{1,0:T(8,128)(2,1)S(1)}, u32[]{:S(2)}, u32[]{:S(2)}) collective-permute-start(bf16[304,512]{1,0:T(8,128)(2,1)S(1)} %get-tuple-element.265), channel_id=1, source_target_pairs={{0,2},{2,0},{1,3},{3,1},{4,6},{6,4},{5,7},{7,5},{8,10},{10,8},{9,1... | collective-permute-start | bytes 933896 | tf_op jit(solution)/shard_map/ppermute | solution.py:604
  180.1 2.8 %copy.34 = bf16[2,14,14,2048]{3,0,2,1:T(2,128)(2,1)} copy(bf16[2,14,14,2048]{3,2,1,0:T(8,128)(2,1)S(1)} %image.1) | data formatting | bytes 3211264 | tf_op jit(solution)/shard_map/image/pallas_call | solution.py:55
  182.9 2.0 back_input.3
  184.9 1.5 collective-permute-done.68.refs_2_
  187.3 2.7 %collective-permute-start.69 = (bf16[304,512]{1,0:T(8,128)(2,1)S(1)}, bf16[304,512]{1,0:T(8,128)(2,1)S(1)}, u32[]{:S(2)}, u32[]{:S(2)}) collective-permute-start(bf16[304,512]{1,0:T(8,128)(2,1)S(1)} %get-tuple-element.275), channel_id=1, source_target_pairs={{0,24},{2,10},{4,28},{6,14},{8,0},{10,18},{12,4},{14,22},{16,8},{1... | collective-permute-start | bytes 933896 | tf_op jit(solution)/shard_map/ppermute | solution.py:617
  191.4 2.8 %copy.33 = bf16[2,14,14,2048]{3,0,2,1:T(2,128)(2,1)} copy(bf16[2,14,14,2048]{3,2,1,0:T(8,128)(2,1)S(1)} %back_input.3) | data formatting | bytes 3211264 | tf_op jit(solution)/shard_map/optimization_barrier | solution.py:40
  194.9 2.7 %collective-permute-done.70.mine_x = bf16[128,1024]{1,0:T(8,128)(2,1)S(1)} collective-permute-done((bf16[128,1024]{1,0:T(8,128)(2,1)S(1)}, bf16[128,1024]{1,0:T(8,128)(2,1)S(1)}, u32[]{:S(2)}, u32[]{:S(2)}) %collective-permute-start.70) | collective-permute-done | bytes 262176 | tf_op jit(solution)/shard_map/ppermute | solution.py:604
  201.7 3.6 %collective-permute-done.73.mine_x = bf16[304,512]{1,0:T(8,128)(2,1)S(1)} collective-permute-done((bf16[304,512]{1,0:T(8,128)(2,1)S(1)}, bf16[304,512]{1,0:T(8,128)(2,1)S(1)}, u32[]{:S(2)}, u32[]{:S(2)}) %collective-permute-start.73) | collective-permute-done | bytes 311328 | tf_op jit(solution)/shard_map/ppermute | solution.py:604
  205.3 1.6 collective-permute-done.77.other_x
  (157 shorter events, 53.3 us)
Async XLA Ops:
  3.8 10.6 %collective-permute-start.1 = (bf16[304,512]{1,0:T(8,128)(2,1)}, bf16[304,512]{1,0:T(8,128)(2,1)S(1)}, u32[]{:S(2)}, u32[]{:S(2)}) collective-permute-start(bf16[304,512]{1,0:T(8,128)(2,1)} %pack.1.refs_0_), channel_id=1, source_target_pairs={{0,4},{4,0},{8,12},{12,8},{16,20},{20,16},{24,28},{28,24},{1,5},{5... | collective-permute-start | bytes 933896 | tf_op jit(solution)/shard_map/ppermute | solution.py:621
  6.9 10.9 %collective-permute-start = (bf16[304,512]{1,0:T(8,128)(2,1)}, bf16[304,512]{1,0:T(8,128)(2,1)S(1)}, u32[]{:S(2)}, u32[]{:S(2)}) collective-permute-start(bf16[304,512]{1,0:T(8,128)(2,1)} %pack.1.refs_0_), channel_id=1, source_target_pairs={{0,8},{2,26},{4,12},{6,30},{8,16},{10,2},{12,20},{14,6},{16,24},{1... | collective-permute-start | bytes 933896 | tf_op jit(solution)/shard_map/ppermute | solution.py:617
  17.8 13.0 %collective-permute-start.5 = (bf16[448,2048]{1,0:T(8,128)(2,1)S(1)}, bf16[448,2048]{1,0:T(8,128)(2,1)S(1)}, u32[]{:S(2)}, u32[]{:S(2)}) collective-permute-start(bf16[448,2048]{1,0:T(8,128)(2,1)S(1)} %bitcast.16), channel_id=1, source_target_pairs={{0,1},{1,0},{2,3},{3,2},{4,5},{5,4},{6,7},{7,6},{8,9},{9,8},{10,11... | collective-permute-start | bytes 5505032 | tf_op jit(solution)/shard_map/ppermute | solution.py:599
  17.8 9.8 %collective-permute-start.4 = (bf16[304,512]{1,0:T(8,128)(2,1)S(1)}, bf16[304,512]{1,0:T(8,128)(2,1)S(1)}, u32[]{:S(2)}, u32[]{:S(2)}) collective-permute-start(bf16[304,512]{1,0:T(8,128)(2,1)S(1)} %collective-permute-done.refs_1_), channel_id=1, source_target_pairs={{0,4},{4,0},{8,12},{12,8},{16,20},{20,16},{24,28},{28,24},{1,5},{5... | collective-permute-start | bytes 933896 | tf_op jit(solution)/shard_map/ppermute | solution.py:621
  18.3 9.5 %collective-permute-start.3 = (bf16[304,512]{1,0:T(8,128)(2,1)S(1)}, bf16[304,512]{1,0:T(8,128)(2,1)S(1)}, u32[]{:S(2)}, u32[]{:S(2)}) collective-permute-start(bf16[304,512]{1,0:T(8,128)(2,1)S(1)} %collective-permute-done.refs_1_), channel_id=1, source_target_pairs={{0,2},{2,0},{1,3},{3,1},{4,6},{6,4},{5,7},{7,5},{8,10},{10,8},{9,1... | collective-permute-start | bytes 933896 | tf_op jit(solution)/shard_map/ppermute | solution.py:604
  19.1 11.6 %collective-permute-start.2 = (bf16[304,512]{1,0:T(8,128)(2,1)S(1)}, bf16[304,512]{1,0:T(8,128)(2,1)S(1)}, u32[]{:S(2)}, u32[]{:S(2)}) collective-permute-start(bf16[304,512]{1,0:T(8,128)(2,1)S(1)} %collective-permute-done.refs_1_), channel_id=1, source_target_pairs={{0,8},{2,26},{4,12},{6,30},{8,16},{10,2},{12,20},{14,6},{16,24},{1... | collective-permute-start | bytes 933896 | tf_op jit(solution)/shard_map/ppermute | solution.py:617
  30.8 10.7 %collective-permute-start.8 = (bf16[304,512]{1,0:T(8,128)(2,1)S(1)}, bf16[304,512]{1,0:T(8,128)(2,1)S(1)}, u32[]{:S(2)}, u32[]{:S(2)}) collective-permute-start(bf16[304,512]{1,0:T(8,128)(2,1)S(1)} %collective-permute-done.2.refs_3_), channel_id=1, source_target_pairs={{0,4},{4,0},{8,12},{12,8},{16,20},{20,16},{24,28},{28,24},{1,5},{5... | collective-permute-start | bytes 933896 | tf_op jit(solution)/shard_map/ppermute | solution.py:621
  32.3 9.1 %collective-permute-start.7 = (bf16[304,512]{1,0:T(8,128)(2,1)S(1)}, bf16[304,512]{1,0:T(8,128)(2,1)S(1)}, u32[]{:S(2)}, u32[]{:S(2)}) collective-permute-start(bf16[304,512]{1,0:T(8,128)(2,1)S(1)} %collective-permute-done.4.refs_5_), channel_id=1, source_target_pairs={{0,2},{2,0},{1,3},{3,1},{4,6},{6,4},{5,7},{7,5},{8,10},{10,8},{9,1... | collective-permute-start | bytes 933896 | tf_op jit(solution)/shard_map/ppermute | solution.py:604
  32.3 9.1 %collective-permute-start.9 = (bf16[128,1024]{1,0:T(8,128)(2,1)S(1)}, bf16[128,1024]{1,0:T(8,128)(2,1)S(1)}, u32[]{:S(2)}, u32[]{:S(2)}) collective-permute-start(bf16[128,1024]{1,0:T(8,128)(2,1)S(1)} %constant_dynamic-slice_fusion.refs_0_), channel_id=1, source_target_pairs={{0,8},{2,26},{4,12},{6,30},{8,16},{10,2},{12,20},{14,6},{16,24},{1... | collective-permute-start | bytes 786440 | tf_op jit(solution)/shard_map/ppermute | solution.py:617
  32.3 20.8 %collective-permute-start.14 = (bf16[128,1024]{1,0:T(8,128)(2,1)S(1)}, bf16[128,1024]{1,0:T(8,128)(2,1)S(1)}, u32[]{:S(2)}, u32[]{:S(2)}) collective-permute-start(bf16[128,1024]{1,0:T(8,128)(2,1)S(1)} %constant_dynamic-slice_fusion.refs_0_), channel_id=1, source_target_pairs={{0,4},{4,0},{8,12},{12,8},{16,20},{20,16},{24,28},{28,24},{1,5},{5... | collective-permute-start | bytes 786440 | tf_op jit(solution)/shard_map/ppermute | solution.py:621
  41.4 11.7 %collective-permute-start.13 = (bf16[128,1024]{1,0:T(8,128)(2,1)S(1)}, bf16[128,1024]{1,0:T(8,128)(2,1)S(1)}, u32[]{:S(2)}, u32[]{:S(2)}) collective-permute-start(bf16[128,1024]{1,0:T(8,128)(2,1)S(1)} %collective-permute-done.9.refs_1_), channel_id=1, source_target_pairs={{0,8},{2,26},{4,12},{6,30},{8,16},{10,2},{12,20},{14,6},{16,24},{1... | collective-permute-start | bytes 786440 | tf_op jit(solution)/shard_map/ppermute | solution.py:617
  44.1 6.2 %collective-permute-start.12 = (f32[3,512]{1,0:T(4,128)S(1)}, f32[3,512]{1,0:T(4,128)S(1)}, u32[]{:S(2)}, u32[]{:S(2)}) collective-permute-start(f32[3,512]{1,0:T(4,128)S(1)} %get-tuple-element.179), channel_id=1, source_target_pairs={{0,6},{2,4},{4,2},{6,0},{8,14},{10,12},{12,10},{14,8},{16,22},{18,... | collective-permute-start | bytes 18440 | tf_op jit(solution)/shard_map/ppermute | solution.py:609
  48.6 3.7 %collective-permute-start.11 = (f32[3,512]{1,0:T(4,128)S(1)}, f32[3,512]{1,0:T(4,128)S(1)}, u32[]{:S(2)}, u32[]{:S(2)}) collective-permute-start(f32[3,512]{1,0:T(4,128)S(1)} %get-tuple-element.179), channel_id=1, source_target_pairs={{0,4},{2,6},{4,0},{6,2},{8,12},{10,14},{12,8},{14,10},{16,20},{18,... | collective-permute-start | bytes 18440 | tf_op jit(solution)/shard_map/ppermute | solution.py:609
  49.5 3.7 %collective-permute-start.10 = (f32[3,512]{1,0:T(4,128)S(1)}, f32[3,512]{1,0:T(4,128)S(1)}, u32[]{:S(2)}, u32[]{:S(2)}) collective-permute-start(f32[3,512]{1,0:T(4,128)S(1)} %get-tuple-element.179), channel_id=1, source_target_pairs={{0,2},{2,0},{4,6},{6,4},{8,10},{10,8},{12,14},{14,12},{16,18},{18,... | collective-permute-start | bytes 18440 | tf_op jit(solution)/shard_map/ppermute | solution.py:609
  53.1 8.4 %collective-permute-start.18 = (bf16[128,1024]{1,0:T(8,128)(2,1)S(1)}, bf16[128,1024]{1,0:T(8,128)(2,1)S(1)}, u32[]{:S(2)}, u32[]{:S(2)}) collective-permute-start(bf16[128,1024]{1,0:T(8,128)(2,1)S(1)} %collective-permute-done.9.refs_1_), channel_id=1, source_target_pairs={{0,4},{4,0},{8,12},{12,8},{16,20},{20,16},{24,28},{28,24},{1,5},{5... | collective-permute-start | bytes 786440 | tf_op jit(solution)/shard_map/ppermute | solution.py:621
  54.4 5.4 %collective-permute-start.17 = (f32[3,512]{1,0:T(4,128)S(1)}, f32[3,512]{1,0:T(4,128)S(1)}, u32[]{:S(2)}, u32[]{:S(2)}) collective-permute-start(f32[3,512]{1,0:T(4,128)S(1)} %add_add_fusion.5), channel_id=1, source_target_pairs={{0,24},{2,26},{4,28},{6,30},{8,16},{10,18},{12,20},{14,22},{16,8},... | collective-permute-start | bytes 18440 | tf_op jit(solution)/shard_map/ppermute | solution.py:609
  54.4 5.4 %collective-permute-start.16 = (f32[3,512]{1,0:T(4,128)S(1)}, f32[3,512]{1,0:T(4,128)S(1)}, u32[]{:S(2)}, u32[]{:S(2)}) collective-permute-start(f32[3,512]{1,0:T(4,128)S(1)} %add_add_fusion.5), channel_id=1, source_target_pairs={{0,16},{2,18},{4,20},{6,22},{8,24},{10,26},{12,28},{14,30},{16,0},... | collective-permute-start | bytes 18440 | tf_op jit(solution)/shard_map/ppermute | solution.py:609
  54.4 6.0 %collective-permute-start.15 = (f32[3,512]{1,0:T(4,128)S(1)}, f32[3,512]{1,0:T(4,128)S(1)}, u32[]{:S(2)}, u32[]{:S(2)}) collective-permute-start(f32[3,512]{1,0:T(4,128)S(1)} %add_add_fusion.5), channel_id=1, source_target_pairs={{0,8},{2,10},{4,12},{6,14},{8,0},{10,2},{12,4},{14,6},{16,24},{18,... | collective-permute-start | bytes 18440 | tf_op jit(solution)/shard_map/ppermute | solution.py:609
  58.7 7.0 %collective-permute-start.19 = (bf16[128,1024]{1,0:T(8,128)(2,1)S(1)}, bf16[128,1024]{1,0:T(8,128)(2,1)S(1)}, u32[]{:S(2)}, u32[]{:S(2)}) collective-permute-start(bf16[128,1024]{1,0:T(8,128)(2,1)S(1)} %collective-permute-done.9.refs_1_), channel_id=1, source_target_pairs={{0,2},{2,0},{1,3},{3,1},{4,6},{6,4},{5,7},{7,5},{8,10},{10,8},{9,1... | collective-permute-start | bytes 786440 | tf_op jit(solution)/shard_map/ppermute | solution.py:604
  61.5 10.6 %collective-permute-start.23 = (bf16[128,1024]{1,0:T(8,128)(2,1)S(1)}, bf16[128,1024]{1,0:T(8,128)(2,1)S(1)}, u32[]{:S(2)}, u32[]{:S(2)}) collective-permute-start(bf16[128,1024]{1,0:T(8,128)(2,1)S(1)} %collective-permute-done.18.refs_5_), channel_id=1, source_target_pairs={{0,2},{2,0},{1,3},{3,1},{4,6},{6,4},{5,7},{7,5},{8,10},{10,8},{9,1... | collective-permute-start | bytes 786440 | tf_op jit(solution)/shard_map/ppermute | solution.py:604
  61.5 10.6 %collective-permute-start.24 = (bf16[128,1024]{1,0:T(8,128)(2,1)S(1)}, bf16[128,1024]{1,0:T(8,128)(2,1)S(1)}, u32[]{:S(2)}, u32[]{:S(2)}) collective-permute-start(bf16[128,1024]{1,0:T(8,128)(2,1)S(1)} %collective-permute-done.13.refs_3_), channel_id=1, source_target_pairs={{0,4},{4,0},{8,12},{12,8},{16,20},{20,16},{24,28},{28,24},{1,5},{5... | collective-permute-start | bytes 786440 | tf_op jit(solution)/shard_map/ppermute | solution.py:621
  65.8 5.5 %collective-permute-start.22 = (f32[2,512]{1,0:T(2,128)S(1)}, f32[2,512]{1,0:T(2,128)S(1)}, u32[]{:S(2)}, u32[]{:S(2)}) collective-permute-start(f32[2,512]{1,0:T(2,128)S(1)} %get-tuple-element.194), channel_id=1, source_target_pairs={{0,24},{2,26},{4,28},{6,30},{8,16},{10,18},{12,20},{14,22},{16,8},... | collective-permute-start | bytes 12296 | tf_op jit(solution)/shard_map/ppermute | solution.py:609
  67.3 4.5 %collective-permute-start.21 = (f32[2,512]{1,0:T(2,128)S(1)}, f32[2,512]{1,0:T(2,128)S(1)}, u32[]{:S(2)}, u32[]{:S(2)}) collective-permute-start(f32[2,512]{1,0:T(2,128)S(1)} %get-tuple-element.194), channel_id=1, source_target_pairs={{0,16},{2,18},{4,20},{6,22},{8,24},{10,26},{12,28},{14,30},{16,0},... | collective-permute-start | bytes 12296 | tf_op jit(solution)/shard_map/ppermute | solution.py:609
  72.1 4.6 %collective-permute-start.27 = (f32[2,512]{1,0:T(2,128)S(1)}, f32[2,512]{1,0:T(2,128)S(1)}, u32[]{:S(2)}, u32[]{:S(2)}) collective-permute-start(f32[2,512]{1,0:T(2,128)S(1)} %add_add_fusion.11), channel_id=1, source_target_pairs={{0,6},{2,4},{4,2},{6,0},{8,14},{10,12},{12,10},{14,8},{16,22},{18,... | collective-permute-start | bytes 12296 | tf_op jit(solution)/shard_map/ppermute | solution.py:609
  80.8 9.0 %collective-permute-start.32 = (bf16[448,1024]{1,0:T(8,128)(2,1)S(1)}, bf16[448,1024]{1,0:T(8,128)(2,1)S(1)}, u32[]{:S(2)}, u32[]{:S(2)}) collective-permute-start(bf16[448,1024]{1,0:T(8,128)(2,1)S(1)} %far_half.1), channel_id=1, source_target_pairs={{0,1},{1,0},{2,3},{3,2},{4,5},{5,4},{6,7},{7,6},{8,9},{9,8},{10,11... | collective-permute-start | bytes 2752520 | tf_op jit(solution)/shard_map/ppermute | solution.py:599
  84.6 4.6 %collective-permute-start.31 = (f32[2,1024]{1,0:T(2,128)S(1)}, f32[2,1024]{1,0:T(2,128)S(1)}, u32[]{:S(2)}, u32[]{:S(2)}) collective-permute-start(f32[2,1024]{1,0:T(2,128)S(1)} %get-tuple-element.212), channel_id=1, source_target_pairs={{0,6},{2,4},{4,2},{6,0},{8,14},{10,12},{12,10},{14,8},{16,22},{18,... | collective-permute-start | bytes 24584 | tf_op jit(solution)/shard_map/ppermute | solution.py:609
  85.3 3.9 %collective-permute-start.30 = (f32[2,1024]{1,0:T(2,128)S(1)}, f32[2,1024]{1,0:T(2,128)S(1)}, u32[]{:S(2)}, u32[]{:S(2)}) collective-permute-start(f32[2,1024]{1,0:T(2,128)S(1)} %get-tuple-element.212), channel_id=1, source_target_pairs={{0,4},{2,6},{4,0},{6,2},{8,12},{10,14},{12,8},{14,10},{16,20},{18,... | collective-permute-start | bytes 24584 | tf_op jit(solution)/shard_map/ppermute | solution.py:609
  89.8 5.5 %collective-permute-start.35 = (f32[2,1024]{1,0:T(2,128)S(1)}, f32[2,1024]{1,0:T(2,128)S(1)}, u32[]{:S(2)}, u32[]{:S(2)}) collective-permute-start(f32[2,1024]{1,0:T(2,128)S(1)} %add_add_fusion.3), channel_id=1, source_target_pairs={{0,24},{2,26},{4,28},{6,30},{8,16},{10,18},{12,20},{14,22},{16,8},... | collective-permute-start | bytes 24584 | tf_op jit(solution)/shard_map/ppermute | solution.py:609
  92.0 4.5 %collective-permute-start.34 = (f32[2,1024]{1,0:T(2,128)S(1)}, f32[2,1024]{1,0:T(2,128)S(1)}, u32[]{:S(2)}, u32[]{:S(2)}) collective-permute-start(f32[2,1024]{1,0:T(2,128)S(1)} %add_add_fusion.3), channel_id=1, source_target_pairs={{0,16},{2,18},{4,20},{6,22},{8,24},{10,26},{12,28},{14,30},{16,0},... | collective-permute-start | bytes 24584 | tf_op jit(solution)/shard_map/ppermute | solution.py:609
  93.1 3.7 %collective-permute-start.33 = (f32[2,1024]{1,0:T(2,128)S(1)}, f32[2,1024]{1,0:T(2,128)S(1)}, u32[]{:S(2)}, u32[]{:S(2)}) collective-permute-start(f32[2,1024]{1,0:T(2,128)S(1)} %add_add_fusion.3), channel_id=1, source_target_pairs={{0,8},{2,10},{4,12},{6,14},{8,0},{10,2},{12,4},{14,6},{16,24},{18,... | collective-permute-start | bytes 24584 | tf_op jit(solution)/shard_map/ppermute | solution.py:609
  100.2 4.6 %collective-permute-start.38 = (f32[2,1024]{1,0:T(2,128)S(1)}, f32[2,1024]{1,0:T(2,128)S(1)}, u32[]{:S(2)}, u32[]{:S(2)}) collective-permute-start(f32[2,1024]{1,0:T(2,128)S(1)} %get-tuple-element.219), channel_id=1, source_target_pairs={{0,6},{2,4},{4,2},{6,0},{8,14},{10,12},{12,10},{14,8},{16,22},{18,... | collective-permute-start | bytes 24584 | tf_op jit(solution)/shard_map/ppermute | solution.py:609
  103.0 3.7 %collective-permute-start.37 = (f32[2,1024]{1,0:T(2,128)S(1)}, f32[2,1024]{1,0:T(2,128)S(1)}, u32[]{:S(2)}, u32[]{:S(2)}) collective-permute-start(f32[2,1024]{1,0:T(2,128)S(1)} %get-tuple-element.219), channel_id=1, source_target_pairs={{0,4},{2,6},{4,0},{6,2},{8,12},{10,14},{12,8},{14,10},{16,20},{18,... | collective-permute-start | bytes 24584 | tf_op jit(solution)/shard_map/ppermute | solution.py:609
  103.8 3.7 %collective-permute-start.36 = (f32[2,1024]{1,0:T(2,128)S(1)}, f32[2,1024]{1,0:T(2,128)S(1)}, u32[]{:S(2)}, u32[]{:S(2)}) collective-permute-start(f32[2,1024]{1,0:T(2,128)S(1)} %get-tuple-element.219), channel_id=1, source_target_pairs={{0,2},{2,0},{4,6},{6,4},{8,10},{10,8},{12,14},{14,12},{16,18},{18,... | collective-permute-start | bytes 24584 | tf_op jit(solution)/shard_map/ppermute | solution.py:609
  107.5 5.5 %collective-permute-start.41 = (f32[2,1024]{1,0:T(2,128)S(1)}, f32[2,1024]{1,0:T(2,128)S(1)}, u32[]{:S(2)}, u32[]{:S(2)}) collective-permute-start(f32[2,1024]{1,0:T(2,128)S(1)} %add_add_fusion.1), channel_id=1, source_target_pairs={{0,24},{2,26},{4,28},{6,30},{8,16},{10,18},{12,20},{14,22},{16,8},... | collective-permute-start | bytes 24584 | tf_op jit(solution)/shard_map/ppermute | solution.py:609
  109.0 4.5 %collective-permute-start.40 = (f32[2,1024]{1,0:T(2,128)S(1)}, f32[2,1024]{1,0:T(2,128)S(1)}, u32[]{:S(2)}, u32[]{:S(2)}) collective-permute-start(f32[2,1024]{1,0:T(2,128)S(1)} %add_add_fusion.1), channel_id=1, source_target_pairs={{0,16},{2,18},{4,20},{6,22},{8,24},{10,26},{12,28},{14,30},{16,0},... | collective-permute-start | bytes 24584 | tf_op jit(solution)/shard_map/ppermute | solution.py:609
  119.8 6.0 %collective-permute-start.45 = (f32[2,512]{1,0:T(2,128)S(1)}, f32[2,512]{1,0:T(2,128)S(1)}, u32[]{:S(2)}, u32[]{:S(2)}) collective-permute-start(f32[2,512]{1,0:T(2,128)S(1)} %get-tuple-element.223), channel_id=1, source_target_pairs={{0,6},{2,4},{4,2},{6,0},{8,14},{10,12},{12,10},{14,8},{16,22},{18,... | collective-permute-start | bytes 12296 | tf_op jit(solution)/shard_map/ppermute | solution.py:609
  120.5 5.3 %collective-permute-start.44 = (f32[2,512]{1,0:T(2,128)S(1)}, f32[2,512]{1,0:T(2,128)S(1)}, u32[]{:S(2)}, u32[]{:S(2)}) collective-permute-start(f32[2,512]{1,0:T(2,128)S(1)} %get-tuple-element.223), channel_id=1, source_target_pairs={{0,4},{2,6},{4,0},{6,2},{8,12},{10,14},{12,8},{14,10},{16,20},{18,... | collective-permute-start | bytes 12296 | tf_op jit(solution)/shard_map/ppermute | solution.py:609
  121.4 4.4 %collective-permute-start.43 = (f32[2,512]{1,0:T(2,128)S(1)}, f32[2,512]{1,0:T(2,128)S(1)}, u32[]{:S(2)}, u32[]{:S(2)}) collective-permute-start(f32[2,512]{1,0:T(2,128)S(1)} %get-tuple-element.223), channel_id=1, source_target_pairs={{0,2},{2,0},{4,6},{6,4},{8,10},{10,8},{12,14},{14,12},{16,18},{18,... | collective-permute-start | bytes 12296 | tf_op jit(solution)/shard_map/ppermute | solution.py:609
  125.8 9.3 %collective-permute-start.49 = (bf16[128,1024]{1,0:T(8,128)(2,1)S(1)}, bf16[128,1024]{1,0:T(8,128)(2,1)S(1)}, u32[]{:S(2)}, u32[]{:S(2)}) collective-permute-start(bf16[128,1024]{1,0:T(8,128)(2,1)S(1)} %get-tuple-element.229), channel_id=1, source_target_pairs={{0,2},{2,0},{1,3},{3,1},{4,6},{6,4},{5,7},{7,5},{8,10},{10,8},{9,1... | collective-permute-start | bytes 786440 | tf_op jit(solution)/shard_map/ppermute | solution.py:604
  126.9 8.2 %collective-permute-start.50 = (bf16[128,1024]{1,0:T(8,128)(2,1)S(1)}, bf16[128,1024]{1,0:T(8,128)(2,1)S(1)}, u32[]{:S(2)}, u32[]{:S(2)}) collective-permute-start(bf16[128,1024]{1,0:T(8,128)(2,1)S(1)} %get-tuple-element.230), channel_id=1, source_target_pairs={{0,4},{4,0},{8,12},{12,8},{16,20},{20,16},{24,28},{28,24},{1,5},{5... | collective-permute-start | bytes 786440 | tf_op jit(solution)/shard_map/ppermute | solution.py:621
  128.1 5.4 %collective-permute-start.48 = (f32[2,512]{1,0:T(2,128)S(1)}, f32[2,512]{1,0:T(2,128)S(1)}, u32[]{:S(2)}, u32[]{:S(2)}) collective-permute-start(f32[2,512]{1,0:T(2,128)S(1)} %add_add_fusion.9), channel_id=1, source_target_pairs={{0,24},{2,26},{4,28},{6,30},{8,16},{10,18},{12,20},{14,22},{16,8},... | collective-permute-start | bytes 12296 | tf_op jit(solution)/shard_map/ppermute | solution.py:609
  130.5 4.5 %collective-permute-start.47 = (f32[2,512]{1,0:T(2,128)S(1)}, f32[2,512]{1,0:T(2,128)S(1)}, u32[]{:S(2)}, u32[]{:S(2)}) collective-permute-start(f32[2,512]{1,0:T(2,128)S(1)} %add_add_fusion.9), channel_id=1, source_target_pairs={{0,16},{2,18},{4,20},{6,22},{8,24},{10,26},{12,28},{14,30},{16,0},... | collective-permute-start | bytes 12296 | tf_op jit(solution)/shard_map/ppermute | solution.py:609
  139.4 7.6 %collective-permute-start.53 = (f32[2,512]{1,0:T(2,128)S(1)}, f32[2,512]{1,0:T(2,128)S(1)}, u32[]{:S(2)}, u32[]{:S(2)}) collective-permute-start(f32[2,512]{1,0:T(2,128)S(1)} %get-tuple-element.241), channel_id=1, source_target_pairs={{0,6},{2,4},{4,2},{6,0},{8,14},{10,12},{12,10},{14,8},{16,22},{18,... | collective-permute-start | bytes 12296 | tf_op jit(solution)/shard_map/ppermute | solution.py:609
  140.7 6.3 %collective-permute-start.52 = (f32[2,512]{1,0:T(2,128)S(1)}, f32[2,512]{1,0:T(2,128)S(1)}, u32[]{:S(2)}, u32[]{:S(2)}) collective-permute-start(f32[2,512]{1,0:T(2,128)S(1)} %get-tuple-element.241), channel_id=1, source_target_pairs={{0,4},{2,6},{4,0},{6,2},{8,12},{10,14},{12,8},{14,10},{16,20},{18,... | collective-permute-start | bytes 12296 | tf_op jit(solution)/shard_map/ppermute | solution.py:609
  141.9 5.1 %collective-permute-start.51 = (f32[2,512]{1,0:T(2,128)S(1)}, f32[2,512]{1,0:T(2,128)S(1)}, u32[]{:S(2)}, u32[]{:S(2)}) collective-permute-start(f32[2,512]{1,0:T(2,128)S(1)} %get-tuple-element.241), channel_id=1, source_target_pairs={{0,2},{2,0},{4,6},{6,4},{8,10},{10,8},{12,14},{14,12},{16,18},{18,... | collective-permute-start | bytes 12296 | tf_op jit(solution)/shard_map/ppermute | solution.py:609
  143.0 6.4 %collective-permute-start.54 = (bf16[128,1024]{1,0:T(8,128)(2,1)S(1)}, bf16[128,1024]{1,0:T(8,128)(2,1)S(1)}, u32[]{:S(2)}, u32[]{:S(2)}) collective-permute-start(bf16[128,1024]{1,0:T(8,128)(2,1)S(1)} %get-tuple-element.247), channel_id=1, source_target_pairs={{0,24},{2,10},{4,28},{6,14},{8,0},{10,18},{12,4},{14,22},{16,8},{1... | collective-permute-start | bytes 786440 | tf_op jit(solution)/shard_map/ppermute | solution.py:617
  144.4 7.3 %collective-permute-start.55 = (bf16[128,1024]{1,0:T(8,128)(2,1)S(1)}, bf16[128,1024]{1,0:T(8,128)(2,1)S(1)}, u32[]{:S(2)}, u32[]{:S(2)}) collective-permute-start(bf16[128,1024]{1,0:T(8,128)(2,1)S(1)} %get-tuple-element.250), channel_id=1, source_target_pairs={{0,4},{4,0},{8,12},{12,8},{16,20},{20,16},{24,28},{28,24},{1,5},{5... | collective-permute-start | bytes 786440 | tf_op jit(solution)/shard_map/ppermute | solution.py:621
  151.7 9.0 %collective-permute-start.59 = (bf16[128,1024]{1,0:T(8,128)(2,1)S(1)}, bf16[128,1024]{1,0:T(8,128)(2,1)S(1)}, u32[]{:S(2)}, u32[]{:S(2)}) collective-permute-start(bf16[128,1024]{1,0:T(8,128)(2,1)S(1)} %get-tuple-element.252), channel_id=1, source_target_pairs={{0,2},{2,0},{1,3},{3,1},{4,6},{6,4},{5,7},{7,5},{8,10},{10,8},{9,1... | collective-permute-start | bytes 786440 | tf_op jit(solution)/shard_map/ppermute | solution.py:604
  152.2 8.5 %collective-permute-start.60 = (bf16[128,1024]{1,0:T(8,128)(2,1)S(1)}, bf16[128,1024]{1,0:T(8,128)(2,1)S(1)}, u32[]{:S(2)}, u32[]{:S(2)}) collective-permute-start(bf16[128,1024]{1,0:T(8,128)(2,1)S(1)} %get-tuple-element.253), channel_id=1, source_target_pairs={{0,4},{4,0},{8,12},{12,8},{16,20},{20,16},{24,28},{28,24},{1,5},{5... | collective-permute-start | bytes 786440 | tf_op jit(solution)/shard_map/ppermute | solution.py:621
  153.0 5.4 %collective-permute-start.58 = (f32[2,512]{1,0:T(2,128)S(1)}, f32[2,512]{1,0:T(2,128)S(1)}, u32[]{:S(2)}, u32[]{:S(2)}) collective-permute-start(f32[2,512]{1,0:T(2,128)S(1)} %add_add_fusion.7), channel_id=1, source_target_pairs={{0,24},{2,26},{4,28},{6,30},{8,16},{10,18},{12,20},{14,22},{16,8},... | collective-permute-start | bytes 12296 | tf_op jit(solution)/shard_map/ppermute | solution.py:609
  156.1 4.5 %collective-permute-start.57 = (f32[2,512]{1,0:T(2,128)S(1)}, f32[2,512]{1,0:T(2,128)S(1)}, u32[]{:S(2)}, u32[]{:S(2)}) collective-permute-start(f32[2,512]{1,0:T(2,128)S(1)} %add_add_fusion.7), channel_id=1, source_target_pairs={{0,16},{2,18},{4,20},{6,22},{8,24},{10,26},{12,28},{14,30},{16,0},... | collective-permute-start | bytes 12296 | tf_op jit(solution)/shard_map/ppermute | solution.py:609
  163.6 10.6 %collective-permute-start.62 = (bf16[448,2048]{1,0:T(8,128)(2,1)S(1)}, bf16[448,2048]{1,0:T(8,128)(2,1)S(1)}, u32[]{:S(2)}, u32[]{:S(2)}) collective-permute-start(bf16[448,2048]{1,0:T(8,128)(2,1)S(1)} %back_input.2), channel_id=1, source_target_pairs={{0,1},{1,0},{2,3},{3,2},{4,5},{5,4},{6,7},{7,6},{8,9},{9,8},{10,11... | collective-permute-start | bytes 5505032 | tf_op jit(solution)/shard_map/ppermute | solution.py:599
  163.7 16.1 %collective-permute-start.66 = (bf16[448,1024]{1,0:T(8,128)(2,1)S(1)}, bf16[448,1024]{1,0:T(8,128)(2,1)S(1)}, u32[]{:S(2)}, u32[]{:S(2)}) collective-permute-start(bf16[448,1024]{1,0:T(8,128)(2,1)S(1)} %get-tuple-element.269), channel_id=1, source_target_pairs={{0,1},{1,0},{2,3},{3,2},{4,5},{5,4},{6,7},{7,6},{8,9},{9,8},{10,11... | collective-permute-start | bytes 2752520 | tf_op jit(solution)/shard_map/ppermute | solution.py:599
  164.2 10.0 %collective-permute-start.61 = (bf16[304,512]{1,0:T(8,128)(2,1)S(1)}, bf16[304,512]{1,0:T(8,128)(2,1)S(1)}, u32[]{:S(2)}, u32[]{:S(2)}) collective-permute-start(bf16[304,512]{1,0:T(8,128)(2,1)S(1)} %get-tuple-element.257), channel_id=1, source_target_pairs={{0,2},{2,0},{1,3},{3,1},{4,6},{6,4},{5,7},{7,5},{8,10},{10,8},{9,1... | collective-permute-start | bytes 933896 | tf_op jit(solution)/shard_map/ppermute | solution.py:604
  164.3 9.8 %collective-permute-start.64 = (bf16[304,512]{1,0:T(8,128)(2,1)S(1)}, bf16[304,512]{1,0:T(8,128)(2,1)S(1)}, u32[]{:S(2)}, u32[]{:S(2)}) collective-permute-start(bf16[304,512]{1,0:T(8,128)(2,1)S(1)} %get-tuple-element.264), channel_id=1, source_target_pairs={{0,4},{4,0},{8,12},{12,8},{16,20},{20,16},{24,28},{28,24},{1,5},{5... | collective-permute-start | bytes 933896 | tf_op jit(solution)/shard_map/ppermute | solution.py:621
  166.2 8.0 %collective-permute-start.63 = (bf16[128,1024]{1,0:T(8,128)(2,1)S(1)}, bf16[128,1024]{1,0:T(8,128)(2,1)S(1)}, u32[]{:S(2)}, u32[]{:S(2)}) collective-permute-start(bf16[128,1024]{1,0:T(8,128)(2,1)S(1)} %expand_sum.6), channel_id=1, source_target_pairs={{0,24},{2,10},{4,28},{6,14},{8,0},{10,18},{12,4},{14,22},{16,8},{1... | collective-permute-start | bytes 786440 | tf_op jit(solution)/shard_map/ppermute | solution.py:617
  175.2 9.7 %collective-permute-start.65 = (bf16[304,512]{1,0:T(8,128)(2,1)S(1)}, bf16[304,512]{1,0:T(8,128)(2,1)S(1)}, u32[]{:S(2)}, u32[]{:S(2)}) collective-permute-start(bf16[304,512]{1,0:T(8,128)(2,1)S(1)} %get-tuple-element.265), channel_id=1, source_target_pairs={{0,2},{2,0},{1,3},{3,1},{4,6},{6,4},{5,7},{7,5},{8,10},{10,8},{9,1... | collective-permute-start | bytes 933896 | tf_op jit(solution)/shard_map/ppermute | solution.py:604
  178.8 7.6 %collective-permute-start.68 = (bf16[304,512]{1,0:T(8,128)(2,1)S(1)}, bf16[304,512]{1,0:T(8,128)(2,1)S(1)}, u32[]{:S(2)}, u32[]{:S(2)}) collective-permute-start(bf16[304,512]{1,0:T(8,128)(2,1)S(1)} %get-tuple-element.274), channel_id=1, source_target_pairs={{0,4},{4,0},{8,12},{12,8},{16,20},{20,16},{24,28},{28,24},{1,5},{5... | collective-permute-start | bytes 933896 | tf_op jit(solution)/shard_map/ppermute | solution.py:621
  179.1 7.4 %collective-permute-start.67 = (bf16[304,512]{1,0:T(8,128)(2,1)S(1)}, bf16[304,512]{1,0:T(8,128)(2,1)S(1)}, u32[]{:S(2)}, u32[]{:S(2)}) collective-permute-start(bf16[304,512]{1,0:T(8,128)(2,1)S(1)} %get-tuple-element.270), channel_id=1, source_target_pairs={{0,24},{2,10},{4,28},{6,14},{8,0},{10,18},{12,4},{14,22},{16,8},{1... | collective-permute-start | bytes 933896 | tf_op jit(solution)/shard_map/ppermute | solution.py:617
  187.3 10.3 %collective-permute-start.69 = (bf16[304,512]{1,0:T(8,128)(2,1)S(1)}, bf16[304,512]{1,0:T(8,128)(2,1)S(1)}, u32[]{:S(2)}, u32[]{:S(2)}) collective-permute-start(bf16[304,512]{1,0:T(8,128)(2,1)S(1)} %get-tuple-element.275), channel_id=1, source_target_pairs={{0,24},{2,10},{4,28},{6,14},{8,0},{10,18},{12,4},{14,22},{16,8},{1... | collective-permute-start | bytes 933896 | tf_op jit(solution)/shard_map/ppermute | solution.py:617
  190.0 7.6 %collective-permute-start.72 = (bf16[304,512]{1,0:T(8,128)(2,1)S(1)}, bf16[304,512]{1,0:T(8,128)(2,1)S(1)}, u32[]{:S(2)}, u32[]{:S(2)}) collective-permute-start(bf16[304,512]{1,0:T(8,128)(2,1)S(1)} %get-tuple-element.290), channel_id=1, source_target_pairs={{0,4},{4,0},{8,12},{12,8},{16,20},{20,16},{24,28},{28,24},{1,5},{5... | collective-permute-start | bytes 933896 | tf_op jit(solution)/shard_map/ppermute | solution.py:621
  191.1 6.4 %collective-permute-start.70 = (bf16[128,1024]{1,0:T(8,128)(2,1)S(1)}, bf16[128,1024]{1,0:T(8,128)(2,1)S(1)}, u32[]{:S(2)}, u32[]{:S(2)}) collective-permute-start(bf16[128,1024]{1,0:T(8,128)(2,1)S(1)} %expand_sum.7.mine), channel_id=1, source_target_pairs={{0,2},{2,0},{1,3},{3,1},{4,6},{6,4},{5,7},{7,5},{8,10},{10,8},{9,1... | collective-permute-start | bytes 786440 | tf_op jit(solution)/shard_map/ppermute | solution.py:604
  198.0 7.3 %collective-permute-start.73 = (bf16[304,512]{1,0:T(8,128)(2,1)S(1)}, bf16[304,512]{1,0:T(8,128)(2,1)S(1)}, u32[]{:S(2)}, u32[]{:S(2)}) collective-permute-start(bf16[304,512]{1,0:T(8,128)(2,1)S(1)} %block_sum.5.mine), channel_id=1, source_target_pairs={{0,2},{2,0},{1,3},{3,1},{4,6},{6,4},{5,7},{7,5},{8,10},{10,8},{9,1... | collective-permute-start | bytes 933896 | tf_op jit(solution)/shard_map/ppermute | solution.py:604
  199.2 6.1 %collective-permute-start.76 = (bf16[304,512]{1,0:T(8,128)(2,1)S(1)}, bf16[304,512]{1,0:T(8,128)(2,1)S(1)}, u32[]{:S(2)}, u32[]{:S(2)}) collective-permute-start(bf16[304,512]{1,0:T(8,128)(2,1)S(1)} %block_sum.5.mine), channel_id=1, source_target_pairs={{0,1},{1,0},{2,3},{3,2},{4,5},{5,4},{6,7},{7,6},{8,9},{9,8},{10,11... | collective-permute-start | bytes 933896 | tf_op jit(solution)/shard_map/ppermute | solution.py:599
  (19 other events, 92.6 us)

commit v4 on v3

--- a/solution.py
+++ b/solution.py
@@ -59,7 +59,7 @@
         out_specs=[vm] * len(outs),
         scratch_shapes=list(scratch),
         compiler_params=pltpu.CompilerParams(vmem_limit_bytes=vmem << 20),
-        cost_estimate=pl.CostEstimate(flops=flops, bytes_accessed=1 << 20, transcendentals=0),
+        cost_estimate=pl.CostEstimate(flops=0, bytes_accessed=0, transcendentals=0),
         input_output_aliases=dict(aliases),
         name=name,
     )(*args)
@@ -129,24 +129,27 @@
     return pl.ds(pl.multiple_of(owner * depth, 16), depth)
 
 
-def pack_kernel(weight, group, vectors, out, held, row, sems):
+def pack_kernel(weight, group, *refs):
+    vectors, (out, held, *rows, sems) = refs[:6], refs[6:]
     depth, half = weight.shape[0], out.shape[1]
     shard, extra = group.shape[0], out.shape[0] - weight.shape[0]
     columns = part_at(0, half)
-    copies = [
-        pltpu.make_async_copy(group, held, sems.at[0]),
-        pltpu.make_async_copy(vectors, row, sems.at[1]),
-        pltpu.make_async_copy(weight.at[:, columns], out.at[pl.ds(0, depth)], sems.at[2]),
-    ]
+    copies = [pltpu.make_async_copy(group, held, sems.at[0])]
+    copies += [pltpu.make_async_copy(vector, row, sems.at[2 + at]) for at, (vector, row) in enumerate(zip(vectors, rows))]
+    copies.append(pltpu.make_async_copy(weight.at[:, columns], out.at[pl.ds(0, depth)], sems.at[1]))
     for copy in copies:
         copy.start()
-    copies[0].wait()
-    copies[1].wait()
-    below = [held[:, columns].astype(F32), row[...].astype(F32)]
+    for copy in copies[:-1]:
+        copy.wait()
+    below = [held[:, columns].astype(F32)]
+    for begin, end in ((0, 4), (4, 6)):
+        line = [row[...].astype(F32).reshape(1, row.shape[0]) for row in rows[begin:end]]
+        missing = half - sum(piece.shape[1] for piece in line)
+        below.append(jnp.concatenate(line + ([jnp.zeros((1, missing), F32)] if missing else []), axis=1))
     if extra > shard + 2:
         below.append(jnp.zeros((extra - shard - 2, half), F32))
     out[depth : depth + extra, :] = jnp.concatenate(below, axis=0).astype(BF16)
-    copies[2].wait()
+    copies[-1].wait()
 
 
 def turn_kernel(side, valid, x, x_other, turned, mask):
@@ -607,6 +610,7 @@
 
 def sum_chips(values, flips):
     got = [lax.ppermute(values, CHIPS, [(at, at ^ flip) for at in range(16)]) for flip in flips]
+    got = together(*got)
     for other in got:
         values = values + other
     return values
@@ -668,16 +672,12 @@
     def padded(values):
         return jnp.pad(values, ((0, 0), (0, 0), (0, LINE - side), (0, 0))).reshape(rows, channels)
 
-    vectors = jnp.zeros((2 * half,), BF16)
-    for at, vector in (
-        (0, gain_one), (per, shift_one), (2 * per, gain_two), (3 * per, shift_two),
-        (half, gain_three), (half + outer, shift_three),
-    ):
-        vectors = vectors + jnp.pad(vector, (at, 2 * half - at - vector.size))
+    vectors = (gain_one, shift_one, gain_two, shift_two, gain_three, shift_three)
     (own,) = call(
-        pack_kernel, [shape((depth + extra, half), BF16)], [w_reduce, w_group, vectors.reshape(2, half)],
+        pack_kernel, [shape((depth + extra, half), BF16)], [w_reduce, w_group, *vectors],
         anywhere=True, vmem=60, name="pack",
-        scratch=[pltpu.VMEM((shard, width), BF16), pltpu.VMEM((2, half), BF16), pltpu.SemaphoreType.DMA((3,))],
+        scratch=[pltpu.VMEM((shard, width), BF16)] + [pltpu.VMEM(vector.shape, BF16) for vector in vectors]
+        + [pltpu.SemaphoreType.DMA((8,))],
     )
     wide_shape = shape((TAPS, half // BLOCK, BLOCK, BLOCK), BF16)
     expand_own, x = halves(w_expand, core), padded(images)
@@ -694,14 +694,14 @@
     if small:
         first = along(own, 1)
         other = across(own)
-        first, other, x, expand_own = together(first, other, x, expand_own)
-        x_other, valid_other = swap_core(x), swap_core(valid)
+        x_other, valid_other = padded(swap_core(images)), swap_core(valid)
+        first, other, x, x_other, expand_own = together(first, other, x, x_other, expand_own)
         passed, second, first_other = swap_x(first), along(first, 1), across(first)
-        second, passed, first_other, x_other, valid_other = together(second, passed, first_other, x_other, valid_other)
+        second, passed, first_other, valid_other = together(second, passed, first_other, valid_other)
         passed_other, second_other, expand_first = swap_x(first_other), across(second), along(expand_own, 1)
         valid_both, turned, mask = turn(x, x_other, valid_other)
         weights = [own, first, passed, second, other, first_other, passed_other, second_other]
-        *weights, expand_first, turned, mask = together(*weights, expand_first, turned, mask)
+        *weights, turned, mask = together(*weights, turned, mask)
         second, other = along(expand_first, 1), across(expand_own)
         slots, slot_depth = size, depth
     else:
@@ -901,24 +901,22 @@
         )
 
     if small:
-        flat_here = after(flat_one, *moving)
         moving[1], expand_first_own = together(moving[1], expand_first_own)
         moving = [swap_x(moving[0]), across(moving[1])]
         expand_first_own = along(expand_first_own, -1)
-        far_input = swap_core(back_input(rows, flat_here))
-        moving[0], far_input, expand_first_own = together(moving[0], far_input, expand_first_own)
+        shards = own_shards([sums_one, sums_two, sums_three])
+        moving[0], expand_first_own, *shards = together(moving[0], expand_first_own, *shards)
         (own_expand,) = expand_sums(((0, (0, 1)),), [expand_first_own, expand_other])
         first_other, passed, second = sums(((5, (0,)), (2, ()), (3, (1,))), moving)
         moving = [swap_x(passed), along(second, -1), across(first_other)]
-        far_out, second = together(far_out, second)
-        grad_input, output = back_input(0, after(flat_one, second), far_input), pinned(image_of(far_out))
-        moving[0], grad_input, output = together(moving[0], grad_input, output)
+        far_input = swap_core(after(back_input(rows, flat_one), second))
+        output = pinned(image_of(after(far_out, second)))
+        moving[0], output = together(moving[0], output)
         first_own, other = sums(((1, (0, 1, 2)), (4, ())), moving)
         moving = [along(first_own, -1), across(other)]
-        shards = own_shards([after(sums_one, first_own), sums_two, sums_three])
-        grad_input, own_expand = pinned(after(grad_input, first_own)), after(own_expand, first_own)
+        grad_input, own_expand = pinned(back_input(0, after(flat_one, first_own), far_input)), after(own_expand, first_own)
         far_expand = swap_x(own_expand)
-        moving[0], grad_input, far_expand, *shards = together(moving[0], grad_input, far_expand, *shards)
+        moving[0], grad_input, far_expand = together(moving[0], grad_input, far_expand)
         (own_reduce,) = sums(((0, (0, 1)),), moving)
         own_expand, far_expand = after(own_expand, own_reduce), after(far_expand, own_reduce)
         (grad_w_expand,) = join(own_expand, far_expand, [w_expand])

time: 208 us -> 200 us (0.962)
  waiting for transfers between devices: 75 us -> 61.4 us
  starting transfers between devices: 80.3 us -> 85 us
    ppermute x8, waiting for transfers between devices: 21.5 us -> 12.3 us  [along(): return lax.ppermute(values, CHIPS, pairs)]
    ppermute x12, waiting for transfers between devices: 14.5 us -> 10.8 us  [across(): return lax.ppermute(values, 'fsdp', [(f, f ^ 1) for f in range(8)])]
    optimization_barrier x1 -> x0, local copies, waits for them, and re-layouts: 2.82 us -> none  [after(): return lax.optimization_barrier((values,) + others)[0]]
    pallas_call x1 -> x2, local copies, waits for them, and re-layouts: 2.82 us -> 5.64 us  [call(): pl.pallas_call(kernel, out_shape=outs, in_specs=[sm] * scalars + [given]...]
    ppermute x8, starting transfers between devices: 8.36 us -> 11.1 us  [along(): return lax.ppermute(values, CHIPS, pairs)]
    ppermute x10, starting transfers between devices: 6.96 us -> 9.49 us  [swap_x(): return lax.ppermute(values, 'x', SWAP)]
    unnamed x12 -> x13, local copies, waits for them, and re-layouts: 2.81 us -> 4.92 us
  transfers between devices with their start and end apart: 78 -> 78, of which waited for: 46 -> 51; matrix products, arithmetic and copies ran while one was open for 4% -> 6% of each run, Pallas kernels for 11% -> 15%
where the time goes in v4:
time: 200 us
  starting transfers between devices  85 us (42%)
  waiting for transfers between devices  61.4 us (31%)
  Pallas kernels  40.9 us (20%)
  local copies, waits for them, and re-layouts  11.3 us (6%)
    ppermute x36, starting transfers between devices, sum_chips(): lax.ppermute(values, CHIPS, [(at, at ^ flip) for at in range(16)])  47.8 us
    pallas_call x30, Pallas kernels, call(): pl.pallas_call(kernel, out_shape=outs, in_specs=[sm] * scalars + [given]...  40.9 us
    ppermute x36, waiting for transfers between devices, sum_chips(): lax.ppermute(values, CHIPS, [(at, at ^ flip) for at in range(16)])  24.1 us
    ppermute x12, starting transfers between devices, across(): return lax.ppermute(values, 'fsdp', [(f, f ^ 1) for f in range(8)])  14.1 us
    ppermute x8, waiting for transfers between devices, along(): return lax.ppermute(values, CHIPS, pairs)  12.3 us
    ppermute x8, starting transfers between devices, along(): return lax.ppermute(values, CHIPS, pairs)  11.1 us
    ppermute x12, waiting for transfers between devices, across(): return lax.ppermute(values, 'fsdp', [(f, f ^ 1) for f in range(8)])  10.8 us
    ppermute x10, starting transfers between devices, swap_x(): return lax.ppermute(values, 'x', SWAP)  9.49 us
  transfers between devices with their start and end apart: 78, of which 51 were waited for; matrix products, arithmetic and copies ran while one was open for 6% of the time, Pallas kernels for 15%

profile of v4, /device:TPU:0, one launch (start us, length us, event | category | flops | bytes accessed | tf_op | source)
XLA Modules:
  0.0 200.0 jit_solution(16286311706395157287)
XLA Ops:
  1.2 1.9 pack.1.refs_0_
  3.1 2.6 %collective-permute-start.1 = (bf16[304,512]{1,0:T(8,128)(2,1)}, bf16[304,512]{1,0:T(8,128)(2,1)S(1)}, u32[]{:S(2)}, u32[]{:S(2)}) collective-permute-start(bf16[304,512]{1,0:T(8,128)(2,1)} %pack.1.refs_0_), channel_id=1, source_target_pairs={{0,4},{4,0},{8,12},{12,8},{16,20},{20,16},{24,28},{28,24},{1,5},{5... | collective-permute-start | bytes 933896 | tf_op jit(solution)/shard_map/ppermute | solution.py:625
  5.7 1.6 collective-permute-start
  7.3 2.1 %copy.30 = bf16[2,14,14,2048]{3,2,1,0:T(8,128)(2,1)S(1)} copy(bf16[2,14,14,2048]{3,0,2,1:T(2,128)(2,1)} %param.12) | data formatting | bytes 3211264
  9.7 2.1 %copy.31 = bf16[2,14,14,2048]{3,2,1,0:T(8,128)(2,1)S(1)} copy(bf16[2,14,14,2048]{3,0,2,1:T(2,128)(2,1)} %collective-permute-done.2) | data formatting | bytes 3211264
  12.1 1.8 collective-permute-done.1.refs_4_
  13.9 3.4 %collective-permute-done.refs_1_ = bf16[304,512]{1,0:T(8,128)(2,1)S(1)} collective-permute-done((bf16[304,512]{1,0:T(8,128)(2,1)}, bf16[304,512]{1,0:T(8,128)(2,1)S(1)}, u32[]{:S(2)}, u32[]{:S(2)}) %collective-permute-start) | collective-permute-done | bytes 311328 | tf_op jit(solution)/shard_map/ppermute | solution.py:621
  18.9 1.6 collective-permute-start.12
  21.6 4.3 %collective-permute-done.5.refs_5_ = bf16[304,512]{1,0:T(8,128)(2,1)S(1)} collective-permute-done((bf16[304,512]{1,0:T(8,128)(2,1)S(1)}, bf16[304,512]{1,0:T(8,128)(2,1)S(1)}, u32[]{:S(2)}, u32[]{:S(2)}) %collective-permute-start.5) | collective-permute-done | bytes 311328 | tf_op jit(solution)/shard_map/ppermute | solution.py:625
  26.4 4.6 %collective-permute-done.3.refs_3_ = bf16[304,512]{1,0:T(8,128)(2,1)S(1)} collective-permute-done((bf16[304,512]{1,0:T(8,128)(2,1)S(1)}, bf16[304,512]{1,0:T(8,128)(2,1)S(1)}, u32[]{:S(2)}, u32[]{:S(2)}) %collective-permute-start.3) | collective-permute-done | bytes 311328 | tf_op jit(solution)/shard_map/ppermute | solution.py:621
  31.0 1.5 collective-permute-start.8
  33.1 1.6 collective-permute-done.12.refs_1_
  34.8 2.2 %turn.1 = (bf16[2048,896]{1,0:T(8,128)(2,1)S(1)}, f32[896,128]{1,0:T(8,128)S(1)}) custom-call(s32[4]{0:T(128)S(1)} %pad_add_fusion.valid, bf16[448,2048]{1,0:T(8,128)(2,1)S(1)} %bitcast.17, bf16[448,2048]{1,0:T(8,128)(2,1)S(1)} %bitcast.20), custom_call_target="tpu_custom_call" | custom-call | tf_op jit(solution)/shard_map/turn/pallas_call | solution.py:55
  37.0 2.3 %collective-permute-done.8.refs_7_ = bf16[304,512]{1,0:T(8,128)(2,1)S(1)} collective-permute-done((bf16[304,512]{1,0:T(8,128)(2,1)S(1)}, bf16[304,512]{1,0:T(8,128)(2,1)S(1)}, u32[]{:S(2)}, u32[]{:S(2)}) %collective-permute-start.8) | collective-permute-done | bytes 311328 | tf_op jit(solution)/shard_map/ppermute | solution.py:625
  39.4 2.7 %reduce.1 = (f32[896,512]{1,0:T(8,128)S(1)}, f32[3,512]{1,0:T(4,128)S(1)}) custom-call(s32[4]{0:T(128)S(1)} %pad_add_fusion.valid, f32[896,128]{1,0:T(8,128)S(1)} %get-tuple-element.201.mask, bf16[448,2048]{1,0:T(8,128)(2,1)S(1)} %bitcast.18, bf16[448,2048]{1,0:T(8,128)(2,1)S(1)} %bitcast.21, bf16[304,512]{1,0:T(8,128)(2,1)S(1)} %copy-done.2, ...), custom_call_target="tpu_custom_call" | custom-call | tf_op jit(solution)/shard_map/reduce/pallas_call | solution.py:55
  42.1 2.4 %collective-permute-start.11 = (f32[3,512]{1,0:T(4,128)S(1)}, f32[3,512]{1,0:T(4,128)S(1)}, u32[]{:S(2)}, u32[]{:S(2)}) collective-permute-start(f32[3,512]{1,0:T(4,128)S(1)} %get-tuple-element.210), channel_id=1, source_target_pairs={{0,6},{2,4},{4,2},{6,0},{8,14},{10,12},{12,10},{14,8},{16,22},{18,... | collective-permute-start | bytes 18440 | tf_op jit(solution)/shard_map/ppermute | solution.py:612
  46.7 1.5 collective-permute-done.10
  48.7 1.6 collective-permute-start.18
  50.3 2.2 %collective-permute-start.17 = (f32[3,512]{1,0:T(4,128)S(1)}, f32[3,512]{1,0:T(4,128)S(1)}, u32[]{:S(2)}, u32[]{:S(2)}) collective-permute-start(f32[3,512]{1,0:T(4,128)S(1)} %add_add_fusion.5), channel_id=1, source_target_pairs={{0,24},{2,26},{4,28},{6,30},{8,16},{10,18},{12,20},{14,22},{16,8},... | collective-permute-start | bytes 18440 | tf_op jit(solution)/shard_map/ppermute | solution.py:612
  52.6 2.1 %collective-permute-start.15 = (f32[3,512]{1,0:T(4,128)S(1)}, f32[3,512]{1,0:T(4,128)S(1)}, u32[]{:S(2)}, u32[]{:S(2)}) collective-permute-start(f32[3,512]{1,0:T(4,128)S(1)} %add_add_fusion.5), channel_id=1, source_target_pairs={{0,8},{2,10},{4,12},{6,14},{8,0},{10,2},{12,4},{14,6},{16,24},{18,... | collective-permute-start | bytes 18440 | tf_op jit(solution)/shard_map/ppermute | solution.py:612
  57.2 1.8 collective-permute-start.24
  59.0 3.5 %group.3 = (bf16[3,4,256,512]{3,2,1,0:T(8,128)(2,1)S(1)}, f32[896,512]{1,0:T(8,128)S(1)}, f32[2,512]{1,0:T(2,128)S(1)}) custom-call(f32[896,128]{1,0:T(8,128)S(1)} %get-tuple-element.201.mask, f32[3,512]{1,0:T(4,128)S(1)} %add_add_fusion.4.total.first, f32[4,512]{1,0:T(4,128)S(1)} %get-tuple-element.227.vectors, f32[896,512]{1,0:T(8,128)S(1)} %get-tuple-element.228.red, ...), custom_call_target="tpu_custom_call" | custom-call | tf_op jit(solution)/shard_map/group/pallas_call | solution.py:55
  62.5 2.5 %collective-permute-start.22 = (f32[2,512]{1,0:T(2,128)S(1)}, f32[2,512]{1,0:T(2,128)S(1)}, u32[]{:S(2)}, u32[]{:S(2)}) collective-permute-start(f32[2,512]{1,0:T(2,128)S(1)} %get-tuple-element.231), channel_id=1, source_target_pairs={{0,24},{2,26},{4,28},{6,30},{8,16},{10,18},{12,20},{14,22},{16,8},... | collective-permute-start | bytes 12296 | tf_op jit(solution)/shard_map/ppermute | solution.py:612
  65.0 2.0 collective-permute-start.20
  68.0 1.5 collective-permute-done.21
  69.5 1.5 collective-permute-start.27
  71.1 2.0 %collective-permute-start.26 = (f32[2,512]{1,0:T(2,128)S(1)}, f32[2,512]{1,0:T(2,128)S(1)}, u32[]{:S(2)}, u32[]{:S(2)}) collective-permute-start(f32[2,512]{1,0:T(2,128)S(1)} %add_add_fusion.11), channel_id=1, source_target_pairs={{0,4},{2,6},{4,0},{6,2},{8,12},{10,14},{12,8},{14,10},{16,20},{18,... | collective-permute-start | bytes 12296 | tf_op jit(solution)/shard_map/ppermute | solution.py:612
  74.7 2.0 %collective-permute-done.25 = f32[2,512]{1,0:T(2,128)S(1)} collective-permute-done((f32[2,512]{1,0:T(2,128)S(1)}, f32[2,512]{1,0:T(2,128)S(1)}, u32[]{:S(2)}, u32[]{:S(2)}) %collective-permute-start.25) | collective-permute-done | bytes 4128 | tf_op jit(solution)/shard_map/ppermute | solution.py:612
  79.8 2.4 %expand.1 = (bf16[896,1024]{1,0:T(8,128)(2,1)S(1)}, f32[896,1024]{1,0:T(8,128)S(1)}, f32[2,1024]{1,0:T(2,128)S(1)}) custom-call(f32[896,128]{1,0:T(8,128)S(1)} %get-tuple-element.201.mask, bf16[896,512]{1,0:T(8,128)(2,1)S(1)} %act.1.act_mine, bf16[896,512]{1,0:T(8,128)(2,1)S(1)} %collective-permute-done.28.act_far, bf16[1024,1024]{1,0:T(8,128)(2,1)S(1)} %assemble.1.weight), custom_call_target="tpu_custom_call" | custom-call | tf_op jit(solution)/shard_map/expand/pallas_call | solution.py:55
  83.7 2.0 %collective-permute-start.29 = (f32[2,1024]{1,0:T(2,128)S(1)}, f32[2,1024]{1,0:T(2,128)S(1)}, u32[]{:S(2)}, u32[]{:S(2)}) collective-permute-start(f32[2,1024]{1,0:T(2,128)S(1)} %get-tuple-element.255), channel_id=1, source_target_pairs={{0,2},{2,0},{4,6},{6,4},{8,10},{10,8},{12,14},{14,12},{16,18},{18,... | collective-permute-start | bytes 24584 | tf_op jit(solution)/shard_map/ppermute | solution.py:612
  87.3 1.5 collective-permute-start.35
  89.9 1.8 collective-permute-start.33
  93.6 3.4 %output.1 = (bf16[448,1024]{1,0:T(8,128)(2,1)S(1)}, bf16[448,1024]{1,0:T(8,128)(2,1)S(1)}, f32[896,1024]{1,0:T(8,128)S(1)}, f32[2,1024]{1,0:T(2,128)S(1)}) custom-call(s32[4]{0:T(128)S(1)} %pad_add_fusion.valid, f32[2,1024]{1,0:T(2,128)S(1)} %add_add_fusion.2.total, f32[3,512]{1,0:T(4,128)S(1)} %add_add_fusion.4.total.first, ...), custom_call_target="tpu_custom_call" | custom-call | tf_op jit(solution)/shard_map/output/pallas_call | solution.py:55
  97.1 1.8 collective-permute-start.38
  98.9 1.7 collective-permute-start.37
  102.5 1.7 collective-permute-done.36
  104.3 2.5 %collective-permute-start.41 = (f32[2,1024]{1,0:T(2,128)S(1)}, f32[2,1024]{1,0:T(2,128)S(1)}, u32[]{:S(2)}, u32[]{:S(2)}) collective-permute-start(f32[2,1024]{1,0:T(2,128)S(1)} %add_add_fusion.1), channel_id=1, source_target_pairs={{0,24},{2,26},{4,28},{6,30},{8,16},{10,18},{12,20},{14,22},{16,8},... | collective-permute-start | bytes 24584 | tf_op jit(solution)/shard_map/ppermute | solution.py:612
  109.8 1.5 collective-permute-done.40
  111.4 2.2 %back_expand.1 = (bf16[896,1024]{1,0:T(8,128)(2,1)S(1)}, bf16[896,512]{1,0:T(8,128)(2,1)S(1)}) custom-call(f32[896,128]{1,0:T(8,128)S(1)} %get-tuple-element.201.mask, f32[2,1024]{1,0:T(2,128)S(1)} %add_add_fusion.2.total, f32[2,1024]{1,0:T(2,128)S(1)} %add_add_fusion.sums, f32[3,512]{1,0:T(4,128)S(1)} %add_add_fusion.4.total.first, ...), custom_call_target="tpu_custom_call" | custom-call | tf_op jit(solution)/shard_map/back_expand/pallas_call | solution.py:55
  118.8 2.0 %collective-permute-start.43 = (f32[2,512]{1,0:T(2,128)S(1)}, f32[2,512]{1,0:T(2,128)S(1)}, u32[]{:S(2)}, u32[]{:S(2)}) collective-permute-start(f32[2,512]{1,0:T(2,128)S(1)} %get-tuple-element.278), channel_id=1, source_target_pairs={{0,2},{2,0},{4,6},{6,4},{8,10},{10,8},{12,14},{14,12},{16,18},{18,... | collective-permute-start | bytes 12296 | tf_op jit(solution)/shard_map/ppermute | solution.py:612
  120.8 2.4 %weight_expand.1.keep = bf16[1024,1024]{1,0:T(8,128)(2,1)S(1)} custom-call(bf16[896,1024]{1,0:T(8,128)(2,1)S(1)} %get-tuple-element.283.act, bf16[896,1024]{1,0:T(8,128)(2,1)S(1)} %get-tuple-element.276.flat), custom_call_target="tpu_custom_call" | custom-call | tf_op jit(solution)/shard_map/weight_expand/pallas_call | solution.py:55
  124.5 1.7 collective-permute-start.48
  127.2 1.7 collective-permute-start.46
  131.1 2.3 %collective-permute-start.54 = (bf16[128,1024]{1,0:T(8,128)(2,1)S(1)}, bf16[128,1024]{1,0:T(8,128)(2,1)S(1)}, u32[]{:S(2)}, u32[]{:S(2)}) collective-permute-start(bf16[128,1024]{1,0:T(8,128)(2,1)S(1)} %get-tuple-element.311), channel_id=1, source_target_pairs={{0,24},{2,10},{4,28},{6,14},{8,0},{10,18},{12,4},{14,22},{16,8},{1... | collective-permute-start | bytes 786440 | tf_op jit(solution)/shard_map/ppermute | solution.py:621
  133.4 2.0 collective-permute-start.55
  135.3 4.1 %back_group.1 = (bf16[896,512]{1,0:T(8,128)(2,1)S(1)}, f32[896,512]{1,0:T(8,128)S(1)}, f32[2,512]{1,0:T(2,128)S(1)}) custom-call(f32[896,128]{1,0:T(8,128)S(1)} %get-tuple-element.201.mask, f32[2,512]{1,0:T(2,128)S(1)} %add_add_fusion.10.total, f32[2,512]{1,0:T(2,128)S(1)} %add_add_fusion.8.sums, f32[3,512]{1,0:T(4,128)S(1)} %add_add_fusion.4.total.first, ...), custom_call_target="tpu_custom_call" | custom-call | tf_op jit(solution)/shard_map/back_group/pallas_call | solution.py:55
  139.7 1.8 collective-permute-start.52
  141.5 1.5 collective-permute-start.51
  143.1 1.7 weight_group.1.group
  145.3 1.6 collective-permute-start.59
  146.9 1.5 collective-permute-start.58
  148.6 2.7 %collective-permute-start.56 = (f32[2,512]{1,0:T(2,128)S(1)}, f32[2,512]{1,0:T(2,128)S(1)}, u32[]{:S(2)}, u32[]{:S(2)}) collective-permute-start(f32[2,512]{1,0:T(2,128)S(1)} %add_add_fusion.7), channel_id=1, source_target_pairs={{0,8},{2,10},{4,12},{6,14},{8,0},{10,2},{12,4},{14,6},{16,24},{18,... | collective-permute-start | bytes 12296 | tf_op jit(solution)/shard_map/ppermute | solution.py:612
  157.3 2.0 %collective-permute-start.62 = (bf16[128,1024]{1,0:T(8,128)(2,1)S(1)}, bf16[128,1024]{1,0:T(8,128)(2,1)S(1)}, u32[]{:S(2)}, u32[]{:S(2)}) collective-permute-start(bf16[128,1024]{1,0:T(8,128)(2,1)S(1)} %expand_sum.6), channel_id=1, source_target_pairs={{0,24},{2,10},{4,28},{6,14},{8,0},{10,18},{12,4},{14,22},{16,8},{1... | collective-permute-start | bytes 786440 | tf_op jit(solution)/shard_map/ppermute | solution.py:621
  159.5 1.7 back_input.2
  161.7 2.0 collective-permute-done.62.refs_0_
  165.3 2.9 %collective-permute-start.65 = (bf16[304,512]{1,0:T(8,128)(2,1)S(1)}, bf16[304,512]{1,0:T(8,128)(2,1)S(1)}, u32[]{:S(2)}, u32[]{:S(2)}) collective-permute-start(bf16[304,512]{1,0:T(8,128)(2,1)S(1)} %get-tuple-element.338), channel_id=1, source_target_pairs={{0,2},{2,0},{1,3},{3,1},{4,6},{6,4},{5,7},{7,5},{8,10},{10,8},{9,1... | collective-permute-start | bytes 933896 | tf_op jit(solution)/shard_map/ppermute | solution.py:607
  170.2 2.8 %copy.36 = bf16[2,14,14,2048]{3,0,2,1:T(2,128)(2,1)} copy(bf16[2,14,14,2048]{3,2,1,0:T(8,128)(2,1)S(1)} %image.1) | data formatting | bytes 3211264 | tf_op jit(solution)/shard_map/image/pallas_call | solution.py:55
  173.0 2.8 %collective-permute-done.65.refs_0_ = bf16[304,512]{1,0:T(8,128)(2,1)S(1)} collective-permute-done((bf16[304,512]{1,0:T(8,128)(2,1)S(1)}, bf16[304,512]{1,0:T(8,128)(2,1)S(1)}, u32[]{:S(2)}, u32[]{:S(2)}) %collective-permute-start.65) | collective-permute-done | bytes 311328 | tf_op jit(solution)/shard_map/ppermute | solution.py:607
  178.8 2.8 %collective-permute-start.69 = (bf16[304,512]{1,0:T(8,128)(2,1)S(1)}, bf16[304,512]{1,0:T(8,128)(2,1)S(1)}, u32[]{:S(2)}, u32[]{:S(2)}) collective-permute-start(bf16[304,512]{1,0:T(8,128)(2,1)S(1)} %get-tuple-element.347), channel_id=1, source_target_pairs={{0,24},{2,10},{4,28},{6,14},{8,0},{10,18},{12,4},{14,22},{16,8},{1... | collective-permute-start | bytes 933896 | tf_op jit(solution)/shard_map/ppermute | solution.py:621
  183.3 2.0 back_input.3
  185.2 2.8 %copy.35 = bf16[2,14,14,2048]{3,0,2,1:T(2,128)(2,1)} copy(bf16[2,14,14,2048]{3,2,1,0:T(8,128)(2,1)S(1)} %back_input.3) | data formatting | bytes 3211264 | tf_op jit(solution)/shard_map/back_input/pallas_call | solution.py:55
  188.1 1.8 collective-permute-done.71.mine_x
  194.7 2.6 %collective-permute-done.73.mine_x = bf16[304,512]{1,0:T(8,128)(2,1)S(1)} collective-permute-done((bf16[304,512]{1,0:T(8,128)(2,1)S(1)}, bf16[304,512]{1,0:T(8,128)(2,1)S(1)}, u32[]{:S(2)}, u32[]{:S(2)}) %collective-permute-start.73) | collective-permute-done | bytes 311328 | tf_op jit(solution)/shard_map/ppermute | solution.py:607
  197.3 1.6 collective-permute-done.77.other_x
  (157 shorter events, 58.3 us)
Async XLA Ops:
  0.7 9.0 %collective-permute-start.2 = (bf16[2,14,14,2048]{3,0,2,1:T(2,128)(2,1)}, bf16[2,14,14,2048]{3,0,2,1:T(2,128)(2,1)}, u32[]{:S(2)}, u32[]{:S(2)}) collective-permute-start(bf16[2,14,14,2048]{3,0,2,1:T(2,128)(2,1)} %param.12), channel_id=1, source_target_pairs={{0,1},{1,0},{2,3},{3,2},{4,5},{5,4},{6,7},{7,6},{8,9},{9,8},{10,11... | collective-permute-start | bytes 4816904 | tf_op jit(solution)/shard_map/ppermute | solution.py:602
  3.1 10.8 %collective-permute-start.1 = (bf16[304,512]{1,0:T(8,128)(2,1)}, bf16[304,512]{1,0:T(8,128)(2,1)S(1)}, u32[]{:S(2)}, u32[]{:S(2)}) collective-permute-start(bf16[304,512]{1,0:T(8,128)(2,1)} %pack.1.refs_0_), channel_id=1, source_target_pairs={{0,4},{4,0},{8,12},{12,8},{16,20},{20,16},{24,28},{28,24},{1,5},{5... | collective-permute-start | bytes 933896 | tf_op jit(solution)/shard_map/ppermute | solution.py:625
  5.7 11.5 %collective-permute-start = (bf16[304,512]{1,0:T(8,128)(2,1)}, bf16[304,512]{1,0:T(8,128)(2,1)S(1)}, u32[]{:S(2)}, u32[]{:S(2)}) collective-permute-start(bf16[304,512]{1,0:T(8,128)(2,1)} %pack.1.refs_0_), channel_id=1, source_target_pairs={{0,8},{2,26},{4,12},{6,30},{8,16},{10,2},{12,20},{14,6},{16,24},{1... | collective-permute-start | bytes 933896 | tf_op jit(solution)/shard_map/ppermute | solution.py:621
  17.2 8.7 %collective-permute-start.5 = (bf16[304,512]{1,0:T(8,128)(2,1)S(1)}, bf16[304,512]{1,0:T(8,128)(2,1)S(1)}, u32[]{:S(2)}, u32[]{:S(2)}) collective-permute-start(bf16[304,512]{1,0:T(8,128)(2,1)S(1)} %collective-permute-done.refs_1_), channel_id=1, source_target_pairs={{0,4},{4,0},{8,12},{12,8},{16,20},{20,16},{24,28},{28,24},{1,5},{5... | collective-permute-start | bytes 933896 | tf_op jit(solution)/shard_map/ppermute | solution.py:625
  17.8 8.7 %collective-permute-start.4 = (bf16[304,512]{1,0:T(8,128)(2,1)S(1)}, bf16[304,512]{1,0:T(8,128)(2,1)S(1)}, u32[]{:S(2)}, u32[]{:S(2)}) collective-permute-start(bf16[304,512]{1,0:T(8,128)(2,1)S(1)} %collective-permute-done.refs_1_), channel_id=1, source_target_pairs={{0,2},{2,0},{1,3},{3,1},{4,6},{6,4},{5,7},{7,5},{8,10},{10,8},{9,1... | collective-permute-start | bytes 933896 | tf_op jit(solution)/shard_map/ppermute | solution.py:607
  18.6 12.4 %collective-permute-start.3 = (bf16[304,512]{1,0:T(8,128)(2,1)S(1)}, bf16[304,512]{1,0:T(8,128)(2,1)S(1)}, u32[]{:S(2)}, u32[]{:S(2)}) collective-permute-start(bf16[304,512]{1,0:T(8,128)(2,1)S(1)} %collective-permute-done.refs_1_), channel_id=1, source_target_pairs={{0,8},{2,26},{4,12},{6,30},{8,16},{10,2},{12,20},{14,6},{16,24},{1... | collective-permute-start | bytes 933896 | tf_op jit(solution)/shard_map/ppermute | solution.py:621
  18.9 15.7 %collective-permute-start.12 = (bf16[128,1024]{1,0:T(8,128)(2,1)S(1)}, bf16[128,1024]{1,0:T(8,128)(2,1)S(1)}, u32[]{:S(2)}, u32[]{:S(2)}) collective-permute-start(bf16[128,1024]{1,0:T(8,128)(2,1)S(1)} %constant_dynamic-slice_fusion.refs_0_), channel_id=1, source_target_pairs={{0,8},{2,26},{4,12},{6,30},{8,16},{10,2},{12,20},{14,6},{16,24},{1... | collective-permute-start | bytes 786440 | tf_op jit(solution)/shard_map/ppermute | solution.py:621
  31.0 8.3 %collective-permute-start.8 = (bf16[304,512]{1,0:T(8,128)(2,1)S(1)}, bf16[304,512]{1,0:T(8,128)(2,1)S(1)}, u32[]{:S(2)}, u32[]{:S(2)}) collective-permute-start(bf16[304,512]{1,0:T(8,128)(2,1)S(1)} %collective-permute-done.3.refs_3_), channel_id=1, source_target_pairs={{0,4},{4,0},{8,12},{12,8},{16,20},{20,16},{24,28},{28,24},{1,5},{5... | collective-permute-start | bytes 933896 | tf_op jit(solution)/shard_map/ppermute | solution.py:625
  32.5 6.9 %collective-permute-start.7 = (bf16[304,512]{1,0:T(8,128)(2,1)S(1)}, bf16[304,512]{1,0:T(8,128)(2,1)S(1)}, u32[]{:S(2)}, u32[]{:S(2)}) collective-permute-start(bf16[304,512]{1,0:T(8,128)(2,1)S(1)} %collective-permute-done.5.refs_5_), channel_id=1, source_target_pairs={{0,2},{2,0},{1,3},{3,1},{4,6},{6,4},{5,7},{7,5},{8,10},{10,8},{9,1... | collective-permute-start | bytes 933896 | tf_op jit(solution)/shard_map/ppermute | solution.py:607
  32.5 16.2 %collective-permute-start.14 = (bf16[128,1024]{1,0:T(8,128)(2,1)S(1)}, bf16[128,1024]{1,0:T(8,128)(2,1)S(1)}, u32[]{:S(2)}, u32[]{:S(2)}) collective-permute-start(bf16[128,1024]{1,0:T(8,128)(2,1)S(1)} %constant_dynamic-slice_fusion.refs_0_), channel_id=1, source_target_pairs={{0,4},{4,0},{8,12},{12,8},{16,20},{20,16},{24,28},{28,24},{1,5},{5... | collective-permute-start | bytes 786440 | tf_op jit(solution)/shard_map/ppermute | solution.py:625
  34.7 14.1 %collective-permute-start.13 = (bf16[128,1024]{1,0:T(8,128)(2,1)S(1)}, bf16[128,1024]{1,0:T(8,128)(2,1)S(1)}, u32[]{:S(2)}, u32[]{:S(2)}) collective-permute-start(bf16[128,1024]{1,0:T(8,128)(2,1)S(1)} %collective-permute-done.12.refs_1_), channel_id=1, source_target_pairs={{0,8},{2,26},{4,12},{6,30},{8,16},{10,2},{12,20},{14,6},{16,24},{1... | collective-permute-start | bytes 786440 | tf_op jit(solution)/shard_map/ppermute | solution.py:621
  42.1 4.6 %collective-permute-start.11 = (f32[3,512]{1,0:T(4,128)S(1)}, f32[3,512]{1,0:T(4,128)S(1)}, u32[]{:S(2)}, u32[]{:S(2)}) collective-permute-start(f32[3,512]{1,0:T(4,128)S(1)} %get-tuple-element.210), channel_id=1, source_target_pairs={{0,6},{2,4},{4,2},{6,0},{8,14},{10,12},{12,10},{14,8},{16,22},{18,... | collective-permute-start | bytes 18440 | tf_op jit(solution)/shard_map/ppermute | solution.py:612
  44.6 3.7 %collective-permute-start.10 = (f32[3,512]{1,0:T(4,128)S(1)}, f32[3,512]{1,0:T(4,128)S(1)}, u32[]{:S(2)}, u32[]{:S(2)}) collective-permute-start(f32[3,512]{1,0:T(4,128)S(1)} %get-tuple-element.210), channel_id=1, source_target_pairs={{0,4},{2,6},{4,0},{6,2},{8,12},{10,14},{12,8},{14,10},{16,20},{18,... | collective-permute-start | bytes 18440 | tf_op jit(solution)/shard_map/ppermute | solution.py:612
  48.7 8.4 %collective-permute-start.18 = (bf16[128,1024]{1,0:T(8,128)(2,1)S(1)}, bf16[128,1024]{1,0:T(8,128)(2,1)S(1)}, u32[]{:S(2)}, u32[]{:S(2)}) collective-permute-start(bf16[128,1024]{1,0:T(8,128)(2,1)S(1)} %collective-permute-done.12.refs_1_), channel_id=1, source_target_pairs={{0,4},{4,0},{8,12},{12,8},{16,20},{20,16},{24,28},{28,24},{1,5},{5... | collective-permute-start | bytes 786440 | tf_op jit(solution)/shard_map/ppermute | solution.py:625
  50.3 5.4 %collective-permute-start.17 = (f32[3,512]{1,0:T(4,128)S(1)}, f32[3,512]{1,0:T(4,128)S(1)}, u32[]{:S(2)}, u32[]{:S(2)}) collective-permute-start(f32[3,512]{1,0:T(4,128)S(1)} %add_add_fusion.5), channel_id=1, source_target_pairs={{0,24},{2,26},{4,28},{6,30},{8,16},{10,18},{12,20},{14,22},{16,8},... | collective-permute-start | bytes 18440 | tf_op jit(solution)/shard_map/ppermute | solution.py:612
  52.6 4.5 %collective-permute-start.16 = (f32[3,512]{1,0:T(4,128)S(1)}, f32[3,512]{1,0:T(4,128)S(1)}, u32[]{:S(2)}, u32[]{:S(2)}) collective-permute-start(f32[3,512]{1,0:T(4,128)S(1)} %add_add_fusion.5), channel_id=1, source_target_pairs={{0,16},{2,18},{4,20},{6,22},{8,24},{10,26},{12,28},{14,30},{16,0},... | collective-permute-start | bytes 18440 | tf_op jit(solution)/shard_map/ppermute | solution.py:612
  52.6 4.5 %collective-permute-start.15 = (f32[3,512]{1,0:T(4,128)S(1)}, f32[3,512]{1,0:T(4,128)S(1)}, u32[]{:S(2)}, u32[]{:S(2)}) collective-permute-start(f32[3,512]{1,0:T(4,128)S(1)} %add_add_fusion.5), channel_id=1, source_target_pairs={{0,8},{2,10},{4,12},{6,14},{8,0},{10,2},{12,4},{14,6},{16,24},{18,... | collective-permute-start | bytes 18440 | tf_op jit(solution)/shard_map/ppermute | solution.py:612
  54.7 7.8 %collective-permute-start.19 = (bf16[128,1024]{1,0:T(8,128)(2,1)S(1)}, bf16[128,1024]{1,0:T(8,128)(2,1)S(1)}, u32[]{:S(2)}, u32[]{:S(2)}) collective-permute-start(bf16[128,1024]{1,0:T(8,128)(2,1)S(1)} %collective-permute-done.12.refs_1_), channel_id=1, source_target_pairs={{0,2},{2,0},{1,3},{3,1},{4,6},{6,4},{5,7},{7,5},{8,10},{10,8},{9,1... | collective-permute-start | bytes 786440 | tf_op jit(solution)/shard_map/ppermute | solution.py:607
  57.1 12.4 %collective-permute-start.23 = (bf16[128,1024]{1,0:T(8,128)(2,1)S(1)}, bf16[128,1024]{1,0:T(8,128)(2,1)S(1)}, u32[]{:S(2)}, u32[]{:S(2)}) collective-permute-start(bf16[128,1024]{1,0:T(8,128)(2,1)S(1)} %collective-permute-done.18.refs_5_), channel_id=1, source_target_pairs={{0,2},{2,0},{1,3},{3,1},{4,6},{6,4},{5,7},{7,5},{8,10},{10,8},{9,1... | collective-permute-start | bytes 786440 | tf_op jit(solution)/shard_map/ppermute | solution.py:607
  57.2 12.3 %collective-permute-start.24 = (bf16[128,1024]{1,0:T(8,128)(2,1)S(1)}, bf16[128,1024]{1,0:T(8,128)(2,1)S(1)}, u32[]{:S(2)}, u32[]{:S(2)}) collective-permute-start(bf16[128,1024]{1,0:T(8,128)(2,1)S(1)} %collective-permute-done.13.refs_3_), channel_id=1, source_target_pairs={{0,4},{4,0},{8,12},{12,8},{16,20},{20,16},{24,28},{28,24},{1,5},{5... | collective-permute-start | bytes 786440 | tf_op jit(solution)/shard_map/ppermute | solution.py:625
  62.5 5.5 %collective-permute-start.22 = (f32[2,512]{1,0:T(2,128)S(1)}, f32[2,512]{1,0:T(2,128)S(1)}, u32[]{:S(2)}, u32[]{:S(2)}) collective-permute-start(f32[2,512]{1,0:T(2,128)S(1)} %get-tuple-element.231), channel_id=1, source_target_pairs={{0,24},{2,26},{4,28},{6,30},{8,16},{10,18},{12,20},{14,22},{16,8},... | collective-permute-start | bytes 12296 | tf_op jit(solution)/shard_map/ppermute | solution.py:612
  65.0 4.5 %collective-permute-start.21 = (f32[2,512]{1,0:T(2,128)S(1)}, f32[2,512]{1,0:T(2,128)S(1)}, u32[]{:S(2)}, u32[]{:S(2)}) collective-permute-start(f32[2,512]{1,0:T(2,128)S(1)} %get-tuple-element.231), channel_id=1, source_target_pairs={{0,16},{2,18},{4,20},{6,22},{8,24},{10,26},{12,28},{14,30},{16,0},... | collective-permute-start | bytes 12296 | tf_op jit(solution)/shard_map/ppermute | solution.py:612
  65.0 4.5 %collective-permute-start.20 = (f32[2,512]{1,0:T(2,128)S(1)}, f32[2,512]{1,0:T(2,128)S(1)}, u32[]{:S(2)}, u32[]{:S(2)}) collective-permute-start(f32[2,512]{1,0:T(2,128)S(1)} %get-tuple-element.231), channel_id=1, source_target_pairs={{0,8},{2,10},{4,12},{6,14},{8,0},{10,2},{12,4},{14,6},{16,24},{18,... | collective-permute-start | bytes 12296 | tf_op jit(solution)/shard_map/ppermute | solution.py:612
  69.5 4.6 %collective-permute-start.27 = (f32[2,512]{1,0:T(2,128)S(1)}, f32[2,512]{1,0:T(2,128)S(1)}, u32[]{:S(2)}, u32[]{:S(2)}) collective-permute-start(f32[2,512]{1,0:T(2,128)S(1)} %add_add_fusion.11), channel_id=1, source_target_pairs={{0,6},{2,4},{4,2},{6,0},{8,14},{10,12},{12,10},{14,8},{16,22},{18,... | collective-permute-start | bytes 12296 | tf_op jit(solution)/shard_map/ppermute | solution.py:612
  78.3 9.0 %collective-permute-start.32 = (bf16[448,1024]{1,0:T(8,128)(2,1)S(1)}, bf16[448,1024]{1,0:T(8,128)(2,1)S(1)}, u32[]{:S(2)}, u32[]{:S(2)}) collective-permute-start(bf16[448,1024]{1,0:T(8,128)(2,1)S(1)} %far_half.1), channel_id=1, source_target_pairs={{0,1},{1,0},{2,3},{3,2},{4,5},{5,4},{6,7},{7,6},{8,9},{9,8},{10,11... | collective-permute-start | bytes 2752520 | tf_op jit(solution)/shard_map/ppermute | solution.py:602
  82.1 4.6 %collective-permute-start.31 = (f32[2,1024]{1,0:T(2,128)S(1)}, f32[2,1024]{1,0:T(2,128)S(1)}, u32[]{:S(2)}, u32[]{:S(2)}) collective-permute-start(f32[2,1024]{1,0:T(2,128)S(1)} %get-tuple-element.255), channel_id=1, source_target_pairs={{0,6},{2,4},{4,2},{6,0},{8,14},{10,12},{12,10},{14,8},{16,22},{18,... | collective-permute-start | bytes 24584 | tf_op jit(solution)/shard_map/ppermute | solution.py:612
  82.3 4.5 %collective-permute-start.30 = (f32[2,1024]{1,0:T(2,128)S(1)}, f32[2,1024]{1,0:T(2,128)S(1)}, u32[]{:S(2)}, u32[]{:S(2)}) collective-permute-start(f32[2,1024]{1,0:T(2,128)S(1)} %get-tuple-element.255), channel_id=1, source_target_pairs={{0,4},{2,6},{4,0},{6,2},{8,12},{10,14},{12,8},{14,10},{16,20},{18,... | collective-permute-start | bytes 24584 | tf_op jit(solution)/shard_map/ppermute | solution.py:612
  83.7 3.7 %collective-permute-start.29 = (f32[2,1024]{1,0:T(2,128)S(1)}, f32[2,1024]{1,0:T(2,128)S(1)}, u32[]{:S(2)}, u32[]{:S(2)}) collective-permute-start(f32[2,1024]{1,0:T(2,128)S(1)} %get-tuple-element.255), channel_id=1, source_target_pairs={{0,2},{2,0},{4,6},{6,4},{8,10},{10,8},{12,14},{14,12},{16,18},{18,... | collective-permute-start | bytes 24584 | tf_op jit(solution)/shard_map/ppermute | solution.py:612
  87.3 5.5 %collective-permute-start.35 = (f32[2,1024]{1,0:T(2,128)S(1)}, f32[2,1024]{1,0:T(2,128)S(1)}, u32[]{:S(2)}, u32[]{:S(2)}) collective-permute-start(f32[2,1024]{1,0:T(2,128)S(1)} %add_add_fusion.3), channel_id=1, source_target_pairs={{0,24},{2,26},{4,28},{6,30},{8,16},{10,18},{12,20},{14,22},{16,8},... | collective-permute-start | bytes 24584 | tf_op jit(solution)/shard_map/ppermute | solution.py:612
  88.9 4.5 %collective-permute-start.34 = (f32[2,1024]{1,0:T(2,128)S(1)}, f32[2,1024]{1,0:T(2,128)S(1)}, u32[]{:S(2)}, u32[]{:S(2)}) collective-permute-start(f32[2,1024]{1,0:T(2,128)S(1)} %add_add_fusion.3), channel_id=1, source_target_pairs={{0,16},{2,18},{4,20},{6,22},{8,24},{10,26},{12,28},{14,30},{16,0},... | collective-permute-start | bytes 24584 | tf_op jit(solution)/shard_map/ppermute | solution.py:612
  97.1 4.6 %collective-permute-start.38 = (f32[2,1024]{1,0:T(2,128)S(1)}, f32[2,1024]{1,0:T(2,128)S(1)}, u32[]{:S(2)}, u32[]{:S(2)}) collective-permute-start(f32[2,1024]{1,0:T(2,128)S(1)} %get-tuple-element.268), channel_id=1, source_target_pairs={{0,6},{2,4},{4,2},{6,0},{8,14},{10,12},{12,10},{14,8},{16,22},{18,... | collective-permute-start | bytes 24584 | tf_op jit(solution)/shard_map/ppermute | solution.py:612
  104.3 5.5 %collective-permute-start.41 = (f32[2,1024]{1,0:T(2,128)S(1)}, f32[2,1024]{1,0:T(2,128)S(1)}, u32[]{:S(2)}, u32[]{:S(2)}) collective-permute-start(f32[2,1024]{1,0:T(2,128)S(1)} %add_add_fusion.1), channel_id=1, source_target_pairs={{0,24},{2,26},{4,28},{6,30},{8,16},{10,18},{12,20},{14,22},{16,8},... | collective-permute-start | bytes 24584 | tf_op jit(solution)/shard_map/ppermute | solution.py:612
  106.7 4.6 %collective-permute-start.40 = (f32[2,1024]{1,0:T(2,128)S(1)}, f32[2,1024]{1,0:T(2,128)S(1)}, u32[]{:S(2)}, u32[]{:S(2)}) collective-permute-start(f32[2,1024]{1,0:T(2,128)S(1)} %add_add_fusion.1), channel_id=1, source_target_pairs={{0,16},{2,18},{4,20},{6,22},{8,24},{10,26},{12,28},{14,30},{16,0},... | collective-permute-start | bytes 24584 | tf_op jit(solution)/shard_map/ppermute | solution.py:612
  107.6 3.7 %collective-permute-start.39 = (f32[2,1024]{1,0:T(2,128)S(1)}, f32[2,1024]{1,0:T(2,128)S(1)}, u32[]{:S(2)}, u32[]{:S(2)}) collective-permute-start(f32[2,1024]{1,0:T(2,128)S(1)} %add_add_fusion.1), channel_id=1, source_target_pairs={{0,8},{2,10},{4,12},{6,14},{8,0},{10,2},{12,4},{14,6},{16,24},{18,... | collective-permute-start | bytes 24584 | tf_op jit(solution)/shard_map/ppermute | solution.py:612
  117.2 6.0 %collective-permute-start.45 = (f32[2,512]{1,0:T(2,128)S(1)}, f32[2,512]{1,0:T(2,128)S(1)}, u32[]{:S(2)}, u32[]{:S(2)}) collective-permute-start(f32[2,512]{1,0:T(2,128)S(1)} %get-tuple-element.278), channel_id=1, source_target_pairs={{0,6},{2,4},{4,2},{6,0},{8,14},{10,12},{12,10},{14,8},{16,22},{18,... | collective-permute-start | bytes 12296 | tf_op jit(solution)/shard_map/ppermute | solution.py:612
  117.4 5.9 %collective-permute-start.44 = (f32[2,512]{1,0:T(2,128)S(1)}, f32[2,512]{1,0:T(2,128)S(1)}, u32[]{:S(2)}, u32[]{:S(2)}) collective-permute-start(f32[2,512]{1,0:T(2,128)S(1)} %get-tuple-element.278), channel_id=1, source_target_pairs={{0,4},{2,6},{4,0},{6,2},{8,12},{10,14},{12,8},{14,10},{16,20},{18,... | collective-permute-start | bytes 12296 | tf_op jit(solution)/shard_map/ppermute | solution.py:612
  118.8 4.5 %collective-permute-start.43 = (f32[2,512]{1,0:T(2,128)S(1)}, f32[2,512]{1,0:T(2,128)S(1)}, u32[]{:S(2)}, u32[]{:S(2)}) collective-permute-start(f32[2,512]{1,0:T(2,128)S(1)} %get-tuple-element.278), channel_id=1, source_target_pairs={{0,2},{2,0},{4,6},{6,4},{8,10},{10,8},{12,14},{14,12},{16,18},{18,... | collective-permute-start | bytes 12296 | tf_op jit(solution)/shard_map/ppermute | solution.py:612
  123.3 7.6 %collective-permute-start.49 = (bf16[128,1024]{1,0:T(8,128)(2,1)S(1)}, bf16[128,1024]{1,0:T(8,128)(2,1)S(1)}, u32[]{:S(2)}, u32[]{:S(2)}) collective-permute-start(bf16[128,1024]{1,0:T(8,128)(2,1)S(1)} %get-tuple-element.290), channel_id=1, source_target_pairs={{0,2},{2,0},{1,3},{3,1},{4,6},{6,4},{5,7},{7,5},{8,10},{10,8},{9,1... | collective-permute-start | bytes 786440 | tf_op jit(solution)/shard_map/ppermute | solution.py:607
  124.4 6.5 %collective-permute-start.50 = (bf16[128,1024]{1,0:T(8,128)(2,1)S(1)}, bf16[128,1024]{1,0:T(8,128)(2,1)S(1)}, u32[]{:S(2)}, u32[]{:S(2)}) collective-permute-start(bf16[128,1024]{1,0:T(8,128)(2,1)S(1)} %get-tuple-element.291), channel_id=1, source_target_pairs={{0,4},{4,0},{8,12},{12,8},{16,20},{20,16},{24,28},{28,24},{1,5},{5... | collective-permute-start | bytes 786440 | tf_op jit(solution)/shard_map/ppermute | solution.py:625
  124.5 5.4 %collective-permute-start.48 = (f32[2,512]{1,0:T(2,128)S(1)}, f32[2,512]{1,0:T(2,128)S(1)}, u32[]{:S(2)}, u32[]{:S(2)}) collective-permute-start(f32[2,512]{1,0:T(2,128)S(1)} %add_add_fusion.9), channel_id=1, source_target_pairs={{0,24},{2,26},{4,28},{6,30},{8,16},{10,18},{12,20},{14,22},{16,8},... | collective-permute-start | bytes 12296 | tf_op jit(solution)/shard_map/ppermute | solution.py:612
  126.2 4.5 %collective-permute-start.47 = (f32[2,512]{1,0:T(2,128)S(1)}, f32[2,512]{1,0:T(2,128)S(1)}, u32[]{:S(2)}, u32[]{:S(2)}) collective-permute-start(f32[2,512]{1,0:T(2,128)S(1)} %add_add_fusion.9), channel_id=1, source_target_pairs={{0,16},{2,18},{4,20},{6,22},{8,24},{10,26},{12,28},{14,30},{16,0},... | collective-permute-start | bytes 12296 | tf_op jit(solution)/shard_map/ppermute | solution.py:612
  131.1 14.2 %collective-permute-start.54 = (bf16[128,1024]{1,0:T(8,128)(2,1)S(1)}, bf16[128,1024]{1,0:T(8,128)(2,1)S(1)}, u32[]{:S(2)}, u32[]{:S(2)}) collective-permute-start(bf16[128,1024]{1,0:T(8,128)(2,1)S(1)} %get-tuple-element.311), channel_id=1, source_target_pairs={{0,24},{2,10},{4,28},{6,14},{8,0},{10,18},{12,4},{14,22},{16,8},{1... | collective-permute-start | bytes 786440 | tf_op jit(solution)/shard_map/ppermute | solution.py:621
  133.4 11.9 %collective-permute-start.55 = (bf16[128,1024]{1,0:T(8,128)(2,1)S(1)}, bf16[128,1024]{1,0:T(8,128)(2,1)S(1)}, u32[]{:S(2)}, u32[]{:S(2)}) collective-permute-start(bf16[128,1024]{1,0:T(8,128)(2,1)S(1)} %get-tuple-element.314), channel_id=1, source_target_pairs={{0,4},{4,0},{8,12},{12,8},{16,20},{20,16},{24,28},{28,24},{1,5},{5... | collective-permute-start | bytes 786440 | tf_op jit(solution)/shard_map/ppermute | solution.py:625
  139.5 5.3 %collective-permute-start.53 = (f32[2,512]{1,0:T(2,128)S(1)}, f32[2,512]{1,0:T(2,128)S(1)}, u32[]{:S(2)}, u32[]{:S(2)}) collective-permute-start(f32[2,512]{1,0:T(2,128)S(1)} %get-tuple-element.302), channel_id=1, source_target_pairs={{0,6},{2,4},{4,2},{6,0},{8,14},{10,12},{12,10},{14,8},{16,22},{18,... | collective-permute-start | bytes 12296 | tf_op jit(solution)/shard_map/ppermute | solution.py:612
  139.7 5.1 %collective-permute-start.52 = (f32[2,512]{1,0:T(2,128)S(1)}, f32[2,512]{1,0:T(2,128)S(1)}, u32[]{:S(2)}, u32[]{:S(2)}) collective-permute-start(f32[2,512]{1,0:T(2,128)S(1)} %get-tuple-element.302), channel_id=1, source_target_pairs={{0,4},{2,6},{4,0},{6,2},{8,12},{10,14},{12,8},{14,10},{16,20},{18,... | collective-permute-start | bytes 12296 | tf_op jit(solution)/shard_map/ppermute | solution.py:612
  141.5 3.7 %collective-permute-start.51 = (f32[2,512]{1,0:T(2,128)S(1)}, f32[2,512]{1,0:T(2,128)S(1)}, u32[]{:S(2)}, u32[]{:S(2)}) collective-permute-start(f32[2,512]{1,0:T(2,128)S(1)} %get-tuple-element.302), channel_id=1, source_target_pairs={{0,2},{2,0},{4,6},{6,4},{8,10},{10,8},{12,14},{14,12},{16,18},{18,... | collective-permute-start | bytes 12296 | tf_op jit(solution)/shard_map/ppermute | solution.py:612
  145.3 7.8 %collective-permute-start.59 = (bf16[128,1024]{1,0:T(8,128)(2,1)S(1)}, bf16[128,1024]{1,0:T(8,128)(2,1)S(1)}, u32[]{:S(2)}, u32[]{:S(2)}) collective-permute-start(bf16[128,1024]{1,0:T(8,128)(2,1)S(1)} %get-tuple-element.319), channel_id=1, source_target_pairs={{0,2},{2,0},{1,3},{3,1},{4,6},{6,4},{5,7},{7,5},{8,10},{10,8},{9,1... | collective-permute-start | bytes 786440 | tf_op jit(solution)/shard_map/ppermute | solution.py:607
  146.9 7.1 %collective-permute-start.60 = (bf16[128,1024]{1,0:T(8,128)(2,1)S(1)}, bf16[128,1024]{1,0:T(8,128)(2,1)S(1)}, u32[]{:S(2)}, u32[]{:S(2)}) collective-permute-start(bf16[128,1024]{1,0:T(8,128)(2,1)S(1)} %get-tuple-element.320), channel_id=1, source_target_pairs={{0,4},{4,0},{8,12},{12,8},{16,20},{20,16},{24,28},{28,24},{1,5},{5... | collective-permute-start | bytes 786440 | tf_op jit(solution)/shard_map/ppermute | solution.py:625
  146.9 5.4 %collective-permute-start.58 = (f32[2,512]{1,0:T(2,128)S(1)}, f32[2,512]{1,0:T(2,128)S(1)}, u32[]{:S(2)}, u32[]{:S(2)}) collective-permute-start(f32[2,512]{1,0:T(2,128)S(1)} %add_add_fusion.7), channel_id=1, source_target_pairs={{0,24},{2,26},{4,28},{6,30},{8,16},{10,18},{12,20},{14,22},{16,8},... | collective-permute-start | bytes 12296 | tf_op jit(solution)/shard_map/ppermute | solution.py:612
  148.4 4.6 %collective-permute-start.57 = (f32[2,512]{1,0:T(2,128)S(1)}, f32[2,512]{1,0:T(2,128)S(1)}, u32[]{:S(2)}, u32[]{:S(2)}) collective-permute-start(f32[2,512]{1,0:T(2,128)S(1)} %add_add_fusion.7), channel_id=1, source_target_pairs={{0,16},{2,18},{4,20},{6,22},{8,24},{10,26},{12,28},{14,30},{16,0},... | collective-permute-start | bytes 12296 | tf_op jit(solution)/shard_map/ppermute | solution.py:612
  148.6 4.5 %collective-permute-start.56 = (f32[2,512]{1,0:T(2,128)S(1)}, f32[2,512]{1,0:T(2,128)S(1)}, u32[]{:S(2)}, u32[]{:S(2)}) collective-permute-start(f32[2,512]{1,0:T(2,128)S(1)} %add_add_fusion.7), channel_id=1, source_target_pairs={{0,8},{2,10},{4,12},{6,14},{8,0},{10,2},{12,4},{14,6},{16,24},{18,... | collective-permute-start | bytes 12296 | tf_op jit(solution)/shard_map/ppermute | solution.py:612
  155.1 8.6 %collective-permute-start.61 = (bf16[304,512]{1,0:T(8,128)(2,1)S(1)}, bf16[304,512]{1,0:T(8,128)(2,1)S(1)}, u32[]{:S(2)}, u32[]{:S(2)}) collective-permute-start(bf16[304,512]{1,0:T(8,128)(2,1)S(1)} %get-tuple-element.324), channel_id=1, source_target_pairs={{0,2},{2,0},{1,3},{3,1},{4,6},{6,4},{5,7},{7,5},{8,10},{10,8},{9,1... | collective-permute-start | bytes 933896 | tf_op jit(solution)/shard_map/ppermute | solution.py:607
  156.4 7.3 %collective-permute-start.64 = (bf16[304,512]{1,0:T(8,128)(2,1)S(1)}, bf16[304,512]{1,0:T(8,128)(2,1)S(1)}, u32[]{:S(2)}, u32[]{:S(2)}) collective-permute-start(bf16[304,512]{1,0:T(8,128)(2,1)S(1)} %get-tuple-element.337), channel_id=1, source_target_pairs={{0,4},{4,0},{8,12},{12,8},{16,20},{20,16},{24,28},{28,24},{1,5},{5... | collective-permute-start | bytes 933896 | tf_op jit(solution)/shard_map/ppermute | solution.py:625
  157.3 6.4 %collective-permute-start.62 = (bf16[128,1024]{1,0:T(8,128)(2,1)S(1)}, bf16[128,1024]{1,0:T(8,128)(2,1)S(1)}, u32[]{:S(2)}, u32[]{:S(2)}) collective-permute-start(bf16[128,1024]{1,0:T(8,128)(2,1)S(1)} %expand_sum.6), channel_id=1, source_target_pairs={{0,24},{2,10},{4,28},{6,14},{8,0},{10,18},{12,4},{14,22},{16,8},{1... | collective-permute-start | bytes 786440 | tf_op jit(solution)/shard_map/ppermute | solution.py:621
  164.7 18.6 %collective-permute-start.70 = (bf16[448,2048]{1,0:T(8,128)(2,1)S(1)}, bf16[448,2048]{1,0:T(8,128)(2,1)S(1)}, u32[]{:S(2)}, u32[]{:S(2)}) collective-permute-start(bf16[448,2048]{1,0:T(8,128)(2,1)S(1)} %back_input.2), channel_id=1, source_target_pairs={{0,1},{1,0},{2,3},{3,2},{4,5},{5,4},{6,7},{7,6},{8,9},{9,8},{10,11... | collective-permute-start | bytes 5505032 | tf_op jit(solution)/shard_map/ppermute | solution.py:602
  164.8 5.1 %collective-permute-start.66 = (bf16[448,1024]{1,0:T(8,128)(2,1)S(1)}, bf16[448,1024]{1,0:T(8,128)(2,1)S(1)}, u32[]{:S(2)}, u32[]{:S(2)}) collective-permute-start(bf16[448,1024]{1,0:T(8,128)(2,1)S(1)} %get-tuple-element.341), channel_id=1, source_target_pairs={{0,1},{1,0},{2,3},{3,2},{4,5},{5,4},{6,7},{7,6},{8,9},{9,8},{10,11... | collective-permute-start | bytes 2752520 | tf_op jit(solution)/shard_map/ppermute | solution.py:602
  165.3 10.5 %collective-permute-start.65 = (bf16[304,512]{1,0:T(8,128)(2,1)S(1)}, bf16[304,512]{1,0:T(8,128)(2,1)S(1)}, u32[]{:S(2)}, u32[]{:S(2)}) collective-permute-start(bf16[304,512]{1,0:T(8,128)(2,1)S(1)} %get-tuple-element.338), channel_id=1, source_target_pairs={{0,2},{2,0},{1,3},{3,1},{4,6},{6,4},{5,7},{7,5},{8,10},{10,8},{9,1... | collective-permute-start | bytes 933896 | tf_op jit(solution)/shard_map/ppermute | solution.py:607
  168.2 9.1 %collective-permute-start.68 = (bf16[304,512]{1,0:T(8,128)(2,1)S(1)}, bf16[304,512]{1,0:T(8,128)(2,1)S(1)}, u32[]{:S(2)}, u32[]{:S(2)}) collective-permute-start(bf16[304,512]{1,0:T(8,128)(2,1)S(1)} %get-tuple-element.346), channel_id=1, source_target_pairs={{0,4},{4,0},{8,12},{12,8},{16,20},{20,16},{24,28},{28,24},{1,5},{5... | collective-permute-start | bytes 933896 | tf_op jit(solution)/shard_map/ppermute | solution.py:625
  169.2 8.8 %collective-permute-start.67 = (bf16[304,512]{1,0:T(8,128)(2,1)S(1)}, bf16[304,512]{1,0:T(8,128)(2,1)S(1)}, u32[]{:S(2)}, u32[]{:S(2)}) collective-permute-start(bf16[304,512]{1,0:T(8,128)(2,1)S(1)} %get-tuple-element.342), channel_id=1, source_target_pairs={{0,24},{2,10},{4,28},{6,14},{8,0},{10,18},{12,4},{14,22},{16,8},{1... | collective-permute-start | bytes 933896 | tf_op jit(solution)/shard_map/ppermute | solution.py:621
  178.8 11.1 %collective-permute-start.69 = (bf16[304,512]{1,0:T(8,128)(2,1)S(1)}, bf16[304,512]{1,0:T(8,128)(2,1)S(1)}, u32[]{:S(2)}, u32[]{:S(2)}) collective-permute-start(bf16[304,512]{1,0:T(8,128)(2,1)S(1)} %get-tuple-element.347), channel_id=1, source_target_pairs={{0,24},{2,10},{4,28},{6,14},{8,0},{10,18},{12,4},{14,22},{16,8},{1... | collective-permute-start | bytes 933896 | tf_op jit(solution)/shard_map/ppermute | solution.py:621
  181.6 8.2 %collective-permute-start.72 = (bf16[304,512]{1,0:T(8,128)(2,1)S(1)}, bf16[304,512]{1,0:T(8,128)(2,1)S(1)}, u32[]{:S(2)}, u32[]{:S(2)}) collective-permute-start(bf16[304,512]{1,0:T(8,128)(2,1)S(1)} %get-tuple-element.355), channel_id=1, source_target_pairs={{0,4},{4,0},{8,12},{12,8},{16,20},{20,16},{24,28},{28,24},{1,5},{5... | collective-permute-start | bytes 933896 | tf_op jit(solution)/shard_map/ppermute | solution.py:625
  183.2 6.6 %collective-permute-start.71 = (bf16[128,1024]{1,0:T(8,128)(2,1)S(1)}, bf16[128,1024]{1,0:T(8,128)(2,1)S(1)}, u32[]{:S(2)}, u32[]{:S(2)}) collective-permute-start(bf16[128,1024]{1,0:T(8,128)(2,1)S(1)} %expand_sum.7.mine), channel_id=1, source_target_pairs={{0,2},{2,0},{1,3},{3,1},{4,6},{6,4},{5,7},{7,5},{8,10},{10,8},{9,1... | collective-permute-start | bytes 786440 | tf_op jit(solution)/shard_map/ppermute | solution.py:607
  190.3 7.0 %collective-permute-start.73 = (bf16[304,512]{1,0:T(8,128)(2,1)S(1)}, bf16[304,512]{1,0:T(8,128)(2,1)S(1)}, u32[]{:S(2)}, u32[]{:S(2)}) collective-permute-start(bf16[304,512]{1,0:T(8,128)(2,1)S(1)} %block_sum.5.mine), channel_id=1, source_target_pairs={{0,2},{2,0},{1,3},{3,1},{4,6},{6,4},{5,7},{7,5},{8,10},{10,8},{9,1... | collective-permute-start | bytes 933896 | tf_op jit(solution)/shard_map/ppermute | solution.py:607
  192.2 5.1 %collective-permute-start.76 = (bf16[304,512]{1,0:T(8,128)(2,1)S(1)}, bf16[304,512]{1,0:T(8,128)(2,1)S(1)}, u32[]{:S(2)}, u32[]{:S(2)}) collective-permute-start(bf16[304,512]{1,0:T(8,128)(2,1)S(1)} %block_sum.5.mine), channel_id=1, source_target_pairs={{0,1},{1,0},{2,3},{3,2},{4,5},{5,4},{6,7},{7,6},{8,9},{9,8},{10,11... | collective-permute-start | bytes 933896 | tf_op jit(solution)/shard_map/ppermute | solution.py:602
  (19 other events, 85.8 us)

commit v5 on v4

--- a/solution.py
+++ b/solution.py
@@ -513,16 +513,16 @@
         out[depth:tall, :] = more.astype(BF16)
 
 
-def expand_sum_kernel(places, keep, *refs):
+def expand_sum_kernel(places, depth, keep, *refs):
     arrived, outs = refs[: len(refs) - len(places)], refs[len(refs) - len(places) :]
-    depth = outs[0].shape[0]
-    for out, (block, chosen) in zip(outs, places):
-        value = keep[rows_of(block_owner(block), depth), :]
-        if chosen:
-            value = value.astype(F32)
-            for other in chosen:
-                value = value + arrived[other][...].astype(F32)
-        out[...] = value.astype(BF16)
+    for out, blocks in zip(outs, places):
+        for at, (block, chosen) in enumerate(blocks):
+            value = keep[rows_of(block_owner(block), depth), :]
+            if chosen:
+                value = value.astype(F32)
+                for other, begin in chosen:
+                    value = value + arrived[other][begin * depth : (begin + 1) * depth, :].astype(F32)
+            out[at * depth : (at + 1) * depth, :] = value.astype(BF16)
 
 
 def join_kernel(mine, mine_x, other, other_x, *outs):
@@ -609,11 +609,15 @@
 
 
 def sum_chips(values, flips):
-    got = [lax.ppermute(values, CHIPS, [(at, at ^ flip) for at in range(16)]) for flip in flips]
+    got = []
+    for flip in (*flips, 0):
+        pairs = [(2 * at + core, 2 * (at ^ flip) + 1 - core) for at in range(16) for core in range(2)]
+        got.append(lax.ppermute(values, (*CHIPS, "core"), pairs))
     got = together(*got)
-    for other in got:
-        values = values + other
-    return values
+    total = got[0]
+    for other in got[1:]:
+        total = total + other
+    return total
 
 
 def along(values, way):
@@ -812,19 +816,15 @@
 
     def expand_sums(places, arrived=()):
         return call(
-            functools.partial(expand_sum_kernel, places),
-            [shape((w_expand.shape[0], half_out), BF16)] * len(places),
+            functools.partial(expand_sum_kernel, places, w_expand.shape[0]),
+            [shape((w_expand.shape[0] * len(blocks), half_out), BF16) for blocks in places],
             [expand_term] + list(arrived), name="expand_sum",
         )
 
     if small:
-        middle, *moving = together(middle, *expand_sums(((6, ()), (7, ()))))
+        middle, *moving = together(middle, *expand_sums((((6, ()), (2, ())), ((7, ()), (4, ())))))
         moving = [swap_x(moving[0]), across(moving[1])]
-        sums_two, *moving = together(line_sum(middle), *moving)
-        sums_two, expand_first_other, expand_passed, expand_second, expand_other = together(
-            sums_two, *expand_sums(((5, (0,)), (2, ()), (3, (1,)), (4, ())), moving)
-        )
-        expand_second, expand_other = along(expand_second, -1), across(expand_other)
+        sums_two = line_sum(middle)
     else:
         sums_two = line_sum(middle)
         own_expand = lax.psum_scatter(expand_term, "fsdp", scatter_dimension=0, tiled=True)
@@ -842,14 +842,14 @@
     )
     middle, group_term = together(plane_sum(part), group_term)
     if small:
-        middle, expand_second, expand_first_other, expand_passed, expand_other = together(
-            middle, expand_second, expand_first_other, expand_passed, expand_other
-        )
-        moving = [swap_x(expand_passed), across(expand_first_other)]
+        middle, *moving = together(middle, *moving)
+        middle, expand_first_other, expand_second = together(middle, *expand_sums((((5, ((0, 0),)),), ((3, ((1, 0),)),)), moving))
+        expand_first_other, expand_second = across(expand_first_other), along(expand_second, -1)
     sums_one = line_sum(middle)
     if small:
-        sums_one, *moving = together(sums_one, *moving)
-        (expand_first_own,) = expand_sums(((1, (0, 1, 2)),), moving + [expand_second])
+        sums_one, expand_first_other, expand_second = together(sums_one, expand_first_other, expand_second)
+        expand_passed, expand_other = moving
+        (expand_first_own,) = expand_sums((((1, ((0, 1), (1, 0), (2, 0))),),), (expand_passed, expand_first_other, expand_second))
     tall = depth + extra
     places = ((6, ()), (7, ())) if small else tuple((at, ()) for at in range(size))
     flat_one, *moving = call(
@@ -906,7 +906,7 @@
         expand_first_own = along(expand_first_own, -1)
         shards = own_shards([sums_one, sums_two, sums_three])
         moving[0], expand_first_own, *shards = together(moving[0], expand_first_own, *shards)
-        (own_expand,) = expand_sums(((0, (0, 1)),), [expand_first_own, expand_other])
+        (own_expand,) = expand_sums((((0, ((0, 0), (1, 1))),),), [expand_first_own, expand_other])
         first_other, passed, second = sums(((5, (0,)), (2, ()), (3, (1,))), moving)
         moving = [swap_x(passed), along(second, -1), across(first_other)]
         far_input = swap_core(after(back_input(rows, flat_one), second))

time: 200 us -> 195 us (0.975)
  starting transfers between devices: 85 us -> 81.3 us
    ppermute x36 -> x48, waiting for transfers between devices: 24.1 us -> 20.8 us  [sum_chips(): got.append(lax.ppermute(values, (*CHIPS, 'core'), pairs))]
    ppermute x8, waiting for transfers between devices: 12.3 us -> 14.6 us  [along(): return lax.ppermute(values, CHIPS, pairs)]
    ppermute x36 -> x48, starting transfers between devices: 47.8 us -> 45.6 us  [sum_chips(): got.append(lax.ppermute(values, (*CHIPS, 'core'), pairs))]
    ppermute x10 -> x9, starting transfers between devices: 9.49 us -> 8.09 us  [swap_x(): return lax.ppermute(values, 'x', SWAP)]
    ppermute x12 -> x11, starting transfers between devices: 14.1 us -> 12.8 us  [across(): return lax.ppermute(values, 'fsdp', [(f, f ^ 1) for f in range(8)])]
    ppermute x10 -> x9, waiting for transfers between devices: 7.84 us -> 7.17 us  [swap_x(): return lax.ppermute(values, 'x', SWAP)]
    ppermute x12 -> x11, waiting for transfers between devices: 10.8 us -> 11.3 us  [across(): return lax.ppermute(values, 'fsdp', [(f, f ^ 1) for f in range(8)])]
  transfers between devices with their start and end apart: 78 -> 88, of which waited for: 51 -> 46; matrix products, arithmetic and copies ran while one was open for 6% -> 6% of each run, Pallas kernels for 15% -> 15%
where the time goes in v5:
time: 195 us
  starting transfers between devices  81.3 us (42%)
  waiting for transfers between devices  60 us (31%)
  Pallas kernels  41.2 us (21%)
  local copies, waits for them, and re-layouts  11.3 us (6%)
    ppermute x48, starting transfers between devices, sum_chips(): got.append(lax.ppermute(values, (*CHIPS, 'core'), pairs))  45.6 us
    pallas_call x30, Pallas kernels, call(): pl.pallas_call(kernel, out_shape=outs, in_specs=[sm] * scalars + [given]...  41.2 us
    ppermute x48, waiting for transfers between devices, sum_chips(): got.append(lax.ppermute(values, (*CHIPS, 'core'), pairs))  20.8 us
    ppermute x8, waiting for transfers between devices, along(): return lax.ppermute(values, CHIPS, pairs)  14.6 us
    ppermute x11, starting transfers between devices, across(): return lax.ppermute(values, 'fsdp', [(f, f ^ 1) for f in range(8)])  12.8 us
    ppermute x8, starting transfers between devices, along(): return lax.ppermute(values, CHIPS, pairs)  12.1 us
    ppermute x11, waiting for transfers between devices, across(): return lax.ppermute(values, 'fsdp', [(f, f ^ 1) for f in range(8)])  11.3 us
    ppermute x9, starting transfers between devices, swap_x(): return lax.ppermute(values, 'x', SWAP)  8.09 us
  transfers between devices with their start and end apart: 88, of which 46 were waited for; matrix products, arithmetic and copies ran while one was open for 6% of the time, Pallas kernels for 15%

profile of v5, /device:TPU:0, one launch (start us, length us, event | category | flops | bytes accessed | tf_op | source)
XLA Modules:
  0.0 195.3 jit_solution(1105117527307357889)
XLA Ops:
  1.2 1.9 pack.1.refs_0_
  3.1 2.6 %collective-permute-start.1 = (bf16[304,512]{1,0:T(8,128)(2,1)}, bf16[304,512]{1,0:T(8,128)(2,1)S(1)}, u32[]{:S(2)}, u32[]{:S(2)}) collective-permute-start(bf16[304,512]{1,0:T(8,128)(2,1)} %pack.1.refs_0_), channel_id=1, source_target_pairs={{0,4},{4,0},{8,12},{12,8},{16,20},{20,16},{24,28},{28,24},{1,5},{5... | collective-permute-start | bytes 933896 | tf_op jit(solution)/shard_map/ppermute | solution.py:629
  5.7 1.6 collective-permute-start
  7.3 2.1 %copy.30 = bf16[2,14,14,2048]{3,2,1,0:T(8,128)(2,1)S(1)} copy(bf16[2,14,14,2048]{3,0,2,1:T(2,128)(2,1)} %param.12) | data formatting | bytes 3211264
  9.7 2.1 %copy.31 = bf16[2,14,14,2048]{3,2,1,0:T(8,128)(2,1)S(1)} copy(bf16[2,14,14,2048]{3,0,2,1:T(2,128)(2,1)} %collective-permute-done.2) | data formatting | bytes 3211264
  12.1 1.8 collective-permute-done.1.refs_4_
  13.9 3.4 %collective-permute-done.refs_1_ = bf16[304,512]{1,0:T(8,128)(2,1)S(1)} collective-permute-done((bf16[304,512]{1,0:T(8,128)(2,1)}, bf16[304,512]{1,0:T(8,128)(2,1)S(1)}, u32[]{:S(2)}, u32[]{:S(2)}) %collective-permute-start) | collective-permute-done | bytes 311328 | tf_op jit(solution)/shard_map/ppermute | solution.py:625
  18.9 1.6 collective-permute-start.13
  21.6 4.3 %collective-permute-done.5.refs_5_ = bf16[304,512]{1,0:T(8,128)(2,1)S(1)} collective-permute-done((bf16[304,512]{1,0:T(8,128)(2,1)S(1)}, bf16[304,512]{1,0:T(8,128)(2,1)S(1)}, u32[]{:S(2)}, u32[]{:S(2)}) %collective-permute-start.5) | collective-permute-done | bytes 311328 | tf_op jit(solution)/shard_map/ppermute | solution.py:629
  26.4 4.6 %collective-permute-done.3.refs_3_ = bf16[304,512]{1,0:T(8,128)(2,1)S(1)} collective-permute-done((bf16[304,512]{1,0:T(8,128)(2,1)S(1)}, bf16[304,512]{1,0:T(8,128)(2,1)S(1)}, u32[]{:S(2)}, u32[]{:S(2)}) %collective-permute-start.3) | collective-permute-done | bytes 311328 | tf_op jit(solution)/shard_map/ppermute | solution.py:625
  31.0 1.5 collective-permute-start.8
  33.1 1.6 collective-permute-done.13.refs_1_
  34.8 2.2 %turn.1 = (bf16[2048,896]{1,0:T(8,128)(2,1)S(1)}, f32[896,128]{1,0:T(8,128)S(1)}) custom-call(s32[4]{0:T(128)S(1)} %pad_add_fusion.valid, bf16[448,2048]{1,0:T(8,128)(2,1)S(1)} %bitcast.17, bf16[448,2048]{1,0:T(8,128)(2,1)S(1)} %bitcast.20), custom_call_target="tpu_custom_call" | custom-call | tf_op jit(solution)/shard_map/turn/pallas_call | solution.py:55
  37.0 2.3 %collective-permute-done.8.refs_7_ = bf16[304,512]{1,0:T(8,128)(2,1)S(1)} collective-permute-done((bf16[304,512]{1,0:T(8,128)(2,1)S(1)}, bf16[304,512]{1,0:T(8,128)(2,1)S(1)}, u32[]{:S(2)}, u32[]{:S(2)}) %collective-permute-start.8) | collective-permute-done | bytes 311328 | tf_op jit(solution)/shard_map/ppermute | solution.py:629
  39.4 2.7 %reduce.1 = (f32[896,512]{1,0:T(8,128)S(1)}, f32[3,512]{1,0:T(4,128)S(1)}) custom-call(s32[4]{0:T(128)S(1)} %pad_add_fusion.valid, f32[896,128]{1,0:T(8,128)S(1)} %get-tuple-element.204.mask, bf16[448,2048]{1,0:T(8,128)(2,1)S(1)} %bitcast.18, bf16[448,2048]{1,0:T(8,128)(2,1)S(1)} %bitcast.21, bf16[304,512]{1,0:T(8,128)(2,1)S(1)} %copy-done.2, ...), custom_call_target="tpu_custom_call" | custom-call | tf_op jit(solution)/shard_map/reduce/pallas_call | solution.py:55
  42.2 2.5 %collective-permute-start.11 = (f32[3,512]{1,0:T(4,128)S(1)}, f32[3,512]{1,0:T(4,128)S(1)}, u32[]{:S(2)}, u32[]{:S(2)}) collective-permute-start(f32[3,512]{1,0:T(4,128)S(1)} %get-tuple-element.213), channel_id=1, source_target_pairs={{0,7},{1,6},{2,5},{3,4},{4,3},{5,2},{6,1},{7,0},{8,15},{9,14},{10,... | collective-permute-start | bytes 18440 | tf_op jit(solution)/shard_map/ppermute | solution.py:615
  46.4 1.4 collective-permute-done.10
  48.0 1.6 collective-permute-start.20
  50.2 1.8 collective-permute-start.18
  52.0 1.9 collective-permute-start.16
  58.7 3.5 %group.3 = (bf16[3,4,256,512]{3,2,1,0:T(8,128)(2,1)S(1)}, f32[896,512]{1,0:T(8,128)S(1)}, f32[2,512]{1,0:T(2,128)S(1)}) custom-call(f32[896,128]{1,0:T(8,128)S(1)} %get-tuple-element.204.mask, f32[3,512]{1,0:T(4,128)S(1)} %add_add_fusion.4.total.first, f32[4,512]{1,0:T(4,128)S(1)} %get-tuple-element.232.vectors, f32[896,512]{1,0:T(8,128)S(1)} %get-tuple-element.233.red, ...), custom_call_target="tpu_custom_call" | custom-call | tf_op jit(solution)/shard_map/group/pallas_call | solution.py:55
  62.3 1.9 collective-permute-start.24
  64.4 2.1 %collective-permute-start.22 = (f32[2,512]{1,0:T(2,128)S(1)}, f32[2,512]{1,0:T(2,128)S(1)}, u32[]{:S(2)}, u32[]{:S(2)}) collective-permute-start(f32[2,512]{1,0:T(2,128)S(1)} %get-tuple-element.236), channel_id=1, source_target_pairs={{0,9},{1,8},{2,11},{3,10},{4,13},{5,12},{6,15},{7,14},{8,1},{9,0},... | collective-permute-start | bytes 12296 | tf_op jit(solution)/shard_map/ppermute | solution.py:615
  68.4 2.1 %collective-permute-start.30 = (f32[2,512]{1,0:T(2,128)S(1)}, f32[2,512]{1,0:T(2,128)S(1)}, u32[]{:S(2)}, u32[]{:S(2)}) collective-permute-start(f32[2,512]{1,0:T(2,128)S(1)} %add_add_fusion.11), channel_id=1, source_target_pairs={{0,7},{1,6},{2,5},{3,4},{4,3},{5,2},{6,1},{7,0},{8,15},{9,14},{10,... | collective-permute-start | bytes 12296 | tf_op jit(solution)/shard_map/ppermute | solution.py:615
  77.7 2.4 %expand.1 = (bf16[896,1024]{1,0:T(8,128)(2,1)S(1)}, f32[896,1024]{1,0:T(8,128)S(1)}, f32[2,1024]{1,0:T(2,128)S(1)}) custom-call(f32[896,128]{1,0:T(8,128)S(1)} %get-tuple-element.204.mask, bf16[896,512]{1,0:T(8,128)(2,1)S(1)} %act.1.act_mine, bf16[896,512]{1,0:T(8,128)(2,1)S(1)} %collective-permute-done.32.act_far, bf16[1024,1024]{1,0:T(8,128)(2,1)S(1)} %assemble.1.weight), custom_call_target="tpu_custom_call" | custom-call | tf_op jit(solution)/shard_map/expand/pallas_call | solution.py:55
  81.7 1.7 collective-permute-start.33
  85.2 1.7 collective-permute-start.40
  87.8 1.3 collective-permute-start.38
  91.0 3.4 %output.1 = (bf16[448,1024]{1,0:T(8,128)(2,1)S(1)}, bf16[448,1024]{1,0:T(8,128)(2,1)S(1)}, f32[896,1024]{1,0:T(8,128)S(1)}, f32[2,1024]{1,0:T(2,128)S(1)}) custom-call(s32[4]{0:T(128)S(1)} %pad_add_fusion.valid, f32[2,1024]{1,0:T(2,128)S(1)} %add_add_fusion.2.total, f32[3,512]{1,0:T(4,128)S(1)} %add_add_fusion.4.total.first, ...), custom_call_target="tpu_custom_call" | custom-call | tf_op jit(solution)/shard_map/output/pallas_call | solution.py:55
  94.7 1.6 collective-permute-start.44
  100.9 2.0 %collective-permute-start.48 = (f32[2,1024]{1,0:T(2,128)S(1)}, f32[2,1024]{1,0:T(2,128)S(1)}, u32[]{:S(2)}, u32[]{:S(2)}) collective-permute-start(f32[2,1024]{1,0:T(2,128)S(1)} %add_add_fusion.1), channel_id=1, source_target_pairs={{0,25},{1,24},{2,27},{3,26},{4,29},{5,28},{6,31},{7,30},{8,17},{9,... | collective-permute-start | bytes 24584 | tf_op jit(solution)/shard_map/ppermute | solution.py:615
  106.9 2.2 %back_expand.1 = (bf16[896,1024]{1,0:T(8,128)(2,1)S(1)}, bf16[896,512]{1,0:T(8,128)(2,1)S(1)}) custom-call(f32[896,128]{1,0:T(8,128)S(1)} %get-tuple-element.204.mask, f32[2,1024]{1,0:T(2,128)S(1)} %add_add_fusion.2.total, f32[2,1024]{1,0:T(2,128)S(1)} %add_add_fusion.sums, f32[3,512]{1,0:T(4,128)S(1)} %add_add_fusion.4.total.first, ...), custom_call_target="tpu_custom_call" | custom-call | tf_op jit(solution)/shard_map/back_expand/pallas_call | solution.py:55
  109.6 1.1 back_part.1.mine
  111.7 1.3 back_act.1
  114.7 1.7 collective-permute-start.51
  116.4 2.4 %weight_expand.1.keep = bf16[1024,1024]{1,0:T(8,128)(2,1)S(1)} custom-call(bf16[896,1024]{1,0:T(8,128)(2,1)S(1)} %get-tuple-element.295.act, bf16[896,1024]{1,0:T(8,128)(2,1)S(1)} %get-tuple-element.287.flat), custom_call_target="tpu_custom_call" | custom-call | tf_op jit(solution)/shard_map/weight_expand/pallas_call | solution.py:55
  120.3 2.1 %collective-permute-start.57 = (f32[2,512]{1,0:T(2,128)S(1)}, f32[2,512]{1,0:T(2,128)S(1)}, u32[]{:S(2)}, u32[]{:S(2)}) collective-permute-start(f32[2,512]{1,0:T(2,128)S(1)} %add_add_fusion.9), channel_id=1, source_target_pairs={{0,25},{1,24},{2,27},{3,26},{4,29},{5,28},{6,31},{7,30},{8,17},{9,... | collective-permute-start | bytes 12296 | tf_op jit(solution)/shard_map/ppermute | solution.py:615
  122.9 1.6 collective-permute-start.55
  125.1 1.2 collective-permute-done.56
  126.4 4.2 %back_group.1 = (bf16[896,512]{1,0:T(8,128)(2,1)S(1)}, f32[896,512]{1,0:T(8,128)S(1)}, f32[2,512]{1,0:T(2,128)S(1)}) custom-call(f32[896,128]{1,0:T(8,128)S(1)} %get-tuple-element.204.mask, f32[2,512]{1,0:T(2,128)S(1)} %add_add_fusion.10.total, f32[2,512]{1,0:T(2,128)S(1)} %add_add_fusion.8.sums, f32[3,512]{1,0:T(4,128)S(1)} %add_add_fusion.4.total.first, ...), custom_call_target="tpu_custom_call" | custom-call | tf_op jit(solution)/shard_map/back_group/pallas_call | solution.py:55
  131.0 1.7 collective-permute-start.61
  133.9 1.7 weight_group.1.group
  136.6 1.4 collective-permute-start.69
  138.0 2.2 %collective-permute-start.70 = (bf16[128,1024]{1,0:T(8,128)(2,1)S(1)}, bf16[128,1024]{1,0:T(8,128)(2,1)S(1)}, u32[]{:S(2)}, u32[]{:S(2)}) collective-permute-start(bf16[128,1024]{1,0:T(8,128)(2,1)S(1)} %get-tuple-element.328), channel_id=1, source_target_pairs={{0,24},{2,10},{4,28},{6,14},{8,0},{10,18},{12,4},{14,22},{16,8},{1... | collective-permute-start | bytes 786440 | tf_op jit(solution)/shard_map/ppermute | solution.py:625
  140.2 1.2 collective-permute-start.67
  141.4 3.0 %collective-permute-start.65 = (f32[2,512]{1,0:T(2,128)S(1)}, f32[2,512]{1,0:T(2,128)S(1)}, u32[]{:S(2)}, u32[]{:S(2)}) collective-permute-start(f32[2,512]{1,0:T(2,128)S(1)} %add_add_fusion.7), channel_id=1, source_target_pairs={{0,9},{1,8},{2,11},{3,10},{4,13},{5,12},{6,15},{7,14},{8,1},{9,0},... | collective-permute-start | bytes 12296 | tf_op jit(solution)/shard_map/ppermute | solution.py:615
  144.4 1.9 collective-permute-done.67
  146.3 1.2 back_reduce.1
  147.6 2.7 %collective-permute-start.71 = (bf16[304,512]{1,0:T(8,128)(2,1)S(1)}, bf16[304,512]{1,0:T(8,128)(2,1)S(1)}, u32[]{:S(2)}, u32[]{:S(2)}) collective-permute-start(bf16[304,512]{1,0:T(8,128)(2,1)S(1)} %get-tuple-element.332), channel_id=1, source_target_pairs={{0,2},{2,0},{1,3},{3,1},{4,6},{6,4},{5,7},{7,5},{8,10},{10,8},{9,1... | collective-permute-start | bytes 933896 | tf_op jit(solution)/shard_map/ppermute | solution.py:607
  151.3 1.4 collective-permute-start.72
  152.7 1.7 back_input.2
  155.0 4.0 %collective-permute-done.72.refs_0_ = bf16[128,1024]{1,0:T(8,128)(2,1)S(1)} collective-permute-done((bf16[128,1024]{1,0:T(8,128)(2,1)S(1)}, bf16[128,1024]{1,0:T(8,128)(2,1)S(1)}, u32[]{:S(2)}, u32[]{:S(2)}) %collective-permute-start.72) | collective-permute-done | bytes 262176 | tf_op jit(solution)/shard_map/ppermute | solution.py:625
  161.2 1.6 collective-permute-start.75
  162.7 1.2 collective-permute-start.78
  164.0 1.4 collective-permute-start.77
  166.1 2.8 %copy.36 = bf16[2,14,14,2048]{3,0,2,1:T(2,128)(2,1)} copy(bf16[2,14,14,2048]{3,2,1,0:T(8,128)(2,1)S(1)} %image.1) | data formatting | bytes 3211264 | tf_op jit(solution)/shard_map/image/pallas_call | solution.py:55
  168.9 1.6 collective-permute-done.75.refs_0_
  170.5 1.3 collective-permute-done.78.refs_2_
  173.5 3.6 %collective-permute-start.79 = (bf16[304,512]{1,0:T(8,128)(2,1)S(1)}, bf16[304,512]{1,0:T(8,128)(2,1)S(1)}, u32[]{:S(2)}, u32[]{:S(2)}) collective-permute-start(bf16[304,512]{1,0:T(8,128)(2,1)S(1)} %get-tuple-element.354), channel_id=1, source_target_pairs={{0,24},{2,10},{4,28},{6,14},{8,0},{10,18},{12,4},{14,22},{16,8},{1... | collective-permute-start | bytes 933896 | tf_op jit(solution)/shard_map/ppermute | solution.py:625
  178.3 2.0 %back_input.3 = bf16[2,14,14,2048]{3,2,1,0:T(8,128)(2,1)S(1)} custom-call(bf16[896,512]{1,0:T(8,128)(2,1)S(1)} %get-tuple-element.355.flat, f32[896,1024]{1,0:T(8,128)S(1)} %get-tuple-element.286.grad, bf16[304,512]{1,0:T(8,128)(2,1)S(1)} %copy-done.2, bf16[304,512]{1,0:T(8,128)(2,1)S(1)} %collective-permute-done.refs_1_, ...), custom_call_target="tpu_custom_call" | custom-call | tf_op jit(solution)/shard_map/back_input/pallas_call | solution.py:55
  180.3 2.8 %copy.35 = bf16[2,14,14,2048]{3,0,2,1:T(2,128)(2,1)} copy(bf16[2,14,14,2048]{3,2,1,0:T(8,128)(2,1)S(1)} %back_input.3) | data formatting | bytes 3211264 | tf_op jit(solution)/shard_map/back_input/pallas_call | solution.py:55
  183.1 1.6 collective-permute-done.81.mine_x
  189.2 3.4 %collective-permute-done.83.mine_x = bf16[304,512]{1,0:T(8,128)(2,1)S(1)} collective-permute-done((bf16[304,512]{1,0:T(8,128)(2,1)S(1)}, bf16[304,512]{1,0:T(8,128)(2,1)S(1)}, u32[]{:S(2)}, u32[]{:S(2)}) %collective-permute-start.83) | collective-permute-done | bytes 311328 | tf_op jit(solution)/shard_map/ppermute | solution.py:607
  192.5 1.6 collective-permute-done.87.other_x
  (177 shorter events, 57.9 us)
Async XLA Ops:
  0.7 9.0 %collective-permute-start.2 = (bf16[2,14,14,2048]{3,0,2,1:T(2,128)(2,1)}, bf16[2,14,14,2048]{3,0,2,1:T(2,128)(2,1)}, u32[]{:S(2)}, u32[]{:S(2)}) collective-permute-start(bf16[2,14,14,2048]{3,0,2,1:T(2,128)(2,1)} %param.12), channel_id=1, source_target_pairs={{0,1},{1,0},{2,3},{3,2},{4,5},{5,4},{6,7},{7,6},{8,9},{9,8},{10,11... | collective-permute-start | bytes 4816904 | tf_op jit(solution)/shard_map/ppermute | solution.py:602
  3.1 10.8 %collective-permute-start.1 = (bf16[304,512]{1,0:T(8,128)(2,1)}, bf16[304,512]{1,0:T(8,128)(2,1)S(1)}, u32[]{:S(2)}, u32[]{:S(2)}) collective-permute-start(bf16[304,512]{1,0:T(8,128)(2,1)} %pack.1.refs_0_), channel_id=1, source_target_pairs={{0,4},{4,0},{8,12},{12,8},{16,20},{20,16},{24,28},{28,24},{1,5},{5... | collective-permute-start | bytes 933896 | tf_op jit(solution)/shard_map/ppermute | solution.py:629
  5.7 11.5 %collective-permute-start = (bf16[304,512]{1,0:T(8,128)(2,1)}, bf16[304,512]{1,0:T(8,128)(2,1)S(1)}, u32[]{:S(2)}, u32[]{:S(2)}) collective-permute-start(bf16[304,512]{1,0:T(8,128)(2,1)} %pack.1.refs_0_), channel_id=1, source_target_pairs={{0,8},{2,26},{4,12},{6,30},{8,16},{10,2},{12,20},{14,6},{16,24},{1... | collective-permute-start | bytes 933896 | tf_op jit(solution)/shard_map/ppermute | solution.py:625
  17.2 8.7 %collective-permute-start.5 = (bf16[304,512]{1,0:T(8,128)(2,1)S(1)}, bf16[304,512]{1,0:T(8,128)(2,1)S(1)}, u32[]{:S(2)}, u32[]{:S(2)}) collective-permute-start(bf16[304,512]{1,0:T(8,128)(2,1)S(1)} %collective-permute-done.refs_1_), channel_id=1, source_target_pairs={{0,4},{4,0},{8,12},{12,8},{16,20},{20,16},{24,28},{28,24},{1,5},{5... | collective-permute-start | bytes 933896 | tf_op jit(solution)/shard_map/ppermute | solution.py:629
  17.8 8.7 %collective-permute-start.4 = (bf16[304,512]{1,0:T(8,128)(2,1)S(1)}, bf16[304,512]{1,0:T(8,128)(2,1)S(1)}, u32[]{:S(2)}, u32[]{:S(2)}) collective-permute-start(bf16[304,512]{1,0:T(8,128)(2,1)S(1)} %collective-permute-done.refs_1_), channel_id=1, source_target_pairs={{0,2},{2,0},{1,3},{3,1},{4,6},{6,4},{5,7},{7,5},{8,10},{10,8},{9,1... | collective-permute-start | bytes 933896 | tf_op jit(solution)/shard_map/ppermute | solution.py:607
  18.6 12.4 %collective-permute-start.3 = (bf16[304,512]{1,0:T(8,128)(2,1)S(1)}, bf16[304,512]{1,0:T(8,128)(2,1)S(1)}, u32[]{:S(2)}, u32[]{:S(2)}) collective-permute-start(bf16[304,512]{1,0:T(8,128)(2,1)S(1)} %collective-permute-done.refs_1_), channel_id=1, source_target_pairs={{0,8},{2,26},{4,12},{6,30},{8,16},{10,2},{12,20},{14,6},{16,24},{1... | collective-permute-start | bytes 933896 | tf_op jit(solution)/shard_map/ppermute | solution.py:625
  18.9 15.7 %collective-permute-start.13 = (bf16[128,1024]{1,0:T(8,128)(2,1)S(1)}, bf16[128,1024]{1,0:T(8,128)(2,1)S(1)}, u32[]{:S(2)}, u32[]{:S(2)}) collective-permute-start(bf16[128,1024]{1,0:T(8,128)(2,1)S(1)} %constant_dynamic-slice_fusion.refs_0_), channel_id=1, source_target_pairs={{0,8},{2,26},{4,12},{6,30},{8,16},{10,2},{12,20},{14,6},{16,24},{1... | collective-permute-start | bytes 786440 | tf_op jit(solution)/shard_map/ppermute | solution.py:625
  31.0 8.3 %collective-permute-start.8 = (bf16[304,512]{1,0:T(8,128)(2,1)S(1)}, bf16[304,512]{1,0:T(8,128)(2,1)S(1)}, u32[]{:S(2)}, u32[]{:S(2)}) collective-permute-start(bf16[304,512]{1,0:T(8,128)(2,1)S(1)} %collective-permute-done.3.refs_3_), channel_id=1, source_target_pairs={{0,4},{4,0},{8,12},{12,8},{16,20},{20,16},{24,28},{28,24},{1,5},{5... | collective-permute-start | bytes 933896 | tf_op jit(solution)/shard_map/ppermute | solution.py:629
  32.5 6.9 %collective-permute-start.7 = (bf16[304,512]{1,0:T(8,128)(2,1)S(1)}, bf16[304,512]{1,0:T(8,128)(2,1)S(1)}, u32[]{:S(2)}, u32[]{:S(2)}) collective-permute-start(bf16[304,512]{1,0:T(8,128)(2,1)S(1)} %collective-permute-done.5.refs_5_), channel_id=1, source_target_pairs={{0,2},{2,0},{1,3},{3,1},{4,6},{6,4},{5,7},{7,5},{8,10},{10,8},{9,1... | collective-permute-start | bytes 933896 | tf_op jit(solution)/shard_map/ppermute | solution.py:607
  32.5 15.4 %collective-permute-start.15 = (bf16[128,1024]{1,0:T(8,128)(2,1)S(1)}, bf16[128,1024]{1,0:T(8,128)(2,1)S(1)}, u32[]{:S(2)}, u32[]{:S(2)}) collective-permute-start(bf16[128,1024]{1,0:T(8,128)(2,1)S(1)} %constant_dynamic-slice_fusion.refs_0_), channel_id=1, source_target_pairs={{0,4},{4,0},{8,12},{12,8},{16,20},{20,16},{24,28},{28,24},{1,5},{5... | collective-permute-start | bytes 786440 | tf_op jit(solution)/shard_map/ppermute | solution.py:629
  34.7 13.3 %collective-permute-start.14 = (bf16[128,1024]{1,0:T(8,128)(2,1)S(1)}, bf16[128,1024]{1,0:T(8,128)(2,1)S(1)}, u32[]{:S(2)}, u32[]{:S(2)}) collective-permute-start(bf16[128,1024]{1,0:T(8,128)(2,1)S(1)} %collective-permute-done.13.refs_1_), channel_id=1, source_target_pairs={{0,8},{2,26},{4,12},{6,30},{8,16},{10,2},{12,20},{14,6},{16,24},{1... | collective-permute-start | bytes 786440 | tf_op jit(solution)/shard_map/ppermute | solution.py:625
  42.2 4.2 %collective-permute-start.11 = (f32[3,512]{1,0:T(4,128)S(1)}, f32[3,512]{1,0:T(4,128)S(1)}, u32[]{:S(2)}, u32[]{:S(2)}) collective-permute-start(f32[3,512]{1,0:T(4,128)S(1)} %get-tuple-element.213), channel_id=1, source_target_pairs={{0,7},{1,6},{2,5},{3,4},{4,3},{5,2},{6,1},{7,0},{8,15},{9,14},{10,... | collective-permute-start | bytes 18440 | tf_op jit(solution)/shard_map/ppermute | solution.py:615
  48.0 8.7 %collective-permute-start.20 = (bf16[128,1024]{1,0:T(8,128)(2,1)S(1)}, bf16[128,1024]{1,0:T(8,128)(2,1)S(1)}, u32[]{:S(2)}, u32[]{:S(2)}) collective-permute-start(bf16[128,1024]{1,0:T(8,128)(2,1)S(1)} %collective-permute-done.13.refs_1_), channel_id=1, source_target_pairs={{0,4},{4,0},{8,12},{12,8},{16,20},{20,16},{24,28},{28,24},{1,5},{5... | collective-permute-start | bytes 786440 | tf_op jit(solution)/shard_map/ppermute | solution.py:629
  49.7 12.4 %collective-permute-start.21 = (bf16[128,1024]{1,0:T(8,128)(2,1)S(1)}, bf16[128,1024]{1,0:T(8,128)(2,1)S(1)}, u32[]{:S(2)}, u32[]{:S(2)}) collective-permute-start(bf16[128,1024]{1,0:T(8,128)(2,1)S(1)} %collective-permute-done.13.refs_1_), channel_id=1, source_target_pairs={{0,2},{2,0},{1,3},{3,1},{4,6},{6,4},{5,7},{7,5},{8,10},{10,8},{9,1... | collective-permute-start | bytes 786440 | tf_op jit(solution)/shard_map/ppermute | solution.py:607
  50.2 4.9 %collective-permute-start.18 = (f32[3,512]{1,0:T(4,128)S(1)}, f32[3,512]{1,0:T(4,128)S(1)}, u32[]{:S(2)}, u32[]{:S(2)}) collective-permute-start(f32[3,512]{1,0:T(4,128)S(1)} %add_add_fusion.5), channel_id=1, source_target_pairs={{0,25},{1,24},{2,27},{3,26},{4,29},{5,28},{6,31},{7,30},{8,17},{9,... | collective-permute-start | bytes 18440 | tf_op jit(solution)/shard_map/ppermute | solution.py:615
  52.0 4.0 %collective-permute-start.17 = (f32[3,512]{1,0:T(4,128)S(1)}, f32[3,512]{1,0:T(4,128)S(1)}, u32[]{:S(2)}, u32[]{:S(2)}) collective-permute-start(f32[3,512]{1,0:T(4,128)S(1)} %add_add_fusion.5), channel_id=1, source_target_pairs={{0,17},{1,16},{2,19},{3,18},{4,21},{5,20},{6,23},{7,22},{8,25},{9,... | collective-permute-start | bytes 18440 | tf_op jit(solution)/shard_map/ppermute | solution.py:615
  52.0 4.0 %collective-permute-start.16 = (f32[3,512]{1,0:T(4,128)S(1)}, f32[3,512]{1,0:T(4,128)S(1)}, u32[]{:S(2)}, u32[]{:S(2)}) collective-permute-start(f32[3,512]{1,0:T(4,128)S(1)} %add_add_fusion.5), channel_id=1, source_target_pairs={{0,9},{1,8},{2,11},{3,10},{4,13},{5,12},{6,15},{7,14},{8,1},{9,0},... | collective-permute-start | bytes 18440 | tf_op jit(solution)/shard_map/ppermute | solution.py:615
  56.7 11.5 %collective-permute-start.26 = (bf16[128,1024]{1,0:T(8,128)(2,1)S(1)}, bf16[128,1024]{1,0:T(8,128)(2,1)S(1)}, u32[]{:S(2)}, u32[]{:S(2)}) collective-permute-start(bf16[128,1024]{1,0:T(8,128)(2,1)S(1)} %collective-permute-done.20.refs_5_), channel_id=1, source_target_pairs={{0,2},{2,0},{1,3},{3,1},{4,6},{6,4},{5,7},{7,5},{8,10},{10,8},{9,1... | collective-permute-start | bytes 786440 | tf_op jit(solution)/shard_map/ppermute | solution.py:607
  57.7 10.4 %collective-permute-start.27 = (bf16[128,1024]{1,0:T(8,128)(2,1)S(1)}, bf16[128,1024]{1,0:T(8,128)(2,1)S(1)}, u32[]{:S(2)}, u32[]{:S(2)}) collective-permute-start(bf16[128,1024]{1,0:T(8,128)(2,1)S(1)} %collective-permute-done.14.refs_3_), channel_id=1, source_target_pairs={{0,4},{4,0},{8,12},{12,8},{16,20},{20,16},{24,28},{28,24},{1,5},{5... | collective-permute-start | bytes 786440 | tf_op jit(solution)/shard_map/ppermute | solution.py:629
  62.3 4.9 %collective-permute-start.24 = (f32[2,512]{1,0:T(2,128)S(1)}, f32[2,512]{1,0:T(2,128)S(1)}, u32[]{:S(2)}, u32[]{:S(2)}) collective-permute-start(f32[2,512]{1,0:T(2,128)S(1)} %get-tuple-element.236), channel_id=1, source_target_pairs={{0,25},{1,24},{2,27},{3,26},{4,29},{5,28},{6,31},{7,30},{8,17},{9,... | collective-permute-start | bytes 12296 | tf_op jit(solution)/shard_map/ppermute | solution.py:615
  64.2 4.0 %collective-permute-start.23 = (f32[2,512]{1,0:T(2,128)S(1)}, f32[2,512]{1,0:T(2,128)S(1)}, u32[]{:S(2)}, u32[]{:S(2)}) collective-permute-start(f32[2,512]{1,0:T(2,128)S(1)} %get-tuple-element.236), channel_id=1, source_target_pairs={{0,17},{1,16},{2,19},{3,18},{4,21},{5,20},{6,23},{7,22},{8,25},{9,... | collective-permute-start | bytes 12296 | tf_op jit(solution)/shard_map/ppermute | solution.py:615
  64.4 3.8 %collective-permute-start.22 = (f32[2,512]{1,0:T(2,128)S(1)}, f32[2,512]{1,0:T(2,128)S(1)}, u32[]{:S(2)}, u32[]{:S(2)}) collective-permute-start(f32[2,512]{1,0:T(2,128)S(1)} %get-tuple-element.236), channel_id=1, source_target_pairs={{0,9},{1,8},{2,11},{3,10},{4,13},{5,12},{6,15},{7,14},{8,1},{9,0},... | collective-permute-start | bytes 12296 | tf_op jit(solution)/shard_map/ppermute | solution.py:615
  68.2 3.4 %collective-permute-start.31 = (f32[2,512]{1,0:T(2,128)S(1)}, f32[2,512]{1,0:T(2,128)S(1)}, u32[]{:S(2)}, u32[]{:S(2)}) collective-permute-start(f32[2,512]{1,0:T(2,128)S(1)} %add_add_fusion.11), channel_id=1, source_target_pairs={{0,1},{1,0},{2,3},{3,2},{4,5},{5,4},{6,7},{7,6},{8,9},{9,8},{10,11... | collective-permute-start | bytes 12296 | tf_op jit(solution)/shard_map/ppermute | solution.py:615
  68.4 4.0 %collective-permute-start.30 = (f32[2,512]{1,0:T(2,128)S(1)}, f32[2,512]{1,0:T(2,128)S(1)}, u32[]{:S(2)}, u32[]{:S(2)}) collective-permute-start(f32[2,512]{1,0:T(2,128)S(1)} %add_add_fusion.11), channel_id=1, source_target_pairs={{0,7},{1,6},{2,5},{3,4},{4,3},{5,2},{6,1},{7,0},{8,15},{9,14},{10,... | collective-permute-start | bytes 12296 | tf_op jit(solution)/shard_map/ppermute | solution.py:615
  76.6 8.2 %collective-permute-start.37 = (bf16[448,1024]{1,0:T(8,128)(2,1)S(1)}, bf16[448,1024]{1,0:T(8,128)(2,1)S(1)}, u32[]{:S(2)}, u32[]{:S(2)}) collective-permute-start(bf16[448,1024]{1,0:T(8,128)(2,1)S(1)} %far_half.1), channel_id=1, source_target_pairs={{0,1},{1,0},{2,3},{3,2},{4,5},{5,4},{6,7},{7,6},{8,9},{9,8},{10,11... | collective-permute-start | bytes 2752520 | tf_op jit(solution)/shard_map/ppermute | solution.py:602
  80.0 3.4 %collective-permute-start.36 = (f32[2,1024]{1,0:T(2,128)S(1)}, f32[2,1024]{1,0:T(2,128)S(1)}, u32[]{:S(2)}, u32[]{:S(2)}) collective-permute-start(f32[2,1024]{1,0:T(2,128)S(1)} %get-tuple-element.262), channel_id=1, source_target_pairs={{0,1},{1,0},{2,3},{3,2},{4,5},{5,4},{6,7},{7,6},{8,9},{9,8},{10,11... | collective-permute-start | bytes 24584 | tf_op jit(solution)/shard_map/ppermute | solution.py:615
  80.5 4.0 %collective-permute-start.35 = (f32[2,1024]{1,0:T(2,128)S(1)}, f32[2,1024]{1,0:T(2,128)S(1)}, u32[]{:S(2)}, u32[]{:S(2)}) collective-permute-start(f32[2,1024]{1,0:T(2,128)S(1)} %get-tuple-element.262), channel_id=1, source_target_pairs={{0,7},{1,6},{2,5},{3,4},{4,3},{5,2},{6,1},{7,0},{8,15},{9,14},{10,... | collective-permute-start | bytes 24584 | tf_op jit(solution)/shard_map/ppermute | solution.py:615
  80.8 3.7 %collective-permute-start.34 = (f32[2,1024]{1,0:T(2,128)S(1)}, f32[2,1024]{1,0:T(2,128)S(1)}, u32[]{:S(2)}, u32[]{:S(2)}) collective-permute-start(f32[2,1024]{1,0:T(2,128)S(1)} %get-tuple-element.262), channel_id=1, source_target_pairs={{0,5},{1,4},{2,7},{3,6},{4,1},{5,0},{6,3},{7,2},{8,13},{9,12},{10,... | collective-permute-start | bytes 24584 | tf_op jit(solution)/shard_map/ppermute | solution.py:615
  84.8 4.3 %collective-permute-start.41 = (f32[2,1024]{1,0:T(2,128)S(1)}, f32[2,1024]{1,0:T(2,128)S(1)}, u32[]{:S(2)}, u32[]{:S(2)}) collective-permute-start(f32[2,1024]{1,0:T(2,128)S(1)} %add_add_fusion.3), channel_id=1, source_target_pairs={{0,1},{1,0},{2,3},{3,2},{4,5},{5,4},{6,7},{7,6},{8,9},{9,8},{10,11... | collective-permute-start | bytes 24584 | tf_op jit(solution)/shard_map/ppermute | solution.py:615
  85.2 4.9 %collective-permute-start.40 = (f32[2,1024]{1,0:T(2,128)S(1)}, f32[2,1024]{1,0:T(2,128)S(1)}, u32[]{:S(2)}, u32[]{:S(2)}) collective-permute-start(f32[2,1024]{1,0:T(2,128)S(1)} %add_add_fusion.3), channel_id=1, source_target_pairs={{0,25},{1,24},{2,27},{3,26},{4,29},{5,28},{6,31},{7,30},{8,17},{9,... | collective-permute-start | bytes 24584 | tf_op jit(solution)/shard_map/ppermute | solution.py:615
  86.9 4.0 %collective-permute-start.39 = (f32[2,1024]{1,0:T(2,128)S(1)}, f32[2,1024]{1,0:T(2,128)S(1)}, u32[]{:S(2)}, u32[]{:S(2)}) collective-permute-start(f32[2,1024]{1,0:T(2,128)S(1)} %add_add_fusion.3), channel_id=1, source_target_pairs={{0,17},{1,16},{2,19},{3,18},{4,21},{5,20},{6,23},{7,22},{8,25},{9,... | collective-permute-start | bytes 24584 | tf_op jit(solution)/shard_map/ppermute | solution.py:615
  94.4 3.4 %collective-permute-start.45 = (f32[2,1024]{1,0:T(2,128)S(1)}, f32[2,1024]{1,0:T(2,128)S(1)}, u32[]{:S(2)}, u32[]{:S(2)}) collective-permute-start(f32[2,1024]{1,0:T(2,128)S(1)} %get-tuple-element.277), channel_id=1, source_target_pairs={{0,1},{1,0},{2,3},{3,2},{4,5},{5,4},{6,7},{7,6},{8,9},{9,8},{10,11... | collective-permute-start | bytes 24584 | tf_op jit(solution)/shard_map/ppermute | solution.py:615
  94.7 4.0 %collective-permute-start.44 = (f32[2,1024]{1,0:T(2,128)S(1)}, f32[2,1024]{1,0:T(2,128)S(1)}, u32[]{:S(2)}, u32[]{:S(2)}) collective-permute-start(f32[2,1024]{1,0:T(2,128)S(1)} %get-tuple-element.277), channel_id=1, source_target_pairs={{0,7},{1,6},{2,5},{3,4},{4,3},{5,2},{6,1},{7,0},{8,15},{9,14},{10,... | collective-permute-start | bytes 24584 | tf_op jit(solution)/shard_map/ppermute | solution.py:615
  100.5 4.3 %collective-permute-start.49 = (f32[2,1024]{1,0:T(2,128)S(1)}, f32[2,1024]{1,0:T(2,128)S(1)}, u32[]{:S(2)}, u32[]{:S(2)}) collective-permute-start(f32[2,1024]{1,0:T(2,128)S(1)} %add_add_fusion.1), channel_id=1, source_target_pairs={{0,1},{1,0},{2,3},{3,2},{4,5},{5,4},{6,7},{7,6},{8,9},{9,8},{10,11... | collective-permute-start | bytes 24584 | tf_op jit(solution)/shard_map/ppermute | solution.py:615
  100.9 4.9 %collective-permute-start.48 = (f32[2,1024]{1,0:T(2,128)S(1)}, f32[2,1024]{1,0:T(2,128)S(1)}, u32[]{:S(2)}, u32[]{:S(2)}) collective-permute-start(f32[2,1024]{1,0:T(2,128)S(1)} %add_add_fusion.1), channel_id=1, source_target_pairs={{0,25},{1,24},{2,27},{3,26},{4,29},{5,28},{6,31},{7,30},{8,17},{9,... | collective-permute-start | bytes 24584 | tf_op jit(solution)/shard_map/ppermute | solution.py:615
  102.9 4.0 %collective-permute-start.47 = (f32[2,1024]{1,0:T(2,128)S(1)}, f32[2,1024]{1,0:T(2,128)S(1)}, u32[]{:S(2)}, u32[]{:S(2)}) collective-permute-start(f32[2,1024]{1,0:T(2,128)S(1)} %add_add_fusion.1), channel_id=1, source_target_pairs={{0,17},{1,16},{2,19},{3,18},{4,21},{5,20},{6,23},{7,22},{8,25},{9,... | collective-permute-start | bytes 24584 | tf_op jit(solution)/shard_map/ppermute | solution.py:615
  113.0 5.9 %collective-permute-start.54 = (f32[2,512]{1,0:T(2,128)S(1)}, f32[2,512]{1,0:T(2,128)S(1)}, u32[]{:S(2)}, u32[]{:S(2)}) collective-permute-start(f32[2,512]{1,0:T(2,128)S(1)} %get-tuple-element.289), channel_id=1, source_target_pairs={{0,1},{1,0},{2,3},{3,2},{4,5},{5,4},{6,7},{7,6},{8,9},{9,8},{10,11... | collective-permute-start | bytes 12296 | tf_op jit(solution)/shard_map/ppermute | solution.py:615
  113.4 5.5 %collective-permute-start.53 = (f32[2,512]{1,0:T(2,128)S(1)}, f32[2,512]{1,0:T(2,128)S(1)}, u32[]{:S(2)}, u32[]{:S(2)}) collective-permute-start(f32[2,512]{1,0:T(2,128)S(1)} %get-tuple-element.289), channel_id=1, source_target_pairs={{0,7},{1,6},{2,5},{3,4},{4,3},{5,2},{6,1},{7,0},{8,15},{9,14},{10,... | collective-permute-start | bytes 12296 | tf_op jit(solution)/shard_map/ppermute | solution.py:615
  113.7 5.2 %collective-permute-start.52 = (f32[2,512]{1,0:T(2,128)S(1)}, f32[2,512]{1,0:T(2,128)S(1)}, u32[]{:S(2)}, u32[]{:S(2)}) collective-permute-start(f32[2,512]{1,0:T(2,128)S(1)} %get-tuple-element.289), channel_id=1, source_target_pairs={{0,5},{1,4},{2,7},{3,6},{4,1},{5,0},{6,3},{7,2},{8,13},{9,12},{10,... | collective-permute-start | bytes 12296 | tf_op jit(solution)/shard_map/ppermute | solution.py:615
  114.7 4.2 %collective-permute-start.51 = (f32[2,512]{1,0:T(2,128)S(1)}, f32[2,512]{1,0:T(2,128)S(1)}, u32[]{:S(2)}, u32[]{:S(2)}) collective-permute-start(f32[2,512]{1,0:T(2,128)S(1)} %get-tuple-element.289), channel_id=1, source_target_pairs={{0,3},{1,2},{2,1},{3,0},{4,7},{5,6},{6,5},{7,4},{8,11},{9,10},{10,... | collective-permute-start | bytes 12296 | tf_op jit(solution)/shard_map/ppermute | solution.py:615
  118.9 17.5 %collective-permute-start.63 = (bf16[256,1024]{1,0:T(8,128)(2,1)S(1)}, bf16[256,1024]{1,0:T(8,128)(2,1)S(1)}, u32[]{:S(2)}, u32[]{:S(2)}) collective-permute-start(bf16[256,1024]{1,0:T(8,128)(2,1)S(1)} %get-tuple-element.315), channel_id=1, source_target_pairs={{0,2},{2,0},{1,3},{3,1},{4,6},{6,4},{5,7},{7,5},{8,10},{10,8},{9,1... | collective-permute-start | bytes 1572872 | tf_op jit(solution)/shard_map/ppermute | solution.py:607
  119.6 16.8 %collective-permute-start.64 = (bf16[256,1024]{1,0:T(8,128)(2,1)S(1)}, bf16[256,1024]{1,0:T(8,128)(2,1)S(1)}, u32[]{:S(2)}, u32[]{:S(2)}) collective-permute-start(bf16[256,1024]{1,0:T(8,128)(2,1)S(1)} %get-tuple-element.316), channel_id=1, source_target_pairs={{0,4},{4,0},{8,12},{12,8},{16,20},{20,16},{24,28},{28,24},{1,5},{5... | collective-permute-start | bytes 1572872 | tf_op jit(solution)/shard_map/ppermute | solution.py:629
  120.3 4.8 %collective-permute-start.57 = (f32[2,512]{1,0:T(2,128)S(1)}, f32[2,512]{1,0:T(2,128)S(1)}, u32[]{:S(2)}, u32[]{:S(2)}) collective-permute-start(f32[2,512]{1,0:T(2,128)S(1)} %add_add_fusion.9), channel_id=1, source_target_pairs={{0,25},{1,24},{2,27},{3,26},{4,29},{5,28},{6,31},{7,30},{8,17},{9,... | collective-permute-start | bytes 12296 | tf_op jit(solution)/shard_map/ppermute | solution.py:615
  122.4 4.0 %collective-permute-start.56 = (f32[2,512]{1,0:T(2,128)S(1)}, f32[2,512]{1,0:T(2,128)S(1)}, u32[]{:S(2)}, u32[]{:S(2)}) collective-permute-start(f32[2,512]{1,0:T(2,128)S(1)} %add_add_fusion.9), channel_id=1, source_target_pairs={{0,17},{1,16},{2,19},{3,18},{4,21},{5,20},{6,23},{7,22},{8,25},{9,... | collective-permute-start | bytes 12296 | tf_op jit(solution)/shard_map/ppermute | solution.py:615
  122.9 3.5 %collective-permute-start.55 = (f32[2,512]{1,0:T(2,128)S(1)}, f32[2,512]{1,0:T(2,128)S(1)}, u32[]{:S(2)}, u32[]{:S(2)}) collective-permute-start(f32[2,512]{1,0:T(2,128)S(1)} %add_add_fusion.9), channel_id=1, source_target_pairs={{0,9},{1,8},{2,11},{3,10},{4,13},{5,12},{6,15},{7,14},{8,1},{9,0},... | collective-permute-start | bytes 12296 | tf_op jit(solution)/shard_map/ppermute | solution.py:615
  131.0 4.7 %collective-permute-start.61 = (f32[2,512]{1,0:T(2,128)S(1)}, f32[2,512]{1,0:T(2,128)S(1)}, u32[]{:S(2)}, u32[]{:S(2)}) collective-permute-start(f32[2,512]{1,0:T(2,128)S(1)} %get-tuple-element.305), channel_id=1, source_target_pairs={{0,7},{1,6},{2,5},{3,4},{4,3},{5,2},{6,1},{7,0},{8,15},{9,14},{10,... | collective-permute-start | bytes 12296 | tf_op jit(solution)/shard_map/ppermute | solution.py:615
  136.6 9.7 %collective-permute-start.69 = (bf16[128,1024]{1,0:T(8,128)(2,1)S(1)}, bf16[128,1024]{1,0:T(8,128)(2,1)S(1)}, u32[]{:S(2)}, u32[]{:S(2)}) collective-permute-start(bf16[128,1024]{1,0:T(8,128)(2,1)S(1)} %get-tuple-element.327), channel_id=1, source_target_pairs={{0,4},{4,0},{8,12},{12,8},{16,20},{20,16},{24,28},{28,24},{1,5},{5... | collective-permute-start | bytes 786440 | tf_op jit(solution)/shard_map/ppermute | solution.py:629
  138.0 8.3 %collective-permute-start.70 = (bf16[128,1024]{1,0:T(8,128)(2,1)S(1)}, bf16[128,1024]{1,0:T(8,128)(2,1)S(1)}, u32[]{:S(2)}, u32[]{:S(2)}) collective-permute-start(bf16[128,1024]{1,0:T(8,128)(2,1)S(1)} %get-tuple-element.328), channel_id=1, source_target_pairs={{0,24},{2,10},{4,28},{6,14},{8,0},{10,18},{12,4},{14,22},{16,8},{1... | collective-permute-start | bytes 786440 | tf_op jit(solution)/shard_map/ppermute | solution.py:625
  140.2 6.1 %collective-permute-start.67 = (f32[2,512]{1,0:T(2,128)S(1)}, f32[2,512]{1,0:T(2,128)S(1)}, u32[]{:S(2)}, u32[]{:S(2)}) collective-permute-start(f32[2,512]{1,0:T(2,128)S(1)} %add_add_fusion.7), channel_id=1, source_target_pairs={{0,25},{1,24},{2,27},{3,26},{4,29},{5,28},{6,31},{7,30},{8,17},{9,... | collective-permute-start | bytes 12296 | tf_op jit(solution)/shard_map/ppermute | solution.py:615
  141.4 4.8 %collective-permute-start.66 = (f32[2,512]{1,0:T(2,128)S(1)}, f32[2,512]{1,0:T(2,128)S(1)}, u32[]{:S(2)}, u32[]{:S(2)}) collective-permute-start(f32[2,512]{1,0:T(2,128)S(1)} %add_add_fusion.7), channel_id=1, source_target_pairs={{0,17},{1,16},{2,19},{3,18},{4,21},{5,20},{6,23},{7,22},{8,25},{9,... | collective-permute-start | bytes 12296 | tf_op jit(solution)/shard_map/ppermute | solution.py:615
  141.4 4.8 %collective-permute-start.65 = (f32[2,512]{1,0:T(2,128)S(1)}, f32[2,512]{1,0:T(2,128)S(1)}, u32[]{:S(2)}, u32[]{:S(2)}) collective-permute-start(f32[2,512]{1,0:T(2,128)S(1)} %add_add_fusion.7), channel_id=1, source_target_pairs={{0,9},{1,8},{2,11},{3,10},{4,13},{5,12},{6,15},{7,14},{8,1},{9,0},... | collective-permute-start | bytes 12296 | tf_op jit(solution)/shard_map/ppermute | solution.py:615
  147.6 11.5 %collective-permute-start.71 = (bf16[304,512]{1,0:T(8,128)(2,1)S(1)}, bf16[304,512]{1,0:T(8,128)(2,1)S(1)}, u32[]{:S(2)}, u32[]{:S(2)}) collective-permute-start(bf16[304,512]{1,0:T(8,128)(2,1)S(1)} %get-tuple-element.332), channel_id=1, source_target_pairs={{0,2},{2,0},{1,3},{3,1},{4,6},{6,4},{5,7},{7,5},{8,10},{10,8},{9,1... | collective-permute-start | bytes 933896 | tf_op jit(solution)/shard_map/ppermute | solution.py:607
  150.4 9.2 %collective-permute-start.74 = (bf16[304,512]{1,0:T(8,128)(2,1)S(1)}, bf16[304,512]{1,0:T(8,128)(2,1)S(1)}, u32[]{:S(2)}, u32[]{:S(2)}) collective-permute-start(bf16[304,512]{1,0:T(8,128)(2,1)S(1)} %get-tuple-element.344), channel_id=1, source_target_pairs={{0,4},{4,0},{8,12},{12,8},{16,20},{20,16},{24,28},{28,24},{1,5},{5... | collective-permute-start | bytes 933896 | tf_op jit(solution)/shard_map/ppermute | solution.py:629
  151.3 7.8 %collective-permute-start.72 = (bf16[128,1024]{1,0:T(8,128)(2,1)S(1)}, bf16[128,1024]{1,0:T(8,128)(2,1)S(1)}, u32[]{:S(2)}, u32[]{:S(2)}) collective-permute-start(bf16[128,1024]{1,0:T(8,128)(2,1)S(1)} %expand_sum.6), channel_id=1, source_target_pairs={{0,24},{2,10},{4,28},{6,14},{8,0},{10,18},{12,4},{14,22},{16,8},{1... | collective-permute-start | bytes 786440 | tf_op jit(solution)/shard_map/ppermute | solution.py:625
  160.6 17.7 %collective-permute-start.80 = (bf16[448,2048]{1,0:T(8,128)(2,1)S(1)}, bf16[448,2048]{1,0:T(8,128)(2,1)S(1)}, u32[]{:S(2)}, u32[]{:S(2)}) collective-permute-start(bf16[448,2048]{1,0:T(8,128)(2,1)S(1)} %back_input.2), channel_id=1, source_target_pairs={{0,1},{1,0},{2,3},{3,2},{4,5},{5,4},{6,7},{7,6},{8,9},{9,8},{10,11... | collective-permute-start | bytes 5505032 | tf_op jit(solution)/shard_map/ppermute | solution.py:602
  160.7 5.1 %collective-permute-start.76 = (bf16[448,1024]{1,0:T(8,128)(2,1)S(1)}, bf16[448,1024]{1,0:T(8,128)(2,1)S(1)}, u32[]{:S(2)}, u32[]{:S(2)}) collective-permute-start(bf16[448,1024]{1,0:T(8,128)(2,1)S(1)} %get-tuple-element.348), channel_id=1, source_target_pairs={{0,1},{1,0},{2,3},{3,2},{4,5},{5,4},{6,7},{7,6},{8,9},{9,8},{10,11... | collective-permute-start | bytes 2752520 | tf_op jit(solution)/shard_map/ppermute | solution.py:602
  161.2 9.3 %collective-permute-start.75 = (bf16[304,512]{1,0:T(8,128)(2,1)S(1)}, bf16[304,512]{1,0:T(8,128)(2,1)S(1)}, u32[]{:S(2)}, u32[]{:S(2)}) collective-permute-start(bf16[304,512]{1,0:T(8,128)(2,1)S(1)} %get-tuple-element.345), channel_id=1, source_target_pairs={{0,2},{2,0},{1,3},{3,1},{4,6},{6,4},{5,7},{7,5},{8,10},{10,8},{9,1... | collective-permute-start | bytes 933896 | tf_op jit(solution)/shard_map/ppermute | solution.py:607
  162.7 9.1 %collective-permute-start.78 = (bf16[304,512]{1,0:T(8,128)(2,1)S(1)}, bf16[304,512]{1,0:T(8,128)(2,1)S(1)}, u32[]{:S(2)}, u32[]{:S(2)}) collective-permute-start(bf16[304,512]{1,0:T(8,128)(2,1)S(1)} %get-tuple-element.353), channel_id=1, source_target_pairs={{0,4},{4,0},{8,12},{12,8},{16,20},{20,16},{24,28},{28,24},{1,5},{5... | collective-permute-start | bytes 933896 | tf_op jit(solution)/shard_map/ppermute | solution.py:629
  164.0 8.8 %collective-permute-start.77 = (bf16[304,512]{1,0:T(8,128)(2,1)S(1)}, bf16[304,512]{1,0:T(8,128)(2,1)S(1)}, u32[]{:S(2)}, u32[]{:S(2)}) collective-permute-start(bf16[304,512]{1,0:T(8,128)(2,1)S(1)} %get-tuple-element.349), channel_id=1, source_target_pairs={{0,24},{2,10},{4,28},{6,14},{8,0},{10,18},{12,4},{14,22},{16,8},{1... | collective-permute-start | bytes 933896 | tf_op jit(solution)/shard_map/ppermute | solution.py:625
  173.5 11.1 %collective-permute-start.79 = (bf16[304,512]{1,0:T(8,128)(2,1)S(1)}, bf16[304,512]{1,0:T(8,128)(2,1)S(1)}, u32[]{:S(2)}, u32[]{:S(2)}) collective-permute-start(bf16[304,512]{1,0:T(8,128)(2,1)S(1)} %get-tuple-element.354), channel_id=1, source_target_pairs={{0,24},{2,10},{4,28},{6,14},{8,0},{10,18},{12,4},{14,22},{16,8},{1... | collective-permute-start | bytes 933896 | tf_op jit(solution)/shard_map/ppermute | solution.py:625
  177.1 7.9 %collective-permute-start.82 = (bf16[304,512]{1,0:T(8,128)(2,1)S(1)}, bf16[304,512]{1,0:T(8,128)(2,1)S(1)}, u32[]{:S(2)}, u32[]{:S(2)}) collective-permute-start(bf16[304,512]{1,0:T(8,128)(2,1)S(1)} %get-tuple-element.361), channel_id=1, source_target_pairs={{0,4},{4,0},{8,12},{12,8},{16,20},{20,16},{24,28},{28,24},{1,5},{5... | collective-permute-start | bytes 933896 | tf_op jit(solution)/shard_map/ppermute | solution.py:629
  178.2 6.4 %collective-permute-start.81 = (bf16[128,1024]{1,0:T(8,128)(2,1)S(1)}, bf16[128,1024]{1,0:T(8,128)(2,1)S(1)}, u32[]{:S(2)}, u32[]{:S(2)}) collective-permute-start(bf16[128,1024]{1,0:T(8,128)(2,1)S(1)} %expand_sum.7.mine), channel_id=1, source_target_pairs={{0,2},{2,0},{1,3},{3,1},{4,6},{6,4},{5,7},{7,5},{8,10},{10,8},{9,1... | collective-permute-start | bytes 786440 | tf_op jit(solution)/shard_map/ppermute | solution.py:607
  185.5 7.0 %collective-permute-start.83 = (bf16[304,512]{1,0:T(8,128)(2,1)S(1)}, bf16[304,512]{1,0:T(8,128)(2,1)S(1)}, u32[]{:S(2)}, u32[]{:S(2)}) collective-permute-start(bf16[304,512]{1,0:T(8,128)(2,1)S(1)} %block_sum.5.mine), channel_id=1, source_target_pairs={{0,2},{2,0},{1,3},{3,1},{4,6},{6,4},{5,7},{7,5},{8,10},{10,8},{9,1... | collective-permute-start | bytes 933896 | tf_op jit(solution)/shard_map/ppermute | solution.py:607
  186.7 5.8 %collective-permute-start.86 = (bf16[304,512]{1,0:T(8,128)(2,1)S(1)}, bf16[304,512]{1,0:T(8,128)(2,1)S(1)}, u32[]{:S(2)}, u32[]{:S(2)}) collective-permute-start(bf16[304,512]{1,0:T(8,128)(2,1)S(1)} %block_sum.5.mine), channel_id=1, source_target_pairs={{0,1},{1,0},{2,3},{3,2},{4,5},{5,4},{6,7},{7,6},{8,9},{9,8},{10,11... | collective-permute-start | bytes 933896 | tf_op jit(solution)/shard_map/ppermute | solution.py:602
  (29 other events, 107.0 us)

commit v6 on v5

--- a/solution.py
+++ b/solution.py
@@ -163,29 +163,34 @@
         mask[image * rows : (image + 1) * rows, :] = jnp.where(inside, valid[image].astype(F32), 0.0)
 
 
-def reduce_kernel(slots, depth, side, valid, mask, x, x_other, *refs):
-    weights, (red, stats) = refs[:slots], refs[slots:]
+def reduce_kernel(slots, depth, side, last, valid, mask, x, x_other, *refs):
+    weights, refs = refs[: len(slots)], refs[len(slots) :]
+    before, red = (None, refs[0]) if len(refs) == 1 + last else refs[:2]
     half, rows = red.shape[1], x.shape[0]
     for at in range(0, half, BLOCK):
         sums = [0.0, 0.0]
         for begin, pixels in ((0, x), (rows, x_other)):
-            total = None
-            for slot in range(slots):
-                if slots == 1:
+            here = (slice(begin, begin + rows), slice(at, at + BLOCK))
+            total = None if before is None else before[here]
+            for slot, weight in zip(slots, weights):
+                if slot is None:
                     piece = pixels[...]
                 else:
                     piece = pixels[:, pl.ds(pl.multiple_of(block_owner(slot) * depth, 128), depth)]
-                term = dot(piece, weights[slot][0:depth, at : at + BLOCK])
+                term = dot(piece, weight[0:depth, at : at + BLOCK])
                 total = term if total is None else total + term
-            red[begin : begin + rows, at : at + BLOCK] = total
-            masked = total * across_lanes(mask[begin : begin + rows, :], BLOCK)
-            sums = [sums[0] + column_sums(masked), sums[1] + column_sums(masked * total)]
-        stats[0:1, at : at + BLOCK] = sums[0]
-        stats[1:2, at : at + BLOCK] = sums[1]
-    pixels = valid[0].astype(F32)
-    for image in range(1, valid.shape[0]):
-        pixels = pixels + valid[image].astype(F32)
-    stats[2:3, :] = jnp.full((1, half), 1.0, F32) * (pixels * (side * side))
+            red[here] = total
+            if last:
+                masked = total * across_lanes(mask[begin : begin + rows, :], BLOCK)
+                sums = [sums[0] + column_sums(masked), sums[1] + column_sums(masked * total)]
+        if last:
+            refs[-1][0:1, at : at + BLOCK] = sums[0]
+            refs[-1][1:2, at : at + BLOCK] = sums[1]
+    if last:
+        pixels = valid[0].astype(F32)
+        for image in range(1, valid.shape[0]):
+            pixels = pixels + valid[image].astype(F32)
+        refs[-1][2:3, :] = jnp.full((1, half), 1.0, F32) * (pixels * (side * side))
 
 
 def spread_kernel(slots, depth, *refs):
@@ -498,19 +503,24 @@
     block_sum_kernel(small, places, turned, group, flat, *outs)
 
 
-def block_sum_kernel(small, places, turned, group, flat, *refs):
-    arrived, outs = refs[: len(refs) - len(places)], refs[len(refs) - len(places) :]
+def block_sum_kernel(small, places, turned, group, flat, *outs):
     tall, half = outs[0].shape
     depth = tall - group.shape[1]
-    for out, (block, chosen) in zip(outs, places):
+    for out, block in zip(outs, places):
         owner = block_owner(block) if small else block
-        value = dot(turned[rows_of(owner, depth), :], flat[...])
-        more = group[owner].astype(F32)
-        for other in chosen:
-            value = value + arrived[other][0:depth, :].astype(F32)
-            more = more + arrived[other][depth:tall, :].astype(F32)
-        out[0:depth, :] = value.astype(BF16)
-        out[depth:tall, :] = more.astype(BF16)
+        out[0:depth, :] = dot(turned[rows_of(owner, depth), :], flat[...]).astype(out.dtype)
+        out[depth:tall, :] = group[owner].astype(out.dtype)
+
+
+def arrived_kernel(numbers, *refs):
+    terms, arrived, outs = refs[: len(numbers)], refs[len(numbers) : -len(numbers)], refs[-len(numbers) :]
+    at = 0
+    for out, term, number in zip(outs, terms, numbers):
+        value = term[...]
+        for other in arrived[at : at + number]:
+            value = value + other[...].astype(F32)
+        out[...] = value.astype(BF16)
+        at += number
 
 
 def expand_sum_kernel(places, depth, keep, *refs):
@@ -668,7 +678,7 @@
         return sum_chips(values, (1, 2, 3)) if small else lax.psum(values, CHIPS)
 
     def line_sum(values):
-        return sum_chips(values, (4, 8, 12)) if small else values
+        return sum_chips(values, (4, 12, 8)) if small else values
 
     def everywhere(values):
         return line_sum(plane_sum(values))
@@ -695,9 +705,18 @@
         )
         return valid_both, turned, mask
 
+    pixels, across_cores = 2 * rows, 2 * count
+
+    def reduce_part(slots, last, depth, weights, *before):
+        return call(
+            functools.partial(reduce_kernel, slots, depth, side, last),
+            [shape((pixels, half), F32), shape((3, half), F32)][: 1 + last],
+            [valid_both, mask, x, x_other, *weights, *before], scalars=1, name="reduce", flops=2 * rows * width * channels,
+        )
+
     if small:
+        other = across(own)
         first = along(own, 1)
-        other = across(own)
         x_other, valid_other = padded(swap_core(images)), swap_core(valid)
         first, other, x, x_other, expand_own = together(first, other, x, x_other, expand_own)
         passed, second, first_other = swap_x(first), along(first, 1), across(first)
@@ -705,7 +724,8 @@
         passed_other, second_other, expand_first = swap_x(first_other), across(second), along(expand_own, 1)
         valid_both, turned, mask = turn(x, x_other, valid_other)
         weights = [own, first, passed, second, other, first_other, passed_other, second_other]
-        *weights, turned, mask = together(*weights, turned, mask)
+        (before,) = reduce_part((0, 1, 2, 3, 4, 5), False, depth, weights[:6])
+        turned, mask, before, *weights[6:] = together(turned, mask, before, *weights[6:])
         second, other = along(expand_first, 1), across(expand_own)
         slots, slot_depth = size, depth
     else:
@@ -715,12 +735,11 @@
         weights = [whole[:, :depth].reshape(channels, half)]
         slots, slot_depth = 1, channels
 
-    pixels, across_cores = 2 * rows, 2 * count
-    red, part = call(
-        functools.partial(reduce_kernel, slots, slot_depth, side),
-        [shape((pixels, half), F32), shape((3, half), F32)],
-        [valid_both, mask, x, x_other, *weights], scalars=1, name="reduce", flops=2 * rows * width * channels,
-    )
+
+    if small:
+        red, part = reduce_part((6, 7), True, depth, weights[6:], before)
+    else:
+        red, part = reduce_part((None,), True, channels, weights)
     if small:
         wide, wide_turned, inner_vectors, outer_vectors = call(
             functools.partial(spread_kernel, slots, depth),
@@ -735,7 +754,7 @@
         middle, second, other, expand_first = together(middle, second, other, expand_first)
         first_other, passed = across(expand_first), swap_x(expand_first)
         first = line_sum(middle)
-        first, first_other, second = together(first, first_other, second)
+        first, second = together(first, second)
         second_other, passed_other = across(second), swap_x(first_other)
     else:
         packed = whole[:, depth:]
@@ -851,7 +870,7 @@
         expand_passed, expand_other = moving
         (expand_first_own,) = expand_sums((((1, ((0, 1), (1, 0), (2, 0))),),), (expand_passed, expand_first_other, expand_second))
     tall = depth + extra
-    places = ((6, ()), (7, ())) if small else tuple((at, ()) for at in range(size))
+    places = (6, 7) if small else tuple(range(size))
     flat_one, *moving = call(
         functools.partial(back_reduce_kernel, small, places),
         [shape((pixels, half), BF16)] + [shape((tall, half), BF16)] * len(places),
@@ -859,12 +878,19 @@
         name="back_reduce", flops=2 * rows * depth * width * len(places),
     )
 
-    def sums(places, arrived):
+    def terms_of(places):
         return call(
             functools.partial(block_sum_kernel, small, places),
-            [shape((tall, half), BF16)] * len(places),
-            [turned, group_term, flat_one] + list(arrived),
+            [shape((tall, half), F32)] * len(places),
+            [turned, group_term, flat_one],
             name="block_sum", flops=2 * rows * depth * width * len(places),
+        )
+
+    def sums(terms, *arrived):
+        numbers = tuple(len(some) for some in arrived)
+        return call(
+            functools.partial(arrived_kernel, numbers), [shape((tall, half), BF16)] * len(terms),
+            [*terms, *(value for some in arrived for value in some)], name="arrived",
         )
 
     def back_input(begin, flat, *far):
@@ -904,20 +930,21 @@
         moving[1], expand_first_own = together(moving[1], expand_first_own)
         moving = [swap_x(moving[0]), across(moving[1])]
         expand_first_own = along(expand_first_own, -1)
+        terms = terms_of((5, 2, 3, 1, 4, 0))
         shards = own_shards([sums_one, sums_two, sums_three])
         moving[0], expand_first_own, *shards = together(moving[0], expand_first_own, *shards)
         (own_expand,) = expand_sums((((0, ((0, 0), (1, 1))),),), [expand_first_own, expand_other])
-        first_other, passed, second = sums(((5, (0,)), (2, ()), (3, (1,))), moving)
+        first_other, passed, second = sums(terms[0:3], moving[0:1], (), moving[1:2])
         moving = [swap_x(passed), along(second, -1), across(first_other)]
         far_input = swap_core(after(back_input(rows, flat_one), second))
         output = pinned(image_of(after(far_out, second)))
         moving[0], output = together(moving[0], output)
-        first_own, other = sums(((1, (0, 1, 2)), (4, ())), moving)
+        first_own, other = sums(terms[3:5], moving, ())
         moving = [along(first_own, -1), across(other)]
         grad_input, own_expand = pinned(back_input(0, after(flat_one, first_own), far_input)), after(own_expand, first_own)
         far_expand = swap_x(own_expand)
         moving[0], grad_input, far_expand = together(moving[0], grad_input, far_expand)
-        (own_reduce,) = sums(((0, (0, 1)),), moving)
+        (own_reduce,) = sums(terms[5:6], moving)
         own_expand, far_expand = after(own_expand, own_reduce), after(far_expand, own_reduce)
         (grad_w_expand,) = join(own_expand, far_expand, [w_expand])
         far_reduce, grad_w_expand = together(swap_x(own_reduce), grad_w_expand)

time: 195 us -> 193 us (0.990)
  starting transfers between devices: 81.3 us -> 78 us
    ppermute x48, waiting for transfers between devices: 20.8 us -> 24.6 us  [sum_chips(): got.append(lax.ppermute(values, (*CHIPS, 'core'), pairs))]
    ppermute x48, starting transfers between devices: 45.6 us -> 42.1 us  [sum_chips(): got.append(lax.ppermute(values, (*CHIPS, 'core'), pairs))]
    ppermute x11, waiting for transfers between devices: 11.3 us -> 8.7 us  [across(): return lax.ppermute(values, 'fsdp', [(f, f ^ 1) for f in range(8)])]
    pallas_call x30 -> x32, Pallas kernels: 41.2 us -> 42 us  [call(): pl.pallas_call(kernel, out_shape=outs, in_specs=[sm] * scalars + [given]...]
  transfers between devices with their start and end apart: 88 -> 88, of which waited for: 46 -> 52; matrix products, arithmetic and copies ran while one was open for 6% -> 6% of each run, Pallas kernels for 15% -> 17%
where the time goes in v6:
time: 193 us; the launch traced here: 192 us
  starting transfers between devices  78 us (40%)
  waiting for transfers between devices  59.6 us (31%)
  Pallas kernels  42 us (22%)
  local copies, waits for them, and re-layouts  11.4 us (6%)
    ppermute x48, starting transfers between devices, sum_chips(): got.append(lax.ppermute(values, (*CHIPS, 'core'), pairs))  42.1 us
    pallas_call x32, Pallas kernels, call(): pl.pallas_call(kernel, out_shape=outs, in_specs=[sm] * scalars + [given]...  42 us
    ppermute x48, waiting for transfers between devices, sum_chips(): got.append(lax.ppermute(values, (*CHIPS, 'core'), pairs))  24.6 us
    ppermute x8, waiting for transfers between devices, along(): return lax.ppermute(values, CHIPS, pairs)  12.8 us
    ppermute x11, starting transfers between devices, across(): return lax.ppermute(values, 'fsdp', [(f, f ^ 1) for f in range(8)])  12.6 us
    ppermute x8, starting transfers between devices, along(): return lax.ppermute(values, CHIPS, pairs)  11.6 us
    ppermute x9, starting transfers between devices, swap_x(): return lax.ppermute(values, 'x', SWAP)  9.11 us
    ppermute x11, waiting for transfers between devices, across(): return lax.ppermute(values, 'fsdp', [(f, f ^ 1) for f in range(8)])  8.7 us
  transfers between devices with their start and end apart: 88, of which 52 were waited for; matrix products, arithmetic and copies ran while one was open for 6% of the time, Pallas kernels for 17%

profile of v6, /device:TPU:0, one launch (start us, length us, event | category | flops | bytes accessed | tf_op | source)
XLA Modules:
  0.0 192.3 jit_solution(15741357981647373016)
XLA Ops:
  1.2 1.9 pack.1.refs_0_
  3.1 2.6 %collective-permute-start.1 = (bf16[304,512]{1,0:T(8,128)(2,1)}, bf16[304,512]{1,0:T(8,128)(2,1)S(1)}, u32[]{:S(2)}, u32[]{:S(2)}) collective-permute-start(bf16[304,512]{1,0:T(8,128)(2,1)} %pack.1.refs_0_), channel_id=1, source_target_pairs={{0,4},{4,0},{8,12},{12,8},{16,20},{20,16},{24,28},{28,24},{1,5},{5... | collective-permute-start | bytes 933896 | tf_op jit(solution)/shard_map/ppermute | solution.py:639
  5.7 1.6 collective-permute-start
  7.3 2.1 %copy.30 = bf16[2,14,14,2048]{3,2,1,0:T(8,128)(2,1)S(1)} copy(bf16[2,14,14,2048]{3,0,2,1:T(2,128)(2,1)} %param.12) | data formatting | bytes 3211264
  9.7 2.1 %copy.31 = bf16[2,14,14,2048]{3,2,1,0:T(8,128)(2,1)S(1)} copy(bf16[2,14,14,2048]{3,0,2,1:T(2,128)(2,1)} %collective-permute-done.2) | data formatting | bytes 3211264
  12.1 1.8 collective-permute-done.1.refs_4_
  13.9 3.4 %collective-permute-done.refs_1_ = bf16[304,512]{1,0:T(8,128)(2,1)S(1)} collective-permute-done((bf16[304,512]{1,0:T(8,128)(2,1)}, bf16[304,512]{1,0:T(8,128)(2,1)S(1)}, u32[]{:S(2)}, u32[]{:S(2)}) %collective-permute-start) | collective-permute-done | bytes 311328 | tf_op jit(solution)/shard_map/ppermute | solution.py:635
  18.9 1.6 collective-permute-start.13
  21.6 4.3 %collective-permute-done.5.refs_5_ = bf16[304,512]{1,0:T(8,128)(2,1)S(1)} collective-permute-done((bf16[304,512]{1,0:T(8,128)(2,1)S(1)}, bf16[304,512]{1,0:T(8,128)(2,1)S(1)}, u32[]{:S(2)}, u32[]{:S(2)}) %collective-permute-start.5) | collective-permute-done | bytes 311328 | tf_op jit(solution)/shard_map/ppermute | solution.py:639
  26.4 4.6 %collective-permute-done.3.refs_3_ = bf16[304,512]{1,0:T(8,128)(2,1)S(1)} collective-permute-done((bf16[304,512]{1,0:T(8,128)(2,1)S(1)}, bf16[304,512]{1,0:T(8,128)(2,1)S(1)}, u32[]{:S(2)}, u32[]{:S(2)}) %collective-permute-start.3) | collective-permute-done | bytes 311328 | tf_op jit(solution)/shard_map/ppermute | solution.py:635
  31.0 1.5 collective-permute-start.8
  33.1 1.6 collective-permute-done.13.refs_1_
  34.8 2.2 %turn.1 = (bf16[2048,896]{1,0:T(8,128)(2,1)S(1)}, f32[896,128]{1,0:T(8,128)S(1)}) custom-call(s32[4]{0:T(128)S(1)} %pad_add_fusion.valid, bf16[448,2048]{1,0:T(8,128)(2,1)S(1)} %bitcast.17, bf16[448,2048]{1,0:T(8,128)(2,1)S(1)} %bitcast.21), custom_call_target="tpu_custom_call" | custom-call | tf_op jit(solution)/shard_map/turn/pallas_call | solution.py:55
  37.0 2.1 %reduce.2.refs_2_ = f32[896,512]{1,0:T(8,128)S(1)} custom-call(s32[4]{0:T(128)S(1)} %pad_add_fusion.valid, f32[896,128]{1,0:T(8,128)S(1)} %get-tuple-element.204.mask, bf16[448,2048]{1,0:T(8,128)(2,1)S(1)} %bitcast.18, bf16[448,2048]{1,0:T(8,128)(2,1)S(1)} %bitcast.22, bf16[304,512]{1,0:T(8,128)(2,1)S(1)} %copy-done.2, ...), custom_call_target="tpu_custom_call" | custom-call | tf_op jit(solution)/shard_map/reduce/pallas_call | solution.py:55
  39.4 1.3 reduce.3
  40.9 4.6 %collective-permute-start.11 = (f32[3,512]{1,0:T(4,128)S(1)}, f32[3,512]{1,0:T(4,128)S(1)}, u32[]{:S(2)}, u32[]{:S(2)}) collective-permute-start(f32[3,512]{1,0:T(4,128)S(1)} %get-tuple-element.208), channel_id=1, source_target_pairs={{0,7},{1,6},{2,5},{3,4},{4,3},{5,2},{6,1},{7,0},{8,15},{9,14},{10,... | collective-permute-start | bytes 18440 | tf_op jit(solution)/shard_map/ppermute | solution.py:625
  46.9 1.7 collective-permute-done.10
  48.8 1.6 collective-permute-start.25
  52.2 1.5 collective-permute-start.16
  54.7 1.3 collective-permute-done.17
  58.1 3.5 %group.3 = (bf16[3,4,256,512]{3,2,1,0:T(8,128)(2,1)S(1)}, f32[896,512]{1,0:T(8,128)S(1)}, f32[2,512]{1,0:T(2,128)S(1)}) custom-call(f32[896,128]{1,0:T(8,128)S(1)} %get-tuple-element.204.mask, f32[3,512]{1,0:T(4,128)S(1)} %add_add_fusion.4.total.first, f32[4,512]{1,0:T(4,128)S(1)} %get-tuple-element.226.vectors, f32[896,512]{1,0:T(8,128)S(1)} %get-tuple-element.227.red, ...), custom_call_target="tpu_custom_call" | custom-call | tf_op jit(solution)/shard_map/group/pallas_call | solution.py:55
  62.6 2.5 %collective-permute-start.22 = (f32[2,512]{1,0:T(2,128)S(1)}, f32[2,512]{1,0:T(2,128)S(1)}, u32[]{:S(2)}, u32[]{:S(2)}) collective-permute-start(f32[2,512]{1,0:T(2,128)S(1)} %get-tuple-element.231), channel_id=1, source_target_pairs={{0,25},{1,24},{2,27},{3,26},{4,29},{5,28},{6,31},{7,30},{8,17},{9,... | collective-permute-start | bytes 12296 | tf_op jit(solution)/shard_map/ppermute | solution.py:625
  65.7 1.7 collective-permute-done.22
  70.1 1.4 collective-permute-start.28
  76.2 2.3 %expand.1 = (bf16[896,1024]{1,0:T(8,128)(2,1)S(1)}, f32[896,1024]{1,0:T(8,128)S(1)}, f32[2,1024]{1,0:T(2,128)S(1)}) custom-call(f32[896,128]{1,0:T(8,128)S(1)} %get-tuple-element.204.mask, bf16[896,512]{1,0:T(8,128)(2,1)S(1)} %act.1.act_mine, bf16[896,512]{1,0:T(8,128)(2,1)S(1)} %collective-permute-done.32.act_far, bf16[1024,1024]{1,0:T(8,128)(2,1)S(1)} %assemble.1.weight), custom_call_target="tpu_custom_call" | custom-call | tf_op jit(solution)/shard_map/expand/pallas_call | solution.py:55
  78.8 2.7 %collective-permute-start.35 = (f32[2,1024]{1,0:T(2,128)S(1)}, f32[2,1024]{1,0:T(2,128)S(1)}, u32[]{:S(2)}, u32[]{:S(2)}) collective-permute-start(f32[2,1024]{1,0:T(2,128)S(1)} %get-tuple-element.256), channel_id=1, source_target_pairs={{0,7},{1,6},{2,5},{3,4},{4,3},{5,2},{6,1},{7,0},{8,15},{9,14},{10,... | collective-permute-start | bytes 24584 | tf_op jit(solution)/shard_map/ppermute | solution.py:625
  82.8 1.7 collective-permute-done.34
  85.3 2.2 %collective-permute-start.39 = (f32[2,1024]{1,0:T(2,128)S(1)}, f32[2,1024]{1,0:T(2,128)S(1)}, u32[]{:S(2)}, u32[]{:S(2)}) collective-permute-start(f32[2,1024]{1,0:T(2,128)S(1)} %add_add_fusion.3), channel_id=1, source_target_pairs={{0,25},{1,24},{2,27},{3,26},{4,29},{5,28},{6,31},{7,30},{8,17},{9,... | collective-permute-start | bytes 24584 | tf_op jit(solution)/shard_map/ppermute | solution.py:625
  90.6 3.4 %output.1 = (bf16[448,1024]{1,0:T(8,128)(2,1)S(1)}, bf16[448,1024]{1,0:T(8,128)(2,1)S(1)}, f32[896,1024]{1,0:T(8,128)S(1)}, f32[2,1024]{1,0:T(2,128)S(1)}) custom-call(s32[4]{0:T(128)S(1)} %pad_add_fusion.valid, f32[2,1024]{1,0:T(2,128)S(1)} %add_add_fusion.2.total, f32[3,512]{1,0:T(4,128)S(1)} %add_add_fusion.4.total.first, ...), custom_call_target="tpu_custom_call" | custom-call | tf_op jit(solution)/shard_map/output/pallas_call | solution.py:55
  94.4 1.9 collective-permute-start.44
  100.5 1.8 collective-permute-start.47
  104.1 1.4 collective-permute-done.47
  105.5 2.2 %back_expand.1 = (bf16[896,1024]{1,0:T(8,128)(2,1)S(1)}, bf16[896,512]{1,0:T(8,128)(2,1)S(1)}) custom-call(f32[896,128]{1,0:T(8,128)S(1)} %get-tuple-element.204.mask, f32[2,1024]{1,0:T(2,128)S(1)} %add_add_fusion.2.total, f32[2,1024]{1,0:T(2,128)S(1)} %add_add_fusion.sums, f32[3,512]{1,0:T(4,128)S(1)} %add_add_fusion.4.total.first, ...), custom_call_target="tpu_custom_call" | custom-call | tf_op jit(solution)/shard_map/back_expand/pallas_call | solution.py:55
  110.2 1.3 back_act.1
  111.9 2.5 %collective-permute-start.53 = (f32[2,512]{1,0:T(2,128)S(1)}, f32[2,512]{1,0:T(2,128)S(1)}, u32[]{:S(2)}, u32[]{:S(2)}) collective-permute-start(f32[2,512]{1,0:T(2,128)S(1)} %get-tuple-element.283), channel_id=1, source_target_pairs={{0,7},{1,6},{2,5},{3,4},{4,3},{5,2},{6,1},{7,0},{8,15},{9,14},{10,... | collective-permute-start | bytes 12296 | tf_op jit(solution)/shard_map/ppermute | solution.py:625
  114.9 2.4 %weight_expand.1.keep = bf16[1024,1024]{1,0:T(8,128)(2,1)S(1)} custom-call(bf16[896,1024]{1,0:T(8,128)(2,1)S(1)} %get-tuple-element.289.act, bf16[896,1024]{1,0:T(8,128)(2,1)S(1)} %get-tuple-element.281.flat), custom_call_target="tpu_custom_call" | custom-call | tf_op jit(solution)/shard_map/weight_expand/pallas_call | solution.py:55
  117.7 1.5 collective-permute-start.63
  119.3 1.5 collective-permute-start.64
  121.5 1.4 collective-permute-start.56
  122.9 1.2 collective-permute-start.55
  124.7 1.6 collective-permute-done.56
  126.3 4.1 %back_group.1 = (bf16[896,512]{1,0:T(8,128)(2,1)S(1)}, f32[896,512]{1,0:T(8,128)S(1)}, f32[2,512]{1,0:T(2,128)S(1)}) custom-call(f32[896,128]{1,0:T(8,128)S(1)} %get-tuple-element.204.mask, f32[2,512]{1,0:T(2,128)S(1)} %add_add_fusion.10.total, f32[2,512]{1,0:T(2,128)S(1)} %add_add_fusion.8.sums, f32[3,512]{1,0:T(4,128)S(1)} %add_add_fusion.4.total.first, ...), custom_call_target="tpu_custom_call" | custom-call | tf_op jit(solution)/shard_map/back_group/pallas_call | solution.py:55
  131.7 1.6 collective-permute-start.60
  133.9 1.7 weight_group.1.group
  137.1 1.8 collective-permute-start.70
  139.1 2.1 %collective-permute-start.66 = (f32[2,512]{1,0:T(2,128)S(1)}, f32[2,512]{1,0:T(2,128)S(1)}, u32[]{:S(2)}, u32[]{:S(2)}) collective-permute-start(f32[2,512]{1,0:T(2,128)S(1)} %add_add_fusion.7), channel_id=1, source_target_pairs={{0,25},{1,24},{2,27},{3,26},{4,29},{5,28},{6,31},{7,30},{8,17},{9,... | collective-permute-start | bytes 12296 | tf_op jit(solution)/shard_map/ppermute | solution.py:625
  142.3 2.5 %collective-permute-done.67 = f32[2,512]{1,0:T(2,128)S(1)} collective-permute-done((f32[2,512]{1,0:T(2,128)S(1)}, f32[2,512]{1,0:T(2,128)S(1)}, u32[]{:S(2)}, u32[]{:S(2)}) %collective-permute-start.67) | collective-permute-done | bytes 4128 | tf_op jit(solution)/shard_map/ppermute | solution.py:625
  145.3 1.2 back_reduce.1
  146.5 2.8 %collective-permute-start.71 = (bf16[304,512]{1,0:T(8,128)(2,1)S(1)}, bf16[304,512]{1,0:T(8,128)(2,1)S(1)}, u32[]{:S(2)}, u32[]{:S(2)}) collective-permute-start(bf16[304,512]{1,0:T(8,128)(2,1)S(1)} %get-tuple-element.329), channel_id=1, source_target_pairs={{0,2},{2,0},{1,3},{3,1},{4,6},{6,4},{5,7},{7,5},{8,10},{10,8},{9,1... | collective-permute-start | bytes 933896 | tf_op jit(solution)/shard_map/ppermute | solution.py:617
  149.5 1.6 collective-permute-start.74
  152.2 1.8 block_sum.1
  154.0 1.7 back_input.2
  156.2 2.6 %collective-permute-done.72.refs_0_ = bf16[128,1024]{1,0:T(8,128)(2,1)S(1)} collective-permute-done((bf16[128,1024]{1,0:T(8,128)(2,1)S(1)}, bf16[128,1024]{1,0:T(8,128)(2,1)S(1)}, u32[]{:S(2)}, u32[]{:S(2)}) %collective-permute-start.72) | collective-permute-done | bytes 262176 | tf_op jit(solution)/shard_map/ppermute | solution.py:635
  159.6 2.1 %collective-permute-start.75 = (bf16[304,512]{1,0:T(8,128)(2,1)S(1)}, bf16[304,512]{1,0:T(8,128)(2,1)S(1)}, u32[]{:S(2)}, u32[]{:S(2)}) collective-permute-start(bf16[304,512]{1,0:T(8,128)(2,1)S(1)} %get-tuple-element.342), channel_id=1, source_target_pairs={{0,2},{2,0},{1,3},{3,1},{4,6},{6,4},{5,7},{7,5},{8,10},{10,8},{9,1... | collective-permute-start | bytes 933896 | tf_op jit(solution)/shard_map/ppermute | solution.py:617
  162.2 1.7 collective-permute-start.77
  164.5 2.8 %copy.36 = bf16[2,14,14,2048]{3,0,2,1:T(2,128)(2,1)} copy(bf16[2,14,14,2048]{3,2,1,0:T(8,128)(2,1)S(1)} %image.1) | data formatting | bytes 3211264 | tf_op jit(solution)/shard_map/image/pallas_call | solution.py:55
  167.3 2.0 %collective-permute-done.75.refs_2_ = bf16[304,512]{1,0:T(8,128)(2,1)S(1)} collective-permute-done((bf16[304,512]{1,0:T(8,128)(2,1)S(1)}, bf16[304,512]{1,0:T(8,128)(2,1)S(1)}, u32[]{:S(2)}, u32[]{:S(2)}) %collective-permute-start.75) | collective-permute-done | bytes 311328 | tf_op jit(solution)/shard_map/ppermute | solution.py:617
  169.3 1.5 collective-permute-done.78.refs_4_
  171.2 3.6 %collective-permute-start.79 = (bf16[304,512]{1,0:T(8,128)(2,1)S(1)}, bf16[304,512]{1,0:T(8,128)(2,1)S(1)}, u32[]{:S(2)}, u32[]{:S(2)}) collective-permute-start(bf16[304,512]{1,0:T(8,128)(2,1)S(1)} %get-tuple-element.353), channel_id=1, source_target_pairs={{0,24},{2,10},{4,28},{6,14},{8,0},{10,18},{12,4},{14,22},{16,8},{1... | collective-permute-start | bytes 933896 | tf_op jit(solution)/shard_map/ppermute | solution.py:635
  176.0 2.0 %back_input.3 = bf16[2,14,14,2048]{3,2,1,0:T(8,128)(2,1)S(1)} custom-call(bf16[896,512]{1,0:T(8,128)(2,1)S(1)} %get-tuple-element.354.flat, f32[896,1024]{1,0:T(8,128)S(1)} %get-tuple-element.280.grad, bf16[304,512]{1,0:T(8,128)(2,1)S(1)} %copy-done.2, bf16[304,512]{1,0:T(8,128)(2,1)S(1)} %collective-permute-done.refs_1_, ...), custom_call_target="tpu_custom_call" | custom-call | tf_op jit(solution)/shard_map/back_input/pallas_call | solution.py:55
  177.9 2.8 %copy.35 = bf16[2,14,14,2048]{3,0,2,1:T(2,128)(2,1)} copy(bf16[2,14,14,2048]{3,2,1,0:T(8,128)(2,1)S(1)} %back_input.3) | data formatting | bytes 3211264 | tf_op jit(solution)/shard_map/back_input/pallas_call | solution.py:55
  180.8 1.8 collective-permute-done.81.mine_x
  186.6 3.0 %collective-permute-done.83.mine_x = bf16[304,512]{1,0:T(8,128)(2,1)S(1)} collective-permute-done((bf16[304,512]{1,0:T(8,128)(2,1)S(1)}, bf16[304,512]{1,0:T(8,128)(2,1)S(1)}, u32[]{:S(2)}, u32[]{:S(2)}) %collective-permute-start.83) | collective-permute-done | bytes 311328 | tf_op jit(solution)/shard_map/ppermute | solution.py:617
  189.6 1.6 collective-permute-done.87.other_x
  (179 shorter events, 52.9 us)
Async XLA Ops:
  0.7 9.0 %collective-permute-start.2 = (bf16[2,14,14,2048]{3,0,2,1:T(2,128)(2,1)}, bf16[2,14,14,2048]{3,0,2,1:T(2,128)(2,1)}, u32[]{:S(2)}, u32[]{:S(2)}) collective-permute-start(bf16[2,14,14,2048]{3,0,2,1:T(2,128)(2,1)} %param.12), channel_id=1, source_target_pairs={{0,1},{1,0},{2,3},{3,2},{4,5},{5,4},{6,7},{7,6},{8,9},{9,8},{10,11... | collective-permute-start | bytes 4816904 | tf_op jit(solution)/shard_map/ppermute | solution.py:612
  3.1 10.8 %collective-permute-start.1 = (bf16[304,512]{1,0:T(8,128)(2,1)}, bf16[304,512]{1,0:T(8,128)(2,1)S(1)}, u32[]{:S(2)}, u32[]{:S(2)}) collective-permute-start(bf16[304,512]{1,0:T(8,128)(2,1)} %pack.1.refs_0_), channel_id=1, source_target_pairs={{0,4},{4,0},{8,12},{12,8},{16,20},{20,16},{24,28},{28,24},{1,5},{5... | collective-permute-start | bytes 933896 | tf_op jit(solution)/shard_map/ppermute | solution.py:639
  5.7 11.5 %collective-permute-start = (bf16[304,512]{1,0:T(8,128)(2,1)}, bf16[304,512]{1,0:T(8,128)(2,1)S(1)}, u32[]{:S(2)}, u32[]{:S(2)}) collective-permute-start(bf16[304,512]{1,0:T(8,128)(2,1)} %pack.1.refs_0_), channel_id=1, source_target_pairs={{0,8},{2,26},{4,12},{6,30},{8,16},{10,2},{12,20},{14,6},{16,24},{1... | collective-permute-start | bytes 933896 | tf_op jit(solution)/shard_map/ppermute | solution.py:635
  17.2 8.7 %collective-permute-start.5 = (bf16[304,512]{1,0:T(8,128)(2,1)S(1)}, bf16[304,512]{1,0:T(8,128)(2,1)S(1)}, u32[]{:S(2)}, u32[]{:S(2)}) collective-permute-start(bf16[304,512]{1,0:T(8,128)(2,1)S(1)} %collective-permute-done.refs_1_), channel_id=1, source_target_pairs={{0,4},{4,0},{8,12},{12,8},{16,20},{20,16},{24,28},{28,24},{1,5},{5... | collective-permute-start | bytes 933896 | tf_op jit(solution)/shard_map/ppermute | solution.py:639
  17.8 8.7 %collective-permute-start.4 = (bf16[304,512]{1,0:T(8,128)(2,1)S(1)}, bf16[304,512]{1,0:T(8,128)(2,1)S(1)}, u32[]{:S(2)}, u32[]{:S(2)}) collective-permute-start(bf16[304,512]{1,0:T(8,128)(2,1)S(1)} %collective-permute-done.refs_1_), channel_id=1, source_target_pairs={{0,2},{2,0},{1,3},{3,1},{4,6},{6,4},{5,7},{7,5},{8,10},{10,8},{9,1... | collective-permute-start | bytes 933896 | tf_op jit(solution)/shard_map/ppermute | solution.py:617
  18.6 12.4 %collective-permute-start.3 = (bf16[304,512]{1,0:T(8,128)(2,1)S(1)}, bf16[304,512]{1,0:T(8,128)(2,1)S(1)}, u32[]{:S(2)}, u32[]{:S(2)}) collective-permute-start(bf16[304,512]{1,0:T(8,128)(2,1)S(1)} %collective-permute-done.refs_1_), channel_id=1, source_target_pairs={{0,8},{2,26},{4,12},{6,30},{8,16},{10,2},{12,20},{14,6},{16,24},{1... | collective-permute-start | bytes 933896 | tf_op jit(solution)/shard_map/ppermute | solution.py:635
  18.9 15.7 %collective-permute-start.13 = (bf16[128,1024]{1,0:T(8,128)(2,1)S(1)}, bf16[128,1024]{1,0:T(8,128)(2,1)S(1)}, u32[]{:S(2)}, u32[]{:S(2)}) collective-permute-start(bf16[128,1024]{1,0:T(8,128)(2,1)S(1)} %constant_dynamic-slice_fusion.refs_0_), channel_id=1, source_target_pairs={{0,8},{2,26},{4,12},{6,30},{8,16},{10,2},{12,20},{14,6},{16,24},{1... | collective-permute-start | bytes 786440 | tf_op jit(solution)/shard_map/ppermute | solution.py:635
  31.0 8.3 %collective-permute-start.8 = (bf16[304,512]{1,0:T(8,128)(2,1)S(1)}, bf16[304,512]{1,0:T(8,128)(2,1)S(1)}, u32[]{:S(2)}, u32[]{:S(2)}) collective-permute-start(bf16[304,512]{1,0:T(8,128)(2,1)S(1)} %collective-permute-done.3.refs_3_), channel_id=1, source_target_pairs={{0,4},{4,0},{8,12},{12,8},{16,20},{20,16},{24,28},{28,24},{1,5},{5... | collective-permute-start | bytes 933896 | tf_op jit(solution)/shard_map/ppermute | solution.py:639
  32.5 6.9 %collective-permute-start.7 = (bf16[304,512]{1,0:T(8,128)(2,1)S(1)}, bf16[304,512]{1,0:T(8,128)(2,1)S(1)}, u32[]{:S(2)}, u32[]{:S(2)}) collective-permute-start(bf16[304,512]{1,0:T(8,128)(2,1)S(1)} %collective-permute-done.5.refs_5_), channel_id=1, source_target_pairs={{0,2},{2,0},{1,3},{3,1},{4,6},{6,4},{5,7},{7,5},{8,10},{10,8},{9,1... | collective-permute-start | bytes 933896 | tf_op jit(solution)/shard_map/ppermute | solution.py:617
  32.5 16.2 %collective-permute-start.15 = (bf16[128,1024]{1,0:T(8,128)(2,1)S(1)}, bf16[128,1024]{1,0:T(8,128)(2,1)S(1)}, u32[]{:S(2)}, u32[]{:S(2)}) collective-permute-start(bf16[128,1024]{1,0:T(8,128)(2,1)S(1)} %constant_dynamic-slice_fusion.refs_0_), channel_id=1, source_target_pairs={{0,4},{4,0},{8,12},{12,8},{16,20},{20,16},{24,28},{28,24},{1,5},{5... | collective-permute-start | bytes 786440 | tf_op jit(solution)/shard_map/ppermute | solution.py:639
  34.7 14.1 %collective-permute-start.14 = (bf16[128,1024]{1,0:T(8,128)(2,1)S(1)}, bf16[128,1024]{1,0:T(8,128)(2,1)S(1)}, u32[]{:S(2)}, u32[]{:S(2)}) collective-permute-start(bf16[128,1024]{1,0:T(8,128)(2,1)S(1)} %collective-permute-done.13.refs_1_), channel_id=1, source_target_pairs={{0,8},{2,26},{4,12},{6,30},{8,16},{10,2},{12,20},{14,6},{16,24},{1... | collective-permute-start | bytes 786440 | tf_op jit(solution)/shard_map/ppermute | solution.py:635
  40.8 4.9 %collective-permute-start.12 = (f32[3,512]{1,0:T(4,128)S(1)}, f32[3,512]{1,0:T(4,128)S(1)}, u32[]{:S(2)}, u32[]{:S(2)}) collective-permute-start(f32[3,512]{1,0:T(4,128)S(1)} %get-tuple-element.208), channel_id=1, source_target_pairs={{0,1},{1,0},{2,3},{3,2},{4,5},{5,4},{6,7},{7,6},{8,9},{9,8},{10,11... | collective-permute-start | bytes 18440 | tf_op jit(solution)/shard_map/ppermute | solution.py:625
  40.9 6.0 %collective-permute-start.11 = (f32[3,512]{1,0:T(4,128)S(1)}, f32[3,512]{1,0:T(4,128)S(1)}, u32[]{:S(2)}, u32[]{:S(2)}) collective-permute-start(f32[3,512]{1,0:T(4,128)S(1)} %get-tuple-element.208), channel_id=1, source_target_pairs={{0,7},{1,6},{2,5},{3,4},{4,3},{5,2},{6,1},{7,0},{8,15},{9,14},{10,... | collective-permute-start | bytes 18440 | tf_op jit(solution)/shard_map/ppermute | solution.py:625
  48.8 8.7 %collective-permute-start.25 = (bf16[128,1024]{1,0:T(8,128)(2,1)S(1)}, bf16[128,1024]{1,0:T(8,128)(2,1)S(1)}, u32[]{:S(2)}, u32[]{:S(2)}) collective-permute-start(bf16[128,1024]{1,0:T(8,128)(2,1)S(1)} %collective-permute-done.13.refs_1_), channel_id=1, source_target_pairs={{0,4},{4,0},{8,12},{12,8},{16,20},{20,16},{24,28},{28,24},{1,5},{5... | collective-permute-start | bytes 786440 | tf_op jit(solution)/shard_map/ppermute | solution.py:639
  50.5 11.0 %collective-permute-start.20 = (bf16[128,1024]{1,0:T(8,128)(2,1)S(1)}, bf16[128,1024]{1,0:T(8,128)(2,1)S(1)}, u32[]{:S(2)}, u32[]{:S(2)}) collective-permute-start(bf16[128,1024]{1,0:T(8,128)(2,1)S(1)} %collective-permute-done.13.refs_1_), channel_id=1, source_target_pairs={{0,2},{2,0},{1,3},{3,1},{4,6},{6,4},{5,7},{7,5},{8,10},{10,8},{9,1... | collective-permute-start | bytes 786440 | tf_op jit(solution)/shard_map/ppermute | solution.py:617
  50.7 4.0 %collective-permute-start.18 = (f32[3,512]{1,0:T(4,128)S(1)}, f32[3,512]{1,0:T(4,128)S(1)}, u32[]{:S(2)}, u32[]{:S(2)}) collective-permute-start(f32[3,512]{1,0:T(4,128)S(1)} %add_add_fusion.5), channel_id=1, source_target_pairs={{0,17},{1,16},{2,19},{3,18},{4,21},{5,20},{6,23},{7,22},{8,25},{9,... | collective-permute-start | bytes 18440 | tf_op jit(solution)/shard_map/ppermute | solution.py:625
  51.2 4.9 %collective-permute-start.17 = (f32[3,512]{1,0:T(4,128)S(1)}, f32[3,512]{1,0:T(4,128)S(1)}, u32[]{:S(2)}, u32[]{:S(2)}) collective-permute-start(f32[3,512]{1,0:T(4,128)S(1)} %add_add_fusion.5), channel_id=1, source_target_pairs={{0,25},{1,24},{2,27},{3,26},{4,29},{5,28},{6,31},{7,30},{8,17},{9,... | collective-permute-start | bytes 18440 | tf_op jit(solution)/shard_map/ppermute | solution.py:625
  52.2 3.8 %collective-permute-start.16 = (f32[3,512]{1,0:T(4,128)S(1)}, f32[3,512]{1,0:T(4,128)S(1)}, u32[]{:S(2)}, u32[]{:S(2)}) collective-permute-start(f32[3,512]{1,0:T(4,128)S(1)} %add_add_fusion.5), channel_id=1, source_target_pairs={{0,9},{1,8},{2,11},{3,10},{4,13},{5,12},{6,15},{7,14},{8,1},{9,0},... | collective-permute-start | bytes 18440 | tf_op jit(solution)/shard_map/ppermute | solution.py:625
  56.1 12.1 %collective-permute-start.27 = (bf16[128,1024]{1,0:T(8,128)(2,1)S(1)}, bf16[128,1024]{1,0:T(8,128)(2,1)S(1)}, u32[]{:S(2)}, u32[]{:S(2)}) collective-permute-start(bf16[128,1024]{1,0:T(8,128)(2,1)S(1)} %collective-permute-done.14.refs_3_), channel_id=1, source_target_pairs={{0,4},{4,0},{8,12},{12,8},{16,20},{20,16},{24,28},{28,24},{1,5},{5... | collective-permute-start | bytes 786440 | tf_op jit(solution)/shard_map/ppermute | solution.py:639
  57.5 10.7 %collective-permute-start.26 = (bf16[128,1024]{1,0:T(8,128)(2,1)S(1)}, bf16[128,1024]{1,0:T(8,128)(2,1)S(1)}, u32[]{:S(2)}, u32[]{:S(2)}) collective-permute-start(bf16[128,1024]{1,0:T(8,128)(2,1)S(1)} %collective-permute-done.25.refs_5_), channel_id=1, source_target_pairs={{0,2},{2,0},{1,3},{3,1},{4,6},{6,4},{5,7},{7,5},{8,10},{10,8},{9,1... | collective-permute-start | bytes 786440 | tf_op jit(solution)/shard_map/ppermute | solution.py:617
  61.6 3.5 %collective-permute-start.24 = (f32[2,512]{1,0:T(2,128)S(1)}, f32[2,512]{1,0:T(2,128)S(1)}, u32[]{:S(2)}, u32[]{:S(2)}) collective-permute-start(f32[2,512]{1,0:T(2,128)S(1)} %get-tuple-element.231), channel_id=1, source_target_pairs={{0,1},{1,0},{2,3},{3,2},{4,5},{5,4},{6,7},{7,6},{8,9},{9,8},{10,11... | collective-permute-start | bytes 12296 | tf_op jit(solution)/shard_map/ppermute | solution.py:625
  61.7 4.0 %collective-permute-start.23 = (f32[2,512]{1,0:T(2,128)S(1)}, f32[2,512]{1,0:T(2,128)S(1)}, u32[]{:S(2)}, u32[]{:S(2)}) collective-permute-start(f32[2,512]{1,0:T(2,128)S(1)} %get-tuple-element.231), channel_id=1, source_target_pairs={{0,17},{1,16},{2,19},{3,18},{4,21},{5,20},{6,23},{7,22},{8,25},{9,... | collective-permute-start | bytes 12296 | tf_op jit(solution)/shard_map/ppermute | solution.py:625
  62.6 4.8 %collective-permute-start.22 = (f32[2,512]{1,0:T(2,128)S(1)}, f32[2,512]{1,0:T(2,128)S(1)}, u32[]{:S(2)}, u32[]{:S(2)}) collective-permute-start(f32[2,512]{1,0:T(2,128)S(1)} %get-tuple-element.231), channel_id=1, source_target_pairs={{0,25},{1,24},{2,27},{3,26},{4,29},{5,28},{6,31},{7,30},{8,17},{9,... | collective-permute-start | bytes 12296 | tf_op jit(solution)/shard_map/ppermute | solution.py:625
  68.2 3.4 %collective-permute-start.31 = (f32[2,512]{1,0:T(2,128)S(1)}, f32[2,512]{1,0:T(2,128)S(1)}, u32[]{:S(2)}, u32[]{:S(2)}) collective-permute-start(f32[2,512]{1,0:T(2,128)S(1)} %add_add_fusion.11), channel_id=1, source_target_pairs={{0,1},{1,0},{2,3},{3,2},{4,5},{5,4},{6,7},{7,6},{8,9},{9,8},{10,11... | collective-permute-start | bytes 12296 | tf_op jit(solution)/shard_map/ppermute | solution.py:625
  68.7 3.9 %collective-permute-start.30 = (f32[2,512]{1,0:T(2,128)S(1)}, f32[2,512]{1,0:T(2,128)S(1)}, u32[]{:S(2)}, u32[]{:S(2)}) collective-permute-start(f32[2,512]{1,0:T(2,128)S(1)} %add_add_fusion.11), channel_id=1, source_target_pairs={{0,7},{1,6},{2,5},{3,4},{4,3},{5,2},{6,1},{7,0},{8,15},{9,14},{10,... | collective-permute-start | bytes 12296 | tf_op jit(solution)/shard_map/ppermute | solution.py:625
  75.1 9.8 %collective-permute-start.37 = (bf16[448,1024]{1,0:T(8,128)(2,1)S(1)}, bf16[448,1024]{1,0:T(8,128)(2,1)S(1)}, u32[]{:S(2)}, u32[]{:S(2)}) collective-permute-start(bf16[448,1024]{1,0:T(8,128)(2,1)S(1)} %far_half.1), channel_id=1, source_target_pairs={{0,1},{1,0},{2,3},{3,2},{4,5},{5,4},{6,7},{7,6},{8,9},{9,8},{10,11... | collective-permute-start | bytes 2752520 | tf_op jit(solution)/shard_map/ppermute | solution.py:612
  78.6 3.4 %collective-permute-start.36 = (f32[2,1024]{1,0:T(2,128)S(1)}, f32[2,1024]{1,0:T(2,128)S(1)}, u32[]{:S(2)}, u32[]{:S(2)}) collective-permute-start(f32[2,1024]{1,0:T(2,128)S(1)} %get-tuple-element.256), channel_id=1, source_target_pairs={{0,1},{1,0},{2,3},{3,2},{4,5},{5,4},{6,7},{7,6},{8,9},{9,8},{10,11... | collective-permute-start | bytes 24584 | tf_op jit(solution)/shard_map/ppermute | solution.py:625
  78.8 4.0 %collective-permute-start.35 = (f32[2,1024]{1,0:T(2,128)S(1)}, f32[2,1024]{1,0:T(2,128)S(1)}, u32[]{:S(2)}, u32[]{:S(2)}) collective-permute-start(f32[2,1024]{1,0:T(2,128)S(1)} %get-tuple-element.256), channel_id=1, source_target_pairs={{0,7},{1,6},{2,5},{3,4},{4,3},{5,2},{6,1},{7,0},{8,15},{9,14},{10,... | collective-permute-start | bytes 24584 | tf_op jit(solution)/shard_map/ppermute | solution.py:625
  84.9 3.4 %collective-permute-start.41 = (f32[2,1024]{1,0:T(2,128)S(1)}, f32[2,1024]{1,0:T(2,128)S(1)}, u32[]{:S(2)}, u32[]{:S(2)}) collective-permute-start(f32[2,1024]{1,0:T(2,128)S(1)} %add_add_fusion.3), channel_id=1, source_target_pairs={{0,1},{1,0},{2,3},{3,2},{4,5},{5,4},{6,7},{7,6},{8,9},{9,8},{10,11... | collective-permute-start | bytes 24584 | tf_op jit(solution)/shard_map/ppermute | solution.py:625
  85.3 4.0 %collective-permute-start.40 = (f32[2,1024]{1,0:T(2,128)S(1)}, f32[2,1024]{1,0:T(2,128)S(1)}, u32[]{:S(2)}, u32[]{:S(2)}) collective-permute-start(f32[2,1024]{1,0:T(2,128)S(1)} %add_add_fusion.3), channel_id=1, source_target_pairs={{0,17},{1,16},{2,19},{3,18},{4,21},{5,20},{6,23},{7,22},{8,25},{9,... | collective-permute-start | bytes 24584 | tf_op jit(solution)/shard_map/ppermute | solution.py:625
  85.3 5.0 %collective-permute-start.39 = (f32[2,1024]{1,0:T(2,128)S(1)}, f32[2,1024]{1,0:T(2,128)S(1)}, u32[]{:S(2)}, u32[]{:S(2)}) collective-permute-start(f32[2,1024]{1,0:T(2,128)S(1)} %add_add_fusion.3), channel_id=1, source_target_pairs={{0,25},{1,24},{2,27},{3,26},{4,29},{5,28},{6,31},{7,30},{8,17},{9,... | collective-permute-start | bytes 24584 | tf_op jit(solution)/shard_map/ppermute | solution.py:625
  94.0 3.4 %collective-permute-start.45 = (f32[2,1024]{1,0:T(2,128)S(1)}, f32[2,1024]{1,0:T(2,128)S(1)}, u32[]{:S(2)}, u32[]{:S(2)}) collective-permute-start(f32[2,1024]{1,0:T(2,128)S(1)} %get-tuple-element.271), channel_id=1, source_target_pairs={{0,1},{1,0},{2,3},{3,2},{4,5},{5,4},{6,7},{7,6},{8,9},{9,8},{10,11... | collective-permute-start | bytes 24584 | tf_op jit(solution)/shard_map/ppermute | solution.py:625
  94.4 4.0 %collective-permute-start.44 = (f32[2,1024]{1,0:T(2,128)S(1)}, f32[2,1024]{1,0:T(2,128)S(1)}, u32[]{:S(2)}, u32[]{:S(2)}) collective-permute-start(f32[2,1024]{1,0:T(2,128)S(1)} %get-tuple-element.271), channel_id=1, source_target_pairs={{0,7},{1,6},{2,5},{3,4},{4,3},{5,2},{6,1},{7,0},{8,15},{9,14},{10,... | collective-permute-start | bytes 24584 | tf_op jit(solution)/shard_map/ppermute | solution.py:625
  99.7 3.4 %collective-permute-start.49 = (f32[2,1024]{1,0:T(2,128)S(1)}, f32[2,1024]{1,0:T(2,128)S(1)}, u32[]{:S(2)}, u32[]{:S(2)}) collective-permute-start(f32[2,1024]{1,0:T(2,128)S(1)} %add_add_fusion.1), channel_id=1, source_target_pairs={{0,1},{1,0},{2,3},{3,2},{4,5},{5,4},{6,7},{7,6},{8,9},{9,8},{10,11... | collective-permute-start | bytes 24584 | tf_op jit(solution)/shard_map/ppermute | solution.py:625
  100.1 4.0 %collective-permute-start.48 = (f32[2,1024]{1,0:T(2,128)S(1)}, f32[2,1024]{1,0:T(2,128)S(1)}, u32[]{:S(2)}, u32[]{:S(2)}) collective-permute-start(f32[2,1024]{1,0:T(2,128)S(1)} %add_add_fusion.1), channel_id=1, source_target_pairs={{0,17},{1,16},{2,19},{3,18},{4,21},{5,20},{6,23},{7,22},{8,25},{9,... | collective-permute-start | bytes 24584 | tf_op jit(solution)/shard_map/ppermute | solution.py:625
  100.5 4.9 %collective-permute-start.47 = (f32[2,1024]{1,0:T(2,128)S(1)}, f32[2,1024]{1,0:T(2,128)S(1)}, u32[]{:S(2)}, u32[]{:S(2)}) collective-permute-start(f32[2,1024]{1,0:T(2,128)S(1)} %add_add_fusion.1), channel_id=1, source_target_pairs={{0,25},{1,24},{2,27},{3,26},{4,29},{5,28},{6,31},{7,30},{8,17},{9,... | collective-permute-start | bytes 24584 | tf_op jit(solution)/shard_map/ppermute | solution.py:625
  111.5 5.9 %collective-permute-start.54 = (f32[2,512]{1,0:T(2,128)S(1)}, f32[2,512]{1,0:T(2,128)S(1)}, u32[]{:S(2)}, u32[]{:S(2)}) collective-permute-start(f32[2,512]{1,0:T(2,128)S(1)} %get-tuple-element.283), channel_id=1, source_target_pairs={{0,1},{1,0},{2,3},{3,2},{4,5},{5,4},{6,7},{7,6},{8,9},{9,8},{10,11... | collective-permute-start | bytes 12296 | tf_op jit(solution)/shard_map/ppermute | solution.py:625
  111.9 5.6 %collective-permute-start.53 = (f32[2,512]{1,0:T(2,128)S(1)}, f32[2,512]{1,0:T(2,128)S(1)}, u32[]{:S(2)}, u32[]{:S(2)}) collective-permute-start(f32[2,512]{1,0:T(2,128)S(1)} %get-tuple-element.283), channel_id=1, source_target_pairs={{0,7},{1,6},{2,5},{3,4},{4,3},{5,2},{6,1},{7,0},{8,15},{9,14},{10,... | collective-permute-start | bytes 12296 | tf_op jit(solution)/shard_map/ppermute | solution.py:625
  117.7 18.6 %collective-permute-start.63 = (bf16[256,1024]{1,0:T(8,128)(2,1)S(1)}, bf16[256,1024]{1,0:T(8,128)(2,1)S(1)}, u32[]{:S(2)}, u32[]{:S(2)}) collective-permute-start(bf16[256,1024]{1,0:T(8,128)(2,1)S(1)} %get-tuple-element.309), channel_id=1, source_target_pairs={{0,2},{2,0},{1,3},{3,1},{4,6},{6,4},{5,7},{7,5},{8,10},{10,8},{9,1... | collective-permute-start | bytes 1572872 | tf_op jit(solution)/shard_map/ppermute | solution.py:617
  119.3 17.1 %collective-permute-start.64 = (bf16[256,1024]{1,0:T(8,128)(2,1)S(1)}, bf16[256,1024]{1,0:T(8,128)(2,1)S(1)}, u32[]{:S(2)}, u32[]{:S(2)}) collective-permute-start(bf16[256,1024]{1,0:T(8,128)(2,1)S(1)} %get-tuple-element.310), channel_id=1, source_target_pairs={{0,4},{4,0},{8,12},{12,8},{16,20},{20,16},{24,28},{28,24},{1,5},{5... | collective-permute-start | bytes 1572872 | tf_op jit(solution)/shard_map/ppermute | solution.py:639
  120.8 3.9 %collective-permute-start.57 = (f32[2,512]{1,0:T(2,128)S(1)}, f32[2,512]{1,0:T(2,128)S(1)}, u32[]{:S(2)}, u32[]{:S(2)}) collective-permute-start(f32[2,512]{1,0:T(2,128)S(1)} %add_add_fusion.9), channel_id=1, source_target_pairs={{0,17},{1,16},{2,19},{3,18},{4,21},{5,20},{6,23},{7,22},{8,25},{9,... | collective-permute-start | bytes 12296 | tf_op jit(solution)/shard_map/ppermute | solution.py:625
  121.5 4.8 %collective-permute-start.56 = (f32[2,512]{1,0:T(2,128)S(1)}, f32[2,512]{1,0:T(2,128)S(1)}, u32[]{:S(2)}, u32[]{:S(2)}) collective-permute-start(f32[2,512]{1,0:T(2,128)S(1)} %add_add_fusion.9), channel_id=1, source_target_pairs={{0,25},{1,24},{2,27},{3,26},{4,29},{5,28},{6,31},{7,30},{8,17},{9,... | collective-permute-start | bytes 12296 | tf_op jit(solution)/shard_map/ppermute | solution.py:625
  122.9 3.4 %collective-permute-start.55 = (f32[2,512]{1,0:T(2,128)S(1)}, f32[2,512]{1,0:T(2,128)S(1)}, u32[]{:S(2)}, u32[]{:S(2)}) collective-permute-start(f32[2,512]{1,0:T(2,128)S(1)} %add_add_fusion.9), channel_id=1, source_target_pairs={{0,9},{1,8},{2,11},{3,10},{4,13},{5,12},{6,15},{7,14},{8,1},{9,0},... | collective-permute-start | bytes 12296 | tf_op jit(solution)/shard_map/ppermute | solution.py:625
  131.0 4.6 %collective-permute-start.61 = (f32[2,512]{1,0:T(2,128)S(1)}, f32[2,512]{1,0:T(2,128)S(1)}, u32[]{:S(2)}, u32[]{:S(2)}) collective-permute-start(f32[2,512]{1,0:T(2,128)S(1)} %get-tuple-element.299), channel_id=1, source_target_pairs={{0,7},{1,6},{2,5},{3,4},{4,3},{5,2},{6,1},{7,0},{8,15},{9,14},{10,... | collective-permute-start | bytes 12296 | tf_op jit(solution)/shard_map/ppermute | solution.py:625
  131.7 3.9 %collective-permute-start.60 = (f32[2,512]{1,0:T(2,128)S(1)}, f32[2,512]{1,0:T(2,128)S(1)}, u32[]{:S(2)}, u32[]{:S(2)}) collective-permute-start(f32[2,512]{1,0:T(2,128)S(1)} %get-tuple-element.299), channel_id=1, source_target_pairs={{0,5},{1,4},{2,7},{3,6},{4,1},{5,0},{6,3},{7,2},{8,13},{9,12},{10,... | collective-permute-start | bytes 12296 | tf_op jit(solution)/shard_map/ppermute | solution.py:625
  136.5 8.4 %collective-permute-start.69 = (bf16[128,1024]{1,0:T(8,128)(2,1)S(1)}, bf16[128,1024]{1,0:T(8,128)(2,1)S(1)}, u32[]{:S(2)}, u32[]{:S(2)}) collective-permute-start(bf16[128,1024]{1,0:T(8,128)(2,1)S(1)} %get-tuple-element.321), channel_id=1, source_target_pairs={{0,4},{4,0},{8,12},{12,8},{16,20},{20,16},{24,28},{28,24},{1,5},{5... | collective-permute-start | bytes 786440 | tf_op jit(solution)/shard_map/ppermute | solution.py:639
  137.1 8.2 %collective-permute-start.70 = (bf16[128,1024]{1,0:T(8,128)(2,1)S(1)}, bf16[128,1024]{1,0:T(8,128)(2,1)S(1)}, u32[]{:S(2)}, u32[]{:S(2)}) collective-permute-start(bf16[128,1024]{1,0:T(8,128)(2,1)S(1)} %get-tuple-element.322), channel_id=1, source_target_pairs={{0,24},{2,10},{4,28},{6,14},{8,0},{10,18},{12,4},{14,22},{16,8},{1... | collective-permute-start | bytes 786440 | tf_op jit(solution)/shard_map/ppermute | solution.py:635
  138.9 5.8 %collective-permute-start.67 = (f32[2,512]{1,0:T(2,128)S(1)}, f32[2,512]{1,0:T(2,128)S(1)}, u32[]{:S(2)}, u32[]{:S(2)}) collective-permute-start(f32[2,512]{1,0:T(2,128)S(1)} %add_add_fusion.7), channel_id=1, source_target_pairs={{0,17},{1,16},{2,19},{3,18},{4,21},{5,20},{6,23},{7,22},{8,25},{9,... | collective-permute-start | bytes 12296 | tf_op jit(solution)/shard_map/ppermute | solution.py:625
  139.1 5.7 %collective-permute-start.66 = (f32[2,512]{1,0:T(2,128)S(1)}, f32[2,512]{1,0:T(2,128)S(1)}, u32[]{:S(2)}, u32[]{:S(2)}) collective-permute-start(f32[2,512]{1,0:T(2,128)S(1)} %add_add_fusion.7), channel_id=1, source_target_pairs={{0,25},{1,24},{2,27},{3,26},{4,29},{5,28},{6,31},{7,30},{8,17},{9,... | collective-permute-start | bytes 12296 | tf_op jit(solution)/shard_map/ppermute | solution.py:625
  141.2 3.6 %collective-permute-start.65 = (f32[2,512]{1,0:T(2,128)S(1)}, f32[2,512]{1,0:T(2,128)S(1)}, u32[]{:S(2)}, u32[]{:S(2)}) collective-permute-start(f32[2,512]{1,0:T(2,128)S(1)} %add_add_fusion.7), channel_id=1, source_target_pairs={{0,9},{1,8},{2,11},{3,10},{4,13},{5,12},{6,15},{7,14},{8,1},{9,0},... | collective-permute-start | bytes 12296 | tf_op jit(solution)/shard_map/ppermute | solution.py:625
  146.5 12.3 %collective-permute-start.71 = (bf16[304,512]{1,0:T(8,128)(2,1)S(1)}, bf16[304,512]{1,0:T(8,128)(2,1)S(1)}, u32[]{:S(2)}, u32[]{:S(2)}) collective-permute-start(bf16[304,512]{1,0:T(8,128)(2,1)S(1)} %get-tuple-element.329), channel_id=1, source_target_pairs={{0,2},{2,0},{1,3},{3,1},{4,6},{6,4},{5,7},{7,5},{8,10},{10,8},{9,1... | collective-permute-start | bytes 933896 | tf_op jit(solution)/shard_map/ppermute | solution.py:617
  149.5 9.3 %collective-permute-start.74 = (bf16[304,512]{1,0:T(8,128)(2,1)S(1)}, bf16[304,512]{1,0:T(8,128)(2,1)S(1)}, u32[]{:S(2)}, u32[]{:S(2)}) collective-permute-start(bf16[304,512]{1,0:T(8,128)(2,1)S(1)} %get-tuple-element.341), channel_id=1, source_target_pairs={{0,4},{4,0},{8,12},{12,8},{16,20},{20,16},{24,28},{28,24},{1,5},{5... | collective-permute-start | bytes 933896 | tf_op jit(solution)/shard_map/ppermute | solution.py:639
  151.1 7.7 %collective-permute-start.72 = (bf16[128,1024]{1,0:T(8,128)(2,1)S(1)}, bf16[128,1024]{1,0:T(8,128)(2,1)S(1)}, u32[]{:S(2)}, u32[]{:S(2)}) collective-permute-start(bf16[128,1024]{1,0:T(8,128)(2,1)S(1)} %expand_sum.6), channel_id=1, source_target_pairs={{0,24},{2,10},{4,28},{6,14},{8,0},{10,18},{12,4},{14,22},{16,8},{1... | collective-permute-start | bytes 786440 | tf_op jit(solution)/shard_map/ppermute | solution.py:635
  152.1 3.5 %collective-permute-start.73 = (f32[2,2048]{1,0:T(2,128)S(1)}, f32[2,2048]{1,0:T(2,128)S(1)}, u32[]{:S(2)}, u32[]{:S(2)}) collective-permute-start(f32[2,2048]{1,0:T(2,128)S(1)} %pad_maximum_fusion.near), channel_id=1, source_target_pairs={{0,1},{1,0},{2,3},{3,2},{4,5},{5,4},{6,7},{7,6},{8,9},{9,8},{10,11... | collective-permute-start | bytes 49160 | tf_op jit(solution)/shard_map/ppermute | solution.py:612
  159.0 16.9 %collective-permute-start.80 = (bf16[448,2048]{1,0:T(8,128)(2,1)S(1)}, bf16[448,2048]{1,0:T(8,128)(2,1)S(1)}, u32[]{:S(2)}, u32[]{:S(2)}) collective-permute-start(bf16[448,2048]{1,0:T(8,128)(2,1)S(1)} %back_input.2), channel_id=1, source_target_pairs={{0,1},{1,0},{2,3},{3,2},{4,5},{5,4},{6,7},{7,6},{8,9},{9,8},{10,11... | collective-permute-start | bytes 5505032 | tf_op jit(solution)/shard_map/ppermute | solution.py:612
  159.1 5.1 %collective-permute-start.76 = (bf16[448,1024]{1,0:T(8,128)(2,1)S(1)}, bf16[448,1024]{1,0:T(8,128)(2,1)S(1)}, u32[]{:S(2)}, u32[]{:S(2)}) collective-permute-start(bf16[448,1024]{1,0:T(8,128)(2,1)S(1)} %get-tuple-element.345), channel_id=1, source_target_pairs={{0,1},{1,0},{2,3},{3,2},{4,5},{5,4},{6,7},{7,6},{8,9},{9,8},{10,11... | collective-permute-start | bytes 2752520 | tf_op jit(solution)/shard_map/ppermute | solution.py:612
  159.6 9.7 %collective-permute-start.75 = (bf16[304,512]{1,0:T(8,128)(2,1)S(1)}, bf16[304,512]{1,0:T(8,128)(2,1)S(1)}, u32[]{:S(2)}, u32[]{:S(2)}) collective-permute-start(bf16[304,512]{1,0:T(8,128)(2,1)S(1)} %get-tuple-element.342), channel_id=1, source_target_pairs={{0,2},{2,0},{1,3},{3,1},{4,6},{6,4},{5,7},{7,5},{8,10},{10,8},{9,1... | collective-permute-start | bytes 933896 | tf_op jit(solution)/shard_map/ppermute | solution.py:617
  161.7 9.1 %collective-permute-start.78 = (bf16[304,512]{1,0:T(8,128)(2,1)S(1)}, bf16[304,512]{1,0:T(8,128)(2,1)S(1)}, u32[]{:S(2)}, u32[]{:S(2)}) collective-permute-start(bf16[304,512]{1,0:T(8,128)(2,1)S(1)} %get-tuple-element.352), channel_id=1, source_target_pairs={{0,4},{4,0},{8,12},{12,8},{16,20},{20,16},{24,28},{28,24},{1,5},{5... | collective-permute-start | bytes 933896 | tf_op jit(solution)/shard_map/ppermute | solution.py:639
  162.2 8.8 %collective-permute-start.77 = (bf16[304,512]{1,0:T(8,128)(2,1)S(1)}, bf16[304,512]{1,0:T(8,128)(2,1)S(1)}, u32[]{:S(2)}, u32[]{:S(2)}) collective-permute-start(bf16[304,512]{1,0:T(8,128)(2,1)S(1)} %get-tuple-element.346), channel_id=1, source_target_pairs={{0,24},{2,10},{4,28},{6,14},{8,0},{10,18},{12,4},{14,22},{16,8},{1... | collective-permute-start | bytes 933896 | tf_op jit(solution)/shard_map/ppermute | solution.py:635
  171.2 11.4 %collective-permute-start.79 = (bf16[304,512]{1,0:T(8,128)(2,1)S(1)}, bf16[304,512]{1,0:T(8,128)(2,1)S(1)}, u32[]{:S(2)}, u32[]{:S(2)}) collective-permute-start(bf16[304,512]{1,0:T(8,128)(2,1)S(1)} %get-tuple-element.353), channel_id=1, source_target_pairs={{0,24},{2,10},{4,28},{6,14},{8,0},{10,18},{12,4},{14,22},{16,8},{1... | collective-permute-start | bytes 933896 | tf_op jit(solution)/shard_map/ppermute | solution.py:635
  174.7 7.8 %collective-permute-start.82 = (bf16[304,512]{1,0:T(8,128)(2,1)S(1)}, bf16[304,512]{1,0:T(8,128)(2,1)S(1)}, u32[]{:S(2)}, u32[]{:S(2)}) collective-permute-start(bf16[304,512]{1,0:T(8,128)(2,1)S(1)} %get-tuple-element.361), channel_id=1, source_target_pairs={{0,4},{4,0},{8,12},{12,8},{16,20},{20,16},{24,28},{28,24},{1,5},{5... | collective-permute-start | bytes 933896 | tf_op jit(solution)/shard_map/ppermute | solution.py:639
  175.9 6.6 %collective-permute-start.81 = (bf16[128,1024]{1,0:T(8,128)(2,1)S(1)}, bf16[128,1024]{1,0:T(8,128)(2,1)S(1)}, u32[]{:S(2)}, u32[]{:S(2)}) collective-permute-start(bf16[128,1024]{1,0:T(8,128)(2,1)S(1)} %expand_sum.7.mine), channel_id=1, source_target_pairs={{0,2},{2,0},{1,3},{3,1},{4,6},{6,4},{5,7},{7,5},{8,10},{10,8},{9,1... | collective-permute-start | bytes 786440 | tf_op jit(solution)/shard_map/ppermute | solution.py:617
  182.6 7.0 %collective-permute-start.83 = (bf16[304,512]{1,0:T(8,128)(2,1)S(1)}, bf16[304,512]{1,0:T(8,128)(2,1)S(1)}, u32[]{:S(2)}, u32[]{:S(2)}) collective-permute-start(bf16[304,512]{1,0:T(8,128)(2,1)S(1)} %arrived.5.mine), channel_id=1, source_target_pairs={{0,2},{2,0},{1,3},{3,1},{4,6},{6,4},{5,7},{7,5},{8,10},{10,8},{9,1... | collective-permute-start | bytes 933896 | tf_op jit(solution)/shard_map/ppermute | solution.py:617
  184.1 5.5 %collective-permute-start.86 = (bf16[304,512]{1,0:T(8,128)(2,1)S(1)}, bf16[304,512]{1,0:T(8,128)(2,1)S(1)}, u32[]{:S(2)}, u32[]{:S(2)}) collective-permute-start(bf16[304,512]{1,0:T(8,128)(2,1)S(1)} %arrived.5.mine), channel_id=1, source_target_pairs={{0,1},{1,0},{2,3},{3,2},{4,5},{5,4},{6,7},{7,6},{8,9},{9,8},{10,11... | collective-permute-start | bytes 933896 | tf_op jit(solution)/shard_map/ppermute | solution.py:612
  (29 other events, 105.5 us)

commit v7 on v6

--- a/solution.py
+++ b/solution.py
@@ -152,15 +152,18 @@
     copies[-1].wait()
 
 
-def turn_kernel(side, valid, x, x_other, turned, mask):
+def mask_kernel(side, valid, mask):
+    images = valid.shape[0]
+    rows = mask.shape[0] // images
+    inside = lax.broadcasted_iota(jnp.int32, (rows, LANES), 0) % LINE < side
+    for image in range(images):
+        mask[image * rows : (image + 1) * rows, :] = jnp.where(inside, valid[image].astype(F32), 0.0)
+
+
+def turn_kernel(x, x_other, turned):
     rows = x.shape[0]
     turned[:, 0:rows] = x[...].T
     turned[:, rows : 2 * rows] = x_other[...].T
-    images = valid.shape[0]
-    rows = 2 * rows // images
-    inside = lax.broadcasted_iota(jnp.int32, (rows, LANES), 0) % LINE < side
-    for image in range(images):
-        mask[image * rows : (image + 1) * rows, :] = jnp.where(inside, valid[image].astype(F32), 0.0)
 
 
 def reduce_kernel(slots, depth, side, last, valid, mask, x, x_other, *refs):
@@ -696,14 +699,12 @@
     wide_shape = shape((TAPS, half // BLOCK, BLOCK, BLOCK), BF16)
     expand_own, x = halves(w_expand, core), padded(images)
 
-    def turn(x, x_other, valid_other):
+    def mask_of(valid_other):
         valid_both = jnp.concatenate([valid, valid_other])
-        turned, mask = call(
-            functools.partial(turn_kernel, side),
-            [shape((channels, 2 * rows), BF16), shape((2 * rows, LANES), F32)],
-            [valid_both, x, x_other], scalars=1, name="turn",
+        (mask,) = call(
+            functools.partial(mask_kernel, side), [shape((2 * rows, LANES), F32)], [valid_both], scalars=1, name="mask"
         )
-        return valid_both, turned, mask
+        return valid_both, mask
 
     pixels, across_cores = 2 * rows, 2 * count
 
@@ -722,15 +723,15 @@
         passed, second, first_other = swap_x(first), along(first, 1), across(first)
         second, passed, first_other, valid_other = together(second, passed, first_other, valid_other)
         passed_other, second_other, expand_first = swap_x(first_other), across(second), along(expand_own, 1)
-        valid_both, turned, mask = turn(x, x_other, valid_other)
+        valid_both, mask = mask_of(valid_other)
         weights = [own, first, passed, second, other, first_other, passed_other, second_other]
         (before,) = reduce_part((0, 1, 2, 3, 4, 5), False, depth, weights[:6])
-        turned, mask, before, *weights[6:] = together(turned, mask, before, *weights[6:])
+        mask, before, *weights[6:] = together(mask, before, *weights[6:])
         second, other = along(expand_first, 1), across(expand_own)
         slots, slot_depth = size, depth
     else:
         x_other, valid_other = swap_core(x), swap_core(valid)
-        valid_both, turned, mask = turn(x, x_other, valid_other)
+        valid_both, mask = mask_of(valid_other)
         whole = lax.all_gather(own, "fsdp", axis=0, tiled=False)
         weights = [whole[:, :depth].reshape(channels, half)]
         slots, slot_depth = 1, channels
@@ -809,7 +810,9 @@
         [valid_both, total_three, first, outer_vectors, expanded, x, x_other, cot, cot_far], scalars=1, name="output",
     )
 
-    sums_three = everywhere(part)
+    (turned,) = call(turn_kernel, [shape((channels, pixels), BF16)], [x, after(x_other, part)], name="turn")
+    middle, turned = together(plane_sum(part), turned)
+    sums_three = line_sum(middle)
     flat_three, send = call(
         back_expand_kernel,
         [shape((pixels, half_out), BF16), shape((pixels, half), BF16)],

time: 193 us -> 191 us (0.990)
  waiting for transfers between devices: 59.6 us -> 56.9 us
  local copies, waits for them, and re-layouts: 11.4 us -> 14.1 us
    ppermute x48, waiting for transfers between devices: 24.6 us -> 22.5 us  [sum_chips(): got.append(lax.ppermute(values, (*CHIPS, 'core'), pairs))]
    pallas_call x32 -> x33, Pallas kernels: 42 us -> 42.1 us  [call(): pl.pallas_call(kernel, out_shape=outs, in_specs=[sm] * scalars + [given]...]
  transfers between devices with their start and end apart: 88 -> 88, of which waited for: 52 -> 46; matrix products, arithmetic and copies ran while one was open for 6% -> 7% of each run, Pallas kernels for 17% -> 17%
where the time goes in v7:
time: 191 us
  starting transfers between devices  76.3 us (40%)
  waiting for transfers between devices  56.9 us (30%)
  Pallas kernels  42.1 us (22%)
  local copies, waits for them, and re-layouts  14.1 us (7%)
    pallas_call x33, Pallas kernels, call(): pl.pallas_call(kernel, out_shape=outs, in_specs=[sm] * scalars + [given]...  42.1 us
    ppermute x48, starting transfers between devices, sum_chips(): got.append(lax.ppermute(values, (*CHIPS, 'core'), pairs))  40.4 us
    ppermute x48, waiting for transfers between devices, sum_chips(): got.append(lax.ppermute(values, (*CHIPS, 'core'), pairs))  22.5 us
    ppermute x11, starting transfers between devices, across(): return lax.ppermute(values, 'fsdp', [(f, f ^ 1) for f in range(8)])  12.6 us
    ppermute x8, waiting for transfers between devices, along(): return lax.ppermute(values, CHIPS, pairs)  12.2 us
    ppermute x8, starting transfers between devices, along(): return lax.ppermute(values, CHIPS, pairs)  11 us
    ppermute x9, starting transfers between devices, swap_x(): return lax.ppermute(values, 'x', SWAP)  9.67 us
    ppermute x11, waiting for transfers between devices, across(): return lax.ppermute(values, 'fsdp', [(f, f ^ 1) for f in range(8)])  8.74 us
  transfers between devices with their start and end apart: 88, of which 46 were waited for; matrix products, arithmetic and copies ran while one was open for 7% of the time, Pallas kernels for 17%

profile of v7, /device:TPU:0, one launch (start us, length us, event | category | flops | bytes accessed | tf_op | source)
XLA Modules:
  0.0 190.7 jit_solution(15618501585298118035)
XLA Ops:
  1.2 1.9 pack.1.refs_0_
  3.1 2.6 %collective-permute-start.1 = (bf16[304,512]{1,0:T(8,128)(2,1)}, bf16[304,512]{1,0:T(8,128)(2,1)S(1)}, u32[]{:S(2)}, u32[]{:S(2)}) collective-permute-start(bf16[304,512]{1,0:T(8,128)(2,1)} %pack.1.refs_0_), channel_id=1, source_target_pairs={{0,4},{4,0},{8,12},{12,8},{16,20},{20,16},{24,28},{28,24},{1,5},{5... | collective-permute-start | bytes 933896 | tf_op jit(solution)/shard_map/ppermute | solution.py:642
  5.7 1.6 collective-permute-start
  7.3 3.3 %copy.30 = bf16[2,14,14,2048]{3,2,1,0:T(8,128)(2,1)} copy(bf16[2,14,14,2048]{3,0,2,1:T(2,128)(2,1)} %param.12) | data formatting | bytes 3211264
  10.6 1.7 pad.10.clone
  12.4 2.1 %copy.31 = bf16[2,14,14,2048]{3,2,1,0:T(8,128)(2,1)S(1)} copy(bf16[2,14,14,2048]{3,0,2,1:T(2,128)(2,1)} %collective-permute-done.2) | data formatting | bytes 3211264
  14.8 2.4 %collective-permute-done.refs_1_ = bf16[304,512]{1,0:T(8,128)(2,1)S(1)} collective-permute-done((bf16[304,512]{1,0:T(8,128)(2,1)}, bf16[304,512]{1,0:T(8,128)(2,1)S(1)}, u32[]{:S(2)}, u32[]{:S(2)}) %collective-permute-start) | collective-permute-done | bytes 311328 | tf_op jit(solution)/shard_map/ppermute | solution.py:638
  18.9 1.6 collective-permute-start.13
  21.6 4.3 %collective-permute-done.5.refs_5_ = bf16[304,512]{1,0:T(8,128)(2,1)S(1)} collective-permute-done((bf16[304,512]{1,0:T(8,128)(2,1)S(1)}, bf16[304,512]{1,0:T(8,128)(2,1)S(1)}, u32[]{:S(2)}, u32[]{:S(2)}) %collective-permute-start.5) | collective-permute-done | bytes 311328 | tf_op jit(solution)/shard_map/ppermute | solution.py:642
  26.4 4.6 %collective-permute-done.3.refs_3_ = bf16[304,512]{1,0:T(8,128)(2,1)S(1)} collective-permute-done((bf16[304,512]{1,0:T(8,128)(2,1)S(1)}, bf16[304,512]{1,0:T(8,128)(2,1)S(1)}, u32[]{:S(2)}, u32[]{:S(2)}) %collective-permute-start.3) | collective-permute-done | bytes 311328 | tf_op jit(solution)/shard_map/ppermute | solution.py:638
  31.0 1.5 collective-permute-start.8
  33.1 1.9 collective-permute-done.13.refs_1_
  35.6 2.1 %reduce.2.refs_2_ = f32[896,512]{1,0:T(8,128)S(1)} custom-call(s32[4]{0:T(128)S(1)} %pad_add_fusion.valid, f32[896,128]{1,0:T(8,128)S(1)} %mask.1, bf16[448,2048]{1,0:T(8,128)(2,1)S(1)} %bitcast.17, bf16[448,2048]{1,0:T(8,128)(2,1)S(1)} %bitcast.21, bf16[304,512]{1,0:T(8,128)(2,1)S(1)} %copy-done.2, bf16[304,512]{1,0:T(8,128)(2,1)S(1)} %collective-permute-done.refs_1_, ...), custom_call_target="tpu_custom_call" | custom-call | tf_op jit(solution)/shard_map/reduce/pallas_call | solution.py:55
  37.7 2.0 %collective-permute-done.8.refs_1_.refs_7_ = bf16[304,512]{1,0:T(8,128)(2,1)S(1)} collective-permute-done((bf16[304,512]{1,0:T(8,128)(2,1)S(1)}, bf16[304,512]{1,0:T(8,128)(2,1)S(1)}, u32[]{:S(2)}, u32[]{:S(2)}) %collective-permute-start.8) | collective-permute-done | bytes 311328 | tf_op jit(solution)/shard_map/ppermute | solution.py:642
  39.8 1.4 reduce.3
  41.2 2.6 %collective-permute-start.11 = (f32[3,512]{1,0:T(4,128)S(1)}, f32[3,512]{1,0:T(4,128)S(1)}, u32[]{:S(2)}, u32[]{:S(2)}) collective-permute-start(f32[3,512]{1,0:T(4,128)S(1)} %get-tuple-element.205), channel_id=1, source_target_pairs={{0,7},{1,6},{2,5},{3,4},{4,3},{5,2},{6,1},{7,0},{8,15},{9,14},{10,... | collective-permute-start | bytes 18440 | tf_op jit(solution)/shard_map/ppermute | solution.py:628
  45.4 1.5 collective-permute-done.10
  47.1 1.6 collective-permute-start.25
  49.5 1.3 collective-permute-start.17
  50.8 1.4 collective-permute-start.16
  56.4 3.5 %group.3 = (bf16[3,4,256,512]{3,2,1,0:T(8,128)(2,1)S(1)}, f32[896,512]{1,0:T(8,128)S(1)}, f32[2,512]{1,0:T(2,128)S(1)}) custom-call(f32[896,128]{1,0:T(8,128)S(1)} %mask.1, f32[3,512]{1,0:T(4,128)S(1)} %add_add_fusion.4.total.first, f32[4,512]{1,0:T(4,128)S(1)} %get-tuple-element.223.vectors, f32[896,512]{1,0:T(8,128)S(1)} %get-tuple-element.224.red, ...), custom_call_target="tpu_custom_call" | custom-call | tf_op jit(solution)/shard_map/group/pallas_call | solution.py:55
  60.0 1.9 %collective-permute-start.23 = (f32[2,512]{1,0:T(2,128)S(1)}, f32[2,512]{1,0:T(2,128)S(1)}, u32[]{:S(2)}, u32[]{:S(2)}) collective-permute-start(f32[2,512]{1,0:T(2,128)S(1)} %get-tuple-element.228), channel_id=1, source_target_pairs={{0,17},{1,16},{2,19},{3,18},{4,21},{5,20},{6,23},{7,22},{8,25},{9,... | collective-permute-start | bytes 12296 | tf_op jit(solution)/shard_map/ppermute | solution.py:628
  61.9 1.6 collective-permute-start.22
  64.0 2.8 %collective-permute-done.22 = f32[2,512]{1,0:T(2,128)S(1)} collective-permute-done((f32[2,512]{1,0:T(2,128)S(1)}, f32[2,512]{1,0:T(2,128)S(1)}, u32[]{:S(2)}, u32[]{:S(2)}) %collective-permute-start.22) | collective-permute-done | bytes 4128 | tf_op jit(solution)/shard_map/ppermute | solution.py:628
  68.7 1.5 collective-permute-start.28
  74.8 2.3 %expand.1 = (bf16[896,1024]{1,0:T(8,128)(2,1)S(1)}, f32[896,1024]{1,0:T(8,128)S(1)}, f32[2,1024]{1,0:T(2,128)S(1)}) custom-call(f32[896,128]{1,0:T(8,128)S(1)} %mask.1, bf16[896,512]{1,0:T(8,128)(2,1)S(1)} %act.1.act_mine, bf16[896,512]{1,0:T(8,128)(2,1)S(1)} %collective-permute-done.32.act_far, bf16[1024,1024]{1,0:T(8,128)(2,1)S(1)} %assemble.1.weight), custom_call_target="tpu_custom_call" | custom-call | tf_op jit(solution)/shard_map/expand/pallas_call | solution.py:55
  77.4 2.4 %collective-permute-start.35 = (f32[2,1024]{1,0:T(2,128)S(1)}, f32[2,1024]{1,0:T(2,128)S(1)}, u32[]{:S(2)}, u32[]{:S(2)}) collective-permute-start(f32[2,1024]{1,0:T(2,128)S(1)} %get-tuple-element.253), channel_id=1, source_target_pairs={{0,7},{1,6},{2,5},{3,4},{4,3},{5,2},{6,1},{7,0},{8,15},{9,14},{10,... | collective-permute-start | bytes 24584 | tf_op jit(solution)/shard_map/ppermute | solution.py:628
  81.4 1.5 collective-permute-done.34
  84.2 1.6 collective-permute-start.39
  87.6 1.5 collective-permute-done.39
  89.1 3.4 %output.1 = (bf16[448,1024]{1,0:T(8,128)(2,1)S(1)}, bf16[448,1024]{1,0:T(8,128)(2,1)S(1)}, f32[896,1024]{1,0:T(8,128)S(1)}, f32[2,1024]{1,0:T(2,128)S(1)}) custom-call(s32[4]{0:T(128)S(1)} %pad_add_fusion.valid, f32[2,1024]{1,0:T(2,128)S(1)} %add_add_fusion.2.total, f32[3,512]{1,0:T(4,128)S(1)} %add_add_fusion.4.total.first, ...), custom_call_target="tpu_custom_call" | custom-call | tf_op jit(solution)/shard_map/output/pallas_call | solution.py:55
  92.8 1.8 collective-permute-start.44
  95.9 1.7 turn.1.turned
  99.2 1.8 collective-permute-start.47
  102.5 1.6 collective-permute-done.47
  104.2 2.2 %back_expand.1 = (bf16[896,1024]{1,0:T(8,128)(2,1)S(1)}, bf16[896,512]{1,0:T(8,128)(2,1)S(1)}) custom-call(f32[896,128]{1,0:T(8,128)S(1)} %mask.1, f32[2,1024]{1,0:T(2,128)S(1)} %add_add_fusion.2.total, f32[2,1024]{1,0:T(2,128)S(1)} %add_add_fusion.sums, f32[3,512]{1,0:T(4,128)S(1)} %add_add_fusion.4.total.first, f32[2,1024]{1,0:T(2,128)S(1)} %get-tuple-element.264.vectors, ...), custom_call_target="tpu_custom_call" | custom-call | tf_op jit(solution)/shard_map/back_expand/pallas_call | solution.py:55
  110.5 2.3 %collective-permute-start.53 = (f32[2,512]{1,0:T(2,128)S(1)}, f32[2,512]{1,0:T(2,128)S(1)}, u32[]{:S(2)}, u32[]{:S(2)}) collective-permute-start(f32[2,512]{1,0:T(2,128)S(1)} %get-tuple-element.283), channel_id=1, source_target_pairs={{0,7},{1,6},{2,5},{3,4},{4,3},{5,2},{6,1},{7,0},{8,15},{9,14},{10,... | collective-permute-start | bytes 12296 | tf_op jit(solution)/shard_map/ppermute | solution.py:628
  113.6 2.4 %weight_expand.1.keep = bf16[1024,1024]{1,0:T(8,128)(2,1)S(1)} custom-call(bf16[896,1024]{1,0:T(8,128)(2,1)S(1)} %get-tuple-element.289.act, bf16[896,1024]{1,0:T(8,128)(2,1)S(1)} %get-tuple-element.281.flat), custom_call_target="tpu_custom_call" | custom-call | tf_op jit(solution)/shard_map/weight_expand/pallas_call | solution.py:55
  116.3 1.4 collective-permute-start.63
  117.6 1.5 collective-permute-start.64
  119.9 1.5 collective-permute-start.56
  123.1 1.6 collective-permute-done.56
  124.7 4.1 %back_group.1 = (bf16[896,512]{1,0:T(8,128)(2,1)S(1)}, f32[896,512]{1,0:T(8,128)S(1)}, f32[2,512]{1,0:T(2,128)S(1)}) custom-call(f32[896,128]{1,0:T(8,128)S(1)} %mask.1, f32[2,512]{1,0:T(2,128)S(1)} %add_add_fusion.10.total, f32[2,512]{1,0:T(2,128)S(1)} %add_add_fusion.8.sums, f32[3,512]{1,0:T(4,128)S(1)} %add_add_fusion.4.total.first, ...), custom_call_target="tpu_custom_call" | custom-call | tf_op jit(solution)/shard_map/back_group/pallas_call | solution.py:55
  130.2 1.5 collective-permute-start.60
  132.3 1.7 weight_group.1.group
  135.5 1.9 collective-permute-start.70
  137.6 2.0 %collective-permute-start.66 = (f32[2,512]{1,0:T(2,128)S(1)}, f32[2,512]{1,0:T(2,128)S(1)}, u32[]{:S(2)}, u32[]{:S(2)}) collective-permute-start(f32[2,512]{1,0:T(2,128)S(1)} %add_add_fusion.7), channel_id=1, source_target_pairs={{0,25},{1,24},{2,27},{3,26},{4,29},{5,28},{6,31},{7,30},{8,17},{9,... | collective-permute-start | bytes 12296 | tf_op jit(solution)/shard_map/ppermute | solution.py:628
  140.7 2.5 %collective-permute-done.67 = f32[2,512]{1,0:T(2,128)S(1)} collective-permute-done((f32[2,512]{1,0:T(2,128)S(1)}, f32[2,512]{1,0:T(2,128)S(1)}, u32[]{:S(2)}, u32[]{:S(2)}) %collective-permute-start.67) | collective-permute-done | bytes 4128 | tf_op jit(solution)/shard_map/ppermute | solution.py:628
  144.9 2.9 %collective-permute-start.71 = (bf16[304,512]{1,0:T(8,128)(2,1)S(1)}, bf16[304,512]{1,0:T(8,128)(2,1)S(1)}, u32[]{:S(2)}, u32[]{:S(2)}) collective-permute-start(bf16[304,512]{1,0:T(8,128)(2,1)S(1)} %get-tuple-element.329), channel_id=1, source_target_pairs={{0,2},{2,0},{1,3},{3,1},{4,6},{6,4},{5,7},{7,5},{8,10},{10,8},{9,1... | collective-permute-start | bytes 933896 | tf_op jit(solution)/shard_map/ppermute | solution.py:620
  148.0 1.5 collective-permute-start.74
  150.5 1.8 block_sum.1
  152.4 1.7 back_input.2
  154.7 2.6 %collective-permute-done.72.refs_0_ = bf16[128,1024]{1,0:T(8,128)(2,1)S(1)} collective-permute-done((bf16[128,1024]{1,0:T(8,128)(2,1)S(1)}, bf16[128,1024]{1,0:T(8,128)(2,1)S(1)}, u32[]{:S(2)}, u32[]{:S(2)}) %collective-permute-start.72) | collective-permute-done | bytes 262176 | tf_op jit(solution)/shard_map/ppermute | solution.py:638
  158.0 2.1 %collective-permute-start.75 = (bf16[304,512]{1,0:T(8,128)(2,1)S(1)}, bf16[304,512]{1,0:T(8,128)(2,1)S(1)}, u32[]{:S(2)}, u32[]{:S(2)}) collective-permute-start(bf16[304,512]{1,0:T(8,128)(2,1)S(1)} %get-tuple-element.342), channel_id=1, source_target_pairs={{0,2},{2,0},{1,3},{3,1},{4,6},{6,4},{5,7},{7,5},{8,10},{10,8},{9,1... | collective-permute-start | bytes 933896 | tf_op jit(solution)/shard_map/ppermute | solution.py:620
  160.7 1.6 collective-permute-start.77
  162.9 2.8 %copy.36 = bf16[2,14,14,2048]{3,0,2,1:T(2,128)(2,1)} copy(bf16[2,14,14,2048]{3,2,1,0:T(8,128)(2,1)S(1)} %image.1) | data formatting | bytes 3211264 | tf_op jit(solution)/shard_map/image/pallas_call | solution.py:55
  165.7 2.0 %collective-permute-done.75.refs_2_ = bf16[304,512]{1,0:T(8,128)(2,1)S(1)} collective-permute-done((bf16[304,512]{1,0:T(8,128)(2,1)S(1)}, bf16[304,512]{1,0:T(8,128)(2,1)S(1)}, u32[]{:S(2)}, u32[]{:S(2)}) %collective-permute-start.75) | collective-permute-done | bytes 311328 | tf_op jit(solution)/shard_map/ppermute | solution.py:620
  167.7 1.5 collective-permute-done.78.refs_4_
  169.6 3.4 %collective-permute-start.79 = (bf16[304,512]{1,0:T(8,128)(2,1)S(1)}, bf16[304,512]{1,0:T(8,128)(2,1)S(1)}, u32[]{:S(2)}, u32[]{:S(2)}) collective-permute-start(bf16[304,512]{1,0:T(8,128)(2,1)S(1)} %get-tuple-element.353), channel_id=1, source_target_pairs={{0,24},{2,10},{4,28},{6,14},{8,0},{10,18},{12,4},{14,22},{16,8},{1... | collective-permute-start | bytes 933896 | tf_op jit(solution)/shard_map/ppermute | solution.py:638
  174.3 2.0 %back_input.3 = bf16[2,14,14,2048]{3,2,1,0:T(8,128)(2,1)S(1)} custom-call(bf16[896,512]{1,0:T(8,128)(2,1)S(1)} %get-tuple-element.354.flat, f32[896,1024]{1,0:T(8,128)S(1)} %get-tuple-element.280.grad, bf16[304,512]{1,0:T(8,128)(2,1)S(1)} %copy-done.2, bf16[304,512]{1,0:T(8,128)(2,1)S(1)} %collective-permute-done.refs_1_, ...), custom_call_target="tpu_custom_call" | custom-call | tf_op jit(solution)/shard_map/back_input/pallas_call | solution.py:55
  176.3 2.8 %copy.35 = bf16[2,14,14,2048]{3,0,2,1:T(2,128)(2,1)} copy(bf16[2,14,14,2048]{3,2,1,0:T(8,128)(2,1)S(1)} %back_input.3) | data formatting | bytes 3211264 | tf_op jit(solution)/shard_map/back_input/pallas_call | solution.py:55
  179.1 1.7 collective-permute-done.81.mine_x
  185.0 3.0 %collective-permute-done.83.mine_x = bf16[304,512]{1,0:T(8,128)(2,1)S(1)} collective-permute-done((bf16[304,512]{1,0:T(8,128)(2,1)S(1)}, bf16[304,512]{1,0:T(8,128)(2,1)S(1)}, u32[]{:S(2)}, u32[]{:S(2)}) %collective-permute-start.83) | collective-permute-done | bytes 311328 | tf_op jit(solution)/shard_map/ppermute | solution.py:620
  188.0 1.6 collective-permute-done.87.other_x
  (180 shorter events, 53.3 us)
Async XLA Ops:
  0.7 11.7 %collective-permute-start.2 = (bf16[2,14,14,2048]{3,0,2,1:T(2,128)(2,1)}, bf16[2,14,14,2048]{3,0,2,1:T(2,128)(2,1)}, u32[]{:S(2)}, u32[]{:S(2)}) collective-permute-start(bf16[2,14,14,2048]{3,0,2,1:T(2,128)(2,1)} %param.12), channel_id=1, source_target_pairs={{0,1},{1,0},{2,3},{3,2},{4,5},{5,4},{6,7},{7,6},{8,9},{9,8},{10,11... | collective-permute-start | bytes 4816904 | tf_op jit(solution)/shard_map/ppermute | solution.py:615
  3.1 11.7 %collective-permute-start.1 = (bf16[304,512]{1,0:T(8,128)(2,1)}, bf16[304,512]{1,0:T(8,128)(2,1)S(1)}, u32[]{:S(2)}, u32[]{:S(2)}) collective-permute-start(bf16[304,512]{1,0:T(8,128)(2,1)} %pack.1.refs_0_), channel_id=1, source_target_pairs={{0,4},{4,0},{8,12},{12,8},{16,20},{20,16},{24,28},{28,24},{1,5},{5... | collective-permute-start | bytes 933896 | tf_op jit(solution)/shard_map/ppermute | solution.py:642
  5.7 11.5 %collective-permute-start = (bf16[304,512]{1,0:T(8,128)(2,1)}, bf16[304,512]{1,0:T(8,128)(2,1)S(1)}, u32[]{:S(2)}, u32[]{:S(2)}) collective-permute-start(bf16[304,512]{1,0:T(8,128)(2,1)} %pack.1.refs_0_), channel_id=1, source_target_pairs={{0,8},{2,26},{4,12},{6,30},{8,16},{10,2},{12,20},{14,6},{16,24},{1... | collective-permute-start | bytes 933896 | tf_op jit(solution)/shard_map/ppermute | solution.py:638
  17.2 8.7 %collective-permute-start.5 = (bf16[304,512]{1,0:T(8,128)(2,1)S(1)}, bf16[304,512]{1,0:T(8,128)(2,1)S(1)}, u32[]{:S(2)}, u32[]{:S(2)}) collective-permute-start(bf16[304,512]{1,0:T(8,128)(2,1)S(1)} %collective-permute-done.refs_1_), channel_id=1, source_target_pairs={{0,4},{4,0},{8,12},{12,8},{16,20},{20,16},{24,28},{28,24},{1,5},{5... | collective-permute-start | bytes 933896 | tf_op jit(solution)/shard_map/ppermute | solution.py:642
  17.8 8.7 %collective-permute-start.4 = (bf16[304,512]{1,0:T(8,128)(2,1)S(1)}, bf16[304,512]{1,0:T(8,128)(2,1)S(1)}, u32[]{:S(2)}, u32[]{:S(2)}) collective-permute-start(bf16[304,512]{1,0:T(8,128)(2,1)S(1)} %collective-permute-done.refs_1_), channel_id=1, source_target_pairs={{0,2},{2,0},{1,3},{3,1},{4,6},{6,4},{5,7},{7,5},{8,10},{10,8},{9,1... | collective-permute-start | bytes 933896 | tf_op jit(solution)/shard_map/ppermute | solution.py:620
  18.9 12.1 %collective-permute-start.3 = (bf16[304,512]{1,0:T(8,128)(2,1)S(1)}, bf16[304,512]{1,0:T(8,128)(2,1)S(1)}, u32[]{:S(2)}, u32[]{:S(2)}) collective-permute-start(bf16[304,512]{1,0:T(8,128)(2,1)S(1)} %collective-permute-done.refs_1_), channel_id=1, source_target_pairs={{0,8},{2,26},{4,12},{6,30},{8,16},{10,2},{12,20},{14,6},{16,24},{1... | collective-permute-start | bytes 933896 | tf_op jit(solution)/shard_map/ppermute | solution.py:638
  18.9 16.0 %collective-permute-start.13 = (bf16[128,1024]{1,0:T(8,128)(2,1)S(1)}, bf16[128,1024]{1,0:T(8,128)(2,1)S(1)}, u32[]{:S(2)}, u32[]{:S(2)}) collective-permute-start(bf16[128,1024]{1,0:T(8,128)(2,1)S(1)} %constant_dynamic-slice_fusion.refs_0_), channel_id=1, source_target_pairs={{0,8},{2,26},{4,12},{6,30},{8,16},{10,2},{12,20},{14,6},{16,24},{1... | collective-permute-start | bytes 786440 | tf_op jit(solution)/shard_map/ppermute | solution.py:638
  31.0 8.8 %collective-permute-start.8 = (bf16[304,512]{1,0:T(8,128)(2,1)S(1)}, bf16[304,512]{1,0:T(8,128)(2,1)S(1)}, u32[]{:S(2)}, u32[]{:S(2)}) collective-permute-start(bf16[304,512]{1,0:T(8,128)(2,1)S(1)} %collective-permute-done.3.refs_3_), channel_id=1, source_target_pairs={{0,4},{4,0},{8,12},{12,8},{16,20},{20,16},{24,28},{28,24},{1,5},{5... | collective-permute-start | bytes 933896 | tf_op jit(solution)/shard_map/ppermute | solution.py:642
  32.5 7.2 %collective-permute-start.7 = (bf16[304,512]{1,0:T(8,128)(2,1)S(1)}, bf16[304,512]{1,0:T(8,128)(2,1)S(1)}, u32[]{:S(2)}, u32[]{:S(2)}) collective-permute-start(bf16[304,512]{1,0:T(8,128)(2,1)S(1)} %collective-permute-done.5.refs_5_), channel_id=1, source_target_pairs={{0,2},{2,0},{1,3},{3,1},{4,6},{6,4},{5,7},{7,5},{8,10},{10,8},{9,1... | collective-permute-start | bytes 933896 | tf_op jit(solution)/shard_map/ppermute | solution.py:620
  32.5 14.6 %collective-permute-start.15 = (bf16[128,1024]{1,0:T(8,128)(2,1)S(1)}, bf16[128,1024]{1,0:T(8,128)(2,1)S(1)}, u32[]{:S(2)}, u32[]{:S(2)}) collective-permute-start(bf16[128,1024]{1,0:T(8,128)(2,1)S(1)} %constant_dynamic-slice_fusion.refs_0_), channel_id=1, source_target_pairs={{0,4},{4,0},{8,12},{12,8},{16,20},{20,16},{24,28},{28,24},{1,5},{5... | collective-permute-start | bytes 786440 | tf_op jit(solution)/shard_map/ppermute | solution.py:642
  34.9 12.2 %collective-permute-start.14 = (bf16[128,1024]{1,0:T(8,128)(2,1)S(1)}, bf16[128,1024]{1,0:T(8,128)(2,1)S(1)}, u32[]{:S(2)}, u32[]{:S(2)}) collective-permute-start(bf16[128,1024]{1,0:T(8,128)(2,1)S(1)} %collective-permute-done.13.refs_1_), channel_id=1, source_target_pairs={{0,8},{2,26},{4,12},{6,30},{8,16},{10,2},{12,20},{14,6},{16,24},{1... | collective-permute-start | bytes 786440 | tf_op jit(solution)/shard_map/ppermute | solution.py:638
  41.2 4.2 %collective-permute-start.11 = (f32[3,512]{1,0:T(4,128)S(1)}, f32[3,512]{1,0:T(4,128)S(1)}, u32[]{:S(2)}, u32[]{:S(2)}) collective-permute-start(f32[3,512]{1,0:T(4,128)S(1)} %get-tuple-element.205), channel_id=1, source_target_pairs={{0,7},{1,6},{2,5},{3,4},{4,3},{5,2},{6,1},{7,0},{8,15},{9,14},{10,... | collective-permute-start | bytes 18440 | tf_op jit(solution)/shard_map/ppermute | solution.py:628
  47.1 8.7 %collective-permute-start.25 = (bf16[128,1024]{1,0:T(8,128)(2,1)S(1)}, bf16[128,1024]{1,0:T(8,128)(2,1)S(1)}, u32[]{:S(2)}, u32[]{:S(2)}) collective-permute-start(bf16[128,1024]{1,0:T(8,128)(2,1)S(1)} %collective-permute-done.13.refs_1_), channel_id=1, source_target_pairs={{0,4},{4,0},{8,12},{12,8},{16,20},{20,16},{24,28},{28,24},{1,5},{5... | collective-permute-start | bytes 786440 | tf_op jit(solution)/shard_map/ppermute | solution.py:642
  48.9 11.0 %collective-permute-start.20 = (bf16[128,1024]{1,0:T(8,128)(2,1)S(1)}, bf16[128,1024]{1,0:T(8,128)(2,1)S(1)}, u32[]{:S(2)}, u32[]{:S(2)}) collective-permute-start(bf16[128,1024]{1,0:T(8,128)(2,1)S(1)} %collective-permute-done.13.refs_1_), channel_id=1, source_target_pairs={{0,2},{2,0},{1,3},{3,1},{4,6},{6,4},{5,7},{7,5},{8,10},{10,8},{9,1... | collective-permute-start | bytes 786440 | tf_op jit(solution)/shard_map/ppermute | solution.py:620
  49.4 4.0 %collective-permute-start.18 = (f32[3,512]{1,0:T(4,128)S(1)}, f32[3,512]{1,0:T(4,128)S(1)}, u32[]{:S(2)}, u32[]{:S(2)}) collective-permute-start(f32[3,512]{1,0:T(4,128)S(1)} %add_add_fusion.5), channel_id=1, source_target_pairs={{0,17},{1,16},{2,19},{3,18},{4,21},{5,20},{6,23},{7,22},{8,25},{9,... | collective-permute-start | bytes 18440 | tf_op jit(solution)/shard_map/ppermute | solution.py:628
  49.5 4.9 %collective-permute-start.17 = (f32[3,512]{1,0:T(4,128)S(1)}, f32[3,512]{1,0:T(4,128)S(1)}, u32[]{:S(2)}, u32[]{:S(2)}) collective-permute-start(f32[3,512]{1,0:T(4,128)S(1)} %add_add_fusion.5), channel_id=1, source_target_pairs={{0,25},{1,24},{2,27},{3,26},{4,29},{5,28},{6,31},{7,30},{8,17},{9,... | collective-permute-start | bytes 18440 | tf_op jit(solution)/shard_map/ppermute | solution.py:628
  50.8 3.6 %collective-permute-start.16 = (f32[3,512]{1,0:T(4,128)S(1)}, f32[3,512]{1,0:T(4,128)S(1)}, u32[]{:S(2)}, u32[]{:S(2)}) collective-permute-start(f32[3,512]{1,0:T(4,128)S(1)} %add_add_fusion.5), channel_id=1, source_target_pairs={{0,9},{1,8},{2,11},{3,10},{4,13},{5,12},{6,15},{7,14},{8,1},{9,0},... | collective-permute-start | bytes 18440 | tf_op jit(solution)/shard_map/ppermute | solution.py:628
  54.4 12.4 %collective-permute-start.27 = (bf16[128,1024]{1,0:T(8,128)(2,1)S(1)}, bf16[128,1024]{1,0:T(8,128)(2,1)S(1)}, u32[]{:S(2)}, u32[]{:S(2)}) collective-permute-start(bf16[128,1024]{1,0:T(8,128)(2,1)S(1)} %collective-permute-done.14.refs_3_), channel_id=1, source_target_pairs={{0,4},{4,0},{8,12},{12,8},{16,20},{20,16},{24,28},{28,24},{1,5},{5... | collective-permute-start | bytes 786440 | tf_op jit(solution)/shard_map/ppermute | solution.py:642
  55.8 10.9 %collective-permute-start.26 = (bf16[128,1024]{1,0:T(8,128)(2,1)S(1)}, bf16[128,1024]{1,0:T(8,128)(2,1)S(1)}, u32[]{:S(2)}, u32[]{:S(2)}) collective-permute-start(bf16[128,1024]{1,0:T(8,128)(2,1)S(1)} %collective-permute-done.25.refs_5_), channel_id=1, source_target_pairs={{0,2},{2,0},{1,3},{3,1},{4,6},{6,4},{5,7},{7,5},{8,10},{10,8},{9,1... | collective-permute-start | bytes 786440 | tf_op jit(solution)/shard_map/ppermute | solution.py:620
  59.9 3.6 %collective-permute-start.24 = (f32[2,512]{1,0:T(2,128)S(1)}, f32[2,512]{1,0:T(2,128)S(1)}, u32[]{:S(2)}, u32[]{:S(2)}) collective-permute-start(f32[2,512]{1,0:T(2,128)S(1)} %get-tuple-element.228), channel_id=1, source_target_pairs={{0,1},{1,0},{2,3},{3,2},{4,5},{5,4},{6,7},{7,6},{8,9},{9,8},{10,11... | collective-permute-start | bytes 12296 | tf_op jit(solution)/shard_map/ppermute | solution.py:628
  60.0 4.0 %collective-permute-start.23 = (f32[2,512]{1,0:T(2,128)S(1)}, f32[2,512]{1,0:T(2,128)S(1)}, u32[]{:S(2)}, u32[]{:S(2)}) collective-permute-start(f32[2,512]{1,0:T(2,128)S(1)} %get-tuple-element.228), channel_id=1, source_target_pairs={{0,17},{1,16},{2,19},{3,18},{4,21},{5,20},{6,23},{7,22},{8,25},{9,... | collective-permute-start | bytes 12296 | tf_op jit(solution)/shard_map/ppermute | solution.py:628
  61.9 4.8 %collective-permute-start.22 = (f32[2,512]{1,0:T(2,128)S(1)}, f32[2,512]{1,0:T(2,128)S(1)}, u32[]{:S(2)}, u32[]{:S(2)}) collective-permute-start(f32[2,512]{1,0:T(2,128)S(1)} %get-tuple-element.228), channel_id=1, source_target_pairs={{0,25},{1,24},{2,27},{3,26},{4,29},{5,28},{6,31},{7,30},{8,17},{9,... | collective-permute-start | bytes 12296 | tf_op jit(solution)/shard_map/ppermute | solution.py:628
  66.8 3.4 %collective-permute-start.31 = (f32[2,512]{1,0:T(2,128)S(1)}, f32[2,512]{1,0:T(2,128)S(1)}, u32[]{:S(2)}, u32[]{:S(2)}) collective-permute-start(f32[2,512]{1,0:T(2,128)S(1)} %add_add_fusion.11), channel_id=1, source_target_pairs={{0,1},{1,0},{2,3},{3,2},{4,5},{5,4},{6,7},{7,6},{8,9},{9,8},{10,11... | collective-permute-start | bytes 12296 | tf_op jit(solution)/shard_map/ppermute | solution.py:628
  67.0 3.9 %collective-permute-start.30 = (f32[2,512]{1,0:T(2,128)S(1)}, f32[2,512]{1,0:T(2,128)S(1)}, u32[]{:S(2)}, u32[]{:S(2)}) collective-permute-start(f32[2,512]{1,0:T(2,128)S(1)} %add_add_fusion.11), channel_id=1, source_target_pairs={{0,7},{1,6},{2,5},{3,4},{4,3},{5,2},{6,1},{7,0},{8,15},{9,14},{10,... | collective-permute-start | bytes 12296 | tf_op jit(solution)/shard_map/ppermute | solution.py:628
  73.5 9.8 %collective-permute-start.37 = (bf16[448,1024]{1,0:T(8,128)(2,1)S(1)}, bf16[448,1024]{1,0:T(8,128)(2,1)S(1)}, u32[]{:S(2)}, u32[]{:S(2)}) collective-permute-start(bf16[448,1024]{1,0:T(8,128)(2,1)S(1)} %far_half.1), channel_id=1, source_target_pairs={{0,1},{1,0},{2,3},{3,2},{4,5},{5,4},{6,7},{7,6},{8,9},{9,8},{10,11... | collective-permute-start | bytes 2752520 | tf_op jit(solution)/shard_map/ppermute | solution.py:615
  77.2 3.4 %collective-permute-start.36 = (f32[2,1024]{1,0:T(2,128)S(1)}, f32[2,1024]{1,0:T(2,128)S(1)}, u32[]{:S(2)}, u32[]{:S(2)}) collective-permute-start(f32[2,1024]{1,0:T(2,128)S(1)} %get-tuple-element.253), channel_id=1, source_target_pairs={{0,1},{1,0},{2,3},{3,2},{4,5},{5,4},{6,7},{7,6},{8,9},{9,8},{10,11... | collective-permute-start | bytes 24584 | tf_op jit(solution)/shard_map/ppermute | solution.py:628
  77.4 4.0 %collective-permute-start.35 = (f32[2,1024]{1,0:T(2,128)S(1)}, f32[2,1024]{1,0:T(2,128)S(1)}, u32[]{:S(2)}, u32[]{:S(2)}) collective-permute-start(f32[2,1024]{1,0:T(2,128)S(1)} %get-tuple-element.253), channel_id=1, source_target_pairs={{0,7},{1,6},{2,5},{3,4},{4,3},{5,2},{6,1},{7,0},{8,15},{9,14},{10,... | collective-permute-start | bytes 24584 | tf_op jit(solution)/shard_map/ppermute | solution.py:628
  83.4 3.4 %collective-permute-start.41 = (f32[2,1024]{1,0:T(2,128)S(1)}, f32[2,1024]{1,0:T(2,128)S(1)}, u32[]{:S(2)}, u32[]{:S(2)}) collective-permute-start(f32[2,1024]{1,0:T(2,128)S(1)} %add_add_fusion.3), channel_id=1, source_target_pairs={{0,1},{1,0},{2,3},{3,2},{4,5},{5,4},{6,7},{7,6},{8,9},{9,8},{10,11... | collective-permute-start | bytes 24584 | tf_op jit(solution)/shard_map/ppermute | solution.py:628
  83.6 4.0 %collective-permute-start.40 = (f32[2,1024]{1,0:T(2,128)S(1)}, f32[2,1024]{1,0:T(2,128)S(1)}, u32[]{:S(2)}, u32[]{:S(2)}) collective-permute-start(f32[2,1024]{1,0:T(2,128)S(1)} %add_add_fusion.3), channel_id=1, source_target_pairs={{0,17},{1,16},{2,19},{3,18},{4,21},{5,20},{6,23},{7,22},{8,25},{9,... | collective-permute-start | bytes 24584 | tf_op jit(solution)/shard_map/ppermute | solution.py:628
  84.2 4.9 %collective-permute-start.39 = (f32[2,1024]{1,0:T(2,128)S(1)}, f32[2,1024]{1,0:T(2,128)S(1)}, u32[]{:S(2)}, u32[]{:S(2)}) collective-permute-start(f32[2,1024]{1,0:T(2,128)S(1)} %add_add_fusion.3), channel_id=1, source_target_pairs={{0,25},{1,24},{2,27},{3,26},{4,29},{5,28},{6,31},{7,30},{8,17},{9,... | collective-permute-start | bytes 24584 | tf_op jit(solution)/shard_map/ppermute | solution.py:628
  92.5 5.1 %collective-permute-start.45 = (f32[2,1024]{1,0:T(2,128)S(1)}, f32[2,1024]{1,0:T(2,128)S(1)}, u32[]{:S(2)}, u32[]{:S(2)}) collective-permute-start(f32[2,1024]{1,0:T(2,128)S(1)} %get-tuple-element.268), channel_id=1, source_target_pairs={{0,1},{1,0},{2,3},{3,2},{4,5},{5,4},{6,7},{7,6},{8,9},{9,8},{10,11... | collective-permute-start | bytes 24584 | tf_op jit(solution)/shard_map/ppermute | solution.py:628
  92.8 4.8 %collective-permute-start.44 = (f32[2,1024]{1,0:T(2,128)S(1)}, f32[2,1024]{1,0:T(2,128)S(1)}, u32[]{:S(2)}, u32[]{:S(2)}) collective-permute-start(f32[2,1024]{1,0:T(2,128)S(1)} %get-tuple-element.268), channel_id=1, source_target_pairs={{0,7},{1,6},{2,5},{3,4},{4,3},{5,2},{6,1},{7,0},{8,15},{9,14},{10,... | collective-permute-start | bytes 24584 | tf_op jit(solution)/shard_map/ppermute | solution.py:628
  98.2 3.4 %collective-permute-start.49 = (f32[2,1024]{1,0:T(2,128)S(1)}, f32[2,1024]{1,0:T(2,128)S(1)}, u32[]{:S(2)}, u32[]{:S(2)}) collective-permute-start(f32[2,1024]{1,0:T(2,128)S(1)} %add_add_fusion.1), channel_id=1, source_target_pairs={{0,1},{1,0},{2,3},{3,2},{4,5},{5,4},{6,7},{7,6},{8,9},{9,8},{10,11... | collective-permute-start | bytes 24584 | tf_op jit(solution)/shard_map/ppermute | solution.py:628
  98.5 4.0 %collective-permute-start.48 = (f32[2,1024]{1,0:T(2,128)S(1)}, f32[2,1024]{1,0:T(2,128)S(1)}, u32[]{:S(2)}, u32[]{:S(2)}) collective-permute-start(f32[2,1024]{1,0:T(2,128)S(1)} %add_add_fusion.1), channel_id=1, source_target_pairs={{0,17},{1,16},{2,19},{3,18},{4,21},{5,20},{6,23},{7,22},{8,25},{9,... | collective-permute-start | bytes 24584 | tf_op jit(solution)/shard_map/ppermute | solution.py:628
  99.2 4.9 %collective-permute-start.47 = (f32[2,1024]{1,0:T(2,128)S(1)}, f32[2,1024]{1,0:T(2,128)S(1)}, u32[]{:S(2)}, u32[]{:S(2)}) collective-permute-start(f32[2,1024]{1,0:T(2,128)S(1)} %add_add_fusion.1), channel_id=1, source_target_pairs={{0,25},{1,24},{2,27},{3,26},{4,29},{5,28},{6,31},{7,30},{8,17},{9,... | collective-permute-start | bytes 24584 | tf_op jit(solution)/shard_map/ppermute | solution.py:628
  110.2 5.9 %collective-permute-start.54 = (f32[2,512]{1,0:T(2,128)S(1)}, f32[2,512]{1,0:T(2,128)S(1)}, u32[]{:S(2)}, u32[]{:S(2)}) collective-permute-start(f32[2,512]{1,0:T(2,128)S(1)} %get-tuple-element.283), channel_id=1, source_target_pairs={{0,1},{1,0},{2,3},{3,2},{4,5},{5,4},{6,7},{7,6},{8,9},{9,8},{10,11... | collective-permute-start | bytes 12296 | tf_op jit(solution)/shard_map/ppermute | solution.py:628
  110.5 5.6 %collective-permute-start.53 = (f32[2,512]{1,0:T(2,128)S(1)}, f32[2,512]{1,0:T(2,128)S(1)}, u32[]{:S(2)}, u32[]{:S(2)}) collective-permute-start(f32[2,512]{1,0:T(2,128)S(1)} %get-tuple-element.283), channel_id=1, source_target_pairs={{0,7},{1,6},{2,5},{3,4},{4,3},{5,2},{6,1},{7,0},{8,15},{9,14},{10,... | collective-permute-start | bytes 12296 | tf_op jit(solution)/shard_map/ppermute | solution.py:628
  112.8 3.3 %collective-permute-start.52 = (f32[2,512]{1,0:T(2,128)S(1)}, f32[2,512]{1,0:T(2,128)S(1)}, u32[]{:S(2)}, u32[]{:S(2)}) collective-permute-start(f32[2,512]{1,0:T(2,128)S(1)} %get-tuple-element.283), channel_id=1, source_target_pairs={{0,5},{1,4},{2,7},{3,6},{4,1},{5,0},{6,3},{7,2},{8,13},{9,12},{10,... | collective-permute-start | bytes 12296 | tf_op jit(solution)/shard_map/ppermute | solution.py:628
  116.3 18.5 %collective-permute-start.63 = (bf16[256,1024]{1,0:T(8,128)(2,1)S(1)}, bf16[256,1024]{1,0:T(8,128)(2,1)S(1)}, u32[]{:S(2)}, u32[]{:S(2)}) collective-permute-start(bf16[256,1024]{1,0:T(8,128)(2,1)S(1)} %get-tuple-element.309), channel_id=1, source_target_pairs={{0,2},{2,0},{1,3},{3,1},{4,6},{6,4},{5,7},{7,5},{8,10},{10,8},{9,1... | collective-permute-start | bytes 1572872 | tf_op jit(solution)/shard_map/ppermute | solution.py:620
  117.6 17.1 %collective-permute-start.64 = (bf16[256,1024]{1,0:T(8,128)(2,1)S(1)}, bf16[256,1024]{1,0:T(8,128)(2,1)S(1)}, u32[]{:S(2)}, u32[]{:S(2)}) collective-permute-start(bf16[256,1024]{1,0:T(8,128)(2,1)S(1)} %get-tuple-element.310), channel_id=1, source_target_pairs={{0,4},{4,0},{8,12},{12,8},{16,20},{20,16},{24,28},{28,24},{1,5},{5... | collective-permute-start | bytes 1572872 | tf_op jit(solution)/shard_map/ppermute | solution.py:642
  119.2 3.9 %collective-permute-start.57 = (f32[2,512]{1,0:T(2,128)S(1)}, f32[2,512]{1,0:T(2,128)S(1)}, u32[]{:S(2)}, u32[]{:S(2)}) collective-permute-start(f32[2,512]{1,0:T(2,128)S(1)} %add_add_fusion.9), channel_id=1, source_target_pairs={{0,17},{1,16},{2,19},{3,18},{4,21},{5,20},{6,23},{7,22},{8,25},{9,... | collective-permute-start | bytes 12296 | tf_op jit(solution)/shard_map/ppermute | solution.py:628
  119.9 4.8 %collective-permute-start.56 = (f32[2,512]{1,0:T(2,128)S(1)}, f32[2,512]{1,0:T(2,128)S(1)}, u32[]{:S(2)}, u32[]{:S(2)}) collective-permute-start(f32[2,512]{1,0:T(2,128)S(1)} %add_add_fusion.9), channel_id=1, source_target_pairs={{0,25},{1,24},{2,27},{3,26},{4,29},{5,28},{6,31},{7,30},{8,17},{9,... | collective-permute-start | bytes 12296 | tf_op jit(solution)/shard_map/ppermute | solution.py:628
  121.4 3.3 %collective-permute-start.55 = (f32[2,512]{1,0:T(2,128)S(1)}, f32[2,512]{1,0:T(2,128)S(1)}, u32[]{:S(2)}, u32[]{:S(2)}) collective-permute-start(f32[2,512]{1,0:T(2,128)S(1)} %add_add_fusion.9), channel_id=1, source_target_pairs={{0,9},{1,8},{2,11},{3,10},{4,13},{5,12},{6,15},{7,14},{8,1},{9,0},... | collective-permute-start | bytes 12296 | tf_op jit(solution)/shard_map/ppermute | solution.py:628
  129.4 4.6 %collective-permute-start.61 = (f32[2,512]{1,0:T(2,128)S(1)}, f32[2,512]{1,0:T(2,128)S(1)}, u32[]{:S(2)}, u32[]{:S(2)}) collective-permute-start(f32[2,512]{1,0:T(2,128)S(1)} %get-tuple-element.299), channel_id=1, source_target_pairs={{0,7},{1,6},{2,5},{3,4},{4,3},{5,2},{6,1},{7,0},{8,15},{9,14},{10,... | collective-permute-start | bytes 12296 | tf_op jit(solution)/shard_map/ppermute | solution.py:628
  130.2 3.9 %collective-permute-start.60 = (f32[2,512]{1,0:T(2,128)S(1)}, f32[2,512]{1,0:T(2,128)S(1)}, u32[]{:S(2)}, u32[]{:S(2)}) collective-permute-start(f32[2,512]{1,0:T(2,128)S(1)} %get-tuple-element.299), channel_id=1, source_target_pairs={{0,5},{1,4},{2,7},{3,6},{4,1},{5,0},{6,3},{7,2},{8,13},{9,12},{10,... | collective-permute-start | bytes 12296 | tf_op jit(solution)/shard_map/ppermute | solution.py:628
  134.9 8.4 %collective-permute-start.69 = (bf16[128,1024]{1,0:T(8,128)(2,1)S(1)}, bf16[128,1024]{1,0:T(8,128)(2,1)S(1)}, u32[]{:S(2)}, u32[]{:S(2)}) collective-permute-start(bf16[128,1024]{1,0:T(8,128)(2,1)S(1)} %get-tuple-element.321), channel_id=1, source_target_pairs={{0,4},{4,0},{8,12},{12,8},{16,20},{20,16},{24,28},{28,24},{1,5},{5... | collective-permute-start | bytes 786440 | tf_op jit(solution)/shard_map/ppermute | solution.py:642
  135.5 8.2 %collective-permute-start.70 = (bf16[128,1024]{1,0:T(8,128)(2,1)S(1)}, bf16[128,1024]{1,0:T(8,128)(2,1)S(1)}, u32[]{:S(2)}, u32[]{:S(2)}) collective-permute-start(bf16[128,1024]{1,0:T(8,128)(2,1)S(1)} %get-tuple-element.322), channel_id=1, source_target_pairs={{0,24},{2,10},{4,28},{6,14},{8,0},{10,18},{12,4},{14,22},{16,8},{1... | collective-permute-start | bytes 786440 | tf_op jit(solution)/shard_map/ppermute | solution.py:638
  137.4 5.8 %collective-permute-start.67 = (f32[2,512]{1,0:T(2,128)S(1)}, f32[2,512]{1,0:T(2,128)S(1)}, u32[]{:S(2)}, u32[]{:S(2)}) collective-permute-start(f32[2,512]{1,0:T(2,128)S(1)} %add_add_fusion.7), channel_id=1, source_target_pairs={{0,17},{1,16},{2,19},{3,18},{4,21},{5,20},{6,23},{7,22},{8,25},{9,... | collective-permute-start | bytes 12296 | tf_op jit(solution)/shard_map/ppermute | solution.py:628
  137.6 5.7 %collective-permute-start.66 = (f32[2,512]{1,0:T(2,128)S(1)}, f32[2,512]{1,0:T(2,128)S(1)}, u32[]{:S(2)}, u32[]{:S(2)}) collective-permute-start(f32[2,512]{1,0:T(2,128)S(1)} %add_add_fusion.7), channel_id=1, source_target_pairs={{0,25},{1,24},{2,27},{3,26},{4,29},{5,28},{6,31},{7,30},{8,17},{9,... | collective-permute-start | bytes 12296 | tf_op jit(solution)/shard_map/ppermute | solution.py:628
  139.6 3.7 %collective-permute-start.65 = (f32[2,512]{1,0:T(2,128)S(1)}, f32[2,512]{1,0:T(2,128)S(1)}, u32[]{:S(2)}, u32[]{:S(2)}) collective-permute-start(f32[2,512]{1,0:T(2,128)S(1)} %add_add_fusion.7), channel_id=1, source_target_pairs={{0,9},{1,8},{2,11},{3,10},{4,13},{5,12},{6,15},{7,14},{8,1},{9,0},... | collective-permute-start | bytes 12296 | tf_op jit(solution)/shard_map/ppermute | solution.py:628
  144.9 12.3 %collective-permute-start.71 = (bf16[304,512]{1,0:T(8,128)(2,1)S(1)}, bf16[304,512]{1,0:T(8,128)(2,1)S(1)}, u32[]{:S(2)}, u32[]{:S(2)}) collective-permute-start(bf16[304,512]{1,0:T(8,128)(2,1)S(1)} %get-tuple-element.329), channel_id=1, source_target_pairs={{0,2},{2,0},{1,3},{3,1},{4,6},{6,4},{5,7},{7,5},{8,10},{10,8},{9,1... | collective-permute-start | bytes 933896 | tf_op jit(solution)/shard_map/ppermute | solution.py:620
  148.0 9.3 %collective-permute-start.74 = (bf16[304,512]{1,0:T(8,128)(2,1)S(1)}, bf16[304,512]{1,0:T(8,128)(2,1)S(1)}, u32[]{:S(2)}, u32[]{:S(2)}) collective-permute-start(bf16[304,512]{1,0:T(8,128)(2,1)S(1)} %get-tuple-element.341), channel_id=1, source_target_pairs={{0,4},{4,0},{8,12},{12,8},{16,20},{20,16},{24,28},{28,24},{1,5},{5... | collective-permute-start | bytes 933896 | tf_op jit(solution)/shard_map/ppermute | solution.py:642
  149.5 7.7 %collective-permute-start.72 = (bf16[128,1024]{1,0:T(8,128)(2,1)S(1)}, bf16[128,1024]{1,0:T(8,128)(2,1)S(1)}, u32[]{:S(2)}, u32[]{:S(2)}) collective-permute-start(bf16[128,1024]{1,0:T(8,128)(2,1)S(1)} %expand_sum.6), channel_id=1, source_target_pairs={{0,24},{2,10},{4,28},{6,14},{8,0},{10,18},{12,4},{14,22},{16,8},{1... | collective-permute-start | bytes 786440 | tf_op jit(solution)/shard_map/ppermute | solution.py:638
  150.5 3.6 %collective-permute-start.73 = (f32[2,2048]{1,0:T(2,128)S(1)}, f32[2,2048]{1,0:T(2,128)S(1)}, u32[]{:S(2)}, u32[]{:S(2)}) collective-permute-start(f32[2,2048]{1,0:T(2,128)S(1)} %pad_maximum_fusion.near), channel_id=1, source_target_pairs={{0,1},{1,0},{2,3},{3,2},{4,5},{5,4},{6,7},{7,6},{8,9},{9,8},{10,11... | collective-permute-start | bytes 49160 | tf_op jit(solution)/shard_map/ppermute | solution.py:615
  157.4 16.9 %collective-permute-start.80 = (bf16[448,2048]{1,0:T(8,128)(2,1)S(1)}, bf16[448,2048]{1,0:T(8,128)(2,1)S(1)}, u32[]{:S(2)}, u32[]{:S(2)}) collective-permute-start(bf16[448,2048]{1,0:T(8,128)(2,1)S(1)} %back_input.2), channel_id=1, source_target_pairs={{0,1},{1,0},{2,3},{3,2},{4,5},{5,4},{6,7},{7,6},{8,9},{9,8},{10,11... | collective-permute-start | bytes 5505032 | tf_op jit(solution)/shard_map/ppermute | solution.py:615
  157.5 5.1 %collective-permute-start.76 = (bf16[448,1024]{1,0:T(8,128)(2,1)S(1)}, bf16[448,1024]{1,0:T(8,128)(2,1)S(1)}, u32[]{:S(2)}, u32[]{:S(2)}) collective-permute-start(bf16[448,1024]{1,0:T(8,128)(2,1)S(1)} %get-tuple-element.345), channel_id=1, source_target_pairs={{0,1},{1,0},{2,3},{3,2},{4,5},{5,4},{6,7},{7,6},{8,9},{9,8},{10,11... | collective-permute-start | bytes 2752520 | tf_op jit(solution)/shard_map/ppermute | solution.py:615
  158.0 9.7 %collective-permute-start.75 = (bf16[304,512]{1,0:T(8,128)(2,1)S(1)}, bf16[304,512]{1,0:T(8,128)(2,1)S(1)}, u32[]{:S(2)}, u32[]{:S(2)}) collective-permute-start(bf16[304,512]{1,0:T(8,128)(2,1)S(1)} %get-tuple-element.342), channel_id=1, source_target_pairs={{0,2},{2,0},{1,3},{3,1},{4,6},{6,4},{5,7},{7,5},{8,10},{10,8},{9,1... | collective-permute-start | bytes 933896 | tf_op jit(solution)/shard_map/ppermute | solution.py:620
  160.1 9.1 %collective-permute-start.78 = (bf16[304,512]{1,0:T(8,128)(2,1)S(1)}, bf16[304,512]{1,0:T(8,128)(2,1)S(1)}, u32[]{:S(2)}, u32[]{:S(2)}) collective-permute-start(bf16[304,512]{1,0:T(8,128)(2,1)S(1)} %get-tuple-element.352), channel_id=1, source_target_pairs={{0,4},{4,0},{8,12},{12,8},{16,20},{20,16},{24,28},{28,24},{1,5},{5... | collective-permute-start | bytes 933896 | tf_op jit(solution)/shard_map/ppermute | solution.py:642
  160.7 8.8 %collective-permute-start.77 = (bf16[304,512]{1,0:T(8,128)(2,1)S(1)}, bf16[304,512]{1,0:T(8,128)(2,1)S(1)}, u32[]{:S(2)}, u32[]{:S(2)}) collective-permute-start(bf16[304,512]{1,0:T(8,128)(2,1)S(1)} %get-tuple-element.346), channel_id=1, source_target_pairs={{0,24},{2,10},{4,28},{6,14},{8,0},{10,18},{12,4},{14,22},{16,8},{1... | collective-permute-start | bytes 933896 | tf_op jit(solution)/shard_map/ppermute | solution.py:638
  169.6 11.2 %collective-permute-start.79 = (bf16[304,512]{1,0:T(8,128)(2,1)S(1)}, bf16[304,512]{1,0:T(8,128)(2,1)S(1)}, u32[]{:S(2)}, u32[]{:S(2)}) collective-permute-start(bf16[304,512]{1,0:T(8,128)(2,1)S(1)} %get-tuple-element.353), channel_id=1, source_target_pairs={{0,24},{2,10},{4,28},{6,14},{8,0},{10,18},{12,4},{14,22},{16,8},{1... | collective-permute-start | bytes 933896 | tf_op jit(solution)/shard_map/ppermute | solution.py:638
  173.1 7.8 %collective-permute-start.82 = (bf16[304,512]{1,0:T(8,128)(2,1)S(1)}, bf16[304,512]{1,0:T(8,128)(2,1)S(1)}, u32[]{:S(2)}, u32[]{:S(2)}) collective-permute-start(bf16[304,512]{1,0:T(8,128)(2,1)S(1)} %get-tuple-element.361), channel_id=1, source_target_pairs={{0,4},{4,0},{8,12},{12,8},{16,20},{20,16},{24,28},{28,24},{1,5},{5... | collective-permute-start | bytes 933896 | tf_op jit(solution)/shard_map/ppermute | solution.py:642
  174.3 6.6 %collective-permute-start.81 = (bf16[128,1024]{1,0:T(8,128)(2,1)S(1)}, bf16[128,1024]{1,0:T(8,128)(2,1)S(1)}, u32[]{:S(2)}, u32[]{:S(2)}) collective-permute-start(bf16[128,1024]{1,0:T(8,128)(2,1)S(1)} %expand_sum.7.mine), channel_id=1, source_target_pairs={{0,2},{2,0},{1,3},{3,1},{4,6},{6,4},{5,7},{7,5},{8,10},{10,8},{9,1... | collective-permute-start | bytes 786440 | tf_op jit(solution)/shard_map/ppermute | solution.py:620
  181.0 7.0 %collective-permute-start.83 = (bf16[304,512]{1,0:T(8,128)(2,1)S(1)}, bf16[304,512]{1,0:T(8,128)(2,1)S(1)}, u32[]{:S(2)}, u32[]{:S(2)}) collective-permute-start(bf16[304,512]{1,0:T(8,128)(2,1)S(1)} %arrived.5.mine), channel_id=1, source_target_pairs={{0,2},{2,0},{1,3},{3,1},{4,6},{6,4},{5,7},{7,5},{8,10},{10,8},{9,1... | collective-permute-start | bytes 933896 | tf_op jit(solution)/shard_map/ppermute | solution.py:620
  182.5 5.5 %collective-permute-start.86 = (bf16[304,512]{1,0:T(8,128)(2,1)S(1)}, bf16[304,512]{1,0:T(8,128)(2,1)S(1)}, u32[]{:S(2)}, u32[]{:S(2)}) collective-permute-start(bf16[304,512]{1,0:T(8,128)(2,1)S(1)} %arrived.5.mine), channel_id=1, source_target_pairs={{0,1},{1,0},{2,3},{3,2},{4,5},{5,4},{6,7},{7,6},{8,9},{9,8},{10,11... | collective-permute-start | bytes 933896 | tf_op jit(solution)/shard_map/ppermute | solution.py:615
  (29 other events, 125.0 us)

commit v8 on v7

--- a/solution.py
+++ b/solution.py
@@ -623,7 +623,7 @@
 
 def sum_chips(values, flips):
     got = []
-    for flip in (*flips, 0):
+    for flip in (0, *flips):
         pairs = [(2 * at + core, 2 * (at ^ flip) + 1 - core) for at in range(16) for core in range(2)]
         got.append(lax.ppermute(values, (*CHIPS, "core"), pairs))
     got = together(*got)

time: 191 us -> 189 us (0.990)
  starting transfers between devices: 76.3 us -> 73.3 us
    ppermute x48, starting transfers between devices: 40.4 us -> 38.2 us  [sum_chips(): got.append(lax.ppermute(values, (*CHIPS, 'core'), pairs))]
where the time goes in v8:
time: 189 us
  starting transfers between devices  73.3 us (39%)
  waiting for transfers between devices  58 us (31%)
  Pallas kernels  42 us (22%)
  local copies, waits for them, and re-layouts  14.1 us (7%)
    pallas_call x33, Pallas kernels, call(): pl.pallas_call(kernel, out_shape=outs, in_specs=[sm] * scalars + [given]...  42 us
    ppermute x48, starting transfers between devices, sum_chips(): got.append(lax.ppermute(values, (*CHIPS, 'core'), pairs))  38.2 us
    ppermute x48, waiting for transfers between devices, sum_chips(): got.append(lax.ppermute(values, (*CHIPS, 'core'), pairs))  24.1 us
    ppermute x11, starting transfers between devices, across(): return lax.ppermute(values, 'fsdp', [(f, f ^ 1) for f in range(8)])  12.2 us
    ppermute x8, waiting for transfers between devices, along(): return lax.ppermute(values, CHIPS, pairs)  11.5 us
    ppermute x8, starting transfers between devices, along(): return lax.ppermute(values, CHIPS, pairs)  11 us
    ppermute x9, starting transfers between devices, swap_x(): return lax.ppermute(values, 'x', SWAP)  9.38 us
    ppermute x11, waiting for transfers between devices, across(): return lax.ppermute(values, 'fsdp', [(f, f ^ 1) for f in range(8)])  8.47 us
  transfers between devices with their start and end apart: 88, of which 46 were waited for; matrix products, arithmetic and copies ran while one was open for 7% of the time, Pallas kernels for 17%

profile of v8, /device:TPU:0, one launch (start us, length us, event | category | flops | bytes accessed | tf_op | source)
XLA Modules:
  0.0 188.9 jit_solution(3730006117375158386)
XLA Ops:
  1.2 1.9 pack.1.refs_0_
  3.1 2.6 %collective-permute-start.1 = (bf16[304,512]{1,0:T(8,128)(2,1)}, bf16[304,512]{1,0:T(8,128)(2,1)S(1)}, u32[]{:S(2)}, u32[]{:S(2)}) collective-permute-start(bf16[304,512]{1,0:T(8,128)(2,1)} %pack.1.refs_0_), channel_id=1, source_target_pairs={{0,4},{4,0},{8,12},{12,8},{16,20},{20,16},{24,28},{28,24},{1,5},{5... | collective-permute-start | bytes 933896 | tf_op jit(solution)/shard_map/ppermute | solution.py:642
  5.7 1.6 collective-permute-start
  7.3 3.3 %copy.30 = bf16[2,14,14,2048]{3,2,1,0:T(8,128)(2,1)} copy(bf16[2,14,14,2048]{3,0,2,1:T(2,128)(2,1)} %param.12) | data formatting | bytes 3211264
  10.6 1.7 pad.10.clone
  12.4 2.1 %copy.31 = bf16[2,14,14,2048]{3,2,1,0:T(8,128)(2,1)S(1)} copy(bf16[2,14,14,2048]{3,0,2,1:T(2,128)(2,1)} %collective-permute-done.2) | data formatting | bytes 3211264
  14.8 2.4 %collective-permute-done.refs_1_ = bf16[304,512]{1,0:T(8,128)(2,1)S(1)} collective-permute-done((bf16[304,512]{1,0:T(8,128)(2,1)}, bf16[304,512]{1,0:T(8,128)(2,1)S(1)}, u32[]{:S(2)}, u32[]{:S(2)}) %collective-permute-start) | collective-permute-done | bytes 311328 | tf_op jit(solution)/shard_map/ppermute | solution.py:638
  17.8 1.2 collective-permute-start.4
  18.9 1.6 collective-permute-start.13
  21.6 4.3 %collective-permute-done.5.refs_5_ = bf16[304,512]{1,0:T(8,128)(2,1)S(1)} collective-permute-done((bf16[304,512]{1,0:T(8,128)(2,1)S(1)}, bf16[304,512]{1,0:T(8,128)(2,1)S(1)}, u32[]{:S(2)}, u32[]{:S(2)}) %collective-permute-start.5) | collective-permute-done | bytes 311328 | tf_op jit(solution)/shard_map/ppermute | solution.py:642
  26.4 4.6 %collective-permute-done.3.refs_3_ = bf16[304,512]{1,0:T(8,128)(2,1)S(1)} collective-permute-done((bf16[304,512]{1,0:T(8,128)(2,1)S(1)}, bf16[304,512]{1,0:T(8,128)(2,1)S(1)}, u32[]{:S(2)}, u32[]{:S(2)}) %collective-permute-start.3) | collective-permute-done | bytes 311328 | tf_op jit(solution)/shard_map/ppermute | solution.py:638
  31.0 1.5 collective-permute-start.8
  33.1 1.9 collective-permute-done.13.refs_1_
  35.6 2.1 %reduce.2.refs_2_ = f32[896,512]{1,0:T(8,128)S(1)} custom-call(s32[4]{0:T(128)S(1)} %pad_add_fusion.valid, f32[896,128]{1,0:T(8,128)S(1)} %mask.1, bf16[448,2048]{1,0:T(8,128)(2,1)S(1)} %bitcast.17, bf16[448,2048]{1,0:T(8,128)(2,1)S(1)} %bitcast.21, bf16[304,512]{1,0:T(8,128)(2,1)S(1)} %copy-done.2, bf16[304,512]{1,0:T(8,128)(2,1)S(1)} %collective-permute-done.refs_1_, ...), custom_call_target="tpu_custom_call" | custom-call | tf_op jit(solution)/shard_map/reduce/pallas_call | solution.py:55
  37.7 2.0 %collective-permute-done.8.refs_1_.refs_7_ = bf16[304,512]{1,0:T(8,128)(2,1)S(1)} collective-permute-done((bf16[304,512]{1,0:T(8,128)(2,1)S(1)}, bf16[304,512]{1,0:T(8,128)(2,1)S(1)}, u32[]{:S(2)}, u32[]{:S(2)}) %collective-permute-start.8) | collective-permute-done | bytes 311328 | tf_op jit(solution)/shard_map/ppermute | solution.py:642
  39.8 1.4 reduce.3
  41.2 2.7 %collective-permute-start.11 = (f32[3,512]{1,0:T(4,128)S(1)}, f32[3,512]{1,0:T(4,128)S(1)}, u32[]{:S(2)}, u32[]{:S(2)}) collective-permute-start(f32[3,512]{1,0:T(4,128)S(1)} %get-tuple-element.205), channel_id=1, source_target_pairs={{0,5},{1,4},{2,7},{3,6},{4,1},{5,0},{6,3},{7,2},{8,13},{9,12},{10,... | collective-permute-start | bytes 18440 | tf_op jit(solution)/shard_map/ppermute | solution.py:628
  47.1 1.6 collective-permute-start.25
  50.6 1.7 collective-permute-start.17
  52.6 1.9 collective-permute-done.18
  56.4 3.5 %group.3 = (bf16[3,4,256,512]{3,2,1,0:T(8,128)(2,1)S(1)}, f32[896,512]{1,0:T(8,128)S(1)}, f32[2,512]{1,0:T(2,128)S(1)}) custom-call(f32[896,128]{1,0:T(8,128)S(1)} %mask.1, f32[3,512]{1,0:T(4,128)S(1)} %add_add_fusion.4.total.first, f32[4,512]{1,0:T(4,128)S(1)} %get-tuple-element.223.vectors, f32[896,512]{1,0:T(8,128)S(1)} %get-tuple-element.224.red, ...), custom_call_target="tpu_custom_call" | custom-call | tf_op jit(solution)/shard_map/group/pallas_call | solution.py:55
  60.4 2.6 %collective-permute-start.23 = (f32[2,512]{1,0:T(2,128)S(1)}, f32[2,512]{1,0:T(2,128)S(1)}, u32[]{:S(2)}, u32[]{:S(2)}) collective-permute-start(f32[2,512]{1,0:T(2,128)S(1)} %get-tuple-element.228), channel_id=1, source_target_pairs={{0,25},{1,24},{2,27},{3,26},{4,29},{5,28},{6,31},{7,30},{8,17},{9,... | collective-permute-start | bytes 12296 | tf_op jit(solution)/shard_map/ppermute | solution.py:628
  63.9 1.3 collective-permute-done.23
  66.0 1.6 collective-permute-start.31
  74.2 2.3 %expand.1 = (bf16[896,1024]{1,0:T(8,128)(2,1)S(1)}, f32[896,1024]{1,0:T(8,128)S(1)}, f32[2,1024]{1,0:T(2,128)S(1)}) custom-call(f32[896,128]{1,0:T(8,128)S(1)} %mask.1, bf16[896,512]{1,0:T(8,128)(2,1)S(1)} %act.1.act_mine, bf16[896,512]{1,0:T(8,128)(2,1)S(1)} %collective-permute-done.32.act_far, bf16[1024,1024]{1,0:T(8,128)(2,1)S(1)} %assemble.1.weight), custom_call_target="tpu_custom_call" | custom-call | tf_op jit(solution)/shard_map/expand/pallas_call | solution.py:55
  76.6 1.9 %collective-permute-start.36 = (f32[2,1024]{1,0:T(2,128)S(1)}, f32[2,1024]{1,0:T(2,128)S(1)}, u32[]{:S(2)}, u32[]{:S(2)}) collective-permute-start(f32[2,1024]{1,0:T(2,128)S(1)} %get-tuple-element.253), channel_id=1, source_target_pairs={{0,7},{1,6},{2,5},{3,4},{4,3},{5,2},{6,1},{7,0},{8,15},{9,14},{10,... | collective-permute-start | bytes 24584 | tf_op jit(solution)/shard_map/ppermute | solution.py:628
  82.7 1.9 collective-permute-start.40
  86.1 1.4 collective-permute-done.40
  87.6 3.4 %output.1 = (bf16[448,1024]{1,0:T(8,128)(2,1)S(1)}, bf16[448,1024]{1,0:T(8,128)(2,1)S(1)}, f32[896,1024]{1,0:T(8,128)S(1)}, f32[2,1024]{1,0:T(2,128)S(1)}) custom-call(s32[4]{0:T(128)S(1)} %pad_add_fusion.valid, f32[2,1024]{1,0:T(2,128)S(1)} %add_add_fusion.2.total, f32[3,512]{1,0:T(4,128)S(1)} %add_add_fusion.4.total.first, ...), custom_call_target="tpu_custom_call" | custom-call | tf_op jit(solution)/shard_map/output/pallas_call | solution.py:55
  91.1 1.6 collective-permute-start.45
  94.5 1.7 turn.1.turned
  97.5 1.8 collective-permute-start.48
  100.6 1.9 %collective-permute-done.48 = f32[2,1024]{1,0:T(2,128)S(1)} collective-permute-done((f32[2,1024]{1,0:T(2,128)S(1)}, f32[2,1024]{1,0:T(2,128)S(1)}, u32[]{:S(2)}, u32[]{:S(2)}) %collective-permute-start.48) | collective-permute-done | bytes 8224 | tf_op jit(solution)/shard_map/ppermute | solution.py:628
  102.5 2.2 %back_expand.1 = (bf16[896,1024]{1,0:T(8,128)(2,1)S(1)}, bf16[896,512]{1,0:T(8,128)(2,1)S(1)}) custom-call(f32[896,128]{1,0:T(8,128)S(1)} %mask.1, f32[2,1024]{1,0:T(2,128)S(1)} %add_add_fusion.2.total, f32[2,1024]{1,0:T(2,128)S(1)} %add_add_fusion.sums, f32[3,512]{1,0:T(4,128)S(1)} %add_add_fusion.4.total.first, f32[2,1024]{1,0:T(2,128)S(1)} %get-tuple-element.264.vectors, ...), custom_call_target="tpu_custom_call" | custom-call | tf_op jit(solution)/shard_map/back_expand/pallas_call | solution.py:55
  107.3 1.3 back_act.1
  108.6 1.9 collective-permute-start.54
  112.0 2.4 %weight_expand.1.keep = bf16[1024,1024]{1,0:T(8,128)(2,1)S(1)} custom-call(bf16[896,1024]{1,0:T(8,128)(2,1)S(1)} %get-tuple-element.289.act, bf16[896,1024]{1,0:T(8,128)(2,1)S(1)} %get-tuple-element.281.flat), custom_call_target="tpu_custom_call" | custom-call | tf_op jit(solution)/shard_map/weight_expand/pallas_call | solution.py:55
  114.5 1.2 collective-permute-start.63
  115.7 1.5 collective-permute-start.64
  117.2 2.3 %collective-permute-start.57 = (f32[2,512]{1,0:T(2,128)S(1)}, f32[2,512]{1,0:T(2,128)S(1)}, u32[]{:S(2)}, u32[]{:S(2)}) collective-permute-start(f32[2,512]{1,0:T(2,128)S(1)} %add_add_fusion.9), channel_id=1, source_target_pairs={{0,25},{1,24},{2,27},{3,26},{4,29},{5,28},{6,31},{7,30},{8,17},{9,... | collective-permute-start | bytes 12296 | tf_op jit(solution)/shard_map/ppermute | solution.py:628
  119.6 1.5 collective-permute-done.58
  122.5 4.1 %back_group.1 = (bf16[896,512]{1,0:T(8,128)(2,1)S(1)}, f32[896,512]{1,0:T(8,128)S(1)}, f32[2,512]{1,0:T(2,128)S(1)}) custom-call(f32[896,128]{1,0:T(8,128)S(1)} %mask.1, f32[2,512]{1,0:T(2,128)S(1)} %add_add_fusion.10.total, f32[2,512]{1,0:T(2,128)S(1)} %add_add_fusion.8.sums, f32[3,512]{1,0:T(4,128)S(1)} %add_add_fusion.4.total.first, ...), custom_call_target="tpu_custom_call" | custom-call | tf_op jit(solution)/shard_map/back_group/pallas_call | solution.py:55
  130.9 1.7 weight_group.1.group
  133.5 1.9 %collective-permute-start.70 = (bf16[128,1024]{1,0:T(8,128)(2,1)S(1)}, bf16[128,1024]{1,0:T(8,128)(2,1)S(1)}, u32[]{:S(2)}, u32[]{:S(2)}) collective-permute-start(bf16[128,1024]{1,0:T(8,128)(2,1)S(1)} %get-tuple-element.322), channel_id=1, source_target_pairs={{0,24},{2,10},{4,28},{6,14},{8,0},{10,18},{12,4},{14,22},{16,8},{1... | collective-permute-start | bytes 786440 | tf_op jit(solution)/shard_map/ppermute | solution.py:638
  135.4 2.2 %collective-permute-start.67 = (f32[2,512]{1,0:T(2,128)S(1)}, f32[2,512]{1,0:T(2,128)S(1)}, u32[]{:S(2)}, u32[]{:S(2)}) collective-permute-start(f32[2,512]{1,0:T(2,128)S(1)} %add_add_fusion.7), channel_id=1, source_target_pairs={{0,25},{1,24},{2,27},{3,26},{4,29},{5,28},{6,31},{7,30},{8,17},{9,... | collective-permute-start | bytes 12296 | tf_op jit(solution)/shard_map/ppermute | solution.py:628
  137.9 3.4 %collective-permute-done.68 = f32[2,512]{1,0:T(2,128)S(1)} collective-permute-done((f32[2,512]{1,0:T(2,128)S(1)}, f32[2,512]{1,0:T(2,128)S(1)}, u32[]{:S(2)}, u32[]{:S(2)}) %collective-permute-start.68) | collective-permute-done | bytes 4128 | tf_op jit(solution)/shard_map/ppermute | solution.py:628
  142.9 1.2 back_reduce.1
  144.1 1.9 %collective-permute-start.71 = (bf16[304,512]{1,0:T(8,128)(2,1)S(1)}, bf16[304,512]{1,0:T(8,128)(2,1)S(1)}, u32[]{:S(2)}, u32[]{:S(2)}) collective-permute-start(bf16[304,512]{1,0:T(8,128)(2,1)S(1)} %get-tuple-element.329), channel_id=1, source_target_pairs={{0,2},{2,0},{1,3},{3,1},{4,6},{6,4},{5,7},{7,5},{8,10},{10,8},{9,1... | collective-permute-start | bytes 933896 | tf_op jit(solution)/shard_map/ppermute | solution.py:620
  146.2 1.3 collective-permute-start.74
  147.5 1.2 collective-permute-start.72
  148.7 1.8 block_sum.1
  150.6 1.6 back_input.2
  152.8 2.4 %collective-permute-done.72.refs_0_ = bf16[128,1024]{1,0:T(8,128)(2,1)S(1)} collective-permute-done((bf16[128,1024]{1,0:T(8,128)(2,1)S(1)}, bf16[128,1024]{1,0:T(8,128)(2,1)S(1)}, u32[]{:S(2)}, u32[]{:S(2)}) %collective-permute-start.72) | collective-permute-done | bytes 262176 | tf_op jit(solution)/shard_map/ppermute | solution.py:638
  156.1 2.4 %collective-permute-start.75 = (bf16[304,512]{1,0:T(8,128)(2,1)S(1)}, bf16[304,512]{1,0:T(8,128)(2,1)S(1)}, u32[]{:S(2)}, u32[]{:S(2)}) collective-permute-start(bf16[304,512]{1,0:T(8,128)(2,1)S(1)} %get-tuple-element.342), channel_id=1, source_target_pairs={{0,2},{2,0},{1,3},{3,1},{4,6},{6,4},{5,7},{7,5},{8,10},{10,8},{9,1... | collective-permute-start | bytes 933896 | tf_op jit(solution)/shard_map/ppermute | solution.py:620
  159.0 1.4 collective-permute-start.77
  161.0 2.8 %copy.36 = bf16[2,14,14,2048]{3,0,2,1:T(2,128)(2,1)} copy(bf16[2,14,14,2048]{3,2,1,0:T(8,128)(2,1)S(1)} %image.1) | data formatting | bytes 3211264 | tf_op jit(solution)/shard_map/image/pallas_call | solution.py:55
  163.8 2.3 %collective-permute-done.75.refs_2_ = bf16[304,512]{1,0:T(8,128)(2,1)S(1)} collective-permute-done((bf16[304,512]{1,0:T(8,128)(2,1)S(1)}, bf16[304,512]{1,0:T(8,128)(2,1)S(1)}, u32[]{:S(2)}, u32[]{:S(2)}) %collective-permute-start.75) | collective-permute-done | bytes 311328 | tf_op jit(solution)/shard_map/ppermute | solution.py:620
  166.1 1.5 collective-permute-done.78.refs_4_
  167.9 3.3 %collective-permute-start.79 = (bf16[304,512]{1,0:T(8,128)(2,1)S(1)}, bf16[304,512]{1,0:T(8,128)(2,1)S(1)}, u32[]{:S(2)}, u32[]{:S(2)}) collective-permute-start(bf16[304,512]{1,0:T(8,128)(2,1)S(1)} %get-tuple-element.353), channel_id=1, source_target_pairs={{0,24},{2,10},{4,28},{6,14},{8,0},{10,18},{12,4},{14,22},{16,8},{1... | collective-permute-start | bytes 933896 | tf_op jit(solution)/shard_map/ppermute | solution.py:638
  172.5 2.0 %back_input.3 = bf16[2,14,14,2048]{3,2,1,0:T(8,128)(2,1)S(1)} custom-call(bf16[896,512]{1,0:T(8,128)(2,1)S(1)} %get-tuple-element.354.flat, f32[896,1024]{1,0:T(8,128)S(1)} %get-tuple-element.280.grad, bf16[304,512]{1,0:T(8,128)(2,1)S(1)} %copy-done.2, bf16[304,512]{1,0:T(8,128)(2,1)S(1)} %collective-permute-done.refs_1_, ...), custom_call_target="tpu_custom_call" | custom-call | tf_op jit(solution)/shard_map/back_input/pallas_call | solution.py:55
  174.4 2.8 %copy.35 = bf16[2,14,14,2048]{3,0,2,1:T(2,128)(2,1)} copy(bf16[2,14,14,2048]{3,2,1,0:T(8,128)(2,1)S(1)} %back_input.3) | data formatting | bytes 3211264 | tf_op jit(solution)/shard_map/back_input/pallas_call | solution.py:55
  177.3 1.8 collective-permute-done.81.mine_x
  182.9 3.2 %collective-permute-done.83.mine_x = bf16[304,512]{1,0:T(8,128)(2,1)S(1)} collective-permute-done((bf16[304,512]{1,0:T(8,128)(2,1)S(1)}, bf16[304,512]{1,0:T(8,128)(2,1)S(1)}, u32[]{:S(2)}, u32[]{:S(2)}) %collective-permute-start.83) | collective-permute-done | bytes 311328 | tf_op jit(solution)/shard_map/ppermute | solution.py:620
  186.1 1.6 collective-permute-done.87.other_x
  (180 shorter events, 52.5 us)
Async XLA Ops:
  0.7 11.7 %collective-permute-start.2 = (bf16[2,14,14,2048]{3,0,2,1:T(2,128)(2,1)}, bf16[2,14,14,2048]{3,0,2,1:T(2,128)(2,1)}, u32[]{:S(2)}, u32[]{:S(2)}) collective-permute-start(bf16[2,14,14,2048]{3,0,2,1:T(2,128)(2,1)} %param.12), channel_id=1, source_target_pairs={{0,1},{1,0},{2,3},{3,2},{4,5},{5,4},{6,7},{7,6},{8,9},{9,8},{10,11... | collective-permute-start | bytes 4816904 | tf_op jit(solution)/shard_map/ppermute | solution.py:615
  3.1 11.7 %collective-permute-start.1 = (bf16[304,512]{1,0:T(8,128)(2,1)}, bf16[304,512]{1,0:T(8,128)(2,1)S(1)}, u32[]{:S(2)}, u32[]{:S(2)}) collective-permute-start(bf16[304,512]{1,0:T(8,128)(2,1)} %pack.1.refs_0_), channel_id=1, source_target_pairs={{0,4},{4,0},{8,12},{12,8},{16,20},{20,16},{24,28},{28,24},{1,5},{5... | collective-permute-start | bytes 933896 | tf_op jit(solution)/shard_map/ppermute | solution.py:642
  5.7 11.5 %collective-permute-start = (bf16[304,512]{1,0:T(8,128)(2,1)}, bf16[304,512]{1,0:T(8,128)(2,1)S(1)}, u32[]{:S(2)}, u32[]{:S(2)}) collective-permute-start(bf16[304,512]{1,0:T(8,128)(2,1)} %pack.1.refs_0_), channel_id=1, source_target_pairs={{0,8},{2,26},{4,12},{6,30},{8,16},{10,2},{12,20},{14,6},{16,24},{1... | collective-permute-start | bytes 933896 | tf_op jit(solution)/shard_map/ppermute | solution.py:638
  17.2 8.7 %collective-permute-start.5 = (bf16[304,512]{1,0:T(8,128)(2,1)S(1)}, bf16[304,512]{1,0:T(8,128)(2,1)S(1)}, u32[]{:S(2)}, u32[]{:S(2)}) collective-permute-start(bf16[304,512]{1,0:T(8,128)(2,1)S(1)} %collective-permute-done.refs_1_), channel_id=1, source_target_pairs={{0,4},{4,0},{8,12},{12,8},{16,20},{20,16},{24,28},{28,24},{1,5},{5... | collective-permute-start | bytes 933896 | tf_op jit(solution)/shard_map/ppermute | solution.py:642
  17.8 8.7 %collective-permute-start.4 = (bf16[304,512]{1,0:T(8,128)(2,1)S(1)}, bf16[304,512]{1,0:T(8,128)(2,1)S(1)}, u32[]{:S(2)}, u32[]{:S(2)}) collective-permute-start(bf16[304,512]{1,0:T(8,128)(2,1)S(1)} %collective-permute-done.refs_1_), channel_id=1, source_target_pairs={{0,2},{2,0},{1,3},{3,1},{4,6},{6,4},{5,7},{7,5},{8,10},{10,8},{9,1... | collective-permute-start | bytes 933896 | tf_op jit(solution)/shard_map/ppermute | solution.py:620
  18.9 12.1 %collective-permute-start.3 = (bf16[304,512]{1,0:T(8,128)(2,1)S(1)}, bf16[304,512]{1,0:T(8,128)(2,1)S(1)}, u32[]{:S(2)}, u32[]{:S(2)}) collective-permute-start(bf16[304,512]{1,0:T(8,128)(2,1)S(1)} %collective-permute-done.refs_1_), channel_id=1, source_target_pairs={{0,8},{2,26},{4,12},{6,30},{8,16},{10,2},{12,20},{14,6},{16,24},{1... | collective-permute-start | bytes 933896 | tf_op jit(solution)/shard_map/ppermute | solution.py:638
  18.9 16.0 %collective-permute-start.13 = (bf16[128,1024]{1,0:T(8,128)(2,1)S(1)}, bf16[128,1024]{1,0:T(8,128)(2,1)S(1)}, u32[]{:S(2)}, u32[]{:S(2)}) collective-permute-start(bf16[128,1024]{1,0:T(8,128)(2,1)S(1)} %constant_dynamic-slice_fusion.refs_0_), channel_id=1, source_target_pairs={{0,8},{2,26},{4,12},{6,30},{8,16},{10,2},{12,20},{14,6},{16,24},{1... | collective-permute-start | bytes 786440 | tf_op jit(solution)/shard_map/ppermute | solution.py:638
  31.0 8.8 %collective-permute-start.8 = (bf16[304,512]{1,0:T(8,128)(2,1)S(1)}, bf16[304,512]{1,0:T(8,128)(2,1)S(1)}, u32[]{:S(2)}, u32[]{:S(2)}) collective-permute-start(bf16[304,512]{1,0:T(8,128)(2,1)S(1)} %collective-permute-done.3.refs_3_), channel_id=1, source_target_pairs={{0,4},{4,0},{8,12},{12,8},{16,20},{20,16},{24,28},{28,24},{1,5},{5... | collective-permute-start | bytes 933896 | tf_op jit(solution)/shard_map/ppermute | solution.py:642
  32.5 7.2 %collective-permute-start.7 = (bf16[304,512]{1,0:T(8,128)(2,1)S(1)}, bf16[304,512]{1,0:T(8,128)(2,1)S(1)}, u32[]{:S(2)}, u32[]{:S(2)}) collective-permute-start(bf16[304,512]{1,0:T(8,128)(2,1)S(1)} %collective-permute-done.5.refs_5_), channel_id=1, source_target_pairs={{0,2},{2,0},{1,3},{3,1},{4,6},{6,4},{5,7},{7,5},{8,10},{10,8},{9,1... | collective-permute-start | bytes 933896 | tf_op jit(solution)/shard_map/ppermute | solution.py:620
  32.5 14.5 %collective-permute-start.15 = (bf16[128,1024]{1,0:T(8,128)(2,1)S(1)}, bf16[128,1024]{1,0:T(8,128)(2,1)S(1)}, u32[]{:S(2)}, u32[]{:S(2)}) collective-permute-start(bf16[128,1024]{1,0:T(8,128)(2,1)S(1)} %constant_dynamic-slice_fusion.refs_0_), channel_id=1, source_target_pairs={{0,4},{4,0},{8,12},{12,8},{16,20},{20,16},{24,28},{28,24},{1,5},{5... | collective-permute-start | bytes 786440 | tf_op jit(solution)/shard_map/ppermute | solution.py:642
  34.9 12.1 %collective-permute-start.14 = (bf16[128,1024]{1,0:T(8,128)(2,1)S(1)}, bf16[128,1024]{1,0:T(8,128)(2,1)S(1)}, u32[]{:S(2)}, u32[]{:S(2)}) collective-permute-start(bf16[128,1024]{1,0:T(8,128)(2,1)S(1)} %collective-permute-done.13.refs_1_), channel_id=1, source_target_pairs={{0,8},{2,26},{4,12},{6,30},{8,16},{10,2},{12,20},{14,6},{16,24},{1... | collective-permute-start | bytes 786440 | tf_op jit(solution)/shard_map/ppermute | solution.py:638
  41.1 4.0 %collective-permute-start.12 = (f32[3,512]{1,0:T(4,128)S(1)}, f32[3,512]{1,0:T(4,128)S(1)}, u32[]{:S(2)}, u32[]{:S(2)}) collective-permute-start(f32[3,512]{1,0:T(4,128)S(1)} %get-tuple-element.205), channel_id=1, source_target_pairs={{0,7},{1,6},{2,5},{3,4},{4,3},{5,2},{6,1},{7,0},{8,15},{9,14},{10,... | collective-permute-start | bytes 18440 | tf_op jit(solution)/shard_map/ppermute | solution.py:628
  41.2 4.9 %collective-permute-start.11 = (f32[3,512]{1,0:T(4,128)S(1)}, f32[3,512]{1,0:T(4,128)S(1)}, u32[]{:S(2)}, u32[]{:S(2)}) collective-permute-start(f32[3,512]{1,0:T(4,128)S(1)} %get-tuple-element.205), channel_id=1, source_target_pairs={{0,5},{1,4},{2,7},{3,6},{4,1},{5,0},{6,3},{7,2},{8,13},{9,12},{10,... | collective-permute-start | bytes 18440 | tf_op jit(solution)/shard_map/ppermute | solution.py:628
  43.9 3.1 %collective-permute-start.10 = (f32[3,512]{1,0:T(4,128)S(1)}, f32[3,512]{1,0:T(4,128)S(1)}, u32[]{:S(2)}, u32[]{:S(2)}) collective-permute-start(f32[3,512]{1,0:T(4,128)S(1)} %get-tuple-element.205), channel_id=1, source_target_pairs={{0,3},{1,2},{2,1},{3,0},{4,7},{5,6},{6,5},{7,4},{8,11},{9,10},{10,... | collective-permute-start | bytes 18440 | tf_op jit(solution)/shard_map/ppermute | solution.py:628
  47.1 8.4 %collective-permute-start.25 = (bf16[128,1024]{1,0:T(8,128)(2,1)S(1)}, bf16[128,1024]{1,0:T(8,128)(2,1)S(1)}, u32[]{:S(2)}, u32[]{:S(2)}) collective-permute-start(bf16[128,1024]{1,0:T(8,128)(2,1)S(1)} %collective-permute-done.13.refs_1_), channel_id=1, source_target_pairs={{0,4},{4,0},{8,12},{12,8},{16,20},{20,16},{24,28},{28,24},{1,5},{5... | collective-permute-start | bytes 786440 | tf_op jit(solution)/shard_map/ppermute | solution.py:642
  48.6 4.0 %collective-permute-start.19 = (f32[3,512]{1,0:T(4,128)S(1)}, f32[3,512]{1,0:T(4,128)S(1)}, u32[]{:S(2)}, u32[]{:S(2)}) collective-permute-start(f32[3,512]{1,0:T(4,128)S(1)} %add_add_fusion.5), channel_id=1, source_target_pairs={{0,17},{1,16},{2,19},{3,18},{4,21},{5,20},{6,23},{7,22},{8,25},{9,... | collective-permute-start | bytes 18440 | tf_op jit(solution)/shard_map/ppermute | solution.py:628
  48.6 11.3 %collective-permute-start.20 = (bf16[128,1024]{1,0:T(8,128)(2,1)S(1)}, bf16[128,1024]{1,0:T(8,128)(2,1)S(1)}, u32[]{:S(2)}, u32[]{:S(2)}) collective-permute-start(bf16[128,1024]{1,0:T(8,128)(2,1)S(1)} %collective-permute-done.13.refs_1_), channel_id=1, source_target_pairs={{0,2},{2,0},{1,3},{3,1},{4,6},{6,4},{5,7},{7,5},{8,10},{10,8},{9,1... | collective-permute-start | bytes 786440 | tf_op jit(solution)/shard_map/ppermute | solution.py:620
  49.5 5.0 %collective-permute-start.18 = (f32[3,512]{1,0:T(4,128)S(1)}, f32[3,512]{1,0:T(4,128)S(1)}, u32[]{:S(2)}, u32[]{:S(2)}) collective-permute-start(f32[3,512]{1,0:T(4,128)S(1)} %add_add_fusion.5), channel_id=1, source_target_pairs={{0,25},{1,24},{2,27},{3,26},{4,29},{5,28},{6,31},{7,30},{8,17},{9,... | collective-permute-start | bytes 18440 | tf_op jit(solution)/shard_map/ppermute | solution.py:628
  50.6 3.9 %collective-permute-start.17 = (f32[3,512]{1,0:T(4,128)S(1)}, f32[3,512]{1,0:T(4,128)S(1)}, u32[]{:S(2)}, u32[]{:S(2)}) collective-permute-start(f32[3,512]{1,0:T(4,128)S(1)} %add_add_fusion.5), channel_id=1, source_target_pairs={{0,9},{1,8},{2,11},{3,10},{4,13},{5,12},{6,15},{7,14},{8,1},{9,0},... | collective-permute-start | bytes 18440 | tf_op jit(solution)/shard_map/ppermute | solution.py:628
  54.5 11.5 %collective-permute-start.27 = (bf16[128,1024]{1,0:T(8,128)(2,1)S(1)}, bf16[128,1024]{1,0:T(8,128)(2,1)S(1)}, u32[]{:S(2)}, u32[]{:S(2)}) collective-permute-start(bf16[128,1024]{1,0:T(8,128)(2,1)S(1)} %collective-permute-done.14.refs_3_), channel_id=1, source_target_pairs={{0,4},{4,0},{8,12},{12,8},{16,20},{20,16},{24,28},{28,24},{1,5},{5... | collective-permute-start | bytes 786440 | tf_op jit(solution)/shard_map/ppermute | solution.py:642
  55.5 10.5 %collective-permute-start.26 = (bf16[128,1024]{1,0:T(8,128)(2,1)S(1)}, bf16[128,1024]{1,0:T(8,128)(2,1)S(1)}, u32[]{:S(2)}, u32[]{:S(2)}) collective-permute-start(bf16[128,1024]{1,0:T(8,128)(2,1)S(1)} %collective-permute-done.25.refs_5_), channel_id=1, source_target_pairs={{0,2},{2,0},{1,3},{3,1},{4,6},{6,4},{5,7},{7,5},{8,10},{10,8},{9,1... | collective-permute-start | bytes 786440 | tf_op jit(solution)/shard_map/ppermute | solution.py:620
  59.9 4.0 %collective-permute-start.24 = (f32[2,512]{1,0:T(2,128)S(1)}, f32[2,512]{1,0:T(2,128)S(1)}, u32[]{:S(2)}, u32[]{:S(2)}) collective-permute-start(f32[2,512]{1,0:T(2,128)S(1)} %get-tuple-element.228), channel_id=1, source_target_pairs={{0,17},{1,16},{2,19},{3,18},{4,21},{5,20},{6,23},{7,22},{8,25},{9,... | collective-permute-start | bytes 12296 | tf_op jit(solution)/shard_map/ppermute | solution.py:628
  60.4 4.8 %collective-permute-start.23 = (f32[2,512]{1,0:T(2,128)S(1)}, f32[2,512]{1,0:T(2,128)S(1)}, u32[]{:S(2)}, u32[]{:S(2)}) collective-permute-start(f32[2,512]{1,0:T(2,128)S(1)} %get-tuple-element.228), channel_id=1, source_target_pairs={{0,25},{1,24},{2,27},{3,26},{4,29},{5,28},{6,31},{7,30},{8,17},{9,... | collective-permute-start | bytes 12296 | tf_op jit(solution)/shard_map/ppermute | solution.py:628
  66.0 4.0 %collective-permute-start.31 = (f32[2,512]{1,0:T(2,128)S(1)}, f32[2,512]{1,0:T(2,128)S(1)}, u32[]{:S(2)}, u32[]{:S(2)}) collective-permute-start(f32[2,512]{1,0:T(2,128)S(1)} %add_add_fusion.11), channel_id=1, source_target_pairs={{0,7},{1,6},{2,5},{3,4},{4,3},{5,2},{6,1},{7,0},{8,15},{9,14},{10,... | collective-permute-start | bytes 12296 | tf_op jit(solution)/shard_map/ppermute | solution.py:628
  73.1 9.0 %collective-permute-start.37 = (bf16[448,1024]{1,0:T(8,128)(2,1)S(1)}, bf16[448,1024]{1,0:T(8,128)(2,1)S(1)}, u32[]{:S(2)}, u32[]{:S(2)}) collective-permute-start(bf16[448,1024]{1,0:T(8,128)(2,1)S(1)} %far_half.1), channel_id=1, source_target_pairs={{0,1},{1,0},{2,3},{3,2},{4,5},{5,4},{6,7},{7,6},{8,9},{9,8},{10,11... | collective-permute-start | bytes 2752520 | tf_op jit(solution)/shard_map/ppermute | solution.py:615
  76.6 4.0 %collective-permute-start.36 = (f32[2,1024]{1,0:T(2,128)S(1)}, f32[2,1024]{1,0:T(2,128)S(1)}, u32[]{:S(2)}, u32[]{:S(2)}) collective-permute-start(f32[2,1024]{1,0:T(2,128)S(1)} %get-tuple-element.253), channel_id=1, source_target_pairs={{0,7},{1,6},{2,5},{3,4},{4,3},{5,2},{6,1},{7,0},{8,15},{9,14},{10,... | collective-permute-start | bytes 24584 | tf_op jit(solution)/shard_map/ppermute | solution.py:628
  78.5 3.1 %collective-permute-start.35 = (f32[2,1024]{1,0:T(2,128)S(1)}, f32[2,1024]{1,0:T(2,128)S(1)}, u32[]{:S(2)}, u32[]{:S(2)}) collective-permute-start(f32[2,1024]{1,0:T(2,128)S(1)} %get-tuple-element.253), channel_id=1, source_target_pairs={{0,5},{1,4},{2,7},{3,6},{4,1},{5,0},{6,3},{7,2},{8,13},{9,12},{10,... | collective-permute-start | bytes 24584 | tf_op jit(solution)/shard_map/ppermute | solution.py:628
  82.1 4.1 %collective-permute-start.41 = (f32[2,1024]{1,0:T(2,128)S(1)}, f32[2,1024]{1,0:T(2,128)S(1)}, u32[]{:S(2)}, u32[]{:S(2)}) collective-permute-start(f32[2,1024]{1,0:T(2,128)S(1)} %add_add_fusion.3), channel_id=1, source_target_pairs={{0,17},{1,16},{2,19},{3,18},{4,21},{5,20},{6,23},{7,22},{8,25},{9,... | collective-permute-start | bytes 24584 | tf_op jit(solution)/shard_map/ppermute | solution.py:628
  82.7 4.9 %collective-permute-start.40 = (f32[2,1024]{1,0:T(2,128)S(1)}, f32[2,1024]{1,0:T(2,128)S(1)}, u32[]{:S(2)}, u32[]{:S(2)}) collective-permute-start(f32[2,1024]{1,0:T(2,128)S(1)} %add_add_fusion.3), channel_id=1, source_target_pairs={{0,25},{1,24},{2,27},{3,26},{4,29},{5,28},{6,31},{7,30},{8,17},{9,... | collective-permute-start | bytes 24584 | tf_op jit(solution)/shard_map/ppermute | solution.py:628
  84.5 3.1 %collective-permute-start.39 = (f32[2,1024]{1,0:T(2,128)S(1)}, f32[2,1024]{1,0:T(2,128)S(1)}, u32[]{:S(2)}, u32[]{:S(2)}) collective-permute-start(f32[2,1024]{1,0:T(2,128)S(1)} %add_add_fusion.3), channel_id=1, source_target_pairs={{0,9},{1,8},{2,11},{3,10},{4,13},{5,12},{6,15},{7,14},{8,1},{9,0},... | collective-permute-start | bytes 24584 | tf_op jit(solution)/shard_map/ppermute | solution.py:628
  91.1 5.1 %collective-permute-start.45 = (f32[2,1024]{1,0:T(2,128)S(1)}, f32[2,1024]{1,0:T(2,128)S(1)}, u32[]{:S(2)}, u32[]{:S(2)}) collective-permute-start(f32[2,1024]{1,0:T(2,128)S(1)} %get-tuple-element.268), channel_id=1, source_target_pairs={{0,7},{1,6},{2,5},{3,4},{4,3},{5,2},{6,1},{7,0},{8,15},{9,14},{10,... | collective-permute-start | bytes 24584 | tf_op jit(solution)/shard_map/ppermute | solution.py:628
  92.7 3.5 %collective-permute-start.44 = (f32[2,1024]{1,0:T(2,128)S(1)}, f32[2,1024]{1,0:T(2,128)S(1)}, u32[]{:S(2)}, u32[]{:S(2)}) collective-permute-start(f32[2,1024]{1,0:T(2,128)S(1)} %get-tuple-element.268), channel_id=1, source_target_pairs={{0,5},{1,4},{2,7},{3,6},{4,1},{5,0},{6,3},{7,2},{8,13},{9,12},{10,... | collective-permute-start | bytes 24584 | tf_op jit(solution)/shard_map/ppermute | solution.py:628
  96.5 4.0 %collective-permute-start.49 = (f32[2,1024]{1,0:T(2,128)S(1)}, f32[2,1024]{1,0:T(2,128)S(1)}, u32[]{:S(2)}, u32[]{:S(2)}) collective-permute-start(f32[2,1024]{1,0:T(2,128)S(1)} %add_add_fusion.1), channel_id=1, source_target_pairs={{0,17},{1,16},{2,19},{3,18},{4,21},{5,20},{6,23},{7,22},{8,25},{9,... | collective-permute-start | bytes 24584 | tf_op jit(solution)/shard_map/ppermute | solution.py:628
  97.5 5.0 %collective-permute-start.48 = (f32[2,1024]{1,0:T(2,128)S(1)}, f32[2,1024]{1,0:T(2,128)S(1)}, u32[]{:S(2)}, u32[]{:S(2)}) collective-permute-start(f32[2,1024]{1,0:T(2,128)S(1)} %add_add_fusion.1), channel_id=1, source_target_pairs={{0,25},{1,24},{2,27},{3,26},{4,29},{5,28},{6,31},{7,30},{8,17},{9,... | collective-permute-start | bytes 24584 | tf_op jit(solution)/shard_map/ppermute | solution.py:628
  99.3 3.2 %collective-permute-start.47 = (f32[2,1024]{1,0:T(2,128)S(1)}, f32[2,1024]{1,0:T(2,128)S(1)}, u32[]{:S(2)}, u32[]{:S(2)}) collective-permute-start(f32[2,1024]{1,0:T(2,128)S(1)} %add_add_fusion.1), channel_id=1, source_target_pairs={{0,9},{1,8},{2,11},{3,10},{4,13},{5,12},{6,15},{7,14},{8,1},{9,0},... | collective-permute-start | bytes 24584 | tf_op jit(solution)/shard_map/ppermute | solution.py:628
  108.6 5.9 %collective-permute-start.54 = (f32[2,512]{1,0:T(2,128)S(1)}, f32[2,512]{1,0:T(2,128)S(1)}, u32[]{:S(2)}, u32[]{:S(2)}) collective-permute-start(f32[2,512]{1,0:T(2,128)S(1)} %get-tuple-element.283), channel_id=1, source_target_pairs={{0,7},{1,6},{2,5},{3,4},{4,3},{5,2},{6,1},{7,0},{8,15},{9,14},{10,... | collective-permute-start | bytes 12296 | tf_op jit(solution)/shard_map/ppermute | solution.py:628
  110.5 4.0 %collective-permute-start.53 = (f32[2,512]{1,0:T(2,128)S(1)}, f32[2,512]{1,0:T(2,128)S(1)}, u32[]{:S(2)}, u32[]{:S(2)}) collective-permute-start(f32[2,512]{1,0:T(2,128)S(1)} %get-tuple-element.283), channel_id=1, source_target_pairs={{0,5},{1,4},{2,7},{3,6},{4,1},{5,0},{6,3},{7,2},{8,13},{9,12},{10,... | collective-permute-start | bytes 12296 | tf_op jit(solution)/shard_map/ppermute | solution.py:628
  111.0 3.5 %collective-permute-start.52 = (f32[2,512]{1,0:T(2,128)S(1)}, f32[2,512]{1,0:T(2,128)S(1)}, u32[]{:S(2)}, u32[]{:S(2)}) collective-permute-start(f32[2,512]{1,0:T(2,128)S(1)} %get-tuple-element.283), channel_id=1, source_target_pairs={{0,3},{1,2},{2,1},{3,0},{4,7},{5,6},{6,5},{7,4},{8,11},{9,10},{10,... | collective-permute-start | bytes 12296 | tf_op jit(solution)/shard_map/ppermute | solution.py:628
  114.5 18.2 %collective-permute-start.63 = (bf16[256,1024]{1,0:T(8,128)(2,1)S(1)}, bf16[256,1024]{1,0:T(8,128)(2,1)S(1)}, u32[]{:S(2)}, u32[]{:S(2)}) collective-permute-start(bf16[256,1024]{1,0:T(8,128)(2,1)S(1)} %get-tuple-element.309), channel_id=1, source_target_pairs={{0,2},{2,0},{1,3},{3,1},{4,6},{6,4},{5,7},{7,5},{8,10},{10,8},{9,1... | collective-permute-start | bytes 1572872 | tf_op jit(solution)/shard_map/ppermute | solution.py:620
  115.7 17.0 %collective-permute-start.64 = (bf16[256,1024]{1,0:T(8,128)(2,1)S(1)}, bf16[256,1024]{1,0:T(8,128)(2,1)S(1)}, u32[]{:S(2)}, u32[]{:S(2)}) collective-permute-start(bf16[256,1024]{1,0:T(8,128)(2,1)S(1)} %get-tuple-element.310), channel_id=1, source_target_pairs={{0,4},{4,0},{8,12},{12,8},{16,20},{20,16},{24,28},{28,24},{1,5},{5... | collective-permute-start | bytes 1572872 | tf_op jit(solution)/shard_map/ppermute | solution.py:642
  117.2 3.9 %collective-permute-start.58 = (f32[2,512]{1,0:T(2,128)S(1)}, f32[2,512]{1,0:T(2,128)S(1)}, u32[]{:S(2)}, u32[]{:S(2)}) collective-permute-start(f32[2,512]{1,0:T(2,128)S(1)} %add_add_fusion.9), channel_id=1, source_target_pairs={{0,17},{1,16},{2,19},{3,18},{4,21},{5,20},{6,23},{7,22},{8,25},{9,... | collective-permute-start | bytes 12296 | tf_op jit(solution)/shard_map/ppermute | solution.py:628
  117.2 4.8 %collective-permute-start.57 = (f32[2,512]{1,0:T(2,128)S(1)}, f32[2,512]{1,0:T(2,128)S(1)}, u32[]{:S(2)}, u32[]{:S(2)}) collective-permute-start(f32[2,512]{1,0:T(2,128)S(1)} %add_add_fusion.9), channel_id=1, source_target_pairs={{0,25},{1,24},{2,27},{3,26},{4,29},{5,28},{6,31},{7,30},{8,17},{9,... | collective-permute-start | bytes 12296 | tf_op jit(solution)/shard_map/ppermute | solution.py:628
  126.6 4.0 %collective-permute-start.62 = (f32[2,512]{1,0:T(2,128)S(1)}, f32[2,512]{1,0:T(2,128)S(1)}, u32[]{:S(2)}, u32[]{:S(2)}) collective-permute-start(f32[2,512]{1,0:T(2,128)S(1)} %get-tuple-element.299), channel_id=1, source_target_pairs={{0,7},{1,6},{2,5},{3,4},{4,3},{5,2},{6,1},{7,0},{8,15},{9,14},{10,... | collective-permute-start | bytes 12296 | tf_op jit(solution)/shard_map/ppermute | solution.py:628
  127.7 5.0 %collective-permute-start.61 = (f32[2,512]{1,0:T(2,128)S(1)}, f32[2,512]{1,0:T(2,128)S(1)}, u32[]{:S(2)}, u32[]{:S(2)}) collective-permute-start(f32[2,512]{1,0:T(2,128)S(1)} %get-tuple-element.299), channel_id=1, source_target_pairs={{0,5},{1,4},{2,7},{3,6},{4,1},{5,0},{6,3},{7,2},{8,13},{9,12},{10,... | collective-permute-start | bytes 12296 | tf_op jit(solution)/shard_map/ppermute | solution.py:628
  128.7 4.0 %collective-permute-start.60 = (f32[2,512]{1,0:T(2,128)S(1)}, f32[2,512]{1,0:T(2,128)S(1)}, u32[]{:S(2)}, u32[]{:S(2)}) collective-permute-start(f32[2,512]{1,0:T(2,128)S(1)} %get-tuple-element.299), channel_id=1, source_target_pairs={{0,3},{1,2},{2,1},{3,0},{4,7},{5,6},{6,5},{7,4},{8,11},{9,10},{10,... | collective-permute-start | bytes 12296 | tf_op jit(solution)/shard_map/ppermute | solution.py:628
  132.9 10.0 %collective-permute-start.69 = (bf16[128,1024]{1,0:T(8,128)(2,1)S(1)}, bf16[128,1024]{1,0:T(8,128)(2,1)S(1)}, u32[]{:S(2)}, u32[]{:S(2)}) collective-permute-start(bf16[128,1024]{1,0:T(8,128)(2,1)S(1)} %get-tuple-element.321), channel_id=1, source_target_pairs={{0,4},{4,0},{8,12},{12,8},{16,20},{20,16},{24,28},{28,24},{1,5},{5... | collective-permute-start | bytes 786440 | tf_op jit(solution)/shard_map/ppermute | solution.py:642
  133.5 9.4 %collective-permute-start.70 = (bf16[128,1024]{1,0:T(8,128)(2,1)S(1)}, bf16[128,1024]{1,0:T(8,128)(2,1)S(1)}, u32[]{:S(2)}, u32[]{:S(2)}) collective-permute-start(bf16[128,1024]{1,0:T(8,128)(2,1)S(1)} %get-tuple-element.322), channel_id=1, source_target_pairs={{0,24},{2,10},{4,28},{6,14},{8,0},{10,18},{12,4},{14,22},{16,8},{1... | collective-permute-start | bytes 786440 | tf_op jit(solution)/shard_map/ppermute | solution.py:638
  135.4 5.9 %collective-permute-start.68 = (f32[2,512]{1,0:T(2,128)S(1)}, f32[2,512]{1,0:T(2,128)S(1)}, u32[]{:S(2)}, u32[]{:S(2)}) collective-permute-start(f32[2,512]{1,0:T(2,128)S(1)} %add_add_fusion.7), channel_id=1, source_target_pairs={{0,17},{1,16},{2,19},{3,18},{4,21},{5,20},{6,23},{7,22},{8,25},{9,... | collective-permute-start | bytes 12296 | tf_op jit(solution)/shard_map/ppermute | solution.py:628
  135.4 6.6 %collective-permute-start.67 = (f32[2,512]{1,0:T(2,128)S(1)}, f32[2,512]{1,0:T(2,128)S(1)}, u32[]{:S(2)}, u32[]{:S(2)}) collective-permute-start(f32[2,512]{1,0:T(2,128)S(1)} %add_add_fusion.7), channel_id=1, source_target_pairs={{0,25},{1,24},{2,27},{3,26},{4,29},{5,28},{6,31},{7,30},{8,17},{9,... | collective-permute-start | bytes 12296 | tf_op jit(solution)/shard_map/ppermute | solution.py:628
  137.6 4.5 %collective-permute-start.66 = (f32[2,512]{1,0:T(2,128)S(1)}, f32[2,512]{1,0:T(2,128)S(1)}, u32[]{:S(2)}, u32[]{:S(2)}) collective-permute-start(f32[2,512]{1,0:T(2,128)S(1)} %add_add_fusion.7), channel_id=1, source_target_pairs={{0,9},{1,8},{2,11},{3,10},{4,13},{5,12},{6,15},{7,14},{8,1},{9,0},... | collective-permute-start | bytes 12296 | tf_op jit(solution)/shard_map/ppermute | solution.py:628
  144.1 11.1 %collective-permute-start.71 = (bf16[304,512]{1,0:T(8,128)(2,1)S(1)}, bf16[304,512]{1,0:T(8,128)(2,1)S(1)}, u32[]{:S(2)}, u32[]{:S(2)}) collective-permute-start(bf16[304,512]{1,0:T(8,128)(2,1)S(1)} %get-tuple-element.329), channel_id=1, source_target_pairs={{0,2},{2,0},{1,3},{3,1},{4,6},{6,4},{5,7},{7,5},{8,10},{10,8},{9,1... | collective-permute-start | bytes 933896 | tf_op jit(solution)/shard_map/ppermute | solution.py:620
  146.2 9.2 %collective-permute-start.74 = (bf16[304,512]{1,0:T(8,128)(2,1)S(1)}, bf16[304,512]{1,0:T(8,128)(2,1)S(1)}, u32[]{:S(2)}, u32[]{:S(2)}) collective-permute-start(bf16[304,512]{1,0:T(8,128)(2,1)S(1)} %get-tuple-element.341), channel_id=1, source_target_pairs={{0,4},{4,0},{8,12},{12,8},{16,20},{20,16},{24,28},{28,24},{1,5},{5... | collective-permute-start | bytes 933896 | tf_op jit(solution)/shard_map/ppermute | solution.py:642
  147.5 7.8 %collective-permute-start.72 = (bf16[128,1024]{1,0:T(8,128)(2,1)S(1)}, bf16[128,1024]{1,0:T(8,128)(2,1)S(1)}, u32[]{:S(2)}, u32[]{:S(2)}) collective-permute-start(bf16[128,1024]{1,0:T(8,128)(2,1)S(1)} %expand_sum.6), channel_id=1, source_target_pairs={{0,24},{2,10},{4,28},{6,14},{8,0},{10,18},{12,4},{14,22},{16,8},{1... | collective-permute-start | bytes 786440 | tf_op jit(solution)/shard_map/ppermute | solution.py:638
  148.6 3.6 %collective-permute-start.73 = (f32[2,2048]{1,0:T(2,128)S(1)}, f32[2,2048]{1,0:T(2,128)S(1)}, u32[]{:S(2)}, u32[]{:S(2)}) collective-permute-start(f32[2,2048]{1,0:T(2,128)S(1)} %pad_maximum_fusion.near), channel_id=1, source_target_pairs={{0,1},{1,0},{2,3},{3,2},{4,5},{5,4},{6,7},{7,6},{8,9},{9,8},{10,11... | collective-permute-start | bytes 49160 | tf_op jit(solution)/shard_map/ppermute | solution.py:615
  155.5 17.0 %collective-permute-start.80 = (bf16[448,2048]{1,0:T(8,128)(2,1)S(1)}, bf16[448,2048]{1,0:T(8,128)(2,1)S(1)}, u32[]{:S(2)}, u32[]{:S(2)}) collective-permute-start(bf16[448,2048]{1,0:T(8,128)(2,1)S(1)} %back_input.2), channel_id=1, source_target_pairs={{0,1},{1,0},{2,3},{3,2},{4,5},{5,4},{6,7},{7,6},{8,9},{9,8},{10,11... | collective-permute-start | bytes 5505032 | tf_op jit(solution)/shard_map/ppermute | solution.py:615
  155.6 5.1 %collective-permute-start.76 = (bf16[448,1024]{1,0:T(8,128)(2,1)S(1)}, bf16[448,1024]{1,0:T(8,128)(2,1)S(1)}, u32[]{:S(2)}, u32[]{:S(2)}) collective-permute-start(bf16[448,1024]{1,0:T(8,128)(2,1)S(1)} %get-tuple-element.345), channel_id=1, source_target_pairs={{0,1},{1,0},{2,3},{3,2},{4,5},{5,4},{6,7},{7,6},{8,9},{9,8},{10,11... | collective-permute-start | bytes 2752520 | tf_op jit(solution)/shard_map/ppermute | solution.py:615
  156.1 10.0 %collective-permute-start.75 = (bf16[304,512]{1,0:T(8,128)(2,1)S(1)}, bf16[304,512]{1,0:T(8,128)(2,1)S(1)}, u32[]{:S(2)}, u32[]{:S(2)}) collective-permute-start(bf16[304,512]{1,0:T(8,128)(2,1)S(1)} %get-tuple-element.342), channel_id=1, source_target_pairs={{0,2},{2,0},{1,3},{3,1},{4,6},{6,4},{5,7},{7,5},{8,10},{10,8},{9,1... | collective-permute-start | bytes 933896 | tf_op jit(solution)/shard_map/ppermute | solution.py:620
  158.5 9.1 %collective-permute-start.78 = (bf16[304,512]{1,0:T(8,128)(2,1)S(1)}, bf16[304,512]{1,0:T(8,128)(2,1)S(1)}, u32[]{:S(2)}, u32[]{:S(2)}) collective-permute-start(bf16[304,512]{1,0:T(8,128)(2,1)S(1)} %get-tuple-element.352), channel_id=1, source_target_pairs={{0,4},{4,0},{8,12},{12,8},{16,20},{20,16},{24,28},{28,24},{1,5},{5... | collective-permute-start | bytes 933896 | tf_op jit(solution)/shard_map/ppermute | solution.py:642
  159.0 8.8 %collective-permute-start.77 = (bf16[304,512]{1,0:T(8,128)(2,1)S(1)}, bf16[304,512]{1,0:T(8,128)(2,1)S(1)}, u32[]{:S(2)}, u32[]{:S(2)}) collective-permute-start(bf16[304,512]{1,0:T(8,128)(2,1)S(1)} %get-tuple-element.346), channel_id=1, source_target_pairs={{0,24},{2,10},{4,28},{6,14},{8,0},{10,18},{12,4},{14,22},{16,8},{1... | collective-permute-start | bytes 933896 | tf_op jit(solution)/shard_map/ppermute | solution.py:638
  167.9 11.1 %collective-permute-start.79 = (bf16[304,512]{1,0:T(8,128)(2,1)S(1)}, bf16[304,512]{1,0:T(8,128)(2,1)S(1)}, u32[]{:S(2)}, u32[]{:S(2)}) collective-permute-start(bf16[304,512]{1,0:T(8,128)(2,1)S(1)} %get-tuple-element.353), channel_id=1, source_target_pairs={{0,24},{2,10},{4,28},{6,14},{8,0},{10,18},{12,4},{14,22},{16,8},{1... | collective-permute-start | bytes 933896 | tf_op jit(solution)/shard_map/ppermute | solution.py:638
  171.2 7.8 %collective-permute-start.82 = (bf16[304,512]{1,0:T(8,128)(2,1)S(1)}, bf16[304,512]{1,0:T(8,128)(2,1)S(1)}, u32[]{:S(2)}, u32[]{:S(2)}) collective-permute-start(bf16[304,512]{1,0:T(8,128)(2,1)S(1)} %get-tuple-element.361), channel_id=1, source_target_pairs={{0,4},{4,0},{8,12},{12,8},{16,20},{20,16},{24,28},{28,24},{1,5},{5... | collective-permute-start | bytes 933896 | tf_op jit(solution)/shard_map/ppermute | solution.py:642
  172.4 6.6 %collective-permute-start.81 = (bf16[128,1024]{1,0:T(8,128)(2,1)S(1)}, bf16[128,1024]{1,0:T(8,128)(2,1)S(1)}, u32[]{:S(2)}, u32[]{:S(2)}) collective-permute-start(bf16[128,1024]{1,0:T(8,128)(2,1)S(1)} %expand_sum.7.mine), channel_id=1, source_target_pairs={{0,2},{2,0},{1,3},{3,1},{4,6},{6,4},{5,7},{7,5},{8,10},{10,8},{9,1... | collective-permute-start | bytes 786440 | tf_op jit(solution)/shard_map/ppermute | solution.py:620
  179.2 7.0 %collective-permute-start.83 = (bf16[304,512]{1,0:T(8,128)(2,1)S(1)}, bf16[304,512]{1,0:T(8,128)(2,1)S(1)}, u32[]{:S(2)}, u32[]{:S(2)}) collective-permute-start(bf16[304,512]{1,0:T(8,128)(2,1)S(1)} %arrived.5.mine), channel_id=1, source_target_pairs={{0,2},{2,0},{1,3},{3,1},{4,6},{6,4},{5,7},{7,5},{8,10},{10,8},{9,1... | collective-permute-start | bytes 933896 | tf_op jit(solution)/shard_map/ppermute | solution.py:620
  180.5 5.7 %collective-permute-start.86 = (bf16[304,512]{1,0:T(8,128)(2,1)S(1)}, bf16[304,512]{1,0:T(8,128)(2,1)S(1)}, u32[]{:S(2)}, u32[]{:S(2)}) collective-permute-start(bf16[304,512]{1,0:T(8,128)(2,1)S(1)} %arrived.5.mine), channel_id=1, source_target_pairs={{0,1},{1,0},{2,3},{3,2},{4,5},{5,4},{6,7},{7,6},{8,9},{9,8},{10,11... | collective-permute-start | bytes 933896 | tf_op jit(solution)/shard_map/ppermute | solution.py:615
  (29 other events, 115.6 us)

commit v9 on v8

--- a/solution.py
+++ b/solution.py
@@ -313,7 +313,13 @@
         out[rows_of(block_owner(slot), depth), :] = block[...]
 
 
-def expand_kernel(mask, act_mine, act_far, weight, act, expanded, stats):
+def expand_near_kernel(act_mine, weight, out):
+    rows, half = act_mine.shape
+    for at in range(0, weight.shape[1], BLOCK):
+        out[:, at : at + BLOCK] = dot(act_mine[...], weight[part_at(0, half), at : at + BLOCK])
+
+
+def expand_kernel(mask, act_mine, act_far, weight, near, act, expanded, stats):
     rows, half = act_mine.shape
     middle = rows // 2
     act[:, part_at(0, half)] = act_mine[...]
@@ -323,7 +329,7 @@
         sums = [0.0, 0.0]
         for begin in (0, middle):
             here = slice(begin, begin + middle)
-            value = dot(act[here, :], weight[:, at : at + BLOCK])
+            value = near[here, at : at + BLOCK] + dot(act[here, part_at(1, half)], weight[part_at(1, half), at : at + BLOCK])
             expanded[here, at : at + BLOCK] = value
             masked = value * across_lanes(mask[here, :], BLOCK)
             sums = [sums[0] + column_sums(masked), sums[1] + column_sums(masked * value)]
@@ -793,10 +799,14 @@
         (weight_three,) = call(assemble_kernel, [shape((width, half_out), BF16)], blocks, name="assemble")
     else:
         weight_three = lax.all_gather(expand_own, "fsdp", axis=0, tiled=True)
+    (near,) = call(
+        expand_near_kernel, [shape((pixels, half_out), F32)], [act_mine, weight_three], name="expand_near",
+        flops=rows * width * channels,
+    )
     act_two, expanded, part = call(
         expand_kernel,
         [shape((pixels, width), BF16), shape((pixels, half_out), F32), shape((2, half_out), F32)],
-        [mask, act_mine, act_far, weight_three],
+        [mask, act_mine, act_far, weight_three, near],
         name="expand", flops=2 * rows * width * channels,
     )
     cot = padded(after(cotangent, grouped))

time: 189 us -> 189 us (level)
    pallas_call x33 -> x34, Pallas kernels: 42 us -> 42.5 us  [call(): pl.pallas_call(kernel, out_shape=outs, in_specs=[sm] * scalars + [given]...]
  transfers between devices with their start and end apart: 88 -> 88, of which waited for: 46 -> 45; matrix products, arithmetic and copies ran while one was open for 7% -> 8% of each run, Pallas kernels for 17% -> 17%
where the time goes in v9:
time: 189 us
  starting transfers between devices  73.4 us (39%)
  waiting for transfers between devices  57.2 us (30%)
  Pallas kernels  42.5 us (22%)
  local copies, waits for them, and re-layouts  14.1 us (7%)
    pallas_call x34, Pallas kernels, call(): pl.pallas_call(kernel, out_shape=outs, in_specs=[sm] * scalars + [given]...  42.5 us
    ppermute x48, starting transfers between devices, sum_chips(): got.append(lax.ppermute(values, (*CHIPS, 'core'), pairs))  38.2 us
    ppermute x48, waiting for transfers between devices, sum_chips(): got.append(lax.ppermute(values, (*CHIPS, 'core'), pairs))  24.1 us
    ppermute x11, starting transfers between devices, across(): return lax.ppermute(values, 'fsdp', [(f, f ^ 1) for f in range(8)])  12.2 us
    ppermute x8, waiting for transfers between devices, along(): return lax.ppermute(values, CHIPS, pairs)  11.6 us
    ppermute x8, starting transfers between devices, along(): return lax.ppermute(values, CHIPS, pairs)  11 us
    ppermute x9, starting transfers between devices, swap_x(): return lax.ppermute(values, 'x', SWAP)  9.38 us
    ppermute x11, waiting for transfers between devices, across(): return lax.ppermute(values, 'fsdp', [(f, f ^ 1) for f in range(8)])  8.46 us
  transfers between devices with their start and end apart: 88, of which 45 were waited for; matrix products, arithmetic and copies ran while one was open for 8% of the time, Pallas kernels for 17%

profile of v9, /device:TPU:0, one launch (start us, length us, event | category | flops | bytes accessed | tf_op | source)
XLA Modules:
  0.0 188.6 jit_solution(10440815465904600234)
XLA Ops:
  1.2 1.9 pack.1.refs_0_
  3.1 2.6 %collective-permute-start.1 = (bf16[304,512]{1,0:T(8,128)(2,1)}, bf16[304,512]{1,0:T(8,128)(2,1)S(1)}, u32[]{:S(2)}, u32[]{:S(2)}) collective-permute-start(bf16[304,512]{1,0:T(8,128)(2,1)} %pack.1.refs_0_), channel_id=1, source_target_pairs={{0,4},{4,0},{8,12},{12,8},{16,20},{20,16},{24,28},{28,24},{1,5},{5... | collective-permute-start | bytes 933896 | tf_op jit(solution)/shard_map/ppermute | solution.py:648
  5.7 1.6 collective-permute-start
  7.3 3.3 %copy.30 = bf16[2,14,14,2048]{3,2,1,0:T(8,128)(2,1)} copy(bf16[2,14,14,2048]{3,0,2,1:T(2,128)(2,1)} %param.12) | data formatting | bytes 3211264
  10.6 1.7 pad.10.clone
  12.4 2.1 %copy.31 = bf16[2,14,14,2048]{3,2,1,0:T(8,128)(2,1)S(1)} copy(bf16[2,14,14,2048]{3,0,2,1:T(2,128)(2,1)} %collective-permute-done.2) | data formatting | bytes 3211264
  14.8 2.4 %collective-permute-done.refs_1_ = bf16[304,512]{1,0:T(8,128)(2,1)S(1)} collective-permute-done((bf16[304,512]{1,0:T(8,128)(2,1)}, bf16[304,512]{1,0:T(8,128)(2,1)S(1)}, u32[]{:S(2)}, u32[]{:S(2)}) %collective-permute-start) | collective-permute-done | bytes 311328 | tf_op jit(solution)/shard_map/ppermute | solution.py:644
  17.8 1.2 collective-permute-start.4
  18.9 1.6 collective-permute-start.13
  21.6 4.3 %collective-permute-done.5.refs_5_ = bf16[304,512]{1,0:T(8,128)(2,1)S(1)} collective-permute-done((bf16[304,512]{1,0:T(8,128)(2,1)S(1)}, bf16[304,512]{1,0:T(8,128)(2,1)S(1)}, u32[]{:S(2)}, u32[]{:S(2)}) %collective-permute-start.5) | collective-permute-done | bytes 311328 | tf_op jit(solution)/shard_map/ppermute | solution.py:648
  26.4 4.6 %collective-permute-done.3.refs_3_ = bf16[304,512]{1,0:T(8,128)(2,1)S(1)} collective-permute-done((bf16[304,512]{1,0:T(8,128)(2,1)S(1)}, bf16[304,512]{1,0:T(8,128)(2,1)S(1)}, u32[]{:S(2)}, u32[]{:S(2)}) %collective-permute-start.3) | collective-permute-done | bytes 311328 | tf_op jit(solution)/shard_map/ppermute | solution.py:644
  31.0 1.5 collective-permute-start.8
  33.1 1.9 collective-permute-done.13.refs_1_
  35.6 2.1 %reduce.2.refs_2_ = f32[896,512]{1,0:T(8,128)S(1)} custom-call(s32[4]{0:T(128)S(1)} %pad_add_fusion.valid, f32[896,128]{1,0:T(8,128)S(1)} %mask.1, bf16[448,2048]{1,0:T(8,128)(2,1)S(1)} %bitcast.17, bf16[448,2048]{1,0:T(8,128)(2,1)S(1)} %bitcast.21, bf16[304,512]{1,0:T(8,128)(2,1)S(1)} %copy-done.2, bf16[304,512]{1,0:T(8,128)(2,1)S(1)} %collective-permute-done.refs_1_, ...), custom_call_target="tpu_custom_call" | custom-call | tf_op jit(solution)/shard_map/reduce/pallas_call | solution.py:55
  37.7 2.0 %collective-permute-done.8.refs_1_.refs_7_ = bf16[304,512]{1,0:T(8,128)(2,1)S(1)} collective-permute-done((bf16[304,512]{1,0:T(8,128)(2,1)S(1)}, bf16[304,512]{1,0:T(8,128)(2,1)S(1)}, u32[]{:S(2)}, u32[]{:S(2)}) %collective-permute-start.8) | collective-permute-done | bytes 311328 | tf_op jit(solution)/shard_map/ppermute | solution.py:648
  39.8 1.4 reduce.3
  41.2 2.7 %collective-permute-start.11 = (f32[3,512]{1,0:T(4,128)S(1)}, f32[3,512]{1,0:T(4,128)S(1)}, u32[]{:S(2)}, u32[]{:S(2)}) collective-permute-start(f32[3,512]{1,0:T(4,128)S(1)} %get-tuple-element.205), channel_id=1, source_target_pairs={{0,5},{1,4},{2,7},{3,6},{4,1},{5,0},{6,3},{7,2},{8,13},{9,12},{10,... | collective-permute-start | bytes 18440 | tf_op jit(solution)/shard_map/ppermute | solution.py:634
  47.1 1.6 collective-permute-start.25
  50.6 1.7 collective-permute-start.17
  52.6 1.9 collective-permute-done.18
  56.4 3.5 %group.3 = (bf16[3,4,256,512]{3,2,1,0:T(8,128)(2,1)S(1)}, f32[896,512]{1,0:T(8,128)S(1)}, f32[2,512]{1,0:T(2,128)S(1)}) custom-call(f32[896,128]{1,0:T(8,128)S(1)} %mask.1, f32[3,512]{1,0:T(4,128)S(1)} %add_add_fusion.4.total.first, f32[4,512]{1,0:T(4,128)S(1)} %get-tuple-element.223.vectors, f32[896,512]{1,0:T(8,128)S(1)} %get-tuple-element.224.red, ...), custom_call_target="tpu_custom_call" | custom-call | tf_op jit(solution)/shard_map/group/pallas_call | solution.py:55
  60.4 2.6 %collective-permute-start.23 = (f32[2,512]{1,0:T(2,128)S(1)}, f32[2,512]{1,0:T(2,128)S(1)}, u32[]{:S(2)}, u32[]{:S(2)}) collective-permute-start(f32[2,512]{1,0:T(2,128)S(1)} %get-tuple-element.228), channel_id=1, source_target_pairs={{0,25},{1,24},{2,27},{3,26},{4,29},{5,28},{6,31},{7,30},{8,17},{9,... | collective-permute-start | bytes 12296 | tf_op jit(solution)/shard_map/ppermute | solution.py:634
  63.9 1.3 collective-permute-done.23
  66.0 1.6 collective-permute-start.31
  74.6 1.6 expand.1
  76.3 2.0 %collective-permute-start.36 = (f32[2,1024]{1,0:T(2,128)S(1)}, f32[2,1024]{1,0:T(2,128)S(1)}, u32[]{:S(2)}, u32[]{:S(2)}) collective-permute-start(f32[2,1024]{1,0:T(2,128)S(1)} %get-tuple-element.253), channel_id=1, source_target_pairs={{0,7},{1,6},{2,5},{3,4},{4,3},{5,2},{6,1},{7,0},{8,15},{9,14},{10,... | collective-permute-start | bytes 24584 | tf_op jit(solution)/shard_map/ppermute | solution.py:634
  82.4 1.8 collective-permute-start.40
  85.8 1.4 collective-permute-done.40
  87.4 3.5 %output.1 = (bf16[448,1024]{1,0:T(8,128)(2,1)S(1)}, bf16[448,1024]{1,0:T(8,128)(2,1)S(1)}, f32[896,1024]{1,0:T(8,128)S(1)}, f32[2,1024]{1,0:T(2,128)S(1)}) custom-call(s32[4]{0:T(128)S(1)} %pad_add_fusion.valid, f32[2,1024]{1,0:T(2,128)S(1)} %add_add_fusion.2.total, f32[3,512]{1,0:T(4,128)S(1)} %add_add_fusion.4.total.first, ...), custom_call_target="tpu_custom_call" | custom-call | tf_op jit(solution)/shard_map/output/pallas_call | solution.py:55
  90.8 1.6 collective-permute-start.45
  94.2 1.7 turn.1.turned
  97.2 1.8 collective-permute-start.48
  100.3 1.9 %collective-permute-done.48 = f32[2,1024]{1,0:T(2,128)S(1)} collective-permute-done((f32[2,1024]{1,0:T(2,128)S(1)}, f32[2,1024]{1,0:T(2,128)S(1)}, u32[]{:S(2)}, u32[]{:S(2)}) %collective-permute-start.48) | collective-permute-done | bytes 8224 | tf_op jit(solution)/shard_map/ppermute | solution.py:634
  102.2 2.2 %back_expand.1 = (bf16[896,1024]{1,0:T(8,128)(2,1)S(1)}, bf16[896,512]{1,0:T(8,128)(2,1)S(1)}) custom-call(f32[896,128]{1,0:T(8,128)S(1)} %mask.1, f32[2,1024]{1,0:T(2,128)S(1)} %add_add_fusion.2.total, f32[2,1024]{1,0:T(2,128)S(1)} %add_add_fusion.sums, f32[3,512]{1,0:T(4,128)S(1)} %add_add_fusion.4.total.first, f32[2,1024]{1,0:T(2,128)S(1)} %get-tuple-element.264.vectors, ...), custom_call_target="tpu_custom_call" | custom-call | tf_op jit(solution)/shard_map/back_expand/pallas_call | solution.py:55
  107.0 1.3 back_act.1
  108.3 1.9 collective-permute-start.54
  111.7 2.4 %weight_expand.1.keep = bf16[1024,1024]{1,0:T(8,128)(2,1)S(1)} custom-call(bf16[896,1024]{1,0:T(8,128)(2,1)S(1)} %get-tuple-element.289.act, bf16[896,1024]{1,0:T(8,128)(2,1)S(1)} %get-tuple-element.281.flat), custom_call_target="tpu_custom_call" | custom-call | tf_op jit(solution)/shard_map/weight_expand/pallas_call | solution.py:55
  114.2 1.2 collective-permute-start.63
  115.4 1.5 collective-permute-start.64
  116.9 2.3 %collective-permute-start.57 = (f32[2,512]{1,0:T(2,128)S(1)}, f32[2,512]{1,0:T(2,128)S(1)}, u32[]{:S(2)}, u32[]{:S(2)}) collective-permute-start(f32[2,512]{1,0:T(2,128)S(1)} %add_add_fusion.9), channel_id=1, source_target_pairs={{0,25},{1,24},{2,27},{3,26},{4,29},{5,28},{6,31},{7,30},{8,17},{9,... | collective-permute-start | bytes 12296 | tf_op jit(solution)/shard_map/ppermute | solution.py:634
  119.3 1.5 collective-permute-done.58
  122.2 4.1 %back_group.1 = (bf16[896,512]{1,0:T(8,128)(2,1)S(1)}, f32[896,512]{1,0:T(8,128)S(1)}, f32[2,512]{1,0:T(2,128)S(1)}) custom-call(f32[896,128]{1,0:T(8,128)S(1)} %mask.1, f32[2,512]{1,0:T(2,128)S(1)} %add_add_fusion.10.total, f32[2,512]{1,0:T(2,128)S(1)} %add_add_fusion.8.sums, f32[3,512]{1,0:T(4,128)S(1)} %add_add_fusion.4.total.first, ...), custom_call_target="tpu_custom_call" | custom-call | tf_op jit(solution)/shard_map/back_group/pallas_call | solution.py:55
  130.7 1.7 weight_group.1.group
  133.2 1.9 %collective-permute-start.70 = (bf16[128,1024]{1,0:T(8,128)(2,1)S(1)}, bf16[128,1024]{1,0:T(8,128)(2,1)S(1)}, u32[]{:S(2)}, u32[]{:S(2)}) collective-permute-start(bf16[128,1024]{1,0:T(8,128)(2,1)S(1)} %get-tuple-element.322), channel_id=1, source_target_pairs={{0,24},{2,10},{4,28},{6,14},{8,0},{10,18},{12,4},{14,22},{16,8},{1... | collective-permute-start | bytes 786440 | tf_op jit(solution)/shard_map/ppermute | solution.py:644
  135.1 2.2 %collective-permute-start.67 = (f32[2,512]{1,0:T(2,128)S(1)}, f32[2,512]{1,0:T(2,128)S(1)}, u32[]{:S(2)}, u32[]{:S(2)}) collective-permute-start(f32[2,512]{1,0:T(2,128)S(1)} %add_add_fusion.7), channel_id=1, source_target_pairs={{0,25},{1,24},{2,27},{3,26},{4,29},{5,28},{6,31},{7,30},{8,17},{9,... | collective-permute-start | bytes 12296 | tf_op jit(solution)/shard_map/ppermute | solution.py:634
  137.6 3.4 %collective-permute-done.68 = f32[2,512]{1,0:T(2,128)S(1)} collective-permute-done((f32[2,512]{1,0:T(2,128)S(1)}, f32[2,512]{1,0:T(2,128)S(1)}, u32[]{:S(2)}, u32[]{:S(2)}) %collective-permute-start.68) | collective-permute-done | bytes 4128 | tf_op jit(solution)/shard_map/ppermute | solution.py:634
  142.6 1.2 back_reduce.1
  143.8 1.9 %collective-permute-start.71 = (bf16[304,512]{1,0:T(8,128)(2,1)S(1)}, bf16[304,512]{1,0:T(8,128)(2,1)S(1)}, u32[]{:S(2)}, u32[]{:S(2)}) collective-permute-start(bf16[304,512]{1,0:T(8,128)(2,1)S(1)} %get-tuple-element.329), channel_id=1, source_target_pairs={{0,2},{2,0},{1,3},{3,1},{4,6},{6,4},{5,7},{7,5},{8,10},{10,8},{9,1... | collective-permute-start | bytes 933896 | tf_op jit(solution)/shard_map/ppermute | solution.py:626
  145.9 1.3 collective-permute-start.74
  147.2 1.2 collective-permute-start.72
  148.4 1.8 block_sum.1
  150.3 1.7 back_input.2
  152.5 2.4 %collective-permute-done.72.refs_0_ = bf16[128,1024]{1,0:T(8,128)(2,1)S(1)} collective-permute-done((bf16[128,1024]{1,0:T(8,128)(2,1)S(1)}, bf16[128,1024]{1,0:T(8,128)(2,1)S(1)}, u32[]{:S(2)}, u32[]{:S(2)}) %collective-permute-start.72) | collective-permute-done | bytes 262176 | tf_op jit(solution)/shard_map/ppermute | solution.py:644
  155.8 2.4 %collective-permute-start.75 = (bf16[304,512]{1,0:T(8,128)(2,1)S(1)}, bf16[304,512]{1,0:T(8,128)(2,1)S(1)}, u32[]{:S(2)}, u32[]{:S(2)}) collective-permute-start(bf16[304,512]{1,0:T(8,128)(2,1)S(1)} %get-tuple-element.342), channel_id=1, source_target_pairs={{0,2},{2,0},{1,3},{3,1},{4,6},{6,4},{5,7},{7,5},{8,10},{10,8},{9,1... | collective-permute-start | bytes 933896 | tf_op jit(solution)/shard_map/ppermute | solution.py:626
  158.7 1.5 collective-permute-start.77
  160.7 2.8 %copy.36 = bf16[2,14,14,2048]{3,0,2,1:T(2,128)(2,1)} copy(bf16[2,14,14,2048]{3,2,1,0:T(8,128)(2,1)S(1)} %image.1) | data formatting | bytes 3211264 | tf_op jit(solution)/shard_map/image/pallas_call | solution.py:55
  163.5 2.3 %collective-permute-done.75.refs_2_ = bf16[304,512]{1,0:T(8,128)(2,1)S(1)} collective-permute-done((bf16[304,512]{1,0:T(8,128)(2,1)S(1)}, bf16[304,512]{1,0:T(8,128)(2,1)S(1)}, u32[]{:S(2)}, u32[]{:S(2)}) %collective-permute-start.75) | collective-permute-done | bytes 311328 | tf_op jit(solution)/shard_map/ppermute | solution.py:626
  165.8 1.5 collective-permute-done.78.refs_4_
  167.6 3.3 %collective-permute-start.79 = (bf16[304,512]{1,0:T(8,128)(2,1)S(1)}, bf16[304,512]{1,0:T(8,128)(2,1)S(1)}, u32[]{:S(2)}, u32[]{:S(2)}) collective-permute-start(bf16[304,512]{1,0:T(8,128)(2,1)S(1)} %get-tuple-element.353), channel_id=1, source_target_pairs={{0,24},{2,10},{4,28},{6,14},{8,0},{10,18},{12,4},{14,22},{16,8},{1... | collective-permute-start | bytes 933896 | tf_op jit(solution)/shard_map/ppermute | solution.py:644
  172.2 2.0 %back_input.3 = bf16[2,14,14,2048]{3,2,1,0:T(8,128)(2,1)S(1)} custom-call(bf16[896,512]{1,0:T(8,128)(2,1)S(1)} %get-tuple-element.354.flat, f32[896,1024]{1,0:T(8,128)S(1)} %get-tuple-element.280.grad, bf16[304,512]{1,0:T(8,128)(2,1)S(1)} %copy-done.2, bf16[304,512]{1,0:T(8,128)(2,1)S(1)} %collective-permute-done.refs_1_, ...), custom_call_target="tpu_custom_call" | custom-call | tf_op jit(solution)/shard_map/back_input/pallas_call | solution.py:55
  174.2 2.8 %copy.35 = bf16[2,14,14,2048]{3,0,2,1:T(2,128)(2,1)} copy(bf16[2,14,14,2048]{3,2,1,0:T(8,128)(2,1)S(1)} %back_input.3) | data formatting | bytes 3211264 | tf_op jit(solution)/shard_map/back_input/pallas_call | solution.py:55
  177.0 1.8 collective-permute-done.81.mine_x
  182.7 3.2 %collective-permute-done.83.mine_x = bf16[304,512]{1,0:T(8,128)(2,1)S(1)} collective-permute-done((bf16[304,512]{1,0:T(8,128)(2,1)S(1)}, bf16[304,512]{1,0:T(8,128)(2,1)S(1)}, u32[]{:S(2)}, u32[]{:S(2)}) %collective-permute-start.83) | collective-permute-done | bytes 311328 | tf_op jit(solution)/shard_map/ppermute | solution.py:626
  185.8 1.6 collective-permute-done.87.other_x
  (181 shorter events, 52.9 us)
Async XLA Ops:
  0.7 11.7 %collective-permute-start.2 = (bf16[2,14,14,2048]{3,0,2,1:T(2,128)(2,1)}, bf16[2,14,14,2048]{3,0,2,1:T(2,128)(2,1)}, u32[]{:S(2)}, u32[]{:S(2)}) collective-permute-start(bf16[2,14,14,2048]{3,0,2,1:T(2,128)(2,1)} %param.12), channel_id=1, source_target_pairs={{0,1},{1,0},{2,3},{3,2},{4,5},{5,4},{6,7},{7,6},{8,9},{9,8},{10,11... | collective-permute-start | bytes 4816904 | tf_op jit(solution)/shard_map/ppermute | solution.py:621
  3.1 11.7 %collective-permute-start.1 = (bf16[304,512]{1,0:T(8,128)(2,1)}, bf16[304,512]{1,0:T(8,128)(2,1)S(1)}, u32[]{:S(2)}, u32[]{:S(2)}) collective-permute-start(bf16[304,512]{1,0:T(8,128)(2,1)} %pack.1.refs_0_), channel_id=1, source_target_pairs={{0,4},{4,0},{8,12},{12,8},{16,20},{20,16},{24,28},{28,24},{1,5},{5... | collective-permute-start | bytes 933896 | tf_op jit(solution)/shard_map/ppermute | solution.py:648
  5.7 11.5 %collective-permute-start = (bf16[304,512]{1,0:T(8,128)(2,1)}, bf16[304,512]{1,0:T(8,128)(2,1)S(1)}, u32[]{:S(2)}, u32[]{:S(2)}) collective-permute-start(bf16[304,512]{1,0:T(8,128)(2,1)} %pack.1.refs_0_), channel_id=1, source_target_pairs={{0,8},{2,26},{4,12},{6,30},{8,16},{10,2},{12,20},{14,6},{16,24},{1... | collective-permute-start | bytes 933896 | tf_op jit(solution)/shard_map/ppermute | solution.py:644
  17.2 8.7 %collective-permute-start.5 = (bf16[304,512]{1,0:T(8,128)(2,1)S(1)}, bf16[304,512]{1,0:T(8,128)(2,1)S(1)}, u32[]{:S(2)}, u32[]{:S(2)}) collective-permute-start(bf16[304,512]{1,0:T(8,128)(2,1)S(1)} %collective-permute-done.refs_1_), channel_id=1, source_target_pairs={{0,4},{4,0},{8,12},{12,8},{16,20},{20,16},{24,28},{28,24},{1,5},{5... | collective-permute-start | bytes 933896 | tf_op jit(solution)/shard_map/ppermute | solution.py:648
  17.8 8.7 %collective-permute-start.4 = (bf16[304,512]{1,0:T(8,128)(2,1)S(1)}, bf16[304,512]{1,0:T(8,128)(2,1)S(1)}, u32[]{:S(2)}, u32[]{:S(2)}) collective-permute-start(bf16[304,512]{1,0:T(8,128)(2,1)S(1)} %collective-permute-done.refs_1_), channel_id=1, source_target_pairs={{0,2},{2,0},{1,3},{3,1},{4,6},{6,4},{5,7},{7,5},{8,10},{10,8},{9,1... | collective-permute-start | bytes 933896 | tf_op jit(solution)/shard_map/ppermute | solution.py:626
  18.9 12.1 %collective-permute-start.3 = (bf16[304,512]{1,0:T(8,128)(2,1)S(1)}, bf16[304,512]{1,0:T(8,128)(2,1)S(1)}, u32[]{:S(2)}, u32[]{:S(2)}) collective-permute-start(bf16[304,512]{1,0:T(8,128)(2,1)S(1)} %collective-permute-done.refs_1_), channel_id=1, source_target_pairs={{0,8},{2,26},{4,12},{6,30},{8,16},{10,2},{12,20},{14,6},{16,24},{1... | collective-permute-start | bytes 933896 | tf_op jit(solution)/shard_map/ppermute | solution.py:644
  18.9 16.0 %collective-permute-start.13 = (bf16[128,1024]{1,0:T(8,128)(2,1)S(1)}, bf16[128,1024]{1,0:T(8,128)(2,1)S(1)}, u32[]{:S(2)}, u32[]{:S(2)}) collective-permute-start(bf16[128,1024]{1,0:T(8,128)(2,1)S(1)} %constant_dynamic-slice_fusion.refs_0_), channel_id=1, source_target_pairs={{0,8},{2,26},{4,12},{6,30},{8,16},{10,2},{12,20},{14,6},{16,24},{1... | collective-permute-start | bytes 786440 | tf_op jit(solution)/shard_map/ppermute | solution.py:644
  31.0 8.8 %collective-permute-start.8 = (bf16[304,512]{1,0:T(8,128)(2,1)S(1)}, bf16[304,512]{1,0:T(8,128)(2,1)S(1)}, u32[]{:S(2)}, u32[]{:S(2)}) collective-permute-start(bf16[304,512]{1,0:T(8,128)(2,1)S(1)} %collective-permute-done.3.refs_3_), channel_id=1, source_target_pairs={{0,4},{4,0},{8,12},{12,8},{16,20},{20,16},{24,28},{28,24},{1,5},{5... | collective-permute-start | bytes 933896 | tf_op jit(solution)/shard_map/ppermute | solution.py:648
  32.5 7.2 %collective-permute-start.7 = (bf16[304,512]{1,0:T(8,128)(2,1)S(1)}, bf16[304,512]{1,0:T(8,128)(2,1)S(1)}, u32[]{:S(2)}, u32[]{:S(2)}) collective-permute-start(bf16[304,512]{1,0:T(8,128)(2,1)S(1)} %collective-permute-done.5.refs_5_), channel_id=1, source_target_pairs={{0,2},{2,0},{1,3},{3,1},{4,6},{6,4},{5,7},{7,5},{8,10},{10,8},{9,1... | collective-permute-start | bytes 933896 | tf_op jit(solution)/shard_map/ppermute | solution.py:626
  32.5 14.5 %collective-permute-start.15 = (bf16[128,1024]{1,0:T(8,128)(2,1)S(1)}, bf16[128,1024]{1,0:T(8,128)(2,1)S(1)}, u32[]{:S(2)}, u32[]{:S(2)}) collective-permute-start(bf16[128,1024]{1,0:T(8,128)(2,1)S(1)} %constant_dynamic-slice_fusion.refs_0_), channel_id=1, source_target_pairs={{0,4},{4,0},{8,12},{12,8},{16,20},{20,16},{24,28},{28,24},{1,5},{5... | collective-permute-start | bytes 786440 | tf_op jit(solution)/shard_map/ppermute | solution.py:648
  34.9 12.1 %collective-permute-start.14 = (bf16[128,1024]{1,0:T(8,128)(2,1)S(1)}, bf16[128,1024]{1,0:T(8,128)(2,1)S(1)}, u32[]{:S(2)}, u32[]{:S(2)}) collective-permute-start(bf16[128,1024]{1,0:T(8,128)(2,1)S(1)} %collective-permute-done.13.refs_1_), channel_id=1, source_target_pairs={{0,8},{2,26},{4,12},{6,30},{8,16},{10,2},{12,20},{14,6},{16,24},{1... | collective-permute-start | bytes 786440 | tf_op jit(solution)/shard_map/ppermute | solution.py:644
  41.1 4.0 %collective-permute-start.12 = (f32[3,512]{1,0:T(4,128)S(1)}, f32[3,512]{1,0:T(4,128)S(1)}, u32[]{:S(2)}, u32[]{:S(2)}) collective-permute-start(f32[3,512]{1,0:T(4,128)S(1)} %get-tuple-element.205), channel_id=1, source_target_pairs={{0,7},{1,6},{2,5},{3,4},{4,3},{5,2},{6,1},{7,0},{8,15},{9,14},{10,... | collective-permute-start | bytes 18440 | tf_op jit(solution)/shard_map/ppermute | solution.py:634
  41.2 4.9 %collective-permute-start.11 = (f32[3,512]{1,0:T(4,128)S(1)}, f32[3,512]{1,0:T(4,128)S(1)}, u32[]{:S(2)}, u32[]{:S(2)}) collective-permute-start(f32[3,512]{1,0:T(4,128)S(1)} %get-tuple-element.205), channel_id=1, source_target_pairs={{0,5},{1,4},{2,7},{3,6},{4,1},{5,0},{6,3},{7,2},{8,13},{9,12},{10,... | collective-permute-start | bytes 18440 | tf_op jit(solution)/shard_map/ppermute | solution.py:634
  43.9 3.1 %collective-permute-start.10 = (f32[3,512]{1,0:T(4,128)S(1)}, f32[3,512]{1,0:T(4,128)S(1)}, u32[]{:S(2)}, u32[]{:S(2)}) collective-permute-start(f32[3,512]{1,0:T(4,128)S(1)} %get-tuple-element.205), channel_id=1, source_target_pairs={{0,3},{1,2},{2,1},{3,0},{4,7},{5,6},{6,5},{7,4},{8,11},{9,10},{10,... | collective-permute-start | bytes 18440 | tf_op jit(solution)/shard_map/ppermute | solution.py:634
  47.1 8.4 %collective-permute-start.25 = (bf16[128,1024]{1,0:T(8,128)(2,1)S(1)}, bf16[128,1024]{1,0:T(8,128)(2,1)S(1)}, u32[]{:S(2)}, u32[]{:S(2)}) collective-permute-start(bf16[128,1024]{1,0:T(8,128)(2,1)S(1)} %collective-permute-done.13.refs_1_), channel_id=1, source_target_pairs={{0,4},{4,0},{8,12},{12,8},{16,20},{20,16},{24,28},{28,24},{1,5},{5... | collective-permute-start | bytes 786440 | tf_op jit(solution)/shard_map/ppermute | solution.py:648
  48.6 4.0 %collective-permute-start.19 = (f32[3,512]{1,0:T(4,128)S(1)}, f32[3,512]{1,0:T(4,128)S(1)}, u32[]{:S(2)}, u32[]{:S(2)}) collective-permute-start(f32[3,512]{1,0:T(4,128)S(1)} %add_add_fusion.5), channel_id=1, source_target_pairs={{0,17},{1,16},{2,19},{3,18},{4,21},{5,20},{6,23},{7,22},{8,25},{9,... | collective-permute-start | bytes 18440 | tf_op jit(solution)/shard_map/ppermute | solution.py:634
  48.6 11.3 %collective-permute-start.20 = (bf16[128,1024]{1,0:T(8,128)(2,1)S(1)}, bf16[128,1024]{1,0:T(8,128)(2,1)S(1)}, u32[]{:S(2)}, u32[]{:S(2)}) collective-permute-start(bf16[128,1024]{1,0:T(8,128)(2,1)S(1)} %collective-permute-done.13.refs_1_), channel_id=1, source_target_pairs={{0,2},{2,0},{1,3},{3,1},{4,6},{6,4},{5,7},{7,5},{8,10},{10,8},{9,1... | collective-permute-start | bytes 786440 | tf_op jit(solution)/shard_map/ppermute | solution.py:626
  49.5 5.0 %collective-permute-start.18 = (f32[3,512]{1,0:T(4,128)S(1)}, f32[3,512]{1,0:T(4,128)S(1)}, u32[]{:S(2)}, u32[]{:S(2)}) collective-permute-start(f32[3,512]{1,0:T(4,128)S(1)} %add_add_fusion.5), channel_id=1, source_target_pairs={{0,25},{1,24},{2,27},{3,26},{4,29},{5,28},{6,31},{7,30},{8,17},{9,... | collective-permute-start | bytes 18440 | tf_op jit(solution)/shard_map/ppermute | solution.py:634
  50.6 3.9 %collective-permute-start.17 = (f32[3,512]{1,0:T(4,128)S(1)}, f32[3,512]{1,0:T(4,128)S(1)}, u32[]{:S(2)}, u32[]{:S(2)}) collective-permute-start(f32[3,512]{1,0:T(4,128)S(1)} %add_add_fusion.5), channel_id=1, source_target_pairs={{0,9},{1,8},{2,11},{3,10},{4,13},{5,12},{6,15},{7,14},{8,1},{9,0},... | collective-permute-start | bytes 18440 | tf_op jit(solution)/shard_map/ppermute | solution.py:634
  54.5 11.5 %collective-permute-start.27 = (bf16[128,1024]{1,0:T(8,128)(2,1)S(1)}, bf16[128,1024]{1,0:T(8,128)(2,1)S(1)}, u32[]{:S(2)}, u32[]{:S(2)}) collective-permute-start(bf16[128,1024]{1,0:T(8,128)(2,1)S(1)} %collective-permute-done.14.refs_3_), channel_id=1, source_target_pairs={{0,4},{4,0},{8,12},{12,8},{16,20},{20,16},{24,28},{28,24},{1,5},{5... | collective-permute-start | bytes 786440 | tf_op jit(solution)/shard_map/ppermute | solution.py:648
  55.5 10.5 %collective-permute-start.26 = (bf16[128,1024]{1,0:T(8,128)(2,1)S(1)}, bf16[128,1024]{1,0:T(8,128)(2,1)S(1)}, u32[]{:S(2)}, u32[]{:S(2)}) collective-permute-start(bf16[128,1024]{1,0:T(8,128)(2,1)S(1)} %collective-permute-done.25.refs_5_), channel_id=1, source_target_pairs={{0,2},{2,0},{1,3},{3,1},{4,6},{6,4},{5,7},{7,5},{8,10},{10,8},{9,1... | collective-permute-start | bytes 786440 | tf_op jit(solution)/shard_map/ppermute | solution.py:626
  59.9 4.0 %collective-permute-start.24 = (f32[2,512]{1,0:T(2,128)S(1)}, f32[2,512]{1,0:T(2,128)S(1)}, u32[]{:S(2)}, u32[]{:S(2)}) collective-permute-start(f32[2,512]{1,0:T(2,128)S(1)} %get-tuple-element.228), channel_id=1, source_target_pairs={{0,17},{1,16},{2,19},{3,18},{4,21},{5,20},{6,23},{7,22},{8,25},{9,... | collective-permute-start | bytes 12296 | tf_op jit(solution)/shard_map/ppermute | solution.py:634
  60.4 4.8 %collective-permute-start.23 = (f32[2,512]{1,0:T(2,128)S(1)}, f32[2,512]{1,0:T(2,128)S(1)}, u32[]{:S(2)}, u32[]{:S(2)}) collective-permute-start(f32[2,512]{1,0:T(2,128)S(1)} %get-tuple-element.228), channel_id=1, source_target_pairs={{0,25},{1,24},{2,27},{3,26},{4,29},{5,28},{6,31},{7,30},{8,17},{9,... | collective-permute-start | bytes 12296 | tf_op jit(solution)/shard_map/ppermute | solution.py:634
  66.0 4.0 %collective-permute-start.31 = (f32[2,512]{1,0:T(2,128)S(1)}, f32[2,512]{1,0:T(2,128)S(1)}, u32[]{:S(2)}, u32[]{:S(2)}) collective-permute-start(f32[2,512]{1,0:T(2,128)S(1)} %add_add_fusion.11), channel_id=1, source_target_pairs={{0,7},{1,6},{2,5},{3,4},{4,3},{5,2},{6,1},{7,0},{8,15},{9,14},{10,... | collective-permute-start | bytes 12296 | tf_op jit(solution)/shard_map/ppermute | solution.py:634
  73.1 8.7 %collective-permute-start.37 = (bf16[448,1024]{1,0:T(8,128)(2,1)S(1)}, bf16[448,1024]{1,0:T(8,128)(2,1)S(1)}, u32[]{:S(2)}, u32[]{:S(2)}) collective-permute-start(bf16[448,1024]{1,0:T(8,128)(2,1)S(1)} %far_half.1), channel_id=1, source_target_pairs={{0,1},{1,0},{2,3},{3,2},{4,5},{5,4},{6,7},{7,6},{8,9},{9,8},{10,11... | collective-permute-start | bytes 2752520 | tf_op jit(solution)/shard_map/ppermute | solution.py:621
  76.3 4.0 %collective-permute-start.36 = (f32[2,1024]{1,0:T(2,128)S(1)}, f32[2,1024]{1,0:T(2,128)S(1)}, u32[]{:S(2)}, u32[]{:S(2)}) collective-permute-start(f32[2,1024]{1,0:T(2,128)S(1)} %get-tuple-element.253), channel_id=1, source_target_pairs={{0,7},{1,6},{2,5},{3,4},{4,3},{5,2},{6,1},{7,0},{8,15},{9,14},{10,... | collective-permute-start | bytes 24584 | tf_op jit(solution)/shard_map/ppermute | solution.py:634
  78.2 3.1 %collective-permute-start.35 = (f32[2,1024]{1,0:T(2,128)S(1)}, f32[2,1024]{1,0:T(2,128)S(1)}, u32[]{:S(2)}, u32[]{:S(2)}) collective-permute-start(f32[2,1024]{1,0:T(2,128)S(1)} %get-tuple-element.253), channel_id=1, source_target_pairs={{0,5},{1,4},{2,7},{3,6},{4,1},{5,0},{6,3},{7,2},{8,13},{9,12},{10,... | collective-permute-start | bytes 24584 | tf_op jit(solution)/shard_map/ppermute | solution.py:634
  81.8 4.1 %collective-permute-start.41 = (f32[2,1024]{1,0:T(2,128)S(1)}, f32[2,1024]{1,0:T(2,128)S(1)}, u32[]{:S(2)}, u32[]{:S(2)}) collective-permute-start(f32[2,1024]{1,0:T(2,128)S(1)} %add_add_fusion.3), channel_id=1, source_target_pairs={{0,17},{1,16},{2,19},{3,18},{4,21},{5,20},{6,23},{7,22},{8,25},{9,... | collective-permute-start | bytes 24584 | tf_op jit(solution)/shard_map/ppermute | solution.py:634
  82.4 4.9 %collective-permute-start.40 = (f32[2,1024]{1,0:T(2,128)S(1)}, f32[2,1024]{1,0:T(2,128)S(1)}, u32[]{:S(2)}, u32[]{:S(2)}) collective-permute-start(f32[2,1024]{1,0:T(2,128)S(1)} %add_add_fusion.3), channel_id=1, source_target_pairs={{0,25},{1,24},{2,27},{3,26},{4,29},{5,28},{6,31},{7,30},{8,17},{9,... | collective-permute-start | bytes 24584 | tf_op jit(solution)/shard_map/ppermute | solution.py:634
  84.2 3.1 %collective-permute-start.39 = (f32[2,1024]{1,0:T(2,128)S(1)}, f32[2,1024]{1,0:T(2,128)S(1)}, u32[]{:S(2)}, u32[]{:S(2)}) collective-permute-start(f32[2,1024]{1,0:T(2,128)S(1)} %add_add_fusion.3), channel_id=1, source_target_pairs={{0,9},{1,8},{2,11},{3,10},{4,13},{5,12},{6,15},{7,14},{8,1},{9,0},... | collective-permute-start | bytes 24584 | tf_op jit(solution)/shard_map/ppermute | solution.py:634
  90.8 5.1 %collective-permute-start.45 = (f32[2,1024]{1,0:T(2,128)S(1)}, f32[2,1024]{1,0:T(2,128)S(1)}, u32[]{:S(2)}, u32[]{:S(2)}) collective-permute-start(f32[2,1024]{1,0:T(2,128)S(1)} %get-tuple-element.268), channel_id=1, source_target_pairs={{0,7},{1,6},{2,5},{3,4},{4,3},{5,2},{6,1},{7,0},{8,15},{9,14},{10,... | collective-permute-start | bytes 24584 | tf_op jit(solution)/shard_map/ppermute | solution.py:634
  92.4 3.5 %collective-permute-start.44 = (f32[2,1024]{1,0:T(2,128)S(1)}, f32[2,1024]{1,0:T(2,128)S(1)}, u32[]{:S(2)}, u32[]{:S(2)}) collective-permute-start(f32[2,1024]{1,0:T(2,128)S(1)} %get-tuple-element.268), channel_id=1, source_target_pairs={{0,5},{1,4},{2,7},{3,6},{4,1},{5,0},{6,3},{7,2},{8,13},{9,12},{10,... | collective-permute-start | bytes 24584 | tf_op jit(solution)/shard_map/ppermute | solution.py:634
  96.2 4.0 %collective-permute-start.49 = (f32[2,1024]{1,0:T(2,128)S(1)}, f32[2,1024]{1,0:T(2,128)S(1)}, u32[]{:S(2)}, u32[]{:S(2)}) collective-permute-start(f32[2,1024]{1,0:T(2,128)S(1)} %add_add_fusion.1), channel_id=1, source_target_pairs={{0,17},{1,16},{2,19},{3,18},{4,21},{5,20},{6,23},{7,22},{8,25},{9,... | collective-permute-start | bytes 24584 | tf_op jit(solution)/shard_map/ppermute | solution.py:634
  97.2 4.9 %collective-permute-start.48 = (f32[2,1024]{1,0:T(2,128)S(1)}, f32[2,1024]{1,0:T(2,128)S(1)}, u32[]{:S(2)}, u32[]{:S(2)}) collective-permute-start(f32[2,1024]{1,0:T(2,128)S(1)} %add_add_fusion.1), channel_id=1, source_target_pairs={{0,25},{1,24},{2,27},{3,26},{4,29},{5,28},{6,31},{7,30},{8,17},{9,... | collective-permute-start | bytes 24584 | tf_op jit(solution)/shard_map/ppermute | solution.py:634
  99.0 3.2 %collective-permute-start.47 = (f32[2,1024]{1,0:T(2,128)S(1)}, f32[2,1024]{1,0:T(2,128)S(1)}, u32[]{:S(2)}, u32[]{:S(2)}) collective-permute-start(f32[2,1024]{1,0:T(2,128)S(1)} %add_add_fusion.1), channel_id=1, source_target_pairs={{0,9},{1,8},{2,11},{3,10},{4,13},{5,12},{6,15},{7,14},{8,1},{9,0},... | collective-permute-start | bytes 24584 | tf_op jit(solution)/shard_map/ppermute | solution.py:634
  108.3 5.9 %collective-permute-start.54 = (f32[2,512]{1,0:T(2,128)S(1)}, f32[2,512]{1,0:T(2,128)S(1)}, u32[]{:S(2)}, u32[]{:S(2)}) collective-permute-start(f32[2,512]{1,0:T(2,128)S(1)} %get-tuple-element.283), channel_id=1, source_target_pairs={{0,7},{1,6},{2,5},{3,4},{4,3},{5,2},{6,1},{7,0},{8,15},{9,14},{10,... | collective-permute-start | bytes 12296 | tf_op jit(solution)/shard_map/ppermute | solution.py:634
  110.2 4.0 %collective-permute-start.53 = (f32[2,512]{1,0:T(2,128)S(1)}, f32[2,512]{1,0:T(2,128)S(1)}, u32[]{:S(2)}, u32[]{:S(2)}) collective-permute-start(f32[2,512]{1,0:T(2,128)S(1)} %get-tuple-element.283), channel_id=1, source_target_pairs={{0,5},{1,4},{2,7},{3,6},{4,1},{5,0},{6,3},{7,2},{8,13},{9,12},{10,... | collective-permute-start | bytes 12296 | tf_op jit(solution)/shard_map/ppermute | solution.py:634
  110.7 3.5 %collective-permute-start.52 = (f32[2,512]{1,0:T(2,128)S(1)}, f32[2,512]{1,0:T(2,128)S(1)}, u32[]{:S(2)}, u32[]{:S(2)}) collective-permute-start(f32[2,512]{1,0:T(2,128)S(1)} %get-tuple-element.283), channel_id=1, source_target_pairs={{0,3},{1,2},{2,1},{3,0},{4,7},{5,6},{6,5},{7,4},{8,11},{9,10},{10,... | collective-permute-start | bytes 12296 | tf_op jit(solution)/shard_map/ppermute | solution.py:634
  114.2 18.2 %collective-permute-start.63 = (bf16[256,1024]{1,0:T(8,128)(2,1)S(1)}, bf16[256,1024]{1,0:T(8,128)(2,1)S(1)}, u32[]{:S(2)}, u32[]{:S(2)}) collective-permute-start(bf16[256,1024]{1,0:T(8,128)(2,1)S(1)} %get-tuple-element.309), channel_id=1, source_target_pairs={{0,2},{2,0},{1,3},{3,1},{4,6},{6,4},{5,7},{7,5},{8,10},{10,8},{9,1... | collective-permute-start | bytes 1572872 | tf_op jit(solution)/shard_map/ppermute | solution.py:626
  115.4 17.1 %collective-permute-start.64 = (bf16[256,1024]{1,0:T(8,128)(2,1)S(1)}, bf16[256,1024]{1,0:T(8,128)(2,1)S(1)}, u32[]{:S(2)}, u32[]{:S(2)}) collective-permute-start(bf16[256,1024]{1,0:T(8,128)(2,1)S(1)} %get-tuple-element.310), channel_id=1, source_target_pairs={{0,4},{4,0},{8,12},{12,8},{16,20},{20,16},{24,28},{28,24},{1,5},{5... | collective-permute-start | bytes 1572872 | tf_op jit(solution)/shard_map/ppermute | solution.py:648
  116.9 3.9 %collective-permute-start.58 = (f32[2,512]{1,0:T(2,128)S(1)}, f32[2,512]{1,0:T(2,128)S(1)}, u32[]{:S(2)}, u32[]{:S(2)}) collective-permute-start(f32[2,512]{1,0:T(2,128)S(1)} %add_add_fusion.9), channel_id=1, source_target_pairs={{0,17},{1,16},{2,19},{3,18},{4,21},{5,20},{6,23},{7,22},{8,25},{9,... | collective-permute-start | bytes 12296 | tf_op jit(solution)/shard_map/ppermute | solution.py:634
  116.9 4.8 %collective-permute-start.57 = (f32[2,512]{1,0:T(2,128)S(1)}, f32[2,512]{1,0:T(2,128)S(1)}, u32[]{:S(2)}, u32[]{:S(2)}) collective-permute-start(f32[2,512]{1,0:T(2,128)S(1)} %add_add_fusion.9), channel_id=1, source_target_pairs={{0,25},{1,24},{2,27},{3,26},{4,29},{5,28},{6,31},{7,30},{8,17},{9,... | collective-permute-start | bytes 12296 | tf_op jit(solution)/shard_map/ppermute | solution.py:634
  126.3 4.0 %collective-permute-start.62 = (f32[2,512]{1,0:T(2,128)S(1)}, f32[2,512]{1,0:T(2,128)S(1)}, u32[]{:S(2)}, u32[]{:S(2)}) collective-permute-start(f32[2,512]{1,0:T(2,128)S(1)} %get-tuple-element.299), channel_id=1, source_target_pairs={{0,7},{1,6},{2,5},{3,4},{4,3},{5,2},{6,1},{7,0},{8,15},{9,14},{10,... | collective-permute-start | bytes 12296 | tf_op jit(solution)/shard_map/ppermute | solution.py:634
  127.4 5.0 %collective-permute-start.61 = (f32[2,512]{1,0:T(2,128)S(1)}, f32[2,512]{1,0:T(2,128)S(1)}, u32[]{:S(2)}, u32[]{:S(2)}) collective-permute-start(f32[2,512]{1,0:T(2,128)S(1)} %get-tuple-element.299), channel_id=1, source_target_pairs={{0,5},{1,4},{2,7},{3,6},{4,1},{5,0},{6,3},{7,2},{8,13},{9,12},{10,... | collective-permute-start | bytes 12296 | tf_op jit(solution)/shard_map/ppermute | solution.py:634
  128.4 4.0 %collective-permute-start.60 = (f32[2,512]{1,0:T(2,128)S(1)}, f32[2,512]{1,0:T(2,128)S(1)}, u32[]{:S(2)}, u32[]{:S(2)}) collective-permute-start(f32[2,512]{1,0:T(2,128)S(1)} %get-tuple-element.299), channel_id=1, source_target_pairs={{0,3},{1,2},{2,1},{3,0},{4,7},{5,6},{6,5},{7,4},{8,11},{9,10},{10,... | collective-permute-start | bytes 12296 | tf_op jit(solution)/shard_map/ppermute | solution.py:634
  132.6 9.9 %collective-permute-start.69 = (bf16[128,1024]{1,0:T(8,128)(2,1)S(1)}, bf16[128,1024]{1,0:T(8,128)(2,1)S(1)}, u32[]{:S(2)}, u32[]{:S(2)}) collective-permute-start(bf16[128,1024]{1,0:T(8,128)(2,1)S(1)} %get-tuple-element.321), channel_id=1, source_target_pairs={{0,4},{4,0},{8,12},{12,8},{16,20},{20,16},{24,28},{28,24},{1,5},{5... | collective-permute-start | bytes 786440 | tf_op jit(solution)/shard_map/ppermute | solution.py:648
  133.2 9.4 %collective-permute-start.70 = (bf16[128,1024]{1,0:T(8,128)(2,1)S(1)}, bf16[128,1024]{1,0:T(8,128)(2,1)S(1)}, u32[]{:S(2)}, u32[]{:S(2)}) collective-permute-start(bf16[128,1024]{1,0:T(8,128)(2,1)S(1)} %get-tuple-element.322), channel_id=1, source_target_pairs={{0,24},{2,10},{4,28},{6,14},{8,0},{10,18},{12,4},{14,22},{16,8},{1... | collective-permute-start | bytes 786440 | tf_op jit(solution)/shard_map/ppermute | solution.py:644
  135.1 5.9 %collective-permute-start.68 = (f32[2,512]{1,0:T(2,128)S(1)}, f32[2,512]{1,0:T(2,128)S(1)}, u32[]{:S(2)}, u32[]{:S(2)}) collective-permute-start(f32[2,512]{1,0:T(2,128)S(1)} %add_add_fusion.7), channel_id=1, source_target_pairs={{0,17},{1,16},{2,19},{3,18},{4,21},{5,20},{6,23},{7,22},{8,25},{9,... | collective-permute-start | bytes 12296 | tf_op jit(solution)/shard_map/ppermute | solution.py:634
  135.1 6.6 %collective-permute-start.67 = (f32[2,512]{1,0:T(2,128)S(1)}, f32[2,512]{1,0:T(2,128)S(1)}, u32[]{:S(2)}, u32[]{:S(2)}) collective-permute-start(f32[2,512]{1,0:T(2,128)S(1)} %add_add_fusion.7), channel_id=1, source_target_pairs={{0,25},{1,24},{2,27},{3,26},{4,29},{5,28},{6,31},{7,30},{8,17},{9,... | collective-permute-start | bytes 12296 | tf_op jit(solution)/shard_map/ppermute | solution.py:634
  137.3 4.4 %collective-permute-start.66 = (f32[2,512]{1,0:T(2,128)S(1)}, f32[2,512]{1,0:T(2,128)S(1)}, u32[]{:S(2)}, u32[]{:S(2)}) collective-permute-start(f32[2,512]{1,0:T(2,128)S(1)} %add_add_fusion.7), channel_id=1, source_target_pairs={{0,9},{1,8},{2,11},{3,10},{4,13},{5,12},{6,15},{7,14},{8,1},{9,0},... | collective-permute-start | bytes 12296 | tf_op jit(solution)/shard_map/ppermute | solution.py:634
  143.8 11.1 %collective-permute-start.71 = (bf16[304,512]{1,0:T(8,128)(2,1)S(1)}, bf16[304,512]{1,0:T(8,128)(2,1)S(1)}, u32[]{:S(2)}, u32[]{:S(2)}) collective-permute-start(bf16[304,512]{1,0:T(8,128)(2,1)S(1)} %get-tuple-element.329), channel_id=1, source_target_pairs={{0,2},{2,0},{1,3},{3,1},{4,6},{6,4},{5,7},{7,5},{8,10},{10,8},{9,1... | collective-permute-start | bytes 933896 | tf_op jit(solution)/shard_map/ppermute | solution.py:626
  145.9 9.2 %collective-permute-start.74 = (bf16[304,512]{1,0:T(8,128)(2,1)S(1)}, bf16[304,512]{1,0:T(8,128)(2,1)S(1)}, u32[]{:S(2)}, u32[]{:S(2)}) collective-permute-start(bf16[304,512]{1,0:T(8,128)(2,1)S(1)} %get-tuple-element.341), channel_id=1, source_target_pairs={{0,4},{4,0},{8,12},{12,8},{16,20},{20,16},{24,28},{28,24},{1,5},{5... | collective-permute-start | bytes 933896 | tf_op jit(solution)/shard_map/ppermute | solution.py:648
  147.2 7.8 %collective-permute-start.72 = (bf16[128,1024]{1,0:T(8,128)(2,1)S(1)}, bf16[128,1024]{1,0:T(8,128)(2,1)S(1)}, u32[]{:S(2)}, u32[]{:S(2)}) collective-permute-start(bf16[128,1024]{1,0:T(8,128)(2,1)S(1)} %expand_sum.6), channel_id=1, source_target_pairs={{0,24},{2,10},{4,28},{6,14},{8,0},{10,18},{12,4},{14,22},{16,8},{1... | collective-permute-start | bytes 786440 | tf_op jit(solution)/shard_map/ppermute | solution.py:644
  148.3 3.6 %collective-permute-start.73 = (f32[2,2048]{1,0:T(2,128)S(1)}, f32[2,2048]{1,0:T(2,128)S(1)}, u32[]{:S(2)}, u32[]{:S(2)}) collective-permute-start(f32[2,2048]{1,0:T(2,128)S(1)} %pad_maximum_fusion.near), channel_id=1, source_target_pairs={{0,1},{1,0},{2,3},{3,2},{4,5},{5,4},{6,7},{7,6},{8,9},{9,8},{10,11... | collective-permute-start | bytes 49160 | tf_op jit(solution)/shard_map/ppermute | solution.py:621
  155.2 17.0 %collective-permute-start.80 = (bf16[448,2048]{1,0:T(8,128)(2,1)S(1)}, bf16[448,2048]{1,0:T(8,128)(2,1)S(1)}, u32[]{:S(2)}, u32[]{:S(2)}) collective-permute-start(bf16[448,2048]{1,0:T(8,128)(2,1)S(1)} %back_input.2), channel_id=1, source_target_pairs={{0,1},{1,0},{2,3},{3,2},{4,5},{5,4},{6,7},{7,6},{8,9},{9,8},{10,11... | collective-permute-start | bytes 5505032 | tf_op jit(solution)/shard_map/ppermute | solution.py:621
  155.3 5.1 %collective-permute-start.76 = (bf16[448,1024]{1,0:T(8,128)(2,1)S(1)}, bf16[448,1024]{1,0:T(8,128)(2,1)S(1)}, u32[]{:S(2)}, u32[]{:S(2)}) collective-permute-start(bf16[448,1024]{1,0:T(8,128)(2,1)S(1)} %get-tuple-element.345), channel_id=1, source_target_pairs={{0,1},{1,0},{2,3},{3,2},{4,5},{5,4},{6,7},{7,6},{8,9},{9,8},{10,11... | collective-permute-start | bytes 2752520 | tf_op jit(solution)/shard_map/ppermute | solution.py:621
  155.8 10.0 %collective-permute-start.75 = (bf16[304,512]{1,0:T(8,128)(2,1)S(1)}, bf16[304,512]{1,0:T(8,128)(2,1)S(1)}, u32[]{:S(2)}, u32[]{:S(2)}) collective-permute-start(bf16[304,512]{1,0:T(8,128)(2,1)S(1)} %get-tuple-element.342), channel_id=1, source_target_pairs={{0,2},{2,0},{1,3},{3,1},{4,6},{6,4},{5,7},{7,5},{8,10},{10,8},{9,1... | collective-permute-start | bytes 933896 | tf_op jit(solution)/shard_map/ppermute | solution.py:626
  158.2 9.1 %collective-permute-start.78 = (bf16[304,512]{1,0:T(8,128)(2,1)S(1)}, bf16[304,512]{1,0:T(8,128)(2,1)S(1)}, u32[]{:S(2)}, u32[]{:S(2)}) collective-permute-start(bf16[304,512]{1,0:T(8,128)(2,1)S(1)} %get-tuple-element.352), channel_id=1, source_target_pairs={{0,4},{4,0},{8,12},{12,8},{16,20},{20,16},{24,28},{28,24},{1,5},{5... | collective-permute-start | bytes 933896 | tf_op jit(solution)/shard_map/ppermute | solution.py:648
  158.7 8.8 %collective-permute-start.77 = (bf16[304,512]{1,0:T(8,128)(2,1)S(1)}, bf16[304,512]{1,0:T(8,128)(2,1)S(1)}, u32[]{:S(2)}, u32[]{:S(2)}) collective-permute-start(bf16[304,512]{1,0:T(8,128)(2,1)S(1)} %get-tuple-element.346), channel_id=1, source_target_pairs={{0,24},{2,10},{4,28},{6,14},{8,0},{10,18},{12,4},{14,22},{16,8},{1... | collective-permute-start | bytes 933896 | tf_op jit(solution)/shard_map/ppermute | solution.py:644
  167.6 11.1 %collective-permute-start.79 = (bf16[304,512]{1,0:T(8,128)(2,1)S(1)}, bf16[304,512]{1,0:T(8,128)(2,1)S(1)}, u32[]{:S(2)}, u32[]{:S(2)}) collective-permute-start(bf16[304,512]{1,0:T(8,128)(2,1)S(1)} %get-tuple-element.353), channel_id=1, source_target_pairs={{0,24},{2,10},{4,28},{6,14},{8,0},{10,18},{12,4},{14,22},{16,8},{1... | collective-permute-start | bytes 933896 | tf_op jit(solution)/shard_map/ppermute | solution.py:644
  170.9 7.8 %collective-permute-start.82 = (bf16[304,512]{1,0:T(8,128)(2,1)S(1)}, bf16[304,512]{1,0:T(8,128)(2,1)S(1)}, u32[]{:S(2)}, u32[]{:S(2)}) collective-permute-start(bf16[304,512]{1,0:T(8,128)(2,1)S(1)} %get-tuple-element.361), channel_id=1, source_target_pairs={{0,4},{4,0},{8,12},{12,8},{16,20},{20,16},{24,28},{28,24},{1,5},{5... | collective-permute-start | bytes 933896 | tf_op jit(solution)/shard_map/ppermute | solution.py:648
  172.1 6.6 %collective-permute-start.81 = (bf16[128,1024]{1,0:T(8,128)(2,1)S(1)}, bf16[128,1024]{1,0:T(8,128)(2,1)S(1)}, u32[]{:S(2)}, u32[]{:S(2)}) collective-permute-start(bf16[128,1024]{1,0:T(8,128)(2,1)S(1)} %expand_sum.7.mine), channel_id=1, source_target_pairs={{0,2},{2,0},{1,3},{3,1},{4,6},{6,4},{5,7},{7,5},{8,10},{10,8},{9,1... | collective-permute-start | bytes 786440 | tf_op jit(solution)/shard_map/ppermute | solution.py:626
  178.9 7.0 %collective-permute-start.83 = (bf16[304,512]{1,0:T(8,128)(2,1)S(1)}, bf16[304,512]{1,0:T(8,128)(2,1)S(1)}, u32[]{:S(2)}, u32[]{:S(2)}) collective-permute-start(bf16[304,512]{1,0:T(8,128)(2,1)S(1)} %arrived.5.mine), channel_id=1, source_target_pairs={{0,2},{2,0},{1,3},{3,1},{4,6},{6,4},{5,7},{7,5},{8,10},{10,8},{9,1... | collective-permute-start | bytes 933896 | tf_op jit(solution)/shard_map/ppermute | solution.py:626
  180.2 5.6 %collective-permute-start.86 = (bf16[304,512]{1,0:T(8,128)(2,1)S(1)}, bf16[304,512]{1,0:T(8,128)(2,1)S(1)}, u32[]{:S(2)}, u32[]{:S(2)}) collective-permute-start(bf16[304,512]{1,0:T(8,128)(2,1)S(1)} %arrived.5.mine), channel_id=1, source_target_pairs={{0,1},{1,0},{2,3},{3,2},{4,5},{5,4},{6,7},{7,6},{8,9},{9,8},{10,11... | collective-permute-start | bytes 933896 | tf_op jit(solution)/shard_map/ppermute | solution.py:621
  (29 other events, 116.0 us)
